TPU v7x, 32 devices: a whole 2x2x4 slice. The times are simulated.
32 devices in a mesh: groups: 2 (over x), slab: 4 (over y, core), rep: 4 (over z).
Axes of the slice: x: 2, y: 2, z: 4, core: 2. Of those that a mesh axis runs over, the one named last changes fastest.
Arguments:
- fields: float32 [8, 5, 8, 4, 128], P(('groups', 'rep'), None, 'slab'), parts along dimension 0, may hold values from -6 to 6
- drop_mass: float32 [8, 4096], P(('groups', 'rep'), 'slab'), parts along dimension 0, may hold values from 0.2 to 2
- drop_vel: float32 [8, 3, 4096], P(('groups', 'rep'), None, 'slab'), parts along dimension 0, may hold values from -6 to 6
- drop_cell: int32 [8, 4096], P(('groups', 'rep'), 'slab'), parts along dimension 0, may hold values from 0 to 1023
- cross_list: int32 [8, 1024], P(('groups', 'rep'), 'slab'), parts along dimension 0, may hold values from 0 to 1023, as said below
- cross_count: int32 [8, 8], P(('groups', 'rep'), 'slab'), parts along dimension 0, may hold values from 0 to 128, as said below
- w_in: bfloat16 [27, 9, 256], replicated, may hold values from -0.375 to 0.375
- w_mid: bfloat16 [27, 256, 256], replicated, may hold values from -0.078125 to 0.078125
- w_out: bfloat16 [256, 5], replicated, may hold values from -0.375 to 0.375
- cotangent: float32 [8, 5, 8, 4, 128], P(('groups', 'rep'), None, 'slab'), parts along dimension 0, may hold values from -6 to 6
Outputs:
- new_fields: float32 [8, 5, 8, 4, 128], P(('groups', 'rep'), None, 'slab'), parts along dimension 0
- grad_first: float32 [54, 9, 256], P('groups'), parts along dimension 0
- grad_middle: float32 [54, 256, 256], P('groups'), parts along dimension 0
- grad_last: float32 [512, 5], P('groups'), parts along dimension 0
There are 2 independent parts, one for each index of `groups`. A program takes and returns all parts, laid end to end along the dimension named above; an argument that names none is the same for every part. Nothing has to cross between parts.
Inputs may be any that keep to these rules, and one draw needn't show every extreme that they name: `cross_list`: within the 256 entries of one slab (up list, then down list) all entries are distinct local droplet numbers. `cross_count`: entries 2j and 2j+1 count the valid leading entries of slab j's up and down lists. In every sample some slab's up count and some slab's down count are 128, and one slab receives 128 droplets from each side. `drop_cell`: A cell is numbered (x * 4 + y) * 128 + z in the local coordinates of the slab the droplet belongs to after the step.
All inputs are finite; a program needn't handle non-finite values.
Results may differ from a plain program's by a relative error of at most 0.0063.
Values may be sent and summed in bfloat16 or wider, within the bound.
No kernel may reach another device: no remote copies, remote signals or barrier semaphores. Data moves between devices by JAX's collectives and lax.ppermute only.
A program may use at most 128 MiB of HBM per device.

v0:
```python
import functools
import math

import jax
import jax.numpy as jnp
from jax import lax
from jax.experimental import pallas as pl
from jax.experimental.pallas import tpu as pltpu
from jax.sharding import PartitionSpec as P

dt_step = 0.2
viscosity = 0.05
drag_rate = 0.5
clip_rms = 0.5

F32 = jnp.float32
BF16 = jnp.bfloat16
VMEM_BYTES = 58 * 2**20
offsets = [(x, y, z) for x in (-1, 0, 1) for y in (-1, 0, 1) for z in (-1, 0, 1)]


def dot(a, b):
    return lax.dot_general(a, b, (((1,), (0,)), ((), ())), preferred_element_type=F32)


def dot_nt(a, b):
    return lax.dot_general(a, b, (((1,), (1,)), ((), ())), preferred_element_type=F32)


def logistic(p):
    return 0.5 * jnp.tanh(0.5 * p) + 0.5


def roll_z(v, by, nz):
    return jnp.concatenate(
        [pltpu.roll(v[:, k : k + nz], by % nz, 1) for k in range(0, v.shape[1], nz)], 1
    )


def ahead_y(v, by, nz):
    if by == 0:
        return v
    cut = (by * nz) % v.shape[1]
    return jnp.concatenate([v[:, cut:], v[:, :cut]], 1)


def flat_cells(ref):
    planes, rows = ref.shape[2], ref.shape[3]
    return jnp.concatenate([ref[0, :, x, y, :] for x in range(planes) for y in range(rows)], 1)


def deposit_kernel(mass, vel, cell, listed, counts, stay, up, down):
    drops = mass.shape[1]
    slots = listed.shape[1]
    half = slots // 2
    k = lax.broadcasted_iota(jnp.int32, (1, slots), 1)
    valid = k < jnp.where(k < half, counts[0, 0], half + counts[0, 1])
    chosen = jnp.where(valid, listed[...], -1)
    member = (lax.broadcasted_iota(jnp.int32, (drops, slots), 0) == chosen).astype(F32).astype(BF16)
    row = lax.broadcasted_iota(jnp.int32, (16, slots), 0)
    column = lax.broadcasted_iota(jnp.int32, (16, slots), 1)
    which = (row == (column >= half).astype(jnp.int32)).astype(F32).astype(BF16)
    mask = dot_nt(which, member)
    goes_up, goes_down = mask[0:1], mask[1:2]
    m = mass[...]
    charges = jnp.concatenate([m, m * vel[0]], 0)
    high = charges.astype(BF16).astype(F32)
    both = jnp.concatenate([high, charges - high], 0)
    rows = jnp.concatenate(
        [both * (1.0 - goes_up - goes_down), both * goes_up, both * goes_down, jnp.zeros_like(both)], 0
    ).astype(BF16)
    chunk = 256
    for start in range(0, stay.shape[1], chunk):
        here = lax.broadcasted_iota(jnp.int32, (chunk, drops), 0) + start
        onehot = (here == cell[...]).astype(F32).astype(BF16)
        got = dot_nt(rows, onehot)
        for i, out in enumerate((stay, up, down)):
            out[:, start : start + chunk] = got[8 * i : 8 * i + 4] + got[8 * i + 4 : 8 * i + 8]


def feature_kernel(stay, below, above, fields, cotangent, feats, drag):
    deposit = stay[...] + below[...] + above[...]
    state = flat_cells(fields)
    force = drag_rate * (deposit[1:4] - deposit[0:1] * state[0:3])
    drag[...] = force
    cells = state.shape[1]
    feats[...] = jnp.concatenate(
        [
            dt_step * flat_cells(cotangent),
            force[2:3],
            jnp.zeros((2, cells), F32),
            state,
            deposit[0:1],
            force[0:2],
        ],
        0,
    ).astype(BF16)


def gather_taps(g2z, x, planes, nz, lead):
    pieces = []
    for ox, oy, oz in offsets:
        xi = lax.rem(x - ox + planes, planes)
        pieces.append(ahead_y(g2z[lead + (oz + 1, xi)], -oy, nz))
    return jnp.concatenate(pieces, 0)


def closure_kernel(
    nz, place, feats, wk, wt, wo, wc, piece, closure, g2z, fcol, w_first, fz, hidden, sums, mid, last
):
    s = pl.program_id(0)
    samples = pl.num_programs(0)
    slabs = feats.shape[0] // samples
    planes = hidden.shape[0]
    per = planes // slabs
    lanes = hidden.shape[2]
    block = wo.shape[0]

    @pl.when(s == 0)
    def _():
        mid[...] = jnp.zeros_like(mid)
        last[...] = jnp.zeros_like(last)
        w_first[...] = wk[...].astype(F32).T.astype(BF16)

    sums[...] = jnp.zeros_like(sums)

    def spread(j, carry):
        f = feats[place[j * samples + s]].astype(F32)
        for h in range(per):
            plane = f[:, h * lanes : (h + 1) * lanes]
            fz[0, j * per + h] = roll_z(plane, 1, nz)
            fz[1, j * per + h] = plane
            fz[2, j * per + h] = roll_z(plane, -1, nz)
        return carry

    lax.fori_loop(0, slabs, spread, 0)

    def first_two(x, carry):
        pieces, ninth = [], []
        for ox, oy, oz in offsets:
            xi = lax.rem(x + ox + planes, planes)
            v = ahead_y(fz[oz + 1, xi], oy, nz)
            pieces.append(v[8:16])
            ninth.append(v[5:6])
        pad = jnp.zeros((256 - 9 * len(offsets), lanes), F32)
        column = jnp.concatenate(pieces + ninth + [pad], 0).astype(BF16)
        fcol[0, x] = column
        pre = dot(w_first[...], column)
        hid = (pre * logistic(pre)).astype(BF16)
        hidden[x] = hid
        prod = dot(wt[...], hid)
        for ox in (-1, 0, 1):
            xi = lax.rem(x - ox + planes, planes)
            for oz in (-1, 0, 1):
                total = None
                for oy in (-1, 0, 1):
                    t = 9 * (ox + 1) + 3 * (oy + 1) + oz + 1
                    v = ahead_y(prod[t * block : (t + 1) * block], oy, nz)
                    total = v if total is None else total + v
                sums[oz + 1, xi] += total
        return carry

    lax.fori_loop(0, planes, first_two, 0)

    def second(j, carry):
        f = feats[place[j * samples + s]]
        for h in range(per):
            x = j * per + h
            here = f[:, h * lanes : (h + 1) * lanes]
            pre = sums[1, x] + roll_z(sums[0, x], 1, nz) + roll_z(sums[2, x], -1, nz)
            sig = logistic(pre)
            hid = (pre * sig).astype(BF16)
            out = dot(wc[...], hid)
            closure[0, x] = jnp.concatenate([out[0:8, : lanes // 2], out[0:8, lanes // 2 :]], 0).astype(BF16)
            grad = dot(wo[...], here) * (sig * (1.0 + pre * (1.0 - sig)))
            last[...] += dot_nt(hid, here)
            rounded = grad.astype(BF16)
            grad = rounded.astype(F32)
            g2z[0, 0, x] = roll_z(grad, -1, nz).astype(BF16)
            g2z[0, 1, x] = rounded
            g2z[0, 2, x] = roll_z(grad, 1, nz).astype(BF16)
        return carry

    lax.fori_loop(0, slabs, second, 0)

    def third(x, carry):
        mid[...] += dot_nt(gather_taps(g2z, x, planes, nz, (0,)), hidden[x])
        return carry

    lax.fori_loop(0, planes, third, 0)

    @pl.when(s == samples - 1)
    def _():
        total = mid[...]
        taps = total.shape[0]
        piece[0:taps] = total.astype(BF16)
        squares = jnp.sum(total * total, keepdims=True)
        high = squares.astype(BF16).astype(F32)
        width = total.shape[1]
        row = lax.broadcasted_iota(jnp.int32, (block, width), 0)
        column = lax.broadcasted_iota(jnp.int32, (block, width), 1)
        extra = jnp.concatenate([last[...], jnp.zeros((block, width - block), F32)], 1)
        extra = jnp.where(column < 5, extra, 0.0)
        extra = jnp.where((row == 0) & (column == 16), high, extra)
        extra = jnp.where((row == 0) & (column == 17), squares - high, extra)
        piece[taps:] = extra.astype(BF16)


def first_kernel(nz, wk, wt, fcol, g2z, out, w_first, w_back):
    planes = fcol.shape[1]

    @pl.when(pl.program_id(0) == 0)
    def _():
        out[...] = jnp.zeros_like(out)
        w_first[...] = wk[...].astype(F32).T.astype(BF16)
        w_back[...] = wt[...].astype(F32).T.astype(BF16)

    def body(x, carry):
        back = dot(w_back[...], gather_taps(g2z, x, planes, nz, (0,)))
        column = fcol[0, x]
        pre = dot(w_first[...], column)
        sig = logistic(pre)
        grad = (back * (sig * (1.0 + pre * (1.0 - sig)))).astype(BF16)
        out[...] += dot_nt(column, grad)
        return carry

    lax.fori_loop(0, planes, body, 0)


def step_kernel(nz, place, fields, drag, closure, feats, out):
    state = flat_cells(fields)
    cells = state.shape[1]
    planes, rows = fields.shape[2], fields.shape[3]
    lanes = cells // planes
    lower = feats[place[0]][8:13, cells - lanes :].astype(F32)
    upper = feats[place[1]][8:13, :lanes].astype(F32)
    wide = jnp.concatenate([lower, state, upper], 1)
    next_x, last_x = wide[:, 2 * lanes :], wide[:, :cells]
    parts = [state[:, i * lanes : (i + 1) * lanes] for i in range(planes)]
    next_y = jnp.concatenate([ahead_y(v, 1, nz) for v in parts], 1)
    last_y = jnp.concatenate([ahead_y(v, -1, nz) for v in parts], 1)
    next_z, last_z = roll_z(state, -1, nz), roll_z(state, 1, nz)
    laplace = next_x + last_x + next_y + last_y + next_z + last_z - 6.0 * state
    advect = -0.5 * (
        state[0:1] * (next_x - last_x) + state[1:2] * (next_y - last_y) + state[2:3] * (next_z - last_z)
    )
    momentum = jnp.concatenate([drag[...], jnp.zeros((2, cells), F32)], 0)
    new = state + dt_step * (viscosity * laplace + advect + closure[0:5, :] + momentum)
    for x in range(planes):
        for y in range(rows):
            at = (x * rows + y) * nz
            out[0, :, x, y, :] = new[:, at : at + nz]


def finish_kernel(count, weight_count, place, *refs):
    pieces, (first, mid_out, first_out, last_out, held, sems, factor) = refs[:count], refs[count:]
    step = pl.program_id(0)
    taps_here = mid_out.shape[0]
    slots = held.shape[0]
    block = mid_out.shape[1] // slots
    rows = held.shape[1] - 16

    @pl.when(step == 0)
    def _():
        copies, at = [], 0
        for i, ref in enumerate(pieces):
            copies.append(pltpu.make_async_copy(ref, held.at[at : at + ref.shape[0]], sems.at[i]))
            at += ref.shape[0]
        for copy in copies:
            copy.start()
        for copy in copies:
            copy.wait()
        raw = first[...]
        squares = jnp.sum(raw * raw, keepdims=True)
        last = []
        for d in range(slots):
            extra = held[place[d], rows:].astype(F32)
            last.append(extra[:, 0:5])
            squares = squares + jnp.sum(extra[0:1, 16:18], keepdims=True)
        last = jnp.concatenate(last, 0)
        squares = squares + jnp.sum(last * last, keepdims=True)
        clip = jnp.minimum(1.0, clip_rms * math.sqrt(weight_count) / jnp.sqrt(squares + 1e-06))
        factor[...] = jnp.broadcast_to(clip, factor.shape)
        last_out[...] = last * clip
        scaled = raw * clip
        for t in range(27):
            first_out[t, 0:8] = scaled[8 * t : 8 * t + 8]
            first_out[t, 8:9] = scaled[216 + t : 217 + t]

    width = mid_out.shape[1]
    eye = (
        lax.broadcasted_iota(jnp.int32, (width, width), 0) == lax.broadcasted_iota(jnp.int32, (width, width), 1)
    ).astype(F32).astype(BF16)
    clip = factor[0:1, 0:1]
    for i in range(taps_here):
        start = pl.multiple_of((step * taps_here + i) * block, block)
        flipped = jnp.concatenate([held[place[d], pl.ds(start, block)] for d in range(slots)], 0)
        mid_out[i] = dot_nt(eye, flipped) * clip


def whole_spec(shape):
    return pl.BlockSpec(shape, lambda *unused: (0,) * len(shape))


SMEM = pl.BlockSpec(memory_space=pltpu.SMEM)
VMEM = pl.BlockSpec(memory_space=pltpu.VMEM)
ANY = pl.BlockSpec(memory_space=pl.ANY)


def params(**more):
    return pltpu.CompilerParams(vmem_limit_bytes=VMEM_BYTES, **more)


def shards(
    fields, drop_mass, drop_vel, drop_cell, cross_list, cross_count, w_in, w_mid, w_out, cotangent
):
    shape = jax.ShapeDtypeStruct
    n_slab, n_rep = lax.axis_size("slab"), lax.axis_size("rep")
    planes, ny, nz = fields.shape[2:]
    cells = planes * ny * nz
    lanes = ny * nz
    hid, cout = w_out.shape
    joined = n_slab * n_rep * 16 <= hid
    team = ("slab", "rep") if joined else ("slab",)
    samples = n_rep if joined else 1
    size = n_slab * samples
    block = hid // size
    fast = joined and n_slab == 4 and n_rep == 4
    slab, rep = lax.axis_index("slab"), lax.axis_index("rep")
    sample = rep if joined else jnp.zeros((), jnp.int32)
    me = slab * samples + sample
    all_planes = n_slab * planes
    everyone = jnp.arange(size, dtype=jnp.int32)

    def trade(v, mask):
        return lax.ppermute(v, team, [(d, d ^ mask) for d in range(size)])

    dense = shape((4, cells), F32)
    stay, up, down = pl.pallas_call(
        deposit_kernel,
        out_shape=(dense, dense, dense),
        in_specs=[VMEM] * 4 + [SMEM],
        out_specs=(VMEM,) * 3,
        compiler_params=params(),
        name="deposit",
    )(drop_mass, drop_vel, drop_cell, cross_list, cross_count)
    from_below = lax.ppermute(up, "slab", [(i, (i + 1) % n_slab) for i in range(n_slab)])
    from_above = lax.ppermute(down, "slab", [((i + 1) % n_slab, i) for i in range(n_slab)])
    own_feats, drag = pl.pallas_call(
        feature_kernel,
        out_shape=(shape((16, cells), BF16), shape((3, cells), F32)),
        in_specs=[VMEM] * 5,
        out_specs=(VMEM,) * 2,
        compiler_params=params(),
        name="features",
    )(stay, from_below, from_above, fields, cotangent)

    if fast:
        order = (8, 1, 2, 4)
        feats = own_feats[None]
        for mask in order:
            feats = jnp.concatenate([feats, trade(feats, mask)], 0)
        apart = me ^ everyone
        feat_place = sum(((apart & mask) != 0).astype(jnp.int32) << i for i, mask in enumerate(order))
    else:
        feats = lax.all_gather(own_feats, team)
        feat_place = everyone

    w_block = lax.dynamic_slice(w_mid, (0, 0, me * block), (27, hid, block))
    wt = jnp.transpose(w_block, (0, 2, 1)).reshape(27 * block, hid)
    wk = jnp.concatenate([w_in[:, :8].reshape(216, hid), w_in[:, 8], jnp.zeros((13, hid), BF16)], 0)
    out_block = lax.dynamic_slice(w_out, (me * block, 0), (block, cout))
    wo = jnp.pad(out_block, ((0, 0), (0, 16 - cout)))
    wc = jnp.pad(out_block.T, ((0, 16 - cout), (0, 0)))

    rows = 27 * block
    piece, closure, g2z, fcol = pl.pallas_call(
        functools.partial(closure_kernel, nz),
        grid=(samples,),
        out_shape=(
            shape((rows + 16, hid), BF16),
            shape((samples, all_planes, 16, lanes // 2), BF16),
            shape((samples, 3, all_planes, block, lanes), BF16),
            shape((samples, all_planes, 256, lanes), BF16),
        ),
        in_specs=[SMEM] + [VMEM] * 5,
        out_specs=(
            whole_spec((rows + 16, hid)),
            pl.BlockSpec((1, all_planes, 16, lanes // 2), lambda s: (s, 0, 0, 0)),
            pl.BlockSpec((1, 3, all_planes, block, lanes), lambda s: (s, 0, 0, 0, 0)),
            pl.BlockSpec((1, all_planes, 256, lanes), lambda s: (s, 0, 0, 0)),
        ),
        scratch_shapes=[
            pltpu.VMEM((hid, 256), BF16),
            pltpu.VMEM((3, all_planes, 16, lanes), F32),
            pltpu.VMEM((all_planes, hid, lanes), BF16),
            pltpu.VMEM((3, all_planes, block, lanes), F32),
            pltpu.VMEM((rows, hid), F32),
            pltpu.VMEM((block, 16), F32),
        ],
        compiler_params=params(),
        name="closure",
    )(feat_place, feats, wk, wt, wo, wc)

    raw_first = pl.pallas_call(
        functools.partial(first_kernel, nz),
        grid=(samples,),
        out_shape=shape((256, hid), F32),
        in_specs=[
            whole_spec((256, hid)),
            whole_spec((rows, hid)),
            pl.BlockSpec((1, all_planes, 256, lanes), lambda s: (s, 0, 0, 0)),
            pl.BlockSpec((1, 3, all_planes, block, lanes), lambda s: (s, 0, 0, 0, 0)),
        ],
        out_specs=whole_spec((256, hid)),
        scratch_shapes=[pltpu.VMEM((hid, 256), BF16), pltpu.VMEM((hid, rows), BF16)],
        compiler_params=params(),
        name="first",
    )(wk, wt, fcol, g2z)

    closure = closure.reshape(samples, n_slab, planes, 16, lanes // 2)
    if fast:
        z = rep
        outer = (z == 0) | (z == 3)

        def line(v, pairs):
            return lax.ppermute(v, "rep", pairs)

        def tie(*values):
            return lax.optimization_barrier(values)

        y0 = trade(piece, 8)
        p1 = line(piece, [(0, 1), (1, 0), (2, 3), (3, 2)])
        p2 = line(piece, [(1, 2), (2, 1)])
        y0, p1, p2 = tie(y0, p1, p2)
        y1 = trade(p1, 8)
        p4 = line(p2, [(1, 0), (2, 3)])
        p3 = line(p1, [(1, 2), (2, 1)])
        y1, p3, p4 = tie(y1, p3, p4)
        q2 = jnp.where(outer, p4, p2)
        y2 = trade(q2, 8)
        p5 = line(p3, [(1, 0), (2, 3)])
        c0 = trade(jnp.stack([piece, y0, p1, y1]), 4)
        y2, p5, c0 = tie(y2, p5, c0)
        q3 = jnp.where(outer, p5, p3)
        y3 = trade(q3, 8)
        c1 = trade(jnp.stack([q2, y2, q3]), 4)
        c2 = trade(y3, 4)
        pieces = [v[None] for v in (piece, y0, p1, y1, q2, y2, q3, y3)] + [c0, c1, c2[None]]
        m2 = jnp.where(outer, 2, 3)
        masks = jnp.stack([jnp.int32(0), jnp.int32(8), jnp.int32(1), jnp.int32(9), m2, m2 | 8, m2 ^ 1, (m2 ^ 1) | 8])
        masks = jnp.concatenate([masks, masks | 4])
        piece_place = jnp.argmax((me ^ everyone)[:, None] == masks[None, :], axis=1).astype(jnp.int32)

        core, y = slab & 1, slab >> 1

        def halves(v, axis, bit):
            low, high = lax.index_in_dim(v, 0, axis, False), lax.index_in_dim(v, 1, axis, False)
            return jnp.where(bit == 0, low, high), jnp.where(bit == 0, high, low)

        raw_keep, raw_send = halves(raw_first.reshape(2, 128, hid), 0, core)
        part = closure.reshape(2, 2, 2, 2, planes * 16, lanes // 2).astype(F32)
        first_stage = True
        for mask, axis, bit in ((4, 3, core), (8, 2, y), (1, 1, z & 1), (2, 0, z >> 1)):
            keep, send = halves(part, axis, bit)
            if not first_stage:
                raw_send = raw_keep = raw_keep.astype(BF16)
            message = jnp.concatenate(
                [raw_send.astype(BF16), send.astype(BF16).reshape(-1, lanes // 2)], 0
            )
            got = trade(message, mask).astype(F32)
            raw_keep = raw_keep.astype(F32) + got[:128]
            part = keep + got[128:].reshape(keep.shape)
            first_stage = False
        other = trade(raw_keep, 4)
        low, high = jnp.where(core == 0, raw_keep, other), jnp.where(core == 0, other, raw_keep)
        raw_first = jnp.concatenate([low, high], 0)
        own_closure = part.reshape(planes, 2, 8, lanes // 2)
    else:
        if not joined:
            raw_first = lax.psum(raw_first, "rep")
            body = lax.psum(piece[:rows].astype(F32), "rep")
            extra = lax.psum(piece[rows:].astype(F32), "rep")
            squares = jnp.sum(body * body)
            high = squares.astype(BF16).astype(F32)
            extra = extra.at[0, 16].set(high).at[0, 17].set(squares - high)
            piece = jnp.concatenate([body, extra], 0).astype(BF16)
        raw_first = lax.psum(raw_first, team)
        pieces = [lax.all_gather(piece, team)]
        piece_place = everyone
        part = jnp.swapaxes(closure, 0, 1).reshape((size,) + closure.shape[2:]).astype(F32)
        own_closure = lax.psum_scatter(part, team, scatter_dimension=0).reshape(planes, 2, 8, lanes // 2)
    own_closure = jnp.transpose(own_closure, (2, 0, 1, 3)).reshape(8, cells)

    near = jnp.stack([(slab + n_slab - 1) % n_slab, (slab + 1) % n_slab]) * samples + sample
    new_fields = pl.pallas_call(
        functools.partial(step_kernel, nz),
        out_shape=shape(fields.shape, F32),
        in_specs=[SMEM] + [VMEM] * 4,
        out_specs=VMEM,
        compiler_params=params(),
        name="step",
    )(jnp.take(feat_place, near), fields, drag, own_closure, feats)

    weight_count = w_in.size + w_mid.size + w_out.size
    step_taps = 3
    grads = pl.pallas_call(
        functools.partial(finish_kernel, len(pieces), weight_count),
        grid=(27 // step_taps,),
        out_shape=(shape((27, hid, hid), F32), shape(w_in.shape, F32), shape(w_out.shape, F32)),
        in_specs=[SMEM] + [ANY] * len(pieces) + [whole_spec((256, hid))],
        out_specs=(
            pl.BlockSpec((step_taps, hid, hid), lambda i: (i, 0, 0)),
            whole_spec(w_in.shape),
            whole_spec(w_out.shape),
        ),
        scratch_shapes=[
            pltpu.VMEM((size, rows + 16, hid), BF16),
            pltpu.SemaphoreType.DMA((len(pieces),)),
            pltpu.VMEM((8, 128), F32),
        ],
        compiler_params=params(),
        name="finish",
    )(piece_place, *pieces, raw_first)
    grad_middle, grad_first, grad_last = grads
    return (new_fields, grad_first, grad_middle, grad_last)


def solution(mesh):
    placed = (
        P(("groups", "rep"), None, "slab", None, None),
        P(("groups", "rep"), "slab"),
        P(("groups", "rep"), None, "slab"),
        P(("groups", "rep"), "slab"),
        P(("groups", "rep"), "slab"),
        P(("groups", "rep"), "slab"),
        P(),
        P(),
        P(),
        P(("groups", "rep"), None, "slab", None, None),
    )
    return jax.shard_map(
        shards,
        mesh=mesh,
        in_specs=placed,
        out_specs=(
            P(("groups", "rep"), None, "slab", None, None),
            P("groups", None, None),
            P("groups", None, None),
            P("groups", None),
        ),
        check_vma=False,
    )
```

profile of v0, /device:TPU:0, one launch (start us, length us, event | category | flops | bytes accessed | tf_op | source)
XLA Modules:
  0.0 174.0 jit_solution(9581042303522219735)
XLA Ops:
  0.6 1.5 copy.32.vel
  2.1 2.3 %deposit.1 = (f32[4,1024]{1,0:T(4,128)}, f32[4,1024]{1,0:T(4,128)}, f32[4,1024]{1,0:T(4,128)}) custom-call(f32[1,1024]{1,0:T(1,128)} %mass.1, f32[1,3,1024]{2,1,0:T(4,128)} %copy.32.vel, s32[1,1024]{1,0:T(1,128)} %cell.1, s32[1,256]{1,0:T(1,128)} %listed.1, s32[1,2]{1,0:T(1,128)} %counts.1), custom_call_target="tpu_custom_call" | custom-call | tf_op jit(solution)/shard_map/deposit/pallas_call | solution.py:339
  4.9 2.0 %collective-permute-start.1 = (f32[4,1024]{1,0:T(4,128)}, f32[4,1024]{1,0:T(4,128)}, u32[]{:S(2)}, u32[]{:S(2)}) collective-permute-start(f32[4,1024]{1,0:T(4,128)} %get-tuple-element.28), channel_id=1, source_target_pairs={{4,0},{8,4},{12,8},{0,12},{5,1},{9,5},{13,9},{1,13},{6,2},{10,6},{... | collective-permute-start | bytes 49160 | tf_op jit(solution)/shard_map/ppermute | solution.py:348
  7.5 1.6 slice.62
  9.1 1.6 copy.54
  10.8 1.8 %dynamic-slice_bitcast_fusion = bf16[27,16,256]{1,2,0:T(8,128)(2,1)} fusion(bf16[27,256,256]{2,1,0:T(8,128)(2,1)S(1)} %copy-done, s32[]{:T(128)S(6)} %select_n.151), kind=kLoop, calls=%fused_computation.1 | loop fusion | bytes 442372 | tf_op jit(solution)/shard_map/transpose | solution.py:370
  12.6 0.8 maximum_maximum_fusion.wk
  13.4 1.5 features.1
  14.9 2.3 %collective-permute-start.2 = (bf16[1,16,1024]{2,1,0:T(8,128)(2,1)}, bf16[1,16,1024]{2,1,0:T(8,128)(2,1)}, u32[]{:S(2)}, u32[]{:S(2)}) collective-permute-start(bf16[1,16,1024]{2,1,0:T(8,128)(2,1)} %bitcast.68), channel_id=1, source_target_pairs={{0,8},{1,9},{2,10},{3,11},{4,12},{5,13},{6,14},{7,15},{8,0},{9,1},... | collective-permute-start | bytes 98312 | tf_op jit(solution)/shard_map/ppermute | solution.py:336
  18.5 2.4 %copy.34 = bf16[27,16,256]{2,1,0:T(8,128)(2,1)} copy(bf16[27,16,256]{1,2,0:T(8,128)(2,1)} %dynamic-slice_bitcast_fusion) | data formatting | bytes 442368 | tf_op jit(solution)/shard_map/transpose | solution.py:370
  21.0 0.8 pad_maximum_fusion.9
  21.8 1.6 collective-permute-start.3
  23.9 2.2 %collective-permute-done.3 = bf16[2,16,1024]{2,1,0:T(8,128)(2,1)S(1)} collective-permute-done((bf16[2,16,1024]{2,1,0:T(8,128)(2,1)S(1)}, bf16[2,16,1024]{2,1,0:T(8,128)(2,1)S(1)}, u32[]{:S(2)}, u32[]{:S(2)}) %collective-permute-start.3) | collective-permute-done | bytes 65568 | tf_op jit(solution)/shard_map/ppermute | solution.py:336
  26.1 0.8 pad_maximum_fusion.5
  26.9 2.7 %collective-permute-start.4 = (bf16[4,16,1024]{2,1,0:T(8,128)(2,1)S(1)}, bf16[4,16,1024]{2,1,0:T(8,128)(2,1)S(1)}, u32[]{:S(2)}, u32[]{:S(2)}) collective-permute-start(bf16[4,16,1024]{2,1,0:T(8,128)(2,1)S(1)} %pad_maximum_fusion.5), channel_id=1, source_target_pairs={{0,2},{1,3},{2,0},{3,1},{4,6},{5,7},{6,4},{7,5},{8,10},{9,11},{10,... | collective-permute-start | bytes 393224 | tf_op jit(solution)/shard_map/ppermute | solution.py:336
  29.6 0.8 constant_dynamic-update-slice_fusion.4
  30.4 3.9 %collective-permute-done.4 = bf16[4,16,1024]{2,1,0:T(8,128)(2,1)S(1)} collective-permute-done((bf16[4,16,1024]{2,1,0:T(8,128)(2,1)S(1)}, bf16[4,16,1024]{2,1,0:T(8,128)(2,1)S(1)}, u32[]{:S(2)}, u32[]{:S(2)}) %collective-permute-start.4) | collective-permute-done | bytes 131104 | tf_op jit(solution)/shard_map/ppermute | solution.py:336
  34.3 0.8 pad_maximum_fusion.2
  35.2 0.8 constant_dynamic-update-slice_fusion.3
  35.9 0.7 collective-permute-done.5
  36.7 0.8 copy-done.4
  37.5 37.2 %closure.1 = (bf16[448,256]{1,0:T(8,128)(2,1)}, bf16[4,8,16,256]{3,2,1,0:T(8,128)(2,1)}, bf16[4,3,8,16,512]{4,3,2,1,0:T(8,128)(2,1)}, bf16[4,8,256,512]{3,2,1,0:T(8,128)(2,1)}) custom-call(s32[16]{0:T(128)} %fusion.10.place, bf16[16,16,1024]{2,1,0:T(8,128)(2,1)} %copy-done.4, bf16[256,256]{1,0:T(8,128)(2,1)} %maximum_maximum_fusion.wk, ...), custom_call_target="tpu_custom_call" | custom-call | tf_op jit(solution)/shard_map/closure/pallas_call | solution.py:377
  74.8 1.0 fusion.14
  75.8 24.0 %first.1 = f32[256,256]{1,0:T(8,128)} custom-call(bf16[256,256]{1,0:T(8,128)(2,1)} %maximum_maximum_fusion.wk, bf16[432,256]{1,0:T(8,128)(2,1)} %bitcast.59, bf16[4,8,256,512]{3,2,1,0:T(8,128)(2,1)} %get-tuple-element.32.fcol, bf16[4,3,8,16,512]{4,3,2,1,0:T(8,128)(2,1)} %get-tuple-element.33.g2z), custom_call_target="tpu_custom_call" | custom-call | tf_op jit(solution)/shard_map/first/pallas_call | solution.py:405
  99.8 1.0 select_convert_fusion.2
  101.8 1.5 collective-permute-done.6
  103.4 0.9 slice.88
  104.3 1.1 bitcast_add_fusion
  106.1 1.0 convert_element_type.91
  107.1 1.0 fusion.2
  109.4 0.8 collective-permute-start.7
  110.2 0.8 iota_reduce_fusion
  111.1 1.3 collective-permute-start.12
  112.4 2.1 %collective-permute-start.11 = (bf16[448,256]{1,0:T(8,128)(2,1)}, bf16[448,256]{1,0:T(8,128)(2,1)}, u32[]{:S(2)}, u32[]{:S(2)}) collective-permute-start(bf16[448,256]{1,0:T(8,128)(2,1)} %get-tuple-element.35), channel_id=1, source_target_pairs={{0,1},{1,0},{2,3},{3,2},{4,5},{5,4},{6,7},{7,6},{8,9},{9,8},{10,11... | collective-permute-start | bytes 688136 | tf_op jit(solution)/shard_map/ppermute | solution.py:427
  114.5 1.5 collective-permute-start.10
  116.1 0.8 slice.92
  116.9 1.0 bitcast_add_fusion.1
  117.9 1.0 convert_element_type.95
  118.9 0.9 fusion.1
  121.7 1.3 collective-permute-start.15
  123.0 1.3 collective-permute-start.14
  124.3 1.5 collective-permute-start.13
  126.9 0.8 slice.96
  127.7 0.9 bitcast_add_fusion.2
  128.6 2.3 %collective-permute-done.15 = bf16[448,256]{1,0:T(8,128)(2,1)} collective-permute-done((bf16[448,256]{1,0:T(8,128)(2,1)}, bf16[448,256]{1,0:T(8,128)(2,1)}, u32[]{:S(2)}, u32[]{:S(2)}) %collective-permute-start.15) | collective-permute-done | bytes 229408 | tf_op jit(solution)/shard_map/ppermute | solution.py:427
  130.9 1.4 pad_maximum_fusion
  132.4 0.9 convert_element_type.100
  133.3 0.9 fusion
  134.2 1.0 broadcast_select_fusion.1
  135.1 1.3 collective-permute-start.16
  136.5 1.3 collective-permute-start.17
  137.8 5.5 %collective-permute-start.9 = (bf16[160,256]{1,0:T(8,128)(2,1)S(1)}, bf16[160,256]{1,0:T(8,128)(2,1)S(1)}, u32[]{:S(2)}, u32[]{:S(2)}) collective-permute-start(bf16[160,256]{1,0:T(8,128)(2,1)S(1)} %pad_maximum_fusion.8), channel_id=1, source_target_pairs={{0,2},{1,3},{2,0},{3,1},{4,6},{5,7},{6,4},{7,5},{8,10},{9,11},{10,... | collective-permute-start | bytes 245768 | tf_op jit(solution)/shard_map/ppermute | solution.py:336
  143.9 4.1 %collective-permute-done.9 = bf16[160,256]{1,0:T(8,128)(2,1)S(1)} collective-permute-done((bf16[160,256]{1,0:T(8,128)(2,1)S(1)}, bf16[160,256]{1,0:T(8,128)(2,1)S(1)}, u32[]{:S(2)}, u32[]{:S(2)}) %collective-permute-start.9) | collective-permute-done | bytes 81952 | tf_op jit(solution)/shard_map/ppermute | solution.py:336
  148.0 2.5 %collective-permute-done.17 = bf16[448,256]{1,0:T(8,128)(2,1)S(1)} collective-permute-done((bf16[448,256]{1,0:T(8,128)(2,1)}, bf16[448,256]{1,0:T(8,128)(2,1)S(1)}, u32[]{:S(2)}, u32[]{:S(2)}) %collective-permute-start.17) | collective-permute-done | bytes 229408 | tf_op jit(solution)/shard_map/ppermute | solution.py:427
  150.6 1.1 collective-permute-start.19
  151.7 0.9 pad_maximum_fusion.1
  153.8 1.8 %step.1 = f32[1,5,2,4,128]{4,3,2,1,0:T(4,128)} custom-call(s32[2]{0:T(128)} %and_select_fusion.place, f32[1,5,2,4,128]{4,3,2,1,0:T(4,128)} %fields.3, f32[3,1024]{1,0:T(4,128)} %get-tuple-element.29.drag, f32[8,1024]{1,0:T(8,128)} %bitcast.77, bf16[16,16,1024]{2,1,0:T(8,128)(2,1)} %copy-done.4), custom_call_target="tpu_custom_call" | custom-call | tf_op jit(solution)/shard_map/step/pallas_call | solution.py:496
  155.6 2.2 %collective-permute-done.19 = bf16[448,256]{1,0:T(8,128)(2,1)S(1)} collective-permute-done((bf16[448,256]{1,0:T(8,128)(2,1)S(1)}, bf16[448,256]{1,0:T(8,128)(2,1)S(1)}, u32[]{:S(2)}, u32[]{:S(2)}) %collective-permute-start.19) | collective-permute-done | bytes 229408 | tf_op jit(solution)/shard_map/ppermute | solution.py:336
  157.9 1.0 broadcast_select_fusion.3
  158.9 0.7 pad_maximum_fusion.3.refs_11_
  160.3 0.8 copy-done.11
  161.1 9.4 %finish.1 = (f32[27,256,256]{2,1,0:T(8,128)}, f32[27,9,256]{2,1,0:T(8,128)}, f32[256,5]{1,0:T(8,128)}) custom-call(s32[16]{0:T(128)} %get-tuple-element.34.place, bf16[1,448,256]{2,1,0:T(8,128)(2,1)} %bitcast.63, bf16[1,448,256]{2,1,0:T(8,128)(2,1)} %bitcast.31.refs_1_, bf16[1,448,256]{2,1,0:T(8,128)(2,1)} %bitcast.32.refs_2_, ...), custom_call_target="tpu_custom_call" | custom-call | tf_op jit(solution)/shard_map/finish/pallas_call | solution.py:507
  170.6 1.9 %copy.42 = f32[27,9,256]{2,0,1:T(8,128)} copy(f32[27,9,256]{2,1,0:T(8,128)} %get-tuple-element.57) | data formatting | bytes 497664
  172.5 1.6 copy.43
  (91 shorter events, 12.1 us)
Async XLA Ops:
  0.6 10.2 %copy-start = (bf16[27,256,256]{2,1,0:T(8,128)(2,1)S(1)}, bf16[27,256,256]{2,1,0:T(8,128)(2,1)}, u32[]{:S(2)}) copy-start(bf16[27,256,256]{2,1,0:T(8,128)(2,1)} %param.17) | copy-start | bytes 10616836
  4.4 9.0 %collective-permute-start = (f32[4,1024]{1,0:T(4,128)}, f32[4,1024]{1,0:T(4,128)}, u32[]{:S(2)}, u32[]{:S(2)}) collective-permute-start(f32[4,1024]{1,0:T(4,128)} %get-tuple-element.27), channel_id=1, source_target_pairs={{0,4},{4,8},{8,12},{12,0},{1,5},{5,9},{9,13},{13,1},{2,6},{6,10},{... | collective-permute-start | bytes 49160 | tf_op jit(solution)/shard_map/ppermute | solution.py:347
  4.9 8.6 %collective-permute-start.1 = (f32[4,1024]{1,0:T(4,128)}, f32[4,1024]{1,0:T(4,128)}, u32[]{:S(2)}, u32[]{:S(2)}) collective-permute-start(f32[4,1024]{1,0:T(4,128)} %get-tuple-element.28), channel_id=1, source_target_pairs={{4,0},{8,4},{12,8},{0,12},{5,1},{9,5},{13,9},{1,13},{6,2},{10,6},{... | collective-permute-start | bytes 49160 | tf_op jit(solution)/shard_map/ppermute | solution.py:348
  10.7 1.9 %copy-start.14 = (bf16[27,8,256]{2,1,0:T(8,128)(2,1)S(1)}, bf16[27,8,256]{2,1,0:T(8,128)(2,1)}, u32[]{:S(2)}) copy-start(bf16[27,8,256]{2,1,0:T(8,128)(2,1)} %copy.54) | copy-start | bytes 331780
  10.7 2.6 %copy-start.17 = (bf16[256,5]{0,1:T(8,128)(2,1)S(1)}, bf16[256,5]{0,1:T(8,128)(2,1)}, u32[]{:S(2)}) copy-start(bf16[256,5]{0,1:T(8,128)(2,1)} %param.18) | copy-start | bytes 7684
  14.9 6.2 %collective-permute-start.2 = (bf16[1,16,1024]{2,1,0:T(8,128)(2,1)}, bf16[1,16,1024]{2,1,0:T(8,128)(2,1)}, u32[]{:S(2)}, u32[]{:S(2)}) collective-permute-start(bf16[1,16,1024]{2,1,0:T(8,128)(2,1)} %bitcast.68), channel_id=1, source_target_pairs={{0,8},{1,9},{2,10},{3,11},{4,12},{5,13},{6,14},{7,15},{8,0},{9,1},... | collective-permute-start | bytes 98312 | tf_op jit(solution)/shard_map/ppermute | solution.py:336
  21.8 4.3 %collective-permute-start.3 = (bf16[2,16,1024]{2,1,0:T(8,128)(2,1)S(1)}, bf16[2,16,1024]{2,1,0:T(8,128)(2,1)S(1)}, u32[]{:S(2)}, u32[]{:S(2)}) collective-permute-start(bf16[2,16,1024]{2,1,0:T(8,128)(2,1)S(1)} %pad_maximum_fusion.9), channel_id=1, source_target_pairs={{0,1},{1,0},{2,3},{3,2},{4,5},{5,4},{6,7},{7,6},{8,9},{9,8},{10,11... | collective-permute-start | bytes 196616 | tf_op jit(solution)/shard_map/ppermute | solution.py:336
  26.9 7.3 %collective-permute-start.4 = (bf16[4,16,1024]{2,1,0:T(8,128)(2,1)S(1)}, bf16[4,16,1024]{2,1,0:T(8,128)(2,1)S(1)}, u32[]{:S(2)}, u32[]{:S(2)}) collective-permute-start(bf16[4,16,1024]{2,1,0:T(8,128)(2,1)S(1)} %pad_maximum_fusion.5), channel_id=1, source_target_pairs={{0,2},{1,3},{2,0},{3,1},{4,6},{5,7},{6,4},{7,5},{8,10},{9,11},{10,... | collective-permute-start | bytes 393224 | tf_op jit(solution)/shard_map/ppermute | solution.py:336
  35.1 1.6 collective-permute-start.5
  36.7 0.8 copy-start.4
  75.8 25.0 %copy-start.2 = (f32[2,2,2,1,32,256]{5,4,3,2,1,0:T(8,128)}, f32[2,2,2,1,32,256]{5,4,3,2,1,0:T(8,128)S(1)}, u32[]{:S(2)}) copy-start(f32[2,2,2,1,32,256]{5,4,3,2,1,0:T(8,128)S(1)} %get-tuple-element.62) | copy-start | bytes 786436
  75.8 25.0 %copy-start.3 = (f32[2,2,2,1,32,256]{5,4,3,2,1,0:T(8,128)}, f32[2,2,2,1,32,256]{5,4,3,2,1,0:T(8,128)S(1)}, u32[]{:S(2)}) copy-start(f32[2,2,2,1,32,256]{5,4,3,2,1,0:T(8,128)S(1)} %get-tuple-element.63) | copy-start | bytes 786436
  99.8 26.0 %copy-start.1 = (s32[16]{0:T(128)S(1)}, s32[16]{0:T(128)}, u32[]{:S(2)}) copy-start(s32[16]{0:T(128)} %fusion.10.place) | copy-start | bytes 196
  101.6 1.8 %collective-permute-start.6 = (bf16[384,256]{1,0:T(8,128)(2,1)}, bf16[384,256]{1,0:T(8,128)(2,1)}, u32[]{:S(2)}, u32[]{:S(2)}) collective-permute-start(bf16[384,256]{1,0:T(8,128)(2,1)} %pad_maximum_fusion.4), channel_id=1, source_target_pairs={{0,4},{1,5},{2,6},{3,7},{4,0},{5,1},{6,2},{7,3},{8,12},{9,13},{10,... | collective-permute-start | bytes 589832 | tf_op jit(solution)/shard_map/ppermute | solution.py:336
  105.4 0.7 copy-start.7
  108.1 0.6 copy-start.13
  109.4 6.7 %collective-permute-start.7 = (bf16[256,256]{1,0:T(8,128)(2,1)}, bf16[256,256]{1,0:T(8,128)(2,1)}, u32[]{:S(2)}, u32[]{:S(2)}) collective-permute-start(bf16[256,256]{1,0:T(8,128)(2,1)} %pad_maximum_fusion.6), channel_id=1, source_target_pairs={{0,8},{1,9},{2,10},{3,11},{4,12},{5,13},{6,14},{7,15},{8,0},{9,1},... | collective-permute-start | bytes 393224 | tf_op jit(solution)/shard_map/ppermute | solution.py:336
  111.1 10.1 %collective-permute-start.12 = (bf16[448,256]{1,0:T(8,128)(2,1)}, bf16[448,256]{1,0:T(8,128)(2,1)}, u32[]{:S(2)}, u32[]{:S(2)}) collective-permute-start(bf16[448,256]{1,0:T(8,128)(2,1)} %get-tuple-element.35), channel_id=1, source_target_pairs={{1,2},{2,1},{5,6},{6,5},{9,10},{10,9},{13,14},{14,13},{17,18},{18,... | collective-permute-start | bytes 688136 | tf_op jit(solution)/shard_map/ppermute | solution.py:427
  112.4 8.7 %collective-permute-start.11 = (bf16[448,256]{1,0:T(8,128)(2,1)}, bf16[448,256]{1,0:T(8,128)(2,1)}, u32[]{:S(2)}, u32[]{:S(2)}) collective-permute-start(bf16[448,256]{1,0:T(8,128)(2,1)} %get-tuple-element.35), channel_id=1, source_target_pairs={{0,1},{1,0},{2,3},{3,2},{4,5},{5,4},{6,7},{7,6},{8,9},{9,8},{10,11... | collective-permute-start | bytes 688136 | tf_op jit(solution)/shard_map/ppermute | solution.py:427
  114.5 7.1 %collective-permute-start.10 = (bf16[448,256]{1,0:T(8,128)(2,1)}, bf16[448,256]{1,0:T(8,128)(2,1)}, u32[]{:S(2)}, u32[]{:S(2)}) collective-permute-start(bf16[448,256]{1,0:T(8,128)(2,1)} %get-tuple-element.35), channel_id=1, source_target_pairs={{0,8},{1,9},{2,10},{3,11},{4,12},{5,13},{6,14},{7,15},{8,0},{9,1},... | collective-permute-start | bytes 688136 | tf_op jit(solution)/shard_map/ppermute | solution.py:336
  117.9 1.8 %copy-start.10 = (f32[2,2,32,256]{3,2,0,1:T(8,128)}, f32[2,2,32,256]{3,2,0,1:T(8,128)S(1)}, u32[]{:S(2)}) copy-start(f32[2,2,32,256]{3,2,0,1:T(8,128)S(1)} %bitcast_add_fusion.1) | copy-start | bytes 393220
  119.8 0.6 copy-start.12
  121.0 5.9 %collective-permute-start.8 = (bf16[192,256]{1,0:T(8,128)(2,1)}, bf16[192,256]{1,0:T(8,128)(2,1)}, u32[]{:S(2)}, u32[]{:S(2)}) collective-permute-start(bf16[192,256]{1,0:T(8,128)(2,1)} %pad_maximum_fusion.7), channel_id=1, source_target_pairs={{0,1},{1,0},{2,3},{3,2},{4,5},{5,4},{6,7},{7,6},{8,9},{9,8},{10,11... | collective-permute-start | bytes 294920 | tf_op jit(solution)/shard_map/ppermute | solution.py:336
  121.7 9.2 %collective-permute-start.15 = (bf16[448,256]{1,0:T(8,128)(2,1)}, bf16[448,256]{1,0:T(8,128)(2,1)}, u32[]{:S(2)}, u32[]{:S(2)}) collective-permute-start(bf16[448,256]{1,0:T(8,128)(2,1)} %collective-permute-done.12), channel_id=1, source_target_pairs={{1,0},{2,3},{5,4},{6,7},{9,8},{10,11},{13,12},{14,15},{17,16},{18,... | collective-permute-start | bytes 688136 | tf_op jit(solution)/shard_map/ppermute | solution.py:427
  123.0 7.9 %collective-permute-start.14 = (bf16[448,256]{1,0:T(8,128)(2,1)}, bf16[448,256]{1,0:T(8,128)(2,1)}, u32[]{:S(2)}, u32[]{:S(2)}) collective-permute-start(bf16[448,256]{1,0:T(8,128)(2,1)} %collective-permute-done.11), channel_id=1, source_target_pairs={{1,2},{2,1},{5,6},{6,5},{9,10},{10,9},{13,14},{14,13},{17,18},{18,... | collective-permute-start | bytes 688136 | tf_op jit(solution)/shard_map/ppermute | solution.py:427
  124.3 6.6 %collective-permute-start.13 = (bf16[448,256]{1,0:T(8,128)(2,1)}, bf16[448,256]{1,0:T(8,128)(2,1)}, u32[]{:S(2)}, u32[]{:S(2)}) collective-permute-start(bf16[448,256]{1,0:T(8,128)(2,1)} %collective-permute-done.11), channel_id=1, source_target_pairs={{0,8},{1,9},{2,10},{3,11},{4,12},{5,13},{6,14},{7,15},{8,0},{9,1},... | collective-permute-start | bytes 688136 | tf_op jit(solution)/shard_map/ppermute | solution.py:336
  132.3 18.2 %collective-permute-start.18 = (bf16[4,448,256]{2,1,0:T(8,128)(2,1)S(1)}, bf16[4,448,256]{2,1,0:T(8,128)(2,1)S(1)}, u32[]{:S(2)}, u32[]{:S(2)}) collective-permute-start(bf16[4,448,256]{2,1,0:T(8,128)(2,1)S(1)} %pad_maximum_fusion), channel_id=1, source_target_pairs={{0,4},{1,5},{2,6},{3,7},{4,0},{5,1},{6,2},{7,3},{8,12},{9,13},{10,... | collective-permute-start | bytes 2752520 | tf_op jit(solution)/shard_map/ppermute | solution.py:336
  135.1 25.1 %copy-start.5 = (bf16[448,256]{1,0:T(8,128)(2,1)}, bf16[448,256]{1,0:T(8,128)(2,1)S(1)}, u32[]{:S(2)}) copy-start(bf16[448,256]{1,0:T(8,128)(2,1)S(1)} %broadcast_select_fusion.1) | copy-start | bytes 688132
  135.1 12.9 %collective-permute-start.16 = (bf16[448,256]{1,0:T(8,128)(2,1)S(1)}, bf16[448,256]{1,0:T(8,128)(2,1)S(1)}, u32[]{:S(2)}, u32[]{:S(2)}) collective-permute-start(bf16[448,256]{1,0:T(8,128)(2,1)S(1)} %broadcast_select_fusion.1), channel_id=1, source_target_pairs={{0,8},{1,9},{2,10},{3,11},{4,12},{5,13},{6,14},{7,15},{8,0},{9,1},... | collective-permute-start | bytes 688136 | tf_op jit(solution)/shard_map/ppermute | solution.py:336
  136.5 14.0 %collective-permute-start.17 = (bf16[448,256]{1,0:T(8,128)(2,1)}, bf16[448,256]{1,0:T(8,128)(2,1)S(1)}, u32[]{:S(2)}, u32[]{:S(2)}) collective-permute-start(bf16[448,256]{1,0:T(8,128)(2,1)} %collective-permute-done.14), channel_id=1, source_target_pairs={{1,0},{2,3},{5,4},{6,7},{9,8},{10,11},{13,12},{14,15},{17,16},{18,... | collective-permute-start | bytes 688136 | tf_op jit(solution)/shard_map/ppermute | solution.py:427
  137.8 10.2 %collective-permute-start.9 = (bf16[160,256]{1,0:T(8,128)(2,1)S(1)}, bf16[160,256]{1,0:T(8,128)(2,1)S(1)}, u32[]{:S(2)}, u32[]{:S(2)}) collective-permute-start(bf16[160,256]{1,0:T(8,128)(2,1)S(1)} %pad_maximum_fusion.8), channel_id=1, source_target_pairs={{0,2},{1,3},{2,0},{3,1},{4,6},{5,7},{6,4},{7,5},{8,10},{9,11},{10,... | collective-permute-start | bytes 245768 | tf_op jit(solution)/shard_map/ppermute | solution.py:336
  148.0 12.2 %copy-start.9 = (bf16[448,256]{1,0:T(8,128)(2,1)}, bf16[448,256]{1,0:T(8,128)(2,1)S(1)}, u32[]{:S(2)}) copy-start(bf16[448,256]{1,0:T(8,128)(2,1)S(1)} %collective-permute-done.16) | copy-start | bytes 688132
  150.5 9.8 %copy-start.8 = (bf16[4,448,256]{2,1,0:T(8,128)(2,1)}, bf16[4,448,256]{2,1,0:T(8,128)(2,1)S(1)}, u32[]{:S(2)}) copy-start(bf16[4,448,256]{2,1,0:T(8,128)(2,1)S(1)} %collective-permute-done.18.refs_8_) | copy-start | bytes 2752516
  150.6 9.7 %copy-start.6 = (bf16[448,256]{1,0:T(8,128)(2,1)}, bf16[448,256]{1,0:T(8,128)(2,1)S(1)}, u32[]{:S(2)}) copy-start(bf16[448,256]{1,0:T(8,128)(2,1)S(1)} %broadcast_select_fusion) | copy-start | bytes 688132
  150.6 7.3 %collective-permute-start.19 = (bf16[448,256]{1,0:T(8,128)(2,1)S(1)}, bf16[448,256]{1,0:T(8,128)(2,1)S(1)}, u32[]{:S(2)}, u32[]{:S(2)}) collective-permute-start(bf16[448,256]{1,0:T(8,128)(2,1)S(1)} %broadcast_select_fusion), channel_id=1, source_target_pairs={{0,8},{1,9},{2,10},{3,11},{4,12},{5,13},{6,14},{7,15},{8,0},{9,1},... | collective-permute-start | bytes 688136 | tf_op jit(solution)/shard_map/ppermute | solution.py:336
  152.6 7.0 %collective-permute-start.20 = (bf16[3,448,256]{2,1,0:T(8,128)(2,1)}, bf16[3,448,256]{2,1,0:T(8,128)(2,1)S(1)}, u32[]{:S(2)}, u32[]{:S(2)}) collective-permute-start(bf16[3,448,256]{2,1,0:T(8,128)(2,1)} %pad_maximum_fusion.1), channel_id=1, source_target_pairs={{0,4},{1,5},{2,6},{3,7},{4,0},{5,1},{6,2},{7,3},{8,12},{9,13},{10,... | collective-permute-start | bytes 2064392 | tf_op jit(solution)/shard_map/ppermute | solution.py:336
  152.6 5.2 %collective-permute-start.22 = (f32[128,256]{1,0:T(8,128)S(1)}, f32[128,256]{1,0:T(8,128)}, u32[]{:S(2)}, u32[]{:S(2)}) collective-permute-start(f32[128,256]{1,0:T(8,128)S(1)} %slice_add_fusion), channel_id=1, source_target_pairs={{0,4},{1,5},{2,6},{3,7},{4,0},{5,1},{6,2},{7,3},{8,12},{9,13},{10,... | collective-permute-start | bytes 393224 | tf_op jit(solution)/shard_map/ppermute | solution.py:336
  157.8 2.4 %copy-start.15 = (bf16[448,256]{1,0:T(8,128)(2,1)}, bf16[448,256]{1,0:T(8,128)(2,1)S(1)}, u32[]{:S(2)}) copy-start(bf16[448,256]{1,0:T(8,128)(2,1)S(1)} %collective-permute-done.19) | copy-start | bytes 688132
  157.8 1.7 %collective-permute-start.21 = (bf16[448,256]{1,0:T(8,128)(2,1)S(1)}, bf16[448,256]{1,0:T(8,128)(2,1)S(1)}, u32[]{:S(2)}, u32[]{:S(2)}) collective-permute-start(bf16[448,256]{1,0:T(8,128)(2,1)S(1)} %collective-permute-done.19), channel_id=1, source_target_pairs={{0,4},{1,5},{2,6},{3,7},{4,0},{5,1},{6,2},{7,3},{8,12},{9,13},{10,... | collective-permute-start | bytes 688136 | tf_op jit(solution)/shard_map/ppermute | solution.py:336
  159.6 0.7 copy-start.16
  160.3 0.9 copy-start.11
where the time goes:
time: 175 us; the launch traced here: 174 us
  Pallas kernels  76.3 us (44%)
  starting transfers between devices  29.1 us (17%)
  local copies, waits for them, and re-layouts  24.7 us (14%)
  other arithmetic  22.4 us (13%)
  waiting for transfers between devices  20.5 us (12%)
    pallas_call x1, Pallas kernels, shards(): pl.pallas_call(functools.partial(closure_kernel, nz), grid=(samples,), ou...  37.2 us
    pallas_call x1, Pallas kernels, shards(): pl.pallas_call(functools.partial(first_kernel, nz), grid=(samples,), out_...  24 us
    ppermute x16, starting transfers between devices, trade(): return lax.ppermute(v, team, [(d, d ^ mask) for d in range(size)])  19.3 us
    ppermute x16, waiting for transfers between devices, trade(): return lax.ppermute(v, team, [(d, d ^ mask) for d in range(size)])  15.8 us
    unnamed x44, local copies, waits for them, and re-layouts  10.8 us
    pallas_call x1, Pallas kernels, shards(): pl.pallas_call(functools.partial(finish_kernel, len(pieces), weight_count...  9.44 us
    ppermute x5, starting transfers between devices, line(): return lax.ppermute(v, 'rep', pairs)  7.39 us
    ppermute x5, waiting for transfers between devices, line(): return lax.ppermute(v, 'rep', pairs)  4.77 us
  transfers between devices with their start and end apart: 23, of which 10 were waited for; matrix products, arithmetic and copies ran while one was open for 15% of the time, Pallas kernels for 1%

commit v1 on v0

v1 whole, which is shorter than its diff:
```python
import functools
import math

import jax
import jax.numpy as jnp
from jax import lax
from jax.experimental import pallas as pl
from jax.experimental.pallas import tpu as pltpu
from jax.sharding import PartitionSpec as P

dt_step = 0.2
viscosity = 0.05
drag_rate = 0.5
clip_rms = 0.5

F32 = jnp.float32
BF16 = jnp.bfloat16
VMEM_BYTES = 58 * 2**20
offsets = [(x, y, z) for x in (-1, 0, 1) for y in (-1, 0, 1) for z in (-1, 0, 1)]


def dot(a, b):
    return lax.dot_general(a, b, (((1,), (0,)), ((), ())), preferred_element_type=F32)


def dot_nt(a, b):
    return lax.dot_general(a, b, (((1,), (1,)), ((), ())), preferred_element_type=F32)


def logistic(p):
    return 0.5 * jnp.tanh(0.5 * p) + 0.5


def roll_z(v, by, nz):
    return jnp.concatenate(
        [pltpu.roll(v[:, k : k + nz], by % nz, 1) for k in range(0, v.shape[1], nz)], 1
    )


def ahead_y(v, by, nz):
    if by == 0:
        return v
    cut = (by * nz) % v.shape[1]
    return jnp.concatenate([v[:, cut:], v[:, :cut]], 1)


def flat_cells(ref):
    planes, rows = ref.shape[2], ref.shape[3]
    return jnp.concatenate([ref[0, :, x, y, :] for x in range(planes) for y in range(rows)], 1)


def deposit_kernel(mass, vel, cell, listed, counts, stay, up, down):
    drops = mass.shape[1]
    slots = listed.shape[1]
    half = slots // 2
    k = lax.broadcasted_iota(jnp.int32, (1, slots), 1)
    valid = k < jnp.where(k < half, counts[0, 0], half + counts[0, 1])
    chosen = jnp.where(valid, listed[...], -1)
    member = (lax.broadcasted_iota(jnp.int32, (drops, slots), 0) == chosen).astype(F32).astype(BF16)
    row = lax.broadcasted_iota(jnp.int32, (16, slots), 0)
    column = lax.broadcasted_iota(jnp.int32, (16, slots), 1)
    which = (row == (column >= half).astype(jnp.int32)).astype(F32).astype(BF16)
    mask = dot_nt(which, member)
    goes_up, goes_down = mask[0:1], mask[1:2]
    m = mass[...]
    charges = jnp.concatenate([m] + [m * vel[i] for i in range(vel.shape[0])], 0)
    high = charges.astype(BF16).astype(F32)
    both = jnp.concatenate([high, charges - high], 0)
    rows = jnp.concatenate(
        [both * (1.0 - goes_up - goes_down), both * goes_up, both * goes_down, jnp.zeros_like(both)], 0
    ).astype(BF16)
    chunk = 256
    for start in range(0, stay.shape[1], chunk):
        here = lax.broadcasted_iota(jnp.int32, (chunk, drops), 0) + start
        onehot = (here == cell[...]).astype(F32).astype(BF16)
        got = dot_nt(rows, onehot)
        for i, out in enumerate((stay, up, down)):
            out[:, start : start + chunk] = got[8 * i : 8 * i + 4] + got[8 * i + 4 : 8 * i + 8]


def feature_kernel(stay, below, above, fields, cotangent, feats, drag):
    deposit = stay[...] + below[...] + above[...]
    state = flat_cells(fields)
    force = drag_rate * (deposit[1:4] - deposit[0:1] * state[0:3])
    drag[...] = force
    cells = state.shape[1]
    feats[...] = jnp.concatenate(
        [
            dt_step * flat_cells(cotangent),
            force[2:3],
            jnp.zeros((2, cells), F32),
            state,
            deposit[0:1],
            force[0:2],
        ],
        0,
    ).astype(BF16)


def tap_rows():
    r = lax.broadcasted_iota(jnp.int32, (288, 256), 0)
    k = lax.broadcasted_iota(jnp.int32, (288, 256), 1)
    c, t = r >> 5, r & 31
    ox = (t >= 9).astype(jnp.int32) + (t >= 18).astype(jnp.int32)
    q = t - 9 * ox
    ninth = jnp.where(q < 8, 216 + 8 * ox + q, 240 + ox)
    at = jnp.where(c < 8, 8 * t + c, ninth)
    return ((at == k) & (t < 27)).astype(F32).astype(BF16)


def weight_kernel(me, w_in, w_mid, w_out, wt, w_back, w_first, wo, wc):
    block, hid = wo.shape[0], wt.shape[1]
    row = lax.broadcasted_iota(jnp.int32, (block, hid), 0)
    column = lax.broadcasted_iota(jnp.int32, (block, hid), 1)
    chosen = (column == row + me[0] * block).astype(F32).astype(BF16)
    for t in range(27):
        wt[t * block : (t + 1) * block] = dot_nt(chosen, w_mid[t]).astype(BF16)
    w_back[...] = wt[...].astype(F32).T.astype(BF16)
    pad = jnp.zeros((5, hid), F32)
    tall = jnp.concatenate([v for c in range(9) for v in (w_in[c].astype(F32), pad)], 0)
    w_first[...] = dot(tall.T.astype(BF16), tap_rows()).astype(BF16)
    wide = w_out[...].astype(F32)
    wide = jnp.concatenate([wide, jnp.zeros((16 - wide.shape[0], hid), F32)], 0).astype(BF16)
    wo[...] = dot_nt(chosen, wide).astype(BF16)
    wc[...] = dot_nt(wide, chosen).astype(BF16)


def moved(v, ox, oy, nz, lanes):
    planes = v.shape[1] // lanes
    parts = []
    for x in range(planes):
        at = ((x + ox) % planes) * lanes
        parts.append(ahead_y(v[:, at : at + lanes], oy, nz))
    return parts


def all_taps(g2z, nz, lanes):
    taps = [moved(g2z[0, oz + 1], -ox, -oy, nz, lanes) for ox, oy, oz in offsets]
    return [jnp.concatenate([tap[x] for tap in taps], 0) for x in range(len(taps[0]))]


def closure_kernel(
    nz, lanes, place, feats, w_first, wt, wo, wc, piece, closure, g2z, fcol, fz, eighth, ninth, hidden, sums, mid, last
):
    s = pl.program_id(0)
    samples = pl.num_programs(0)
    slabs = feats.shape[0] // samples
    cells = hidden.shape[1]
    planes = cells // lanes
    per = planes // slabs
    block = wo.shape[0]
    group = 4

    @pl.when(s == 0)
    def _():
        mid[...] = jnp.zeros_like(mid)
        last[...] = jnp.zeros_like(last)

    sums[...] = jnp.zeros_like(sums)
    sub = lax.broadcasted_iota(jnp.int32, (8, lanes), 0)
    for j in range(slabs):
        f = feats[place[j * samples + s]].astype(F32)
        at = slice(j * per * lanes, (j + 1) * per * lanes)
        fz[0, :, at] = roll_z(f, 1, nz)
        fz[1, :, at] = f
        fz[2, :, at] = roll_z(f, -1, nz)
    for x in range(planes):
        at = slice(x * lanes, (x + 1) * lanes)
        rows = [jnp.broadcast_to(fz[oz + 1, 5:6, at], (8, lanes)) for oz in (-1, 0, 1)]
        tile = ahead_y(rows[0], -1, nz)
        for q in range(1, 8):
            tile = jnp.where(sub == q, ahead_y(rows[q % 3], q // 3 - 1, nz), tile)
        eighth[:, at] = tile
        ninth[:, at] = ahead_y(rows[2], 1, nz)

    for x in range(planes):
        at = slice(x * lanes, (x + 1) * lanes)
        near = [slice(((x + ox) % planes) * lanes, ((x + ox) % planes + 1) * lanes) for ox in (-1, 0, 1)]
        pieces = [ahead_y(fz[oz + 1, 8:16, near[ox + 1]], oy, nz) for ox, oy, oz in offsets]
        pieces += [eighth[:, n] for n in near]
        tail = jnp.where(sub == 0, ninth[:, near[0]], jnp.where(sub == 1, ninth[:, near[1]], ninth[:, near[2]]))
        pieces += [jnp.where(sub < 3, tail, 0.0), jnp.zeros((8, lanes), F32)]
        column = jnp.concatenate(pieces, 0).astype(BF16)
        fcol[0, :, at] = column
        pre = dot(w_first[...], column)
        hid = (pre * logistic(pre)).astype(BF16)
        hidden[:, at] = hid
        prod = dot(wt[...], hid)
        for ox in (-1, 0, 1):
            to = near[1 - ox]
            for oz in (-1, 0, 1):
                total = None
                for oy in (-1, 0, 1):
                    t = 9 * (ox + 1) + 3 * (oy + 1) + oz + 1
                    v = ahead_y(prod[t * block : (t + 1) * block], oy, nz)
                    total = v if total is None else total + v
                sums[oz + 1, :, to] += total

    for j in range(slabs):
        here = feats[place[j * samples + s]]
        at = slice(j * per * lanes, (j + 1) * per * lanes)
        pre = sums[1, :, at] + roll_z(sums[0, :, at], 1, nz) + roll_z(sums[2, :, at], -1, nz)
        sig = logistic(pre)
        hid = (pre * sig).astype(BF16)
        out = dot(wc[...], hid)
        for h in range(per):
            for k in range(2):
                start = h * lanes + k * (lanes // 2)
                closure[0, j * per + h, 8 * k : 8 * k + 8] = out[0:8, start : start + lanes // 2].astype(BF16)
        grad = dot(wo[...], here) * (sig * (1.0 + pre * (1.0 - sig)))
        last[...] += dot_nt(here, hid)
        rounded = grad.astype(BF16)
        grad = rounded.astype(F32)
        g2z[0, 0, :, at] = roll_z(grad, -1, nz).astype(BF16)
        g2z[0, 1, :, at] = rounded
        g2z[0, 2, :, at] = roll_z(grad, 1, nz).astype(BF16)

    columns = all_taps(g2z, nz, lanes)
    for x in range(0, planes, group):
        at = slice(x * lanes, (x + group) * lanes)
        mid[...] += dot_nt(jnp.concatenate(columns[x : x + group], 1), hidden[:, at])

    @pl.when(s == samples - 1)
    def _():
        total = mid[...]
        taps = total.shape[0]
        piece[0:taps] = total.astype(BF16)
        squares = jnp.sum(total * total, keepdims=True)
        high = squares.astype(BF16).astype(F32)
        width = total.shape[1]
        row = lax.broadcasted_iota(jnp.int32, (block, width), 0)
        column = lax.broadcasted_iota(jnp.int32, (block, width), 1)
        extra = jnp.concatenate([last[...], jnp.zeros((block, width - block), F32)], 1)
        extra = jnp.where(row < 5, extra, 0.0)
        extra = jnp.where((row == 8) & (column == 0), high, extra)
        extra = jnp.where((row == 8) & (column == 1), squares - high, extra)
        piece[taps:] = extra.astype(BF16)


def first_kernel(nz, lanes, w_first, w_back, fcol, g2z, out):
    @pl.when(pl.program_id(0) == 0)
    def _():
        out[...] = jnp.zeros_like(out)

    columns = all_taps(g2z, nz, lanes)
    group = 2
    for x in range(0, len(columns), group):
        at = slice(x * lanes, (x + group) * lanes)
        back = dot(w_back[...], jnp.concatenate(columns[x : x + group], 1))
        column = fcol[0, :, at]
        pre = dot(w_first[...], column)
        sig = logistic(pre)
        grad = (back * (sig * (1.0 + pre * (1.0 - sig)))).astype(BF16)
        out[...] += dot_nt(column, grad)


def split_kernel(core, one, two, closure, message, keep, kept):
    half = keep.shape[0]
    mine = pl.multiple_of(core[0] * half, half)
    theirs = pl.multiple_of((1 - core[0]) * half, half)
    keep[...] = one[pl.ds(mine, half)] + two[pl.ds(mine, half)]
    message[0:half] = (one[pl.ds(theirs, half)] + two[pl.ds(theirs, half)]).astype(BF16)
    samples, planes = closure.shape[:2]
    at = 0
    for s in range(samples):
        for y in range(planes // 4):
            for p in range(2):
                kept[at : at + 16] = closure[s, 4 * y + 2 * core[0] + p].astype(F32)
                message[half + at : half + at + 16] = closure[s, 4 * y + 2 * (1 - core[0]) + p]
                at += 16


def merge_kernel(bit, got, mine, kept, message, keep):
    half = 128
    message[0:half] = (mine[0:half].astype(F32) + got[0:half].astype(F32)).astype(BF16)
    for o in range(keep.shape[0] // 32):
        a = pl.multiple_of((2 * o + bit[0]) * 32, 32)
        b = pl.multiple_of((2 * o + 1 - bit[0]) * 32, 32)
        keep[o * 32 : o * 32 + 32] = kept[pl.ds(a, 32)] + got[pl.ds(half + a, 32)].astype(F32)
        message[half + o * 32 : half + o * 32 + 32] = (
            kept[pl.ds(b, 32)] + got[pl.ds(half + b, 32)].astype(F32)
        ).astype(BF16)


def total_kernel(got, mine, kept, half, closure):
    half[...] = (mine[0:128].astype(F32) + got[0:128].astype(F32)).astype(BF16)
    closure[...] = kept[...] + got[128:].astype(F32)


def step_kernel(nz, place, fields, drag, closure, feats, out):
    state = flat_cells(fields)
    cells = state.shape[1]
    planes, rows = fields.shape[2], fields.shape[3]
    lanes = cells // planes
    lower = feats[place[0]][8:13, cells - lanes :].astype(F32)
    upper = feats[place[1]][8:13, :lanes].astype(F32)
    wide = jnp.concatenate([lower, state, upper], 1)
    next_x, last_x = wide[:, 2 * lanes :], wide[:, :cells]
    parts = [state[:, i * lanes : (i + 1) * lanes] for i in range(planes)]
    next_y = jnp.concatenate([ahead_y(v, 1, nz) for v in parts], 1)
    last_y = jnp.concatenate([ahead_y(v, -1, nz) for v in parts], 1)
    next_z, last_z = roll_z(state, -1, nz), roll_z(state, 1, nz)
    laplace = next_x + last_x + next_y + last_y + next_z + last_z - 6.0 * state
    advect = -0.5 * (
        state[0:1] * (next_x - last_x) + state[1:2] * (next_y - last_y) + state[2:3] * (next_z - last_z)
    )
    momentum = jnp.concatenate([drag[...], jnp.zeros((2, cells), F32)], 0)
    closed = jnp.concatenate([closure[k : k + 5] for k in range(0, closure.shape[0], 8)], 1)
    new = state + dt_step * (viscosity * laplace + advect + closed + momentum)
    for x in range(planes):
        for y in range(rows):
            at = (x * rows + y) * nz
            out[0, :, x, y, :] = new[:, at : at + nz]


def finish_kernel(count, weight_count, place, core, *refs):
    pieces, (own, other, mid_out, first_out, last_out, held, sems, factor) = refs[:count], refs[count:]
    step = pl.program_id(0)
    taps_here = mid_out.shape[0]
    slots = held.shape[0]
    block = mid_out.shape[1] // slots
    rows = held.shape[1] - 16

    @pl.when(step == 0)
    def _():
        copies, at = [], 0
        for i, ref in enumerate(pieces):
            copies.append(pltpu.make_async_copy(ref, held.at[at : at + ref.shape[0]], sems.at[i]))
            at += ref.shape[0]
        for copy in copies:
            copy.start()
        a, b = own[...].astype(F32), other[...].astype(F32)
        swapped = core[0] == 1
        raw = jnp.concatenate([jnp.where(swapped, b, a), jnp.where(swapped, a, b)], 0)
        squares = jnp.sum(raw * raw, keepdims=True)
        ordered = dot(tap_rows(), raw.astype(BF16))
        for copy in copies:
            copy.wait()
        last = []
        for d in range(slots):
            extra = held[place[d], rows:].astype(F32)
            last.append(extra[0:5, 0:block])
            squares = squares + jnp.sum(extra[8:9, 0:2], keepdims=True)
        last = jnp.concatenate(last, 1)
        squares = squares + jnp.sum(last * last, keepdims=True)
        clip = jnp.minimum(1.0, clip_rms * math.sqrt(weight_count) / jnp.sqrt(squares + 1e-06))
        factor[...] = jnp.broadcast_to(clip, factor.shape)
        last_out[...] = last * clip
        ordered = ordered * clip
        for c in range(first_out.shape[0]):
            first_out[c] = ordered[32 * c : 32 * c + 27]

    width = mid_out.shape[1]
    eye = (
        lax.broadcasted_iota(jnp.int32, (width, width), 0) == lax.broadcasted_iota(jnp.int32, (width, width), 1)
    ).astype(F32).astype(BF16)
    clip = factor[0:1, 0:1]
    for i in range(taps_here):
        start = pl.multiple_of((step * taps_here + i) * block, block)
        flipped = jnp.concatenate([held[place[d], pl.ds(start, block)] for d in range(slots)], 0)
        mid_out[i] = dot_nt(eye, flipped) * clip


def whole_spec(shape):
    return pl.BlockSpec(shape, lambda *unused: (0,) * len(shape))


SMEM = pl.BlockSpec(memory_space=pltpu.SMEM)
VMEM = pl.BlockSpec(memory_space=pltpu.VMEM)
ANY = pl.BlockSpec(memory_space=pl.ANY)


def cost(flops):
    return pl.CostEstimate(flops=int(flops), bytes_accessed=2**22, transcendentals=0)


def params(**more):
    return pltpu.CompilerParams(vmem_limit_bytes=VMEM_BYTES, **more)


def shards(
    fields, drop_mass, drop_vel, drop_cell, cross_list, cross_count, w_in, w_mid, w_out, cotangent
):
    shape = jax.ShapeDtypeStruct
    n_slab, n_rep = lax.axis_size("slab"), lax.axis_size("rep")
    planes, ny, nz = fields.shape[2:]
    cells = planes * ny * nz
    lanes = ny * nz
    hid, cout = w_out.shape
    joined = n_slab * n_rep * 16 <= hid
    team = ("slab", "rep") if joined else ("slab",)
    samples = n_rep if joined else 1
    size = n_slab * samples
    block = hid // size
    fast = joined and n_slab == 4 and n_rep == 4
    slab, rep = lax.axis_index("slab"), lax.axis_index("rep")
    sample = rep if joined else jnp.zeros((), jnp.int32)
    me = slab * samples + sample
    all_planes = n_slab * planes
    everyone = jnp.arange(size, dtype=jnp.int32)

    def trade(v, mask):
        return lax.ppermute(v, team, [(d, d ^ mask) for d in range(size)])

    dense = shape((4, cells), F32)
    stay, up, down = pl.pallas_call(
        deposit_kernel,
        out_shape=(dense, dense, dense),
        in_specs=[VMEM] * 4 + [SMEM],
        out_specs=(VMEM,) * 3,
        compiler_params=params(),
        name="deposit",
    )(drop_mass, jnp.transpose(drop_vel, (1, 0, 2)), drop_cell, cross_list, cross_count)
    from_below = lax.ppermute(up, "slab", [(i, (i + 1) % n_slab) for i in range(n_slab)])
    from_above = lax.ppermute(down, "slab", [((i + 1) % n_slab, i) for i in range(n_slab)])
    own_feats, drag = pl.pallas_call(
        feature_kernel,
        out_shape=(shape((16, cells), BF16), shape((3, cells), F32)),
        in_specs=[VMEM] * 5,
        out_specs=(VMEM,) * 2,
        compiler_params=params(),
        name="features",
    )(stay, from_below, from_above, fields, cotangent)

    if fast:
        order = (8, 2, 1, 4)
        feats = own_feats[None]
        for mask in order:
            feats = jnp.concatenate([feats, trade(feats, mask)], 0)
        apart = me ^ everyone
        feat_place = sum(((apart & mask) != 0).astype(jnp.int32) << i for i, mask in enumerate(order))
    else:
        feats = lax.all_gather(own_feats, team)
        feat_place = everyone

    rows = 27 * block
    wt, w_back, w_first, wo, wc = pl.pallas_call(
        weight_kernel,
        out_shape=(
            shape((rows, hid), BF16),
            shape((hid, rows), BF16),
            shape((hid, 256), BF16),
            shape((block, 16), BF16),
            shape((16, block), BF16),
        ),
        in_specs=[SMEM] + [VMEM] * 3,
        out_specs=(VMEM,) * 5,
        compiler_params=params(),
        cost_estimate=cost(1.5e9),
        name="weights",
    )(me[None], jnp.transpose(w_in, (1, 0, 2)), w_mid, w_out.T)

    team_cells = all_planes * lanes
    piece, closure, g2z, fcol = pl.pallas_call(
        functools.partial(closure_kernel, nz, lanes),
        grid=(samples,),
        out_shape=(
            shape((rows + 16, hid), BF16),
            shape((samples, all_planes, 16, lanes // 2), BF16),
            shape((samples, 3, block, team_cells), BF16),
            shape((samples, 256, team_cells), BF16),
        ),
        in_specs=[SMEM] + [VMEM] * 5,
        out_specs=(
            whole_spec((rows + 16, hid)),
            pl.BlockSpec((1, all_planes, 16, lanes // 2), lambda s: (s, 0, 0, 0)),
            pl.BlockSpec((1, 3, block, team_cells), lambda s: (s, 0, 0, 0)),
            pl.BlockSpec((1, 256, team_cells), lambda s: (s, 0, 0)),
        ),
        scratch_shapes=[
            pltpu.VMEM((3, 16, team_cells), F32),
            pltpu.VMEM((8, team_cells), F32),
            pltpu.VMEM((8, team_cells), F32),
            pltpu.VMEM((hid, team_cells), BF16),
            pltpu.VMEM((3, block, team_cells), F32),
            pltpu.VMEM((rows, hid), F32),
            pltpu.VMEM((16, block), F32),
        ],
        compiler_params=params(),
        cost_estimate=cost(9e9),
        name="closure",
    )(feat_place, feats, w_first, wt, wo, wc)

    def first_part(lo, count, fcol, g2z):
        return pl.pallas_call(
            functools.partial(first_kernel, nz, lanes),
            grid=(count,),
            out_shape=shape((256, hid), F32),
            in_specs=[
                whole_spec((hid, 256)),
                whole_spec((hid, rows)),
                pl.BlockSpec((1, 256, team_cells), lambda s: (s + lo, 0, 0)),
                pl.BlockSpec((1, 3, block, team_cells), lambda s: (s + lo, 0, 0, 0)),
            ],
            out_specs=whole_spec((256, hid)),
            compiler_params=params(),
            cost_estimate=cost(7.6e9 * count / samples),
            name="first",
        )(w_first, w_back, fcol, g2z)

    if fast:
        z = rep
        outer = (z == 0) | (z == 3)

        def line(v, pairs):
            return lax.ppermute(v, "rep", pairs)

        def tie(*values):
            return lax.optimization_barrier(values)

        core, y = slab & 1, slab >> 1
        y0 = trade(piece, 8)
        p1 = line(piece, [(0, 1), (1, 0), (2, 3), (3, 2)])
        p2 = line(piece, [(1, 2), (2, 1)])
        half_one = first_part(0, samples // 2, fcol, g2z)
        y0, p1, p2, half_one, fcol, g2z = tie(y0, p1, p2, half_one, fcol, g2z)
        p4 = line(p2, [(1, 0), (2, 3)])
        p3 = line(p1, [(1, 2), (2, 1)])
        y1 = trade(p1, 8)
        half_two = first_part(samples // 2, samples - samples // 2, fcol, g2z)

        def exchanged(count):
            return (shape((128 + 32 * count, hid), BF16), shape((32 * count, hid), F32))

        message, keep, kept = pl.pallas_call(
            split_kernel,
            out_shape=(exchanged(8)[0], shape((128, hid), F32), exchanged(8)[1]),
            in_specs=[SMEM] + [VMEM] * 3,
            out_specs=(VMEM,) * 3,
            compiler_params=params(),
            name="split",
        )(core[None], half_one, half_two, closure)
        y1, p3, p4, message = tie(y1, p3, p4, message)
        got = trade(message, 4)
        q2 = jnp.where(outer, p4, p2)
        y2 = trade(q2, 8)
        p5 = line(p3, [(1, 0), (2, 3)])
        c0 = trade(jnp.stack([piece, y0, p1, y1]), 4)

        def merge(count, bit, got, mine, kept):
            return pl.pallas_call(
                merge_kernel,
                out_shape=exchanged(count),
                in_specs=[SMEM] + [VMEM] * 3,
                out_specs=(VMEM,) * 2,
                compiler_params=params(),
                name="merge",
            )(bit[None], got, mine, kept)

        message, kept = merge(4, y, got, keep, kept)
        got = trade(message, 8)
        y2, p5, c0, got = tie(y2, p5, c0, got)
        q3 = jnp.where(outer, p5, p3)
        y3 = trade(q3, 8)
        c1 = trade(jnp.stack([q2, y2, q3]), 4)
        message, kept = merge(2, z & 1, got, message, kept)
        got = trade(message, 1)
        message, kept = merge(1, z >> 1, got, message, kept)
        got = trade(message, 2)
        own, own_closure = pl.pallas_call(
            total_kernel,
            out_shape=(shape((128, hid), BF16), shape((32, hid), F32)),
            in_specs=[VMEM] * 3,
            out_specs=(VMEM,) * 2,
            compiler_params=params(),
            name="total",
        )(got, message, kept)
        other = trade(own, 4)
        c2 = trade(y3, 4)
        pieces = [v[None] for v in (piece, y0, p1, y1, q2, y2, q3, y3)] + [c0, c1, c2[None]]
        m2 = jnp.where(outer, 2, 3)
        masks = jnp.stack([jnp.int32(0), jnp.int32(8), jnp.int32(1), jnp.int32(9), m2, m2 | 8, m2 ^ 1, (m2 ^ 1) | 8])
        masks = jnp.concatenate([masks, masks | 4])
        piece_place = jnp.argmax((me ^ everyone)[:, None] == masks[None, :], axis=1).astype(jnp.int32)
    else:
        raw_first = first_part(0, samples, fcol, g2z)
        core = jnp.zeros((), jnp.int32)
        if not joined:
            raw_first = lax.psum(raw_first, "rep")
            body = lax.psum(piece[:rows].astype(F32), "rep")
            extra = lax.psum(piece[rows:].astype(F32), "rep")
            squares = jnp.sum(body * body)
            high = squares.astype(BF16).astype(F32)
            extra = extra.at[8, 0].set(high).at[8, 1].set(squares - high)
            piece = jnp.concatenate([body, extra], 0).astype(BF16)
        raw_first = lax.psum(raw_first, team).astype(BF16)
        own, other = raw_first[:128], raw_first[128:]
        pieces = [lax.all_gather(piece, team)]
        piece_place = everyone
        part = closure.reshape(samples, n_slab, planes * 16, lanes // 2)
        part = jnp.swapaxes(part, 0, 1).reshape(size, planes * 16, lanes // 2).astype(F32)
        own_closure = lax.psum_scatter(part, team, scatter_dimension=0)

    near = jnp.stack([(slab + n_slab - 1) % n_slab, (slab + 1) % n_slab]) * samples + sample
    new_fields = pl.pallas_call(
        functools.partial(step_kernel, nz),
        out_shape=shape(fields.shape, F32),
        in_specs=[SMEM] + [VMEM] * 4,
        out_specs=VMEM,
        compiler_params=params(),
        name="step",
    )(jnp.take(feat_place, near), fields, drag, own_closure, feats)

    weight_count = w_in.size + w_mid.size + w_out.size
    step_taps = 3
    grad_middle, grad_first, grad_last = pl.pallas_call(
        functools.partial(finish_kernel, len(pieces), weight_count),
        grid=(27 // step_taps,),
        out_shape=(shape((27, hid, hid), F32), shape((9, 27, hid), F32), shape((cout, hid), F32)),
        in_specs=[SMEM] * 2 + [ANY] * len(pieces) + [whole_spec((128, hid))] * 2,
        out_specs=(
            pl.BlockSpec((step_taps, hid, hid), lambda i: (i, 0, 0)),
            whole_spec((9, 27, hid)),
            whole_spec((cout, hid)),
        ),
        scratch_shapes=[
            pltpu.VMEM((size, rows + 16, hid), BF16),
            pltpu.SemaphoreType.DMA((len(pieces),)),
            pltpu.VMEM((8, 128), F32),
        ],
        compiler_params=params(),
        name="finish",
    )(piece_place, core[None], *pieces, own, other)
    return (new_fields, jnp.transpose(grad_first, (1, 0, 2)), grad_middle, grad_last.T)


def solution(mesh):
    placed = (
        P(("groups", "rep"), None, "slab", None, None),
        P(("groups", "rep"), "slab"),
        P(("groups", "rep"), None, "slab"),
        P(("groups", "rep"), "slab"),
        P(("groups", "rep"), "slab"),
        P(("groups", "rep"), "slab"),
        P(),
        P(),
        P(),
        P(("groups", "rep"), None, "slab", None, None),
    )
    return jax.shard_map(
        shards,
        mesh=mesh,
        in_specs=placed,
        out_specs=(
            P(("groups", "rep"), None, "slab", None, None),
            P("groups", None, None),
            P("groups", None, None),
            P("groups", None),
        ),
        check_vma=False,
    )
```

time: 175 us -> 132 us (0.75)
  local copies, waits for them, and re-layouts: 24.7 us -> 5.93 us
  other arithmetic: 22.4 us -> 5.51 us
  Pallas kernels: 76.3 us -> 68.1 us
  waiting for transfers between devices: 20.5 us -> 25.4 us
  starting transfers between devices: 29.1 us -> 24.9 us
    pallas_call x2 -> x9, Pallas kernels: 61.3 us -> 53.2 us  [the longest x1 23.4 us: shards(): pl.pallas_call(functools.partial(closure_kernel, nz, lanes), grid=(sample...]
    slice x6 -> x0, local copies, waits for them, and re-layouts: 6.72 us -> none  [the longest x2 3.17 us: shards(): w_in[:, :8].reshape(216, hid)]
    convert_element_type x12 -> x0, other arithmetic: 6.6 us -> none  [the longest x4 2.85 us: shards(): got = trade(message, mask).astype(F32)]
    unnamed x44, local copies, waits for them, and re-layouts: 10.8 us -> 5.11 us
    transpose x3 -> x0, local copies, waits for them, and re-layouts: 4.26 us -> none  [the longest x2 4.19 us: shards(): wt = jnp.transpose(w_block, (0, 2, 1)).reshape(27 * block, hid)]
    add x5 -> x0, other arithmetic: 3.61 us -> none  [the longest x4 3.6 us: shards(): part = keep + got[128:].reshape(keep.shape)]
    concatenate x6 -> x0, other arithmetic: 3.5 us -> none  [the longest x4 2.01 us: shards(): jnp.concatenate([raw_send.astype(BF16), send.astype(BF16).reshape(-1, lan...]
    ppermute x16, starting transfers between devices: 19.3 us -> 17 us  [trade(): return lax.ppermute(v, team, [(d, d ^ mask) for d in range(size)])]
  transfers between devices with their start and end apart: 23 -> 23, of which waited for: 10 -> 9; matrix products, arithmetic and copies ran while one was open for 15% -> 3% of each run, Pallas kernels for 1% -> 24%
where the time goes in v1:
time: 132 us; the launch traced here: 131 us
  Pallas kernels  68.1 us (52%)
  waiting for transfers between devices  25.4 us (19%)
  starting transfers between devices  24.9 us (19%)
  local copies, waits for them, and re-layouts  5.93 us (4%)
  other arithmetic  5.51 us (4%)
    pallas_call x1, Pallas kernels, shards(): pl.pallas_call(functools.partial(closure_kernel, nz, lanes), grid=(sample...  23.4 us
    pallas_call x2, Pallas kernels, first_part(): pl.pallas_call(functools.partial(first_kernel, nz, lanes), grid=(count,),...  17.2 us
    ppermute x16, starting transfers between devices, trade(): return lax.ppermute(v, team, [(d, d ^ mask) for d in range(size)])  17 us
    ppermute x16, waiting for transfers between devices, trade(): return lax.ppermute(v, team, [(d, d ^ mask) for d in range(size)])  16.9 us
    pallas_call x1, Pallas kernels, shards(): pl.pallas_call(functools.partial(finish_kernel, len(pieces), weight_count...  9.33 us
    ppermute x5, waiting for transfers between devices, line(): return lax.ppermute(v, 'rep', pairs)  6.88 us
    ppermute x5, starting transfers between devices, line(): return lax.ppermute(v, 'rep', pairs)  5.5 us
    pallas_call x3, Pallas kernels, merge(): pl.pallas_call(merge_kernel, out_shape=exchanged(count), in_specs=[SMEM]...  5.17 us
  transfers between devices with their start and end apart: 23, of which 9 were waited for; matrix products, arithmetic and copies ran while one was open for 3% of the time, Pallas kernels for 24%

profile of v1, /device:TPU:0, one launch (start us, length us, event | category | flops | bytes accessed | tf_op | source)
XLA Modules:
  0.0 131.1 jit_solution(411302293861344369)
XLA Ops:
  0.6 2.3 %deposit.1 = (f32[4,1024]{1,0:T(4,128)}, f32[4,1024]{1,0:T(4,128)}, f32[4,1024]{1,0:T(4,128)}) custom-call(f32[1,1024]{1,0:T(1,128)} %mass.1, f32[3,1,1024]{2,1,0:T(1,128)} %bitcast.51, s32[1,1024]{1,0:T(1,128)} %cell.1, s32[1,256]{1,0:T(1,128)} %listed.1, s32[1,2]{1,0:T(1,128)} %counts.1), custom_call_target="tpu_custom_call" | custom-call | tf_op jit(solution)/shard_map/deposit/pallas_call | solution.py:406
  2.9 0.5 collective-permute-start
  3.4 2.0 %collective-permute-start.1 = (f32[4,1024]{1,0:T(4,128)}, f32[4,1024]{1,0:T(4,128)S(1)}, u32[]{:S(2)}, u32[]{:S(2)}) collective-permute-start(f32[4,1024]{1,0:T(4,128)} %get-tuple-element.49), channel_id=1, source_target_pairs={{4,0},{8,4},{12,8},{0,12},{5,1},{9,5},{13,9},{1,13},{6,2},{10,6},{... | collective-permute-start | bytes 49160 | tf_op jit(solution)/shard_map/ppermute | solution.py:415
  5.3 1.6 %collective-permute-done.below = f32[4,1024]{1,0:T(4,128)S(1)} collective-permute-done((f32[4,1024]{1,0:T(4,128)}, f32[4,1024]{1,0:T(4,128)S(1)}, u32[]{:S(2)}, u32[]{:S(2)}) %collective-permute-start) | collective-permute-done | bytes 16416 | tf_op jit(solution)/shard_map/ppermute | solution.py:414
  7.0 0.6 copy-done.18
  7.6 0.0 copy-done.19
  7.6 1.5 %features.1 = (bf16[16,1024]{1,0:T(8,128)(2,1)}, f32[3,1024]{1,0:T(4,128)}) custom-call(f32[4,1024]{1,0:T(4,128)} %get-tuple-element.47.stay, f32[4,1024]{1,0:T(4,128)} %copy-done.18, f32[4,1024]{1,0:T(4,128)} %copy-done.19, f32[1,5,2,4,128]{4,3,2,1,0:T(4,128)} %fields.3, f32[1,5,2,4,128]{4,3,2,1,0:T(4,128)} %cotangent.1), custom_call_target="tpu_custom_call" | custom-call | tf_op jit(solution)/shard_map/features/pallas_call | solution.py:416
  9.0 2.4 %collective-permute-start.2 = (bf16[1,16,1024]{2,1,0:T(8,128)(2,1)}, bf16[1,16,1024]{2,1,0:T(8,128)(2,1)S(1)}, u32[]{:S(2)}, u32[]{:S(2)}) collective-permute-start(bf16[1,16,1024]{2,1,0:T(8,128)(2,1)} %bitcast.45), channel_id=1, source_target_pairs={{0,8},{1,9},{2,10},{3,11},{4,12},{5,13},{6,14},{7,15},{8,0},{9,1},... | collective-permute-start | bytes 98312 | tf_op jit(solution)/shard_map/ppermute | solution.py:403
  11.5 3.9 %weights.1 = (bf16[432,256]{1,0:T(8,128)(2,1)}, bf16[256,432]{1,0:T(8,128)(2,1)}, bf16[256,256]{1,0:T(8,128)(2,1)}, bf16[16,16]{1,0:T(8,128)(2,1)}, bf16[16,16]{1,0:T(8,128)(2,1)}) custom-call(s32[1]{0:T(128)} %bitcast.9.me, bf16[9,27,256]{2,1,0:T(8,128)(2,1)} %bitcast.53, bf16[27,256,256]{2,1,0:T(8,128)(2,1)} %w_mid.1, bf16[5,256]{1,0:T(8,128)(2,1)} %bitcast.55), custom_call_target="tpu_custom_call" | custom-call | flops 1500000000 | bytes 4194304 | tf_op jit(solution)/shard_map/weights/pallas_call | solution.py:437
  15.4 0.8 pad_maximum_fusion.4
  16.2 2.5 %collective-permute-start.3 = (bf16[2,16,1024]{2,1,0:T(8,128)(2,1)S(1)}, bf16[2,16,1024]{2,1,0:T(8,128)(2,1)S(1)}, u32[]{:S(2)}, u32[]{:S(2)}) collective-permute-start(bf16[2,16,1024]{2,1,0:T(8,128)(2,1)S(1)} %pad_maximum_fusion.4), channel_id=1, source_target_pairs={{0,2},{1,3},{2,0},{3,1},{4,6},{5,7},{6,4},{7,5},{8,10},{9,11},{10,... | collective-permute-start | bytes 196616 | tf_op jit(solution)/shard_map/ppermute | solution.py:403
  18.6 0.6 fusion.6.place
  19.2 3.5 %collective-permute-done.3 = bf16[2,16,1024]{2,1,0:T(8,128)(2,1)S(1)} collective-permute-done((bf16[2,16,1024]{2,1,0:T(8,128)(2,1)S(1)}, bf16[2,16,1024]{2,1,0:T(8,128)(2,1)S(1)}, u32[]{:S(2)}, u32[]{:S(2)}) %collective-permute-start.3) | collective-permute-done | bytes 65568 | tf_op jit(solution)/shard_map/ppermute | solution.py:403
  22.7 0.8 pad_maximum_fusion.3
  23.5 0.7 collective-permute-start.4
  24.2 0.8 constant_dynamic-update-slice_fusion.4
  24.9 3.6 %collective-permute-done.4 = bf16[4,16,1024]{2,1,0:T(8,128)(2,1)S(1)} collective-permute-done((bf16[4,16,1024]{2,1,0:T(8,128)(2,1)S(1)}, bf16[4,16,1024]{2,1,0:T(8,128)(2,1)S(1)}, u32[]{:S(2)}, u32[]{:S(2)}) %collective-permute-start.4) | collective-permute-done | bytes 131104 | tf_op jit(solution)/shard_map/ppermute | solution.py:403
  28.5 0.8 pad_maximum_fusion.2
  29.3 0.1 collective-permute-start.5
  29.5 1.5 %collective-permute-done.5 = bf16[8,16,1024]{2,1,0:T(8,128)(2,1)S(1)} collective-permute-done((bf16[8,16,1024]{2,1,0:T(8,128)(2,1)S(1)}, bf16[8,16,1024]{2,1,0:T(8,128)(2,1)S(1)}, u32[]{:S(2)}, u32[]{:S(2)}) %collective-permute-start.5) | collective-permute-done | bytes 262176 | tf_op jit(solution)/shard_map/ppermute | solution.py:403
  31.0 0.8 copy-done.10
  31.8 23.4 %closure.1 = (bf16[448,256]{1,0:T(8,128)(2,1)}, bf16[4,8,16,256]{3,2,1,0:T(8,128)(2,1)}, bf16[4,3,16,4096]{3,2,1,0:T(8,128)(2,1)}, bf16[4,256,4096]{2,1,0:T(8,128)(2,1)}) custom-call(s32[16]{0:T(128)} %fusion.6.place, bf16[16,16,1024]{2,1,0:T(8,128)(2,1)} %copy-done.10, bf16[256,256]{1,0:T(8,128)(2,1)} %get-tuple-element.52.w_first, ...), custom_call_target="tpu_custom_call" | custom-call | flops 8999999488 | bytes 4194304 | tf_op jit(solution)/shard_map/closure/pallas_call | solution.py:454
  55.2 1.0 collective-permute-start.6
  56.2 1.3 collective-permute-start.7
  57.5 0.7 collective-permute-start.8
  58.2 8.6 %first.2.one = f32[256,256]{1,0:T(8,128)} custom-call(bf16[256,256]{1,0:T(8,128)(2,1)} %get-tuple-element.52.w_first, bf16[256,432]{1,0:T(8,128)(2,1)} %get-tuple-element.57.w_back, bf16[4,256,4096]{2,1,0:T(8,128)(2,1)} %get-tuple-element.63.fcol, bf16[4,3,16,4096]{3,2,1,0:T(8,128)(2,1)} %get-tuple-element.64.g2z), custom_call_target="tpu_custom_call" | custom-call | flops 3800000000 | bytes 4194304 | tf_op jit(solution)/shard_map/first/pallas_call | solution.py:485
  66.9 0.8 collective-permute-start.10
  67.7 0.8 collective-permute-start.9
  68.5 1.5 %collective-permute-start.11 = (bf16[448,256]{1,0:T(8,128)(2,1)S(1)}, bf16[448,256]{1,0:T(8,128)(2,1)S(1)}, u32[]{:S(2)}, u32[]{:S(2)}) collective-permute-start(bf16[448,256]{1,0:T(8,128)(2,1)S(1)} %collective-permute-done.8), channel_id=1, source_target_pairs={{1,0},{2,3},{5,4},{6,7},{9,8},{10,11},{13,12},{14,15},{17,16},{18,... | collective-permute-start | bytes 688136 | tf_op jit(solution)/shard_map/ppermute | solution.py:506
  70.0 8.6 %first.3.two = f32[256,256]{1,0:T(8,128)} custom-call(bf16[256,256]{1,0:T(8,128)(2,1)} %get-tuple-element.52.w_first, bf16[256,432]{1,0:T(8,128)(2,1)} %get-tuple-element.57.w_back, bf16[4,256,4096]{2,1,0:T(8,128)(2,1)} %get-tuple-element.63.fcol, bf16[4,3,16,4096]{3,2,1,0:T(8,128)(2,1)} %get-tuple-element.64.g2z), custom_call_target="tpu_custom_call" | custom-call | flops 3800000000 | bytes 4194304 | tf_op jit(solution)/shard_map/first/pallas_call | solution.py:485
  78.6 2.0 %split.1 = (bf16[384,256]{1,0:T(8,128)(2,1)}, f32[128,256]{1,0:T(8,128)}, f32[256,256]{1,0:T(8,128)}) custom-call(s32[1]{0:T(128)} %bitcast.12.core, f32[256,256]{1,0:T(8,128)} %first.2.one, f32[256,256]{1,0:T(8,128)} %first.3.two, bf16[4,8,16,256]{3,2,1,0:T(8,128)(2,1)} %get-tuple-element.65.closure), custom_call_target="tpu_custom_call" | custom-call | tf_op jit(solution)/shard_map/split/pallas_call | solution.py:525
  80.6 0.4 collective-permute-done.11
  81.0 0.1 pad_maximum_fusion
  81.1 0.1 collective-permute-start.14
  81.2 0.5 collective-permute-start.15
  81.8 1.3 collective-permute-start.12
  83.0 1.3 collective-permute-start.13
  84.3 0.1 stack.66
  84.4 0.7 copy-done.13
  85.1 1.8 %merge.3 = (bf16[256,256]{1,0:T(8,128)(2,1)}, f32[128,256]{1,0:T(8,128)}) custom-call(s32[1]{0:T(128)} %bitcast.17.bit, bf16[384,256]{1,0:T(8,128)(2,1)} %copy-done.13, f32[128,256]{1,0:T(8,128)} %get-tuple-element.72.mine, f32[256,256]{1,0:T(8,128)} %get-tuple-element.73.kept), custom_call_target="tpu_custom_call" | custom-call | tf_op jit(solution)/shard_map/merge/pallas_call | solution.py:541
  86.9 0.8 collective-permute-start.16
  87.8 1.7 %collective-permute-done.12 = bf16[448,256]{1,0:T(8,128)(2,1)S(1)} collective-permute-done((bf16[448,256]{1,0:T(8,128)(2,1)S(1)}, bf16[448,256]{1,0:T(8,128)(2,1)S(1)}, u32[]{:S(2)}, u32[]{:S(2)}) %collective-permute-start.12) | collective-permute-done | bytes 229408 | tf_op jit(solution)/shard_map/ppermute | solution.py:403
  89.4 6.5 %collective-permute-done.13 = bf16[448,256]{1,0:T(8,128)(2,1)S(1)} collective-permute-done((bf16[448,256]{1,0:T(8,128)(2,1)S(1)}, bf16[448,256]{1,0:T(8,128)(2,1)S(1)}, u32[]{:S(2)}, u32[]{:S(2)}) %collective-permute-start.13) | collective-permute-done | bytes 229408 | tf_op jit(solution)/shard_map/ppermute | solution.py:506
  95.9 1.0 pad_maximum_fusion.1
  97.0 0.1 concatenate.32
  97.1 0.9 collective-permute-start.19
  97.9 0.7 iota_reduce_fusion
  98.6 1.7 %merge.4 = (bf16[192,256]{1,0:T(8,128)(2,1)}, f32[64,256]{1,0:T(8,128)}) custom-call(s32[1]{0:T(128)} %bitcast.7.bit, bf16[256,256]{1,0:T(8,128)(2,1)} %copy-done.14, bf16[256,256]{1,0:T(8,128)(2,1)} %get-tuple-element.74.mine, f32[128,256]{1,0:T(8,128)} %get-tuple-element.76.kept), custom_call_target="tpu_custom_call" | custom-call | tf_op jit(solution)/shard_map/merge/pallas_call | solution.py:541
  100.4 2.8 %collective-permute-start.17 = (bf16[192,256]{1,0:T(8,128)(2,1)}, bf16[192,256]{1,0:T(8,128)(2,1)S(1)}, u32[]{:S(2)}, u32[]{:S(2)}) collective-permute-start(bf16[192,256]{1,0:T(8,128)(2,1)} %get-tuple-element.77.mine), channel_id=1, source_target_pairs={{0,1},{1,0},{2,3},{3,2},{4,5},{5,4},{6,7},{7,6},{8,9},{9,8},{10,11... | collective-permute-start | bytes 294920 | tf_op jit(solution)/shard_map/ppermute | solution.py:403
  103.2 0.1 fusion.7
  103.3 3.3 %collective-permute-done.17.got = bf16[192,256]{1,0:T(8,128)(2,1)S(1)} collective-permute-done((bf16[192,256]{1,0:T(8,128)(2,1)}, bf16[192,256]{1,0:T(8,128)(2,1)S(1)}, u32[]{:S(2)}, u32[]{:S(2)}) %collective-permute-start.17) | collective-permute-done | bytes 98336 | tf_op jit(solution)/shard_map/ppermute | solution.py:403
  106.6 0.6 copy-done.15
  107.2 1.6 %merge.5 = (bf16[160,256]{1,0:T(8,128)(2,1)}, f32[32,256]{1,0:T(8,128)}) custom-call(s32[1]{0:T(128)} %bitcast.6.bit, bf16[192,256]{1,0:T(8,128)(2,1)} %copy-done.15, bf16[192,256]{1,0:T(8,128)(2,1)} %get-tuple-element.77.mine, f32[64,256]{1,0:T(8,128)} %get-tuple-element.78.kept), custom_call_target="tpu_custom_call" | custom-call | tf_op jit(solution)/shard_map/merge/pallas_call | solution.py:541
  108.8 3.2 %collective-permute-start.18 = (bf16[160,256]{1,0:T(8,128)(2,1)}, bf16[160,256]{1,0:T(8,128)(2,1)S(1)}, u32[]{:S(2)}, u32[]{:S(2)}) collective-permute-start(bf16[160,256]{1,0:T(8,128)(2,1)} %get-tuple-element.79.mine), channel_id=1, source_target_pairs={{0,2},{1,3},{2,0},{3,1},{4,6},{5,7},{6,4},{7,5},{8,10},{9,11},{10,... | collective-permute-start | bytes 245768 | tf_op jit(solution)/shard_map/ppermute | solution.py:403
  112.0 0.6 gather_fusion
  112.7 3.3 %collective-permute-done.18.got = bf16[160,256]{1,0:T(8,128)(2,1)S(1)} collective-permute-done((bf16[160,256]{1,0:T(8,128)(2,1)}, bf16[160,256]{1,0:T(8,128)(2,1)S(1)}, u32[]{:S(2)}, u32[]{:S(2)}) %collective-permute-start.18) | collective-permute-done | bytes 81952 | tf_op jit(solution)/shard_map/ppermute | solution.py:403
  116.0 0.6 copy-done.16
  116.6 1.6 %total.1 = (bf16[128,256]{1,0:T(8,128)(2,1)}, f32[32,256]{1,0:T(8,128)}) custom-call(bf16[160,256]{1,0:T(8,128)(2,1)} %copy-done.16, bf16[160,256]{1,0:T(8,128)(2,1)} %get-tuple-element.79.mine, f32[32,256]{1,0:T(8,128)} %get-tuple-element.80.kept), custom_call_target="tpu_custom_call" | custom-call | tf_op jit(solution)/shard_map/total/pallas_call | solution.py:560
  118.2 0.6 and_select_fusion.place
  118.8 1.8 %step.1 = f32[1,5,2,4,128]{4,3,2,1,0:T(4,128)} custom-call(s32[2]{0:T(128)} %and_select_fusion.place, f32[1,5,2,4,128]{4,3,2,1,0:T(4,128)} %fields.3, f32[3,1024]{1,0:T(4,128)} %get-tuple-element.50.drag, f32[32,256]{1,0:T(8,128)} %get-tuple-element.81.closure, bf16[16,16,1024]{2,1,0:T(8,128)(2,1)} %copy-done.10), custom_call_target="tpu_custom_call" | custom-call | tf_op jit(solution)/shard_map/step/pallas_call | solution.py:595
  120.7 0.5 copy-done.17
  121.3 0.1 copy-done.12
  121.4 0.3 copy-done.9
  121.6 9.3 %finish.1 = (f32[27,256,256]{2,1,0:T(8,128)}, f32[9,27,256]{2,1,0:T(8,128)}, f32[5,256]{1,0:T(8,128)}) custom-call(s32[16]{0:T(128)} %get-tuple-element.82.place, s32[1]{0:T(128)} %bitcast.12.core, bf16[1,448,256]{2,1,0:T(8,128)(2,1)} %bitcast.35, bf16[1,448,256]{2,1,0:T(8,128)(2,1)} %bitcast.38, bf16[1,448,256]{2,1,0:T(8,128)(2,1)} %bitcast.40, ...), custom_call_target="tpu_custom_call" | custom-call | tf_op jit(solution)/shard_map/finish/pallas_call | solution.py:606
  (57 shorter events, 0.2 us)
Async XLA Ops:
  2.9 4.0 %collective-permute-start = (f32[4,1024]{1,0:T(4,128)}, f32[4,1024]{1,0:T(4,128)S(1)}, u32[]{:S(2)}, u32[]{:S(2)}) collective-permute-start(f32[4,1024]{1,0:T(4,128)} %get-tuple-element.48), channel_id=1, source_target_pairs={{0,4},{4,8},{8,12},{12,0},{1,5},{5,9},{9,13},{13,1},{2,6},{6,10},{... | collective-permute-start | bytes 49160 | tf_op jit(solution)/shard_map/ppermute | solution.py:414
  3.4 3.6 %collective-permute-start.1 = (f32[4,1024]{1,0:T(4,128)}, f32[4,1024]{1,0:T(4,128)S(1)}, u32[]{:S(2)}, u32[]{:S(2)}) collective-permute-start(f32[4,1024]{1,0:T(4,128)} %get-tuple-element.49), channel_id=1, source_target_pairs={{4,0},{8,4},{12,8},{0,12},{5,1},{9,5},{13,9},{1,13},{6,2},{10,6},{... | collective-permute-start | bytes 49160 | tf_op jit(solution)/shard_map/ppermute | solution.py:415
  7.0 0.6 copy-start.18
  7.0 0.6 copy-start.19
  9.0 6.4 %collective-permute-start.2 = (bf16[1,16,1024]{2,1,0:T(8,128)(2,1)}, bf16[1,16,1024]{2,1,0:T(8,128)(2,1)S(1)}, u32[]{:S(2)}, u32[]{:S(2)}) collective-permute-start(bf16[1,16,1024]{2,1,0:T(8,128)(2,1)} %bitcast.45), channel_id=1, source_target_pairs={{0,8},{1,9},{2,10},{3,11},{4,12},{5,13},{6,14},{7,15},{8,0},{9,1},... | collective-permute-start | bytes 98312 | tf_op jit(solution)/shard_map/ppermute | solution.py:403
  16.2 6.6 %collective-permute-start.3 = (bf16[2,16,1024]{2,1,0:T(8,128)(2,1)S(1)}, bf16[2,16,1024]{2,1,0:T(8,128)(2,1)S(1)}, u32[]{:S(2)}, u32[]{:S(2)}) collective-permute-start(bf16[2,16,1024]{2,1,0:T(8,128)(2,1)S(1)} %pad_maximum_fusion.4), channel_id=1, source_target_pairs={{0,2},{1,3},{2,0},{3,1},{4,6},{5,7},{6,4},{7,5},{8,10},{9,11},{10,... | collective-permute-start | bytes 196616 | tf_op jit(solution)/shard_map/ppermute | solution.py:403
  23.5 5.0 %collective-permute-start.4 = (bf16[4,16,1024]{2,1,0:T(8,128)(2,1)S(1)}, bf16[4,16,1024]{2,1,0:T(8,128)(2,1)S(1)}, u32[]{:S(2)}, u32[]{:S(2)}) collective-permute-start(bf16[4,16,1024]{2,1,0:T(8,128)(2,1)S(1)} %pad_maximum_fusion.3), channel_id=1, source_target_pairs={{0,1},{1,0},{2,3},{3,2},{4,5},{5,4},{6,7},{7,6},{8,9},{9,8},{10,11... | collective-permute-start | bytes 393224 | tf_op jit(solution)/shard_map/ppermute | solution.py:403
  29.3 1.6 %collective-permute-start.5 = (bf16[8,16,1024]{2,1,0:T(8,128)(2,1)S(1)}, bf16[8,16,1024]{2,1,0:T(8,128)(2,1)S(1)}, u32[]{:S(2)}, u32[]{:S(2)}) collective-permute-start(bf16[8,16,1024]{2,1,0:T(8,128)(2,1)S(1)} %pad_maximum_fusion.2), channel_id=1, source_target_pairs={{0,4},{1,5},{2,6},{3,7},{4,0},{5,1},{6,2},{7,3},{8,12},{9,13},{10,... | collective-permute-start | bytes 786440 | tf_op jit(solution)/shard_map/ppermute | solution.py:403
  31.0 0.9 copy-start.10
  55.2 11.6 %collective-permute-start.6 = (bf16[448,256]{1,0:T(8,128)(2,1)}, bf16[448,256]{1,0:T(8,128)(2,1)S(1)}, u32[]{:S(2)}, u32[]{:S(2)}) collective-permute-start(bf16[448,256]{1,0:T(8,128)(2,1)} %get-tuple-element.56), channel_id=1, source_target_pairs={{0,8},{1,9},{2,10},{3,11},{4,12},{5,13},{6,14},{7,15},{8,0},{9,1},... | collective-permute-start | bytes 688136 | tf_op jit(solution)/shard_map/ppermute | solution.py:403
  56.2 10.6 %collective-permute-start.7 = (bf16[448,256]{1,0:T(8,128)(2,1)}, bf16[448,256]{1,0:T(8,128)(2,1)S(1)}, u32[]{:S(2)}, u32[]{:S(2)}) collective-permute-start(bf16[448,256]{1,0:T(8,128)(2,1)} %get-tuple-element.56), channel_id=1, source_target_pairs={{0,1},{1,0},{2,3},{3,2},{4,5},{5,4},{6,7},{7,6},{8,9},{9,8},{10,11... | collective-permute-start | bytes 688136 | tf_op jit(solution)/shard_map/ppermute | solution.py:506
  57.5 9.3 %collective-permute-start.8 = (bf16[448,256]{1,0:T(8,128)(2,1)}, bf16[448,256]{1,0:T(8,128)(2,1)S(1)}, u32[]{:S(2)}, u32[]{:S(2)}) collective-permute-start(bf16[448,256]{1,0:T(8,128)(2,1)} %get-tuple-element.56), channel_id=1, source_target_pairs={{1,2},{2,1},{5,6},{6,5},{9,10},{10,9},{13,14},{14,13},{17,18},{18,... | collective-permute-start | bytes 688136 | tf_op jit(solution)/shard_map/ppermute | solution.py:506
  66.8 14.2 %copy-start.4 = (bf16[448,256]{1,0:T(8,128)(2,1)S(1)}, bf16[448,256]{1,0:T(8,128)(2,1)}, u32[]{:S(2)}) copy-start(bf16[448,256]{1,0:T(8,128)(2,1)} %get-tuple-element.56) | copy-start | bytes 688132
  66.8 45.2 %copy-start = (s32[16]{0:T(128)S(1)}, s32[16]{0:T(128)}, u32[]{:S(2)}) copy-start(s32[16]{0:T(128)} %fusion.6.place) | copy-start | bytes 196
  66.8 14.2 %copy-start.5 = (bf16[448,256]{1,0:T(8,128)(2,1)}, bf16[448,256]{1,0:T(8,128)(2,1)S(1)}, u32[]{:S(2)}) copy-start(bf16[448,256]{1,0:T(8,128)(2,1)S(1)} %collective-permute-done.6) | copy-start | bytes 688132
  66.8 14.2 %copy-start.6 = (bf16[448,256]{1,0:T(8,128)(2,1)}, bf16[448,256]{1,0:T(8,128)(2,1)S(1)}, u32[]{:S(2)}) copy-start(bf16[448,256]{1,0:T(8,128)(2,1)S(1)} %collective-permute-done.7) | copy-start | bytes 688132
  66.9 13.7 %collective-permute-start.10 = (bf16[448,256]{1,0:T(8,128)(2,1)S(1)}, bf16[448,256]{1,0:T(8,128)(2,1)S(1)}, u32[]{:S(2)}, u32[]{:S(2)}) collective-permute-start(bf16[448,256]{1,0:T(8,128)(2,1)S(1)} %collective-permute-done.7), channel_id=1, source_target_pairs={{1,2},{2,1},{5,6},{6,5},{9,10},{10,9},{13,14},{14,13},{17,18},{18,... | collective-permute-start | bytes 688136 | tf_op jit(solution)/shard_map/ppermute | solution.py:506
  67.7 13.3 %collective-permute-start.9 = (bf16[448,256]{1,0:T(8,128)(2,1)S(1)}, bf16[448,256]{1,0:T(8,128)(2,1)S(1)}, u32[]{:S(2)}, u32[]{:S(2)}) collective-permute-start(bf16[448,256]{1,0:T(8,128)(2,1)S(1)} %collective-permute-done.7), channel_id=1, source_target_pairs={{0,8},{1,9},{2,10},{3,11},{4,12},{5,13},{6,14},{7,15},{8,0},{9,1},... | collective-permute-start | bytes 688136 | tf_op jit(solution)/shard_map/ppermute | solution.py:403
  68.5 12.5 %collective-permute-start.11 = (bf16[448,256]{1,0:T(8,128)(2,1)S(1)}, bf16[448,256]{1,0:T(8,128)(2,1)S(1)}, u32[]{:S(2)}, u32[]{:S(2)}) collective-permute-start(bf16[448,256]{1,0:T(8,128)(2,1)S(1)} %collective-permute-done.8), channel_id=1, source_target_pairs={{1,0},{2,3},{5,4},{6,7},{9,8},{10,11},{13,12},{14,15},{17,16},{18,... | collective-permute-start | bytes 688136 | tf_op jit(solution)/shard_map/ppermute | solution.py:506
  81.0 39.7 %copy-start.7 = (bf16[448,256]{1,0:T(8,128)(2,1)}, bf16[448,256]{1,0:T(8,128)(2,1)S(1)}, u32[]{:S(2)}) copy-start(bf16[448,256]{1,0:T(8,128)(2,1)S(1)} %collective-permute-done.9) | copy-start | bytes 688132
  81.1 14.7 %collective-permute-start.14 = (bf16[4,448,256]{2,1,0:T(8,128)(2,1)S(1)}, bf16[4,448,256]{2,1,0:T(8,128)(2,1)S(1)}, u32[]{:S(2)}, u32[]{:S(2)}) collective-permute-start(bf16[4,448,256]{2,1,0:T(8,128)(2,1)S(1)} %pad_maximum_fusion), channel_id=1, source_target_pairs={{0,4},{1,5},{2,6},{3,7},{4,0},{5,1},{6,2},{7,3},{8,12},{9,13},{10,... | collective-permute-start | bytes 2752520 | tf_op jit(solution)/shard_map/ppermute | solution.py:403
  81.2 3.2 %collective-permute-start.15 = (bf16[384,256]{1,0:T(8,128)(2,1)}, bf16[384,256]{1,0:T(8,128)(2,1)S(1)}, u32[]{:S(2)}, u32[]{:S(2)}) collective-permute-start(bf16[384,256]{1,0:T(8,128)(2,1)} %get-tuple-element.71), channel_id=1, source_target_pairs={{0,4},{1,5},{2,6},{3,7},{4,0},{5,1},{6,2},{7,3},{8,12},{9,13},{10,... | collective-permute-start | bytes 589832 | tf_op jit(solution)/shard_map/ppermute | solution.py:403
  81.7 38.9 %copy-start.1 = (bf16[448,256]{1,0:T(8,128)(2,1)}, bf16[448,256]{1,0:T(8,128)(2,1)S(1)}, u32[]{:S(2)}) copy-start(bf16[448,256]{1,0:T(8,128)(2,1)S(1)} %broadcast_select_fusion.1) | copy-start | bytes 688132
  81.8 7.7 %collective-permute-start.12 = (bf16[448,256]{1,0:T(8,128)(2,1)S(1)}, bf16[448,256]{1,0:T(8,128)(2,1)S(1)}, u32[]{:S(2)}, u32[]{:S(2)}) collective-permute-start(bf16[448,256]{1,0:T(8,128)(2,1)S(1)} %broadcast_select_fusion.1), channel_id=1, source_target_pairs={{0,8},{1,9},{2,10},{3,11},{4,12},{5,13},{6,14},{7,15},{8,0},{9,1},... | collective-permute-start | bytes 688136 | tf_op jit(solution)/shard_map/ppermute | solution.py:403
  83.0 12.9 %collective-permute-start.13 = (bf16[448,256]{1,0:T(8,128)(2,1)S(1)}, bf16[448,256]{1,0:T(8,128)(2,1)S(1)}, u32[]{:S(2)}, u32[]{:S(2)}) collective-permute-start(bf16[448,256]{1,0:T(8,128)(2,1)S(1)} %collective-permute-done.10), channel_id=1, source_target_pairs={{1,0},{2,3},{5,4},{6,7},{9,8},{10,11},{13,12},{14,15},{17,16},{18,... | collective-permute-start | bytes 688136 | tf_op jit(solution)/shard_map/ppermute | solution.py:506
  84.4 0.7 copy-start.13
  86.9 9.0 %collective-permute-start.16 = (bf16[256,256]{1,0:T(8,128)(2,1)}, bf16[256,256]{1,0:T(8,128)(2,1)S(1)}, u32[]{:S(2)}, u32[]{:S(2)}) collective-permute-start(bf16[256,256]{1,0:T(8,128)(2,1)} %get-tuple-element.74.mine), channel_id=1, source_target_pairs={{0,8},{1,9},{2,10},{3,11},{4,12},{5,13},{6,14},{7,15},{8,0},{9,1},... | collective-permute-start | bytes 393224 | tf_op jit(solution)/shard_map/ppermute | solution.py:403
  89.4 31.3 %copy-start.8 = (bf16[448,256]{1,0:T(8,128)(2,1)}, bf16[448,256]{1,0:T(8,128)(2,1)S(1)}, u32[]{:S(2)}) copy-start(bf16[448,256]{1,0:T(8,128)(2,1)S(1)} %collective-permute-done.12) | copy-start | bytes 688132
  95.9 2.8 %copy-start.14 = (bf16[256,256]{1,0:T(8,128)(2,1)}, bf16[256,256]{1,0:T(8,128)(2,1)S(1)}, u32[]{:S(2)}) copy-start(bf16[256,256]{1,0:T(8,128)(2,1)S(1)} %collective-permute-done.16.got) | copy-start | bytes 393220
  95.9 24.8 %copy-start.3 = (bf16[4,448,256]{2,1,0:T(8,128)(2,1)}, bf16[4,448,256]{2,1,0:T(8,128)(2,1)S(1)}, u32[]{:S(2)}) copy-start(bf16[4,448,256]{2,1,0:T(8,128)(2,1)S(1)} %collective-permute-done.14.refs_8_) | copy-start | bytes 2752516
  95.9 24.8 %copy-start.2 = (bf16[448,256]{1,0:T(8,128)(2,1)}, bf16[448,256]{1,0:T(8,128)(2,1)S(1)}, u32[]{:S(2)}) copy-start(bf16[448,256]{1,0:T(8,128)(2,1)S(1)} %broadcast_select_fusion) | copy-start | bytes 688132
  97.0 23.7 %collective-permute-start.20 = (bf16[3,448,256]{2,1,0:T(8,128)(2,1)}, bf16[3,448,256]{2,1,0:T(8,128)(2,1)S(1)}, u32[]{:S(2)}, u32[]{:S(2)}) collective-permute-start(bf16[3,448,256]{2,1,0:T(8,128)(2,1)} %pad_maximum_fusion.1), channel_id=1, source_target_pairs={{0,4},{1,5},{2,6},{3,7},{4,0},{5,1},{6,2},{7,3},{8,12},{9,13},{10,... | collective-permute-start | bytes 2064392 | tf_op jit(solution)/shard_map/ppermute | solution.py:403
  97.1 15.0 %collective-permute-start.19 = (bf16[448,256]{1,0:T(8,128)(2,1)S(1)}, bf16[448,256]{1,0:T(8,128)(2,1)S(1)}, u32[]{:S(2)}, u32[]{:S(2)}) collective-permute-start(bf16[448,256]{1,0:T(8,128)(2,1)S(1)} %broadcast_select_fusion), channel_id=1, source_target_pairs={{0,8},{1,9},{2,10},{3,11},{4,12},{5,13},{6,14},{7,15},{8,0},{9,1},... | collective-permute-start | bytes 688136 | tf_op jit(solution)/shard_map/ppermute | solution.py:403
  100.4 6.2 %collective-permute-start.17 = (bf16[192,256]{1,0:T(8,128)(2,1)}, bf16[192,256]{1,0:T(8,128)(2,1)S(1)}, u32[]{:S(2)}, u32[]{:S(2)}) collective-permute-start(bf16[192,256]{1,0:T(8,128)(2,1)} %get-tuple-element.77.mine), channel_id=1, source_target_pairs={{0,1},{1,0},{2,3},{3,2},{4,5},{5,4},{6,7},{7,6},{8,9},{9,8},{10,11... | collective-permute-start | bytes 294920 | tf_op jit(solution)/shard_map/ppermute | solution.py:403
  106.6 0.6 copy-start.15
  108.8 7.2 %collective-permute-start.18 = (bf16[160,256]{1,0:T(8,128)(2,1)}, bf16[160,256]{1,0:T(8,128)(2,1)S(1)}, u32[]{:S(2)}, u32[]{:S(2)}) collective-permute-start(bf16[160,256]{1,0:T(8,128)(2,1)} %get-tuple-element.79.mine), channel_id=1, source_target_pairs={{0,2},{1,3},{2,0},{3,1},{4,6},{5,7},{6,4},{7,5},{8,10},{9,11},{10,... | collective-permute-start | bytes 245768 | tf_op jit(solution)/shard_map/ppermute | solution.py:403
  112.0 8.7 %copy-start.11 = (bf16[448,256]{1,0:T(8,128)(2,1)}, bf16[448,256]{1,0:T(8,128)(2,1)S(1)}, u32[]{:S(2)}) copy-start(bf16[448,256]{1,0:T(8,128)(2,1)S(1)} %collective-permute-done.19) | copy-start | bytes 688132
  112.0 8.6 %collective-permute-start.21 = (bf16[448,256]{1,0:T(8,128)(2,1)S(1)}, bf16[448,256]{1,0:T(8,128)(2,1)S(1)}, u32[]{:S(2)}, u32[]{:S(2)}) collective-permute-start(bf16[448,256]{1,0:T(8,128)(2,1)S(1)} %collective-permute-done.19), channel_id=1, source_target_pairs={{0,4},{1,5},{2,6},{3,7},{4,0},{5,1},{6,2},{7,3},{8,12},{9,13},{10,... | collective-permute-start | bytes 688136 | tf_op jit(solution)/shard_map/ppermute | solution.py:403
  116.0 0.6 copy-start.16
  118.2 2.4 %collective-permute-start.22 = (bf16[128,256]{1,0:T(8,128)(2,1)}, bf16[128,256]{1,0:T(8,128)(2,1)S(1)}, u32[]{:S(2)}, u32[]{:S(2)}) collective-permute-start(bf16[128,256]{1,0:T(8,128)(2,1)} %get-tuple-element.86.refs_11_), channel_id=1, source_target_pairs={{0,4},{1,5},{2,6},{3,7},{4,0},{5,1},{6,2},{7,3},{8,12},{9,13},{10,... | collective-permute-start | bytes 196616 | tf_op jit(solution)/shard_map/ppermute | solution.py:403
  120.6 0.6 copy-start.17
  120.6 0.7 copy-start.12
  120.7 1.0 copy-start.9

commit v2 on v1

--- a/solution.py
+++ b/solution.py
@@ -118,33 +118,30 @@
     w_back[...] = wt[...].astype(F32).T.astype(BF16)
     pad = jnp.zeros((5, hid), F32)
     tall = jnp.concatenate([v for c in range(9) for v in (w_in[c].astype(F32), pad)], 0)
-    w_first[...] = dot(tall.T.astype(BF16), tap_rows()).astype(BF16)
+    w_first[...] = (0.5 * dot(tall.T.astype(BF16), tap_rows())).astype(BF16)
     wide = w_out[...].astype(F32)
     wide = jnp.concatenate([wide, jnp.zeros((16 - wide.shape[0], hid), F32)], 0).astype(BF16)
     wo[...] = dot_nt(chosen, wide).astype(BF16)
     wc[...] = dot_nt(wide, chosen).astype(BF16)
 
 
-def moved(v, ox, oy, nz, lanes):
-    planes = v.shape[1] // lanes
+def span(x, lanes, count=1):
+    return slice(x * lanes, (x + count) * lanes)
+
+
+def plane_taps(g2z, x, planes, nz, lanes):
     parts = []
-    for x in range(planes):
-        at = ((x + ox) % planes) * lanes
-        parts.append(ahead_y(v[:, at : at + lanes], oy, nz))
-    return parts
-
-
-def all_taps(g2z, nz, lanes):
-    taps = [moved(g2z[0, oz + 1], -ox, -oy, nz, lanes) for ox, oy, oz in offsets]
-    return [jnp.concatenate([tap[x] for tap in taps], 0) for x in range(len(taps[0]))]
-
-
-def closure_kernel(
-    nz, lanes, place, feats, w_first, wt, wo, wc, piece, closure, g2z, fcol, fz, eighth, ninth, hidden, sums, mid, last
-):
+    for ox, oy, oz in offsets:
+        parts.append(ahead_y(g2z[0, oz + 1, :, span((x - ox) % planes, lanes)], -oy, nz))
+    return jnp.concatenate(parts, 0)
+
+
+def closure_kernel(nz, lanes, sources, place, w_first, wt, wo, wc, *refs):
+    arrived, refs = refs[:sources], refs[sources:]
+    piece, closure, g2z, fcol, feats, fz, eighth, ninth, hidden, sums, mid, last = refs
     s = pl.program_id(0)
     samples = pl.num_programs(0)
-    slabs = feats.shape[0] // samples
+    slabs = place.shape[0]
     cells = hidden.shape[1]
     planes = cells // lanes
     per = planes // slabs
@@ -155,17 +152,29 @@
     def _():
         mid[...] = jnp.zeros_like(mid)
         last[...] = jnp.zeros_like(last)
+        at = 0
+        for ref in arrived:
+            feats[at : at + ref.shape[0]] = ref[...]
+            at += ref.shape[0]
 
     sums[...] = jnp.zeros_like(sums)
     sub = lax.broadcasted_iota(jnp.int32, (8, lanes), 0)
-    for j in range(slabs):
-        f = feats[place[j * samples + s]].astype(F32)
-        at = slice(j * per * lanes, (j + 1) * per * lanes)
+
+    def spread(j):
+        f = feats[place[j] + s].astype(F32)
+        at = span(j, per * lanes)
         fz[0, :, at] = roll_z(f, 1, nz)
         fz[1, :, at] = f
         fz[2, :, at] = roll_z(f, -1, nz)
-    for x in range(planes):
-        at = slice(x * lanes, (x + 1) * lanes)
+
+    for j in range(slabs):
+        spread(j)
+
+    def around(x):
+        return [span((x + ox) % planes, lanes) for ox in (-1, 0, 1)]
+
+    def ninth_rows(x):
+        at = span(x, lanes)
         rows = [jnp.broadcast_to(fz[oz + 1, 5:6, at], (8, lanes)) for oz in (-1, 0, 1)]
         tile = ahead_y(rows[0], -1, nz)
         for q in range(1, 8):
@@ -174,18 +183,30 @@
         ninth[:, at] = ahead_y(rows[2], 1, nz)
 
     for x in range(planes):
-        at = slice(x * lanes, (x + 1) * lanes)
-        near = [slice(((x + ox) % planes) * lanes, ((x + ox) % planes + 1) * lanes) for ox in (-1, 0, 1)]
+        ninth_rows(x)
+
+    def patches(x):
+        near = around(x)
         pieces = [ahead_y(fz[oz + 1, 8:16, near[ox + 1]], oy, nz) for ox, oy, oz in offsets]
         pieces += [eighth[:, n] for n in near]
         tail = jnp.where(sub == 0, ninth[:, near[0]], jnp.where(sub == 1, ninth[:, near[1]], ninth[:, near[2]]))
         pieces += [jnp.where(sub < 3, tail, 0.0), jnp.zeros((8, lanes), F32)]
-        column = jnp.concatenate(pieces, 0).astype(BF16)
-        fcol[0, :, at] = column
-        pre = dot(w_first[...], column)
-        hid = (pre * logistic(pre)).astype(BF16)
-        hidden[:, at] = hid
-        prod = dot(wt[...], hid)
+        fcol[0, :, near[1]] = jnp.concatenate(pieces, 0).astype(BF16)
+
+    for x in range(planes):
+        patches(x)
+
+    def first(x):
+        at = span(x, lanes)
+        half = dot(w_first[...], fcol[0, :, at])
+        hidden[:, at] = (half * jnp.tanh(half) + half).astype(BF16)
+
+    for x in range(planes):
+        first(x)
+
+    def second(x):
+        near = around(x)
+        prod = dot(wt[...], hidden[:, near[1]])
         for ox in (-1, 0, 1):
             to = near[1 - ox]
             for oz in (-1, 0, 1):
@@ -196,9 +217,12 @@
                     total = v if total is None else total + v
                 sums[oz + 1, :, to] += total
 
-    for j in range(slabs):
-        here = feats[place[j * samples + s]]
-        at = slice(j * per * lanes, (j + 1) * per * lanes)
+    for x in range(planes):
+        second(x)
+
+    def gradient(j):
+        here = feats[place[j] + s]
+        at = span(j, per * lanes)
         pre = sums[1, :, at] + roll_z(sums[0, :, at], 1, nz) + roll_z(sums[2, :, at], -1, nz)
         sig = logistic(pre)
         hid = (pre * sig).astype(BF16)
@@ -215,10 +239,14 @@
         g2z[0, 1, :, at] = rounded
         g2z[0, 2, :, at] = roll_z(grad, 1, nz).astype(BF16)
 
-    columns = all_taps(g2z, nz, lanes)
-    for x in range(0, planes, group):
-        at = slice(x * lanes, (x + group) * lanes)
-        mid[...] += dot_nt(jnp.concatenate(columns[x : x + group], 1), hidden[:, at])
+    for j in range(slabs):
+        gradient(j)
+
+    @pl.when(s >= 0)
+    def _():
+        for x in range(0, planes, group):
+            columns = [plane_taps(g2z, x + h, planes, nz, lanes) for h in range(group)]
+            mid[...] += dot_nt(jnp.concatenate(columns, 1), hidden[:, span(x, lanes, group)])
 
     @pl.when(s == samples - 1)
     def _():
@@ -242,15 +270,16 @@
     def _():
         out[...] = jnp.zeros_like(out)
 
-    columns = all_taps(g2z, nz, lanes)
+    planes = fcol.shape[2] // lanes
     group = 2
-    for x in range(0, len(columns), group):
-        at = slice(x * lanes, (x + group) * lanes)
-        back = dot(w_back[...], jnp.concatenate(columns[x : x + group], 1))
+    for x in range(0, planes, group):
+        at = span(x, lanes, group)
+        columns = [plane_taps(g2z, x + h, planes, nz, lanes) for h in range(group)]
+        back = dot(w_back[...], jnp.concatenate(columns, 1))
         column = fcol[0, :, at]
-        pre = dot(w_first[...], column)
-        sig = logistic(pre)
-        grad = (back * (sig * (1.0 + pre * (1.0 - sig)))).astype(BF16)
+        half = dot(w_first[...], column)
+        double = 1.0 + jnp.tanh(half)
+        grad = (back * (double * (0.5 + half - 0.5 * half * double))).astype(BF16)
         out[...] += dot_nt(column, grad)
 
 
@@ -259,41 +288,56 @@
     mine = pl.multiple_of(core[0] * half, half)
     theirs = pl.multiple_of((1 - core[0]) * half, half)
     keep[...] = one[pl.ds(mine, half)] + two[pl.ds(mine, half)]
-    message[0:half] = (one[pl.ds(theirs, half)] + two[pl.ds(theirs, half)]).astype(BF16)
+    message[0:half] = one[pl.ds(theirs, half)] + two[pl.ds(theirs, half)]
     samples, planes = closure.shape[:2]
     at = 0
     for s in range(samples):
         for y in range(planes // 4):
             for p in range(2):
                 kept[at : at + 16] = closure[s, 4 * y + 2 * core[0] + p].astype(F32)
-                message[half + at : half + at + 16] = closure[s, 4 * y + 2 * (1 - core[0]) + p]
+                message[half + at : half + at + 16] = closure[s, 4 * y + 2 * (1 - core[0]) + p].astype(F32)
                 at += 16
 
 
 def merge_kernel(bit, got, mine, kept, message, keep):
     half = 128
-    message[0:half] = (mine[0:half].astype(F32) + got[0:half].astype(F32)).astype(BF16)
+    message[0:half] = (mine[...] + got[0:half]).astype(BF16)
     for o in range(keep.shape[0] // 32):
         a = pl.multiple_of((2 * o + bit[0]) * 32, 32)
         b = pl.multiple_of((2 * o + 1 - bit[0]) * 32, 32)
-        keep[o * 32 : o * 32 + 32] = kept[pl.ds(a, 32)] + got[pl.ds(half + a, 32)].astype(F32)
-        message[half + o * 32 : half + o * 32 + 32] = (
-            kept[pl.ds(b, 32)] + got[pl.ds(half + b, 32)].astype(F32)
-        ).astype(BF16)
-
-
-def total_kernel(got, mine, kept, half, closure):
-    half[...] = (mine[0:128].astype(F32) + got[0:128].astype(F32)).astype(BF16)
-    closure[...] = kept[...] + got[128:].astype(F32)
-
-
-def step_kernel(nz, place, fields, drag, closure, feats, out):
+        keep[o * 32 : o * 32 + 32] = kept[pl.ds(a, 32)] + got[pl.ds(half + a, 32)]
+        message[half + o * 32 : half + o * 32 + 32] = (kept[pl.ds(b, 32)] + got[pl.ds(half + b, 32)]).astype(BF16)
+
+
+def fan_kernel(got, mine, kept, keep, *messages):
+    half = 128
+    raw = (mine[0:half].astype(F32) + got[0:half].astype(F32)).astype(BF16)
+    for o in range(4):
+        rows = kept[o * 32 : o * 32 + 32] + got[half + o * 32 : half + o * 32 + 32].astype(F32)
+        if o == 0:
+            keep[...] = rows
+        else:
+            messages[o - 1][0:half] = raw
+            messages[o - 1][half:] = rows.astype(BF16)
+
+
+def total_kernel(mine, kept, one, two, three, half, closure):
+    pair = mine[0:128].astype(F32) + one[0:128].astype(F32)
+    half[...] = pair + (two[0:128].astype(F32) + three[0:128].astype(F32))
+    closure[...] = kept[...] + (one[128:].astype(F32) + two[128:].astype(F32) + three[128:].astype(F32))
+
+
+def step_kernel(nz, place, fields, drag, closure, *refs):
+    sources, out = refs[:-1], refs[-1]
     state = flat_cells(fields)
     cells = state.shape[1]
     planes, rows = fields.shape[2], fields.shape[3]
     lanes = cells // planes
-    lower = feats[place[0]][8:13, cells - lanes :].astype(F32)
-    upper = feats[place[1]][8:13, :lanes].astype(F32)
+    lower, upper = (sources[0][place[i] if len(sources) == 1 else 0].astype(F32) for i in range(2))
+    for g in range(1, len(sources)):
+        other = sources[g][0].astype(F32)
+        lower, upper = (jnp.where(place[i] == g, other, v) for i, v in enumerate((lower, upper)))
+    lower, upper = lower[8:13, cells - lanes :], upper[8:13, :lanes]
     wide = jnp.concatenate([lower, state, upper], 1)
     next_x, last_x = wide[:, 2 * lanes :], wide[:, :cells]
     parts = [state[:, i * lanes : (i + 1) * lanes] for i in range(planes)]
@@ -313,52 +357,59 @@
             out[0, :, x, y, :] = new[:, at : at + nz]
 
 
-def finish_kernel(count, weight_count, place, core, *refs):
-    pieces, (own, other, mid_out, first_out, last_out, held, sems, factor) = refs[:count], refs[count:]
-    step = pl.program_id(0)
-    taps_here = mid_out.shape[0]
+def finish_kernel(count, weight_count, place, core, own, other, *refs):
+    pieces, (mid_out, first_out, last_out, held, done, arrive, leave) = refs[:count], refs[count:]
     slots = held.shape[0]
-    block = mid_out.shape[1] // slots
+    block = done.shape[1] // slots
     rows = held.shape[1] - 16
-
-    @pl.when(step == 0)
-    def _():
-        copies, at = [], 0
-        for i, ref in enumerate(pieces):
-            copies.append(pltpu.make_async_copy(ref, held.at[at : at + ref.shape[0]], sems.at[i]))
-            at += ref.shape[0]
-        for copy in copies:
-            copy.start()
-        a, b = own[...].astype(F32), other[...].astype(F32)
-        swapped = core[0] == 1
-        raw = jnp.concatenate([jnp.where(swapped, b, a), jnp.where(swapped, a, b)], 0)
-        squares = jnp.sum(raw * raw, keepdims=True)
-        ordered = dot(tap_rows(), raw.astype(BF16))
-        for copy in copies:
-            copy.wait()
-        last = []
-        for d in range(slots):
-            extra = held[place[d], rows:].astype(F32)
-            last.append(extra[0:5, 0:block])
-            squares = squares + jnp.sum(extra[8:9, 0:2], keepdims=True)
-        last = jnp.concatenate(last, 1)
-        squares = squares + jnp.sum(last * last, keepdims=True)
-        clip = jnp.minimum(1.0, clip_rms * math.sqrt(weight_count) / jnp.sqrt(squares + 1e-06))
-        factor[...] = jnp.broadcast_to(clip, factor.shape)
-        last_out[...] = last * clip
-        ordered = ordered * clip
-        for c in range(first_out.shape[0]):
-            first_out[c] = ordered[32 * c : 32 * c + 27]
-
-    width = mid_out.shape[1]
+    width = done.shape[1]
+
+    copies, at = [], 0
+    for i, ref in enumerate(pieces):
+        copies.append(pltpu.make_async_copy(ref, held.at[at : at + ref.shape[0]], arrive.at[i]))
+        at += ref.shape[0]
+    for copy in copies:
+        copy.start()
+    a, b = own[...], other[...]
+    swapped = core[0] == 1
+    raw = jnp.concatenate([jnp.where(swapped, b, a), jnp.where(swapped, a, b)], 0)
+    squares = jnp.sum(raw * raw, keepdims=True)
+    high = raw.astype(BF16)
+    ordered = dot(tap_rows(), high) + dot(tap_rows(), (raw - high.astype(F32)).astype(BF16))
+    for copy in copies:
+        copy.wait()
+    last = []
+    for d in range(slots):
+        extra = held[place[d], rows:].astype(F32)
+        last.append(extra[0:5, 0:block])
+        squares = squares + jnp.sum(extra[8:9, 0:2], keepdims=True)
+    last = jnp.concatenate(last, 1)
+    squares = squares + jnp.sum(last * last, keepdims=True)
+    clip = jnp.minimum(1.0, clip_rms * math.sqrt(weight_count) / jnp.sqrt(squares + 1e-06))
+    last_out[...] = last * clip
+    ordered = ordered * clip
+    for c in range(first_out.shape[0]):
+        first_out[c] = ordered[32 * c : 32 * c + 27]
+
     eye = (
         lax.broadcasted_iota(jnp.int32, (width, width), 0) == lax.broadcasted_iota(jnp.int32, (width, width), 1)
     ).astype(F32).astype(BF16)
-    clip = factor[0:1, 0:1]
-    for i in range(taps_here):
-        start = pl.multiple_of((step * taps_here + i) * block, block)
-        flipped = jnp.concatenate([held[place[d], pl.ds(start, block)] for d in range(slots)], 0)
-        mid_out[i] = dot_nt(eye, flipped) * clip
+
+    def leaving(t):
+        return pltpu.make_async_copy(done.at[t], mid_out.at[t], leave.at[t])
+
+    def flip(i, carry):
+        for k in range(3):
+            t = 3 * i + k
+            start = pl.multiple_of(t * block, block)
+            flipped = jnp.concatenate([held[place[d], pl.ds(start, block)] for d in range(slots)], 0)
+            done[t] = dot_nt(eye, flipped) * clip
+            leaving(t).start()
+        return carry
+
+    lax.fori_loop(0, 9, flip, 0)
+    for t in range(27):
+        leaving(t).wait()
 
 
 def whole_spec(shape):
@@ -423,15 +474,17 @@
     )(stay, from_below, from_above, fields, cotangent)
 
     if fast:
-        order = (8, 2, 1, 4)
-        feats = own_feats[None]
-        for mask in order:
-            feats = jnp.concatenate([feats, trade(feats, mask)], 0)
-        apart = me ^ everyone
-        feat_place = sum(((apart & mask) != 0).astype(jnp.int32) << i for i, mask in enumerate(order))
+        near_z = [trade(own_feats, mask) for mask in (1, 2, 3)]
+        mine = jnp.stack([own_feats] + near_z)
+        across = trade(mine, 8)
+        sources = [mine, across, trade(mine, 4), trade(across, 4)]
+        slabs = jnp.arange(n_slab, dtype=jnp.int32)
+        group = 2 * ((slabs ^ slab) & 1) + (((slabs ^ slab) >> 1) & 1)
+        place = group * samples
     else:
-        feats = lax.all_gather(own_feats, team)
-        feat_place = everyone
+        sources = [lax.all_gather(own_feats, team)]
+        group = jnp.arange(n_slab, dtype=jnp.int32)
+        place = group * samples
 
     rows = 27 * block
     wt, w_back, w_first, wo, wc = pl.pallas_call(
@@ -452,7 +505,7 @@
 
     team_cells = all_planes * lanes
     piece, closure, g2z, fcol = pl.pallas_call(
-        functools.partial(closure_kernel, nz, lanes),
+        functools.partial(closure_kernel, nz, lanes, len(sources)),
         grid=(samples,),
         out_shape=(
             shape((rows + 16, hid), BF16),
@@ -460,7 +513,7 @@
             shape((samples, 3, block, team_cells), BF16),
             shape((samples, 256, team_cells), BF16),
         ),
-        in_specs=[SMEM] + [VMEM] * 5,
+        in_specs=[SMEM] + [VMEM] * (4 + len(sources)),
         out_specs=(
             whole_spec((rows + 16, hid)),
             pl.BlockSpec((1, all_planes, 16, lanes // 2), lambda s: (s, 0, 0, 0)),
@@ -468,6 +521,7 @@
             pl.BlockSpec((1, 256, team_cells), lambda s: (s, 0, 0)),
         ),
         scratch_shapes=[
+            pltpu.VMEM((size, 16, cells), BF16),
             pltpu.VMEM((3, 16, team_cells), F32),
             pltpu.VMEM((8, team_cells), F32),
             pltpu.VMEM((8, team_cells), F32),
@@ -479,7 +533,7 @@
         compiler_params=params(),
         cost_estimate=cost(9e9),
         name="closure",
-    )(feat_place, feats, w_first, wt, wo, wc)
+    )(place, w_first, wt, wo, wc, *sources)
 
     def first_part(lo, count, fcol, g2z):
         return pl.pallas_call(
@@ -499,79 +553,75 @@
         )(w_first, w_back, fcol, g2z)
 
     if fast:
-        z = rep
-        outer = (z == 0) | (z == 3)
-
-        def line(v, pairs):
-            return lax.ppermute(v, "rep", pairs)
+        core, y = slab & 1, slab >> 1
+
+        def chip(at):
+            at = at % 8
+            return (0, at) if at < 4 else (1, 7 - at)
+
+        def device(at, c):
+            y, z = chip(at)
+            return (2 * y + c) * n_rep + z
+
+        def around(v, by):
+            return lax.ppermute(v, team, [(device(at, c), device(at + by, c)) for at in range(8) for c in range(2)])
 
         def tie(*values):
             return lax.optimization_barrier(values)
 
-        core, y = slab & 1, slab >> 1
-        y0 = trade(piece, 8)
-        p1 = line(piece, [(0, 1), (1, 0), (2, 3), (3, 2)])
-        p2 = line(piece, [(1, 2), (2, 1)])
+        f1, b1 = around(piece, 1), around(piece, -1)
         half_one = first_part(0, samples // 2, fcol, g2z)
-        y0, p1, p2, half_one, fcol, g2z = tie(y0, p1, p2, half_one, fcol, g2z)
-        p4 = line(p2, [(1, 0), (2, 3)])
-        p3 = line(p1, [(1, 2), (2, 1)])
-        y1 = trade(p1, 8)
+        f1, b1, half_one, fcol, g2z = tie(f1, b1, half_one, fcol, g2z)
+        f2, b2 = around(f1, 1), around(b1, -1)
         half_two = first_part(samples // 2, samples - samples // 2, fcol, g2z)
-
-        def exchanged(count):
-            return (shape((128 + 32 * count, hid), BF16), shape((32 * count, hid), F32))
+        f2, b2, half_two = tie(f2, b2, half_two)
+        f3, b3 = around(f2, 1), around(b2, -1)
 
         message, keep, kept = pl.pallas_call(
             split_kernel,
-            out_shape=(exchanged(8)[0], shape((128, hid), F32), exchanged(8)[1]),
+            out_shape=(shape((384, hid), F32), shape((128, hid), F32), shape((256, hid), F32)),
             in_specs=[SMEM] + [VMEM] * 3,
             out_specs=(VMEM,) * 3,
             compiler_params=params(),
             name="split",
         )(core[None], half_one, half_two, closure)
-        y1, p3, p4, message = tie(y1, p3, p4, message)
         got = trade(message, 4)
-        q2 = jnp.where(outer, p4, p2)
-        y2 = trade(q2, 8)
-        p5 = line(p3, [(1, 0), (2, 3)])
-        c0 = trade(jnp.stack([piece, y0, p1, y1]), 4)
-
-        def merge(count, bit, got, mine, kept):
-            return pl.pallas_call(
-                merge_kernel,
-                out_shape=exchanged(count),
-                in_specs=[SMEM] + [VMEM] * 3,
-                out_specs=(VMEM,) * 2,
-                compiler_params=params(),
-                name="merge",
-            )(bit[None], got, mine, kept)
-
-        message, kept = merge(4, y, got, keep, kept)
+        message, kept = pl.pallas_call(
+            merge_kernel,
+            out_shape=(shape((256, hid), BF16), shape((128, hid), F32)),
+            in_specs=[SMEM] + [VMEM] * 3,
+            out_specs=(VMEM,) * 2,
+            compiler_params=params(),
+            name="merge",
+        )(y[None], got, keep, kept)
         got = trade(message, 8)
-        y2, p5, c0, got = tie(y2, p5, c0, got)
-        q3 = jnp.where(outer, p5, p3)
-        y3 = trade(q3, 8)
-        c1 = trade(jnp.stack([q2, y2, q3]), 4)
-        message, kept = merge(2, z & 1, got, message, kept)
-        got = trade(message, 1)
-        message, kept = merge(1, z >> 1, got, message, kept)
-        got = trade(message, 2)
+        kept, *messages = pl.pallas_call(
+            fan_kernel,
+            out_shape=(shape((32, hid), F32),) + (shape((160, hid), BF16),) * 3,
+            in_specs=[VMEM] * 3,
+            out_specs=(VMEM,) * 4,
+            compiler_params=params(),
+            name="fan",
+        )(got, message, kept)
+        got = [trade(message, mask) for mask, message in zip((1, 2, 3), messages)]
+        f4 = around(f3, 1)
         own, own_closure = pl.pallas_call(
             total_kernel,
-            out_shape=(shape((128, hid), BF16), shape((32, hid), F32)),
-            in_specs=[VMEM] * 3,
+            out_shape=(shape((128, hid), F32), shape((32, hid), F32)),
+            in_specs=[VMEM] * 5,
             out_specs=(VMEM,) * 2,
             compiler_params=params(),
             name="total",
-        )(got, message, kept)
+        )(messages[0], kept, *got)
         other = trade(own, 4)
-        c2 = trade(y3, 4)
-        pieces = [v[None] for v in (piece, y0, p1, y1, q2, y2, q3, y3)] + [c0, c1, c2[None]]
-        m2 = jnp.where(outer, 2, 3)
-        masks = jnp.stack([jnp.int32(0), jnp.int32(8), jnp.int32(1), jnp.int32(9), m2, m2 | 8, m2 ^ 1, (m2 ^ 1) | 8])
-        masks = jnp.concatenate([masks, masks | 4])
-        piece_place = jnp.argmax((me ^ everyone)[:, None] == masks[None, :], axis=1).astype(jnp.int32)
+        pieces = [piece, f1, b1, f2, b2, f3, b3, f4]
+        pieces = [v[None] for v in pieces + [trade(v, 4) for v in pieces]]
+        position = jnp.where(y == 0, rep, 7 - rep)
+        theirs, their_z = everyone // n_rep, everyone % n_rep
+        apart = (jnp.where(theirs < 2, their_z, 7 - their_z) - position) % 8
+        piece_place = jnp.where(apart < 4, 2 * apart, 2 * (8 - apart) - 1)
+        piece_place = jnp.where(apart == 0, 0, piece_place) + 8 * ((theirs ^ slab) & 1)
+        piece_place = piece_place.astype(jnp.int32)
     else:
         raw_first = first_part(0, samples, fcol, g2z)
         core = jnp.zeros((), jnp.int32)
@@ -583,7 +633,7 @@
             high = squares.astype(BF16).astype(F32)
             extra = extra.at[8, 0].set(high).at[8, 1].set(squares - high)
             piece = jnp.concatenate([body, extra], 0).astype(BF16)
-        raw_first = lax.psum(raw_first, team).astype(BF16)
+        raw_first = lax.psum(raw_first, team)
         own, other = raw_first[:128], raw_first[128:]
         pieces = [lax.all_gather(piece, team)]
         piece_place = everyone
@@ -591,36 +641,32 @@
         part = jnp.swapaxes(part, 0, 1).reshape(size, planes * 16, lanes // 2).astype(F32)
         own_closure = lax.psum_scatter(part, team, scatter_dimension=0)
 
-    near = jnp.stack([(slab + n_slab - 1) % n_slab, (slab + 1) % n_slab]) * samples + sample
+    near = jnp.take(group, jnp.stack([(slab + n_slab - 1) % n_slab, (slab + 1) % n_slab]))
+    halo = sources if fast else [sources[0].reshape(n_slab, samples, 16, cells)[:, sample]]
     new_fields = pl.pallas_call(
         functools.partial(step_kernel, nz),
         out_shape=shape(fields.shape, F32),
-        in_specs=[SMEM] + [VMEM] * 4,
+        in_specs=[SMEM] + [VMEM] * (3 + len(halo)),
         out_specs=VMEM,
         compiler_params=params(),
         name="step",
-    )(jnp.take(feat_place, near), fields, drag, own_closure, feats)
+    )(near, fields, drag, own_closure, *halo)
 
     weight_count = w_in.size + w_mid.size + w_out.size
-    step_taps = 3
     grad_middle, grad_first, grad_last = pl.pallas_call(
         functools.partial(finish_kernel, len(pieces), weight_count),
-        grid=(27 // step_taps,),
         out_shape=(shape((27, hid, hid), F32), shape((9, 27, hid), F32), shape((cout, hid), F32)),
-        in_specs=[SMEM] * 2 + [ANY] * len(pieces) + [whole_spec((128, hid))] * 2,
-        out_specs=(
-            pl.BlockSpec((step_taps, hid, hid), lambda i: (i, 0, 0)),
-            whole_spec((9, 27, hid)),
-            whole_spec((cout, hid)),
-        ),
+        in_specs=[SMEM] * 2 + [VMEM] * 2 + [ANY] * len(pieces),
+        out_specs=(ANY, VMEM, VMEM),
         scratch_shapes=[
             pltpu.VMEM((size, rows + 16, hid), BF16),
+            pltpu.VMEM((27, hid, hid), F32),
             pltpu.SemaphoreType.DMA((len(pieces),)),
-            pltpu.VMEM((8, 128), F32),
+            pltpu.SemaphoreType.DMA((27,)),
         ],
         compiler_params=params(),
         name="finish",
-    )(piece_place, core[None], *pieces, own, other)
+    )(piece_place, core[None], own, other, *pieces)
     return (new_fields, jnp.transpose(grad_first, (1, 0, 2)), grad_middle, grad_last.T)
 
 

time: 132 us -> 113 us (0.86)
  Pallas kernels: 68.1 us -> 58.4 us
  other arithmetic: 5.51 us -> 2.53 us
  starting transfers between devices: 24.9 us -> 22.5 us
  local copies, waits for them, and re-layouts: 5.93 us -> 4.18 us
    pallas_call x6 -> x5, Pallas kernels: 32.1 us -> 24 us  [the longest x1 16.4 us: shards(): pl.pallas_call(functools.partial(closure_kernel, nz, lanes, len(sources))...]
    ppermute x5 -> x7, waiting for transfers between devices: 6.88 us -> 0.73 us  [around(): lax.ppermute(v, team, [(device(at, c), device(at + by, c)) for at in rang...]
    ppermute x16 -> x20, waiting for transfers between devices: 16.9 us -> 21.7 us  [trade(): return lax.ppermute(v, team, [(d, d ^ mask) for d in range(size)])]
    ppermute x16 -> x20, starting transfers between devices: 17 us -> 13.6 us  [trade(): return lax.ppermute(v, team, [(d, d ^ mask) for d in range(size)])]
    concatenate x3 -> x0, other arithmetic: 2.32 us -> none  [shards(): feats = jnp.concatenate([feats, trade(feats, mask)], 0)]
    unnamed x44 -> x56, local copies, waits for them, and re-layouts: 5.11 us -> 3.55 us
    ppermute x5 -> x7, starting transfers between devices: 5.5 us -> 6.47 us  [around(): lax.ppermute(v, team, [(device(at, c), device(at + by, c)) for at in rang...]
  transfers between devices with their start and end apart: 23 -> 29, of which waited for: 9 -> 9; matrix products, arithmetic and copies ran while one was open for 3% -> 2% of each run, Pallas kernels for 24% -> 25%
where the time goes in v2:
time: 113 us
  Pallas kernels  58.4 us (52%)
  waiting for transfers between devices  24.1 us (21%)
  starting transfers between devices  22.5 us (20%)
  local copies, waits for them, and re-layouts  4.18 us (4%)
  other arithmetic  2.53 us (2%)
  between operations  1.14 us (1%)
    ppermute x20, waiting for transfers between devices, trade(): return lax.ppermute(v, team, [(d, d ^ mask) for d in range(size)])  21.7 us
    pallas_call x2, Pallas kernels, first_part(): pl.pallas_call(functools.partial(first_kernel, nz, lanes), grid=(count,),...  16.8 us
    pallas_call x1, Pallas kernels, shards(): pl.pallas_call(functools.partial(closure_kernel, nz, lanes, len(sources))...  16.4 us
    ppermute x20, starting transfers between devices, trade(): return lax.ppermute(v, team, [(d, d ^ mask) for d in range(size)])  13.6 us
    pallas_call x1, Pallas kernels, shards(): pl.pallas_call(functools.partial(finish_kernel, len(pieces), weight_count...  8.05 us
    ppermute x7, starting transfers between devices, around(): lax.ppermute(v, team, [(device(at, c), device(at + by, c)) for at in rang...  6.47 us
    pallas_call x1, Pallas kernels, shards(): pl.pallas_call(weight_kernel, out_shape=(shape((rows, hid), BF16), shape(...  3.96 us
    unnamed x56, local copies, waits for them, and re-layouts  3.55 us
  transfers between devices with their start and end apart: 29, of which 9 were waited for; matrix products, arithmetic and copies ran while one was open for 2% of the time, Pallas kernels for 25%

profile of v2, /device:TPU:0, one launch (start us, length us, event | category | flops | bytes accessed | tf_op | source)
XLA Modules:
  0.0 112.9 jit_solution(3497356962780173760)
XLA Ops:
  0.6 2.3 %deposit.1 = (f32[4,1024]{1,0:T(4,128)}, f32[4,1024]{1,0:T(4,128)}, f32[4,1024]{1,0:T(4,128)}) custom-call(f32[1,1024]{1,0:T(1,128)} %mass.1, f32[3,1,1024]{2,1,0:T(1,128)} %bitcast.54, s32[1,1024]{1,0:T(1,128)} %cell.1, s32[1,256]{1,0:T(1,128)} %listed.1, s32[1,2]{1,0:T(1,128)} %counts.1), custom_call_target="tpu_custom_call" | custom-call | tf_op jit(solution)/shard_map/deposit/pallas_call | solution.py:457
  2.9 0.5 collective-permute-start
  3.4 2.0 %collective-permute-start.1 = (f32[4,1024]{1,0:T(4,128)}, f32[4,1024]{1,0:T(4,128)S(1)}, u32[]{:S(2)}, u32[]{:S(2)}) collective-permute-start(f32[4,1024]{1,0:T(4,128)} %get-tuple-element.42), channel_id=1, source_target_pairs={{4,0},{8,4},{12,8},{0,12},{5,1},{9,5},{13,9},{1,13},{6,2},{10,6},{... | collective-permute-start | bytes 49160 | tf_op jit(solution)/shard_map/ppermute | solution.py:466
  5.3 1.6 %collective-permute-done.below = f32[4,1024]{1,0:T(4,128)S(1)} collective-permute-done((f32[4,1024]{1,0:T(4,128)}, f32[4,1024]{1,0:T(4,128)S(1)}, u32[]{:S(2)}, u32[]{:S(2)}) %collective-permute-start) | collective-permute-done | bytes 16416 | tf_op jit(solution)/shard_map/ppermute | solution.py:465
  7.0 0.0 collective-permute-done.1.above
  7.0 0.6 copy-done.26
  7.6 0.0 copy-done.27
  7.6 1.5 %features.1 = (bf16[16,1024]{1,0:T(8,128)(2,1)}, f32[3,1024]{1,0:T(4,128)}) custom-call(f32[4,1024]{1,0:T(4,128)} %get-tuple-element.40.stay, f32[4,1024]{1,0:T(4,128)} %copy-done.26, f32[4,1024]{1,0:T(4,128)} %copy-done.27, f32[1,5,2,4,128]{4,3,2,1,0:T(4,128)} %fields.3, f32[1,5,2,4,128]{4,3,2,1,0:T(4,128)} %cotangent.1), custom_call_target="tpu_custom_call" | custom-call | tf_op jit(solution)/shard_map/features/pallas_call | solution.py:467
  9.0 2.4 %collective-permute-start.2 = (bf16[16,1024]{1,0:T(8,128)(2,1)}, bf16[16,1024]{1,0:T(8,128)(2,1)S(1)}, u32[]{:S(2)}, u32[]{:S(2)}) collective-permute-start(bf16[16,1024]{1,0:T(8,128)(2,1)} %get-tuple-element.48), channel_id=1, source_target_pairs={{0,1},{1,0},{2,3},{3,2},{4,5},{5,4},{6,7},{7,6},{8,9},{9,8},{10,11... | collective-permute-start | bytes 98312 | tf_op jit(solution)/shard_map/ppermute | solution.py:454
  11.4 2.6 %collective-permute-start.3 = (bf16[16,1024]{1,0:T(8,128)(2,1)}, bf16[16,1024]{1,0:T(8,128)(2,1)S(1)}, u32[]{:S(2)}, u32[]{:S(2)}) collective-permute-start(bf16[16,1024]{1,0:T(8,128)(2,1)} %get-tuple-element.48), channel_id=1, source_target_pairs={{0,2},{1,3},{2,0},{3,1},{4,6},{5,7},{6,4},{7,5},{8,10},{9,11},{10,... | collective-permute-start | bytes 98312 | tf_op jit(solution)/shard_map/ppermute | solution.py:454
  14.0 3.3 %collective-permute-done.3 = bf16[16,1024]{1,0:T(8,128)(2,1)S(1)} collective-permute-done((bf16[16,1024]{1,0:T(8,128)(2,1)}, bf16[16,1024]{1,0:T(8,128)(2,1)S(1)}, u32[]{:S(2)}, u32[]{:S(2)}) %collective-permute-start.3) | collective-permute-done | bytes 32800 | tf_op jit(solution)/shard_map/ppermute | solution.py:454
  17.3 2.9 %collective-permute-done.4 = bf16[16,1024]{1,0:T(8,128)(2,1)S(1)} collective-permute-done((bf16[16,1024]{1,0:T(8,128)(2,1)}, bf16[16,1024]{1,0:T(8,128)(2,1)S(1)}, u32[]{:S(2)}, u32[]{:S(2)}) %collective-permute-start.4) | collective-permute-done | bytes 32800 | tf_op jit(solution)/shard_map/ppermute | solution.py:454
  20.2 0.8 pad_maximum_fusion.refs_0_
  21.0 1.3 %collective-permute-start.5 = (bf16[4,16,1024]{2,1,0:T(8,128)(2,1)S(1)}, bf16[4,16,1024]{2,1,0:T(8,128)(2,1)S(1)}, u32[]{:S(2)}, u32[]{:S(2)}) collective-permute-start(bf16[4,16,1024]{2,1,0:T(8,128)(2,1)S(1)} %pad_maximum_fusion.refs_0_), channel_id=1, source_target_pairs={{0,8},{1,9},{2,10},{3,11},{4,12},{5,13},{6,14},{7,15},{8,0},{9,1},... | collective-permute-start | bytes 393224 | tf_op jit(solution)/shard_map/ppermute | solution.py:454
  22.3 0.5 broadcast_multiply_fusion.place
  22.8 0.0 collective-permute-start.6
  22.8 3.8 %collective-permute-done.5.refs_1_ = bf16[4,16,1024]{2,1,0:T(8,128)(2,1)S(1)} collective-permute-done((bf16[4,16,1024]{2,1,0:T(8,128)(2,1)S(1)}, bf16[4,16,1024]{2,1,0:T(8,128)(2,1)S(1)}, u32[]{:S(2)}, u32[]{:S(2)}) %collective-permute-start.5) | collective-permute-done | bytes 131104 | tf_op jit(solution)/shard_map/ppermute | solution.py:454
  26.6 4.0 %weights.1 = (bf16[432,256]{1,0:T(8,128)(2,1)}, bf16[256,432]{1,0:T(8,128)(2,1)}, bf16[256,256]{1,0:T(8,128)(2,1)}, bf16[16,16]{1,0:T(8,128)(2,1)}, bf16[16,16]{1,0:T(8,128)(2,1)}) custom-call(s32[1]{0:T(128)} %bitcast.8.me, bf16[9,27,256]{2,1,0:T(8,128)(2,1)} %bitcast.56, bf16[27,256,256]{2,1,0:T(8,128)(2,1)} %w_mid.1, bf16[5,256]{1,0:T(8,128)(2,1)} %bitcast.58), custom_call_target="tpu_custom_call" | custom-call | flops 1500000000 | bytes 4194304 | tf_op jit(solution)/shard_map/weights/pallas_call | solution.py:490
  30.5 0.0 collective-permute-done.7.refs_3_
  30.6 0.6 copy-done.21
  31.2 0.1 copy-done.22
  31.2 16.4 %closure.1 = (bf16[448,256]{1,0:T(8,128)(2,1)}, bf16[4,8,16,256]{3,2,1,0:T(8,128)(2,1)}, bf16[4,3,16,4096]{3,2,1,0:T(8,128)(2,1)}, bf16[4,256,4096]{2,1,0:T(8,128)(2,1)}) custom-call(s32[4]{0:T(128)} %broadcast_multiply_fusion.place, bf16[256,256]{1,0:T(8,128)(2,1)} %get-tuple-element.44.w_first, bf16[432,256]{1,0:T(8,128)(2,1)} %get-tuple-element.45.wt, ...), custom_call_target="tpu_custom_call" | custom-call | flops 8999999488 | bytes 4194304 | tf_op jit(solution)/shard_map/closure/pallas_call | solution.py:507
  47.7 0.0 collective-permute-start.8
  47.7 2.0 %collective-permute-start.9 = (bf16[448,256]{1,0:T(8,128)(2,1)}, bf16[448,256]{1,0:T(8,128)(2,1)S(1)}, u32[]{:S(2)}, u32[]{:S(2)}) collective-permute-start(bf16[448,256]{1,0:T(8,128)(2,1)} %get-tuple-element.49), channel_id=1, source_target_pairs={{0,8},{4,12},{1,0},{5,4},{2,1},{6,5},{3,2},{7,6},{11,3},{15,7},{10... | collective-permute-start | bytes 688136 | tf_op jit(solution)/shard_map/ppermute | solution.py:567
  49.7 8.4 %first.2.one = f32[256,256]{1,0:T(8,128)} custom-call(bf16[256,256]{1,0:T(8,128)(2,1)} %get-tuple-element.44.w_first, bf16[256,432]{1,0:T(8,128)(2,1)} %get-tuple-element.50.w_back, bf16[4,256,4096]{2,1,0:T(8,128)(2,1)} %get-tuple-element.56.fcol, bf16[4,3,16,4096]{3,2,1,0:T(8,128)(2,1)} %get-tuple-element.57.g2z), custom_call_target="tpu_custom_call" | custom-call | flops 3800000000 | bytes 4194304 | tf_op jit(solution)/shard_map/first/pallas_call | solution.py:539
  58.1 0.1 collective-permute-start.10
  58.2 2.0 %collective-permute-start.11 = (bf16[448,256]{1,0:T(8,128)(2,1)S(1)}, bf16[448,256]{1,0:T(8,128)(2,1)S(1)}, u32[]{:S(2)}, u32[]{:S(2)}) collective-permute-start(bf16[448,256]{1,0:T(8,128)(2,1)S(1)} %collective-permute-done.9), channel_id=1, source_target_pairs={{0,8},{4,12},{1,0},{5,4},{2,1},{6,5},{3,2},{7,6},{11,3},{15,7},{10... | collective-permute-start | bytes 688136 | tf_op jit(solution)/shard_map/ppermute | solution.py:567
  60.2 8.4 %first.3.two = f32[256,256]{1,0:T(8,128)} custom-call(bf16[256,256]{1,0:T(8,128)(2,1)} %get-tuple-element.44.w_first, bf16[256,432]{1,0:T(8,128)(2,1)} %get-tuple-element.50.w_back, bf16[4,256,4096]{2,1,0:T(8,128)(2,1)} %get-tuple-element.56.fcol, bf16[4,3,16,4096]{3,2,1,0:T(8,128)(2,1)} %get-tuple-element.57.g2z), custom_call_target="tpu_custom_call" | custom-call | flops 3800000000 | bytes 4194304 | tf_op jit(solution)/shard_map/first/pallas_call | solution.py:539
  68.7 2.2 %split.1 = (f32[384,256]{1,0:T(8,128)}, f32[128,256]{1,0:T(8,128)}, f32[256,256]{1,0:T(8,128)}) custom-call(s32[1]{0:T(128)} %bitcast.7.core, f32[256,256]{1,0:T(8,128)} %first.2.one, f32[256,256]{1,0:T(8,128)} %first.3.two, bf16[4,8,16,256]{3,2,1,0:T(8,128)(2,1)} %get-tuple-element.59.closure), custom_call_target="tpu_custom_call" | custom-call | tf_op jit(solution)/shard_map/split/pallas_call | solution.py:580
  70.9 0.5 collective-permute-start.21
  71.4 0.1 collective-permute-start.18
  71.4 1.3 %collective-permute-done.12.got = f32[384,256]{1,0:T(8,128)S(1)} collective-permute-done((f32[384,256]{1,0:T(8,128)}, f32[384,256]{1,0:T(8,128)S(1)}, u32[]{:S(2)}, u32[]{:S(2)}) %collective-permute-start.12) | collective-permute-done | bytes 393248 | tf_op jit(solution)/shard_map/ppermute | solution.py:454
  72.8 0.7 copy-done.1
  73.5 1.9 %merge.1 = (bf16[256,256]{1,0:T(8,128)(2,1)}, f32[128,256]{1,0:T(8,128)}) custom-call(s32[1]{0:T(128)} %bitcast.6.bit, f32[384,256]{1,0:T(8,128)} %copy-done.1, f32[128,256]{1,0:T(8,128)} %get-tuple-element.61.mine, f32[256,256]{1,0:T(8,128)} %get-tuple-element.62.kept), custom_call_target="tpu_custom_call" | custom-call | tf_op jit(solution)/shard_map/merge/pallas_call | solution.py:589
  75.4 0.7 collective-permute-start.13
  76.1 5.6 %collective-permute-done.13.got = bf16[256,256]{1,0:T(8,128)(2,1)S(1)} collective-permute-done((bf16[256,256]{1,0:T(8,128)(2,1)}, bf16[256,256]{1,0:T(8,128)(2,1)S(1)}, u32[]{:S(2)}, u32[]{:S(2)}) %collective-permute-start.13) | collective-permute-done | bytes 131104 | tf_op jit(solution)/shard_map/ppermute | solution.py:454
  81.8 0.7 copy-done.19
  82.4 1.8 %fan.1 = (f32[32,256]{1,0:T(8,128)}, bf16[160,256]{1,0:T(8,128)(2,1)}, bf16[160,256]{1,0:T(8,128)(2,1)}, bf16[160,256]{1,0:T(8,128)(2,1)}) custom-call(bf16[256,256]{1,0:T(8,128)(2,1)} %copy-done.19, bf16[256,256]{1,0:T(8,128)(2,1)} %get-tuple-element.63.mine, f32[128,256]{1,0:T(8,128)} %get-tuple-element.64.kept), custom_call_target="tpu_custom_call" | custom-call | tf_op jit(solution)/shard_map/fan/pallas_call | solution.py:598
  84.2 0.6 collective-permute-start.15
  84.7 3.8 %collective-permute-start.16 = (bf16[160,256]{1,0:T(8,128)(2,1)}, bf16[160,256]{1,0:T(8,128)(2,1)S(1)}, u32[]{:S(2)}, u32[]{:S(2)}) collective-permute-start(bf16[160,256]{1,0:T(8,128)(2,1)} %get-tuple-element.68), channel_id=1, source_target_pairs={{0,3},{1,2},{2,1},{3,0},{4,7},{5,6},{6,5},{7,4},{8,11},{9,10},{10,... | collective-permute-start | bytes 245768 | tf_op jit(solution)/shard_map/ppermute | solution.py:454
  88.6 0.1 collective-permute-start.22
  88.7 0.5 collective-permute-start.23
  89.2 0.0 collective-permute-done.14.one
  89.2 0.1 collective-permute-start.24
  89.3 4.7 %collective-permute-done.15.two = bf16[160,256]{1,0:T(8,128)(2,1)S(1)} collective-permute-done((bf16[160,256]{1,0:T(8,128)(2,1)}, bf16[160,256]{1,0:T(8,128)(2,1)S(1)}, u32[]{:S(2)}, u32[]{:S(2)}) %collective-permute-start.15) | collective-permute-done | bytes 81952 | tf_op jit(solution)/shard_map/ppermute | solution.py:454
  94.1 2.3 %collective-permute-start.20 = (bf16[448,256]{1,0:T(8,128)(2,1)S(1)}, bf16[448,256]{1,0:T(8,128)(2,1)S(1)}, u32[]{:S(2)}, u32[]{:S(2)}) collective-permute-start(bf16[448,256]{1,0:T(8,128)(2,1)S(1)} %collective-permute-done.18), channel_id=1, source_target_pairs={{0,1},{4,5},{1,2},{5,6},{2,3},{6,7},{3,11},{7,15},{11,10},{15,14},... | collective-permute-start | bytes 688136 | tf_op jit(solution)/shard_map/ppermute | solution.py:567
  96.4 0.1 fusion.3
  96.4 0.6 gather_fusion
  97.1 1.7 %total.1 = (f32[128,256]{1,0:T(8,128)}, f32[32,256]{1,0:T(8,128)}) custom-call(bf16[160,256]{1,0:T(8,128)(2,1)} %get-tuple-element.65.mine, f32[32,256]{1,0:T(8,128)} %get-tuple-element.66.kept, bf16[160,256]{1,0:T(8,128)(2,1)} %copy-done.23, bf16[160,256]{1,0:T(8,128)(2,1)} %copy-done.24, bf16[160,256]{1,0:T(8,128)(2,1)} %copy-done.25), custom_call_target="tpu_custom_call" | custom-call | tf_op jit(solution)/shard_map/total/pallas_call | solution.py:608
  98.8 0.1 collective-permute-start.25
  98.9 0.5 collective-permute-start.26
  99.4 0.7 collective-permute-done.19
  100.1 0.1 collective-permute-done.20
  100.1 0.4 collective-permute-start.28
  100.6 0.1 collective-permute-start.17
  100.7 0.6 and_select_fusion.3.place
  101.3 0.6 fusion.1.place
  101.8 1.9 %step.1 = f32[1,5,2,4,128]{4,3,2,1,0:T(4,128)} custom-call(s32[2]{0:T(128)} %and_select_fusion.3.place, f32[1,5,2,4,128]{4,3,2,1,0:T(4,128)} %fields.3, f32[3,1024]{1,0:T(4,128)} %get-tuple-element.43.drag, f32[32,256]{1,0:T(8,128)} %get-tuple-element.69.closure, bf16[4,16,1024]{2,1,0:T(8,128)(2,1)} %copy-done, bf16[4,16,1024]{2,1,0:T(8,128)(2,1)} %copy-done.20, ...), custom_call_target="tpu_custom_call" | custom-call | tf_op jit(solution)/shard_map/step/pallas_call | solution.py:646
  103.9 0.5 copy-done.14
  104.4 0.1 copy-done.15
  104.5 0.1 copy-done.16
  104.6 0.1 copy-done.17
  104.6 0.1 copy-done.18
  104.7 8.1 %finish.1 = (f32[27,256,256]{2,1,0:T(8,128)}, f32[9,27,256]{2,1,0:T(8,128)}, f32[5,256]{1,0:T(8,128)}) custom-call(s32[16]{0:T(128)} %fusion.1.place, s32[1]{0:T(128)} %bitcast.7.core, f32[128,256]{1,0:T(8,128)} %get-tuple-element.70.own, f32[128,256]{1,0:T(8,128)} %copy-done.18, bf16[1,448,256]{2,1,0:T(8,128)(2,1)} %bitcast.34, ...), custom_call_target="tpu_custom_call" | custom-call | tf_op jit(solution)/shard_map/finish/pallas_call | solution.py:656
  (70 shorter events, 0.2 us)
Async XLA Ops:
  2.9 4.0 %collective-permute-start = (f32[4,1024]{1,0:T(4,128)}, f32[4,1024]{1,0:T(4,128)S(1)}, u32[]{:S(2)}, u32[]{:S(2)}) collective-permute-start(f32[4,1024]{1,0:T(4,128)} %get-tuple-element.41), channel_id=1, source_target_pairs={{0,4},{4,8},{8,12},{12,0},{1,5},{5,9},{9,13},{13,1},{2,6},{6,10},{... | collective-permute-start | bytes 49160 | tf_op jit(solution)/shard_map/ppermute | solution.py:465
  3.4 3.6 %collective-permute-start.1 = (f32[4,1024]{1,0:T(4,128)}, f32[4,1024]{1,0:T(4,128)S(1)}, u32[]{:S(2)}, u32[]{:S(2)}) collective-permute-start(f32[4,1024]{1,0:T(4,128)} %get-tuple-element.42), channel_id=1, source_target_pairs={{4,0},{8,4},{12,8},{0,12},{5,1},{9,5},{13,9},{1,13},{6,2},{10,6},{... | collective-permute-start | bytes 49160 | tf_op jit(solution)/shard_map/ppermute | solution.py:466
  7.0 0.6 copy-start.26
  7.0 0.6 copy-start.27
  9.0 5.0 %collective-permute-start.2 = (bf16[16,1024]{1,0:T(8,128)(2,1)}, bf16[16,1024]{1,0:T(8,128)(2,1)S(1)}, u32[]{:S(2)}, u32[]{:S(2)}) collective-permute-start(bf16[16,1024]{1,0:T(8,128)(2,1)} %get-tuple-element.48), channel_id=1, source_target_pairs={{0,1},{1,0},{2,3},{3,2},{4,5},{5,4},{6,7},{7,6},{8,9},{9,8},{10,11... | collective-permute-start | bytes 98312 | tf_op jit(solution)/shard_map/ppermute | solution.py:454
  11.4 5.9 %collective-permute-start.3 = (bf16[16,1024]{1,0:T(8,128)(2,1)}, bf16[16,1024]{1,0:T(8,128)(2,1)S(1)}, u32[]{:S(2)}, u32[]{:S(2)}) collective-permute-start(bf16[16,1024]{1,0:T(8,128)(2,1)} %get-tuple-element.48), channel_id=1, source_target_pairs={{0,2},{1,3},{2,0},{3,1},{4,6},{5,7},{6,4},{7,5},{8,10},{9,11},{10,... | collective-permute-start | bytes 98312 | tf_op jit(solution)/shard_map/ppermute | solution.py:454
  14.0 6.2 %collective-permute-start.4 = (bf16[16,1024]{1,0:T(8,128)(2,1)}, bf16[16,1024]{1,0:T(8,128)(2,1)S(1)}, u32[]{:S(2)}, u32[]{:S(2)}) collective-permute-start(bf16[16,1024]{1,0:T(8,128)(2,1)} %get-tuple-element.48), channel_id=1, source_target_pairs={{0,3},{1,2},{2,1},{3,0},{4,7},{5,6},{6,5},{7,4},{8,11},{9,10},{10,... | collective-permute-start | bytes 98312 | tf_op jit(solution)/shard_map/ppermute | solution.py:454
  21.0 9.6 %copy-start = (bf16[4,16,1024]{2,1,0:T(8,128)(2,1)}, bf16[4,16,1024]{2,1,0:T(8,128)(2,1)S(1)}, u32[]{:S(2)}) copy-start(bf16[4,16,1024]{2,1,0:T(8,128)(2,1)S(1)} %pad_maximum_fusion.refs_0_) | copy-start | bytes 393220
  21.0 5.6 %collective-permute-start.5 = (bf16[4,16,1024]{2,1,0:T(8,128)(2,1)S(1)}, bf16[4,16,1024]{2,1,0:T(8,128)(2,1)S(1)}, u32[]{:S(2)}, u32[]{:S(2)}) collective-permute-start(bf16[4,16,1024]{2,1,0:T(8,128)(2,1)S(1)} %pad_maximum_fusion.refs_0_), channel_id=1, source_target_pairs={{0,8},{1,9},{2,10},{3,11},{4,12},{5,13},{6,14},{7,15},{8,0},{9,1},... | collective-permute-start | bytes 393224 | tf_op jit(solution)/shard_map/ppermute | solution.py:454
  22.8 7.7 %collective-permute-start.6 = (bf16[4,16,1024]{2,1,0:T(8,128)(2,1)S(1)}, bf16[4,16,1024]{2,1,0:T(8,128)(2,1)S(1)}, u32[]{:S(2)}, u32[]{:S(2)}) collective-permute-start(bf16[4,16,1024]{2,1,0:T(8,128)(2,1)S(1)} %pad_maximum_fusion.refs_0_), channel_id=1, source_target_pairs={{0,4},{1,5},{2,6},{3,7},{4,0},{5,1},{6,2},{7,3},{8,12},{9,13},{10,... | collective-permute-start | bytes 393224 | tf_op jit(solution)/shard_map/ppermute | solution.py:454
  26.6 4.0 %copy-start.20 = (bf16[4,16,1024]{2,1,0:T(8,128)(2,1)}, bf16[4,16,1024]{2,1,0:T(8,128)(2,1)S(1)}, u32[]{:S(2)}) copy-start(bf16[4,16,1024]{2,1,0:T(8,128)(2,1)S(1)} %collective-permute-done.5.refs_1_) | copy-start | bytes 393220
  26.6 4.0 %collective-permute-start.7 = (bf16[4,16,1024]{2,1,0:T(8,128)(2,1)S(1)}, bf16[4,16,1024]{2,1,0:T(8,128)(2,1)S(1)}, u32[]{:S(2)}, u32[]{:S(2)}) collective-permute-start(bf16[4,16,1024]{2,1,0:T(8,128)(2,1)S(1)} %collective-permute-done.5.refs_1_), channel_id=1, source_target_pairs={{0,4},{1,5},{2,6},{3,7},{4,0},{5,1},{6,2},{7,3},{8,12},{9,13},{10,... | collective-permute-start | bytes 393224 | tf_op jit(solution)/shard_map/ppermute | solution.py:454
  30.5 0.6 copy-start.21
  30.5 0.7 copy-start.22
  47.7 10.4 %collective-permute-start.8 = (bf16[448,256]{1,0:T(8,128)(2,1)}, bf16[448,256]{1,0:T(8,128)(2,1)S(1)}, u32[]{:S(2)}, u32[]{:S(2)}) collective-permute-start(bf16[448,256]{1,0:T(8,128)(2,1)} %get-tuple-element.49), channel_id=1, source_target_pairs={{0,1},{4,5},{1,2},{5,6},{2,3},{6,7},{3,11},{7,15},{11,10},{15,14},... | collective-permute-start | bytes 688136 | tf_op jit(solution)/shard_map/ppermute | solution.py:567
  47.7 10.4 %collective-permute-start.9 = (bf16[448,256]{1,0:T(8,128)(2,1)}, bf16[448,256]{1,0:T(8,128)(2,1)S(1)}, u32[]{:S(2)}, u32[]{:S(2)}) collective-permute-start(bf16[448,256]{1,0:T(8,128)(2,1)} %get-tuple-element.49), channel_id=1, source_target_pairs={{0,8},{4,12},{1,0},{5,4},{2,1},{6,5},{3,2},{7,6},{11,3},{15,7},{10... | collective-permute-start | bytes 688136 | tf_op jit(solution)/shard_map/ppermute | solution.py:567
  58.1 12.8 %copy-start.2 = (bf16[448,256]{1,0:T(8,128)(2,1)S(1)}, bf16[448,256]{1,0:T(8,128)(2,1)}, u32[]{:S(2)}) copy-start(bf16[448,256]{1,0:T(8,128)(2,1)} %get-tuple-element.49) | copy-start | bytes 688132
  58.1 30.4 %copy-start.3 = (bf16[448,256]{1,0:T(8,128)(2,1)}, bf16[448,256]{1,0:T(8,128)(2,1)S(1)}, u32[]{:S(2)}) copy-start(bf16[448,256]{1,0:T(8,128)(2,1)S(1)} %collective-permute-done.8) | copy-start | bytes 688132
  58.1 30.5 %copy-start.4 = (bf16[448,256]{1,0:T(8,128)(2,1)}, bf16[448,256]{1,0:T(8,128)(2,1)S(1)}, u32[]{:S(2)}) copy-start(bf16[448,256]{1,0:T(8,128)(2,1)S(1)} %collective-permute-done.9) | copy-start | bytes 688132
  58.1 10.5 %collective-permute-start.10 = (bf16[448,256]{1,0:T(8,128)(2,1)S(1)}, bf16[448,256]{1,0:T(8,128)(2,1)S(1)}, u32[]{:S(2)}, u32[]{:S(2)}) collective-permute-start(bf16[448,256]{1,0:T(8,128)(2,1)S(1)} %collective-permute-done.8), channel_id=1, source_target_pairs={{0,1},{4,5},{1,2},{5,6},{2,3},{6,7},{3,11},{7,15},{11,10},{15,14},... | collective-permute-start | bytes 688136 | tf_op jit(solution)/shard_map/ppermute | solution.py:567
  58.2 10.4 %collective-permute-start.11 = (bf16[448,256]{1,0:T(8,128)(2,1)S(1)}, bf16[448,256]{1,0:T(8,128)(2,1)S(1)}, u32[]{:S(2)}, u32[]{:S(2)}) collective-permute-start(bf16[448,256]{1,0:T(8,128)(2,1)S(1)} %collective-permute-done.9), channel_id=1, source_target_pairs={{0,8},{4,12},{1,0},{5,4},{2,1},{6,5},{3,2},{7,6},{11,3},{15,7},{10... | collective-permute-start | bytes 688136 | tf_op jit(solution)/shard_map/ppermute | solution.py:567
  68.6 35.2 %copy-start.5 = (bf16[448,256]{1,0:T(8,128)(2,1)}, bf16[448,256]{1,0:T(8,128)(2,1)S(1)}, u32[]{:S(2)}) copy-start(bf16[448,256]{1,0:T(8,128)(2,1)S(1)} %collective-permute-done.10) | copy-start | bytes 688132
  68.7 35.2 %copy-start.6 = (bf16[448,256]{1,0:T(8,128)(2,1)}, bf16[448,256]{1,0:T(8,128)(2,1)S(1)}, u32[]{:S(2)}) copy-start(bf16[448,256]{1,0:T(8,128)(2,1)S(1)} %collective-permute-done.11) | copy-start | bytes 688132
  70.8 1.9 %collective-permute-start.12 = (f32[384,256]{1,0:T(8,128)}, f32[384,256]{1,0:T(8,128)S(1)}, u32[]{:S(2)}, u32[]{:S(2)}) collective-permute-start(f32[384,256]{1,0:T(8,128)} %get-tuple-element.60), channel_id=1, source_target_pairs={{0,4},{1,5},{2,6},{3,7},{4,0},{5,1},{6,2},{7,3},{8,12},{9,13},{10,... | collective-permute-start | bytes 1179656 | tf_op jit(solution)/shard_map/ppermute | solution.py:454
  70.9 17.7 %collective-permute-start.21 = (bf16[448,256]{1,0:T(8,128)(2,1)S(1)}, bf16[448,256]{1,0:T(8,128)(2,1)S(1)}, u32[]{:S(2)}, u32[]{:S(2)}) collective-permute-start(bf16[448,256]{1,0:T(8,128)(2,1)S(1)} %copy-done.2), channel_id=1, source_target_pairs={{0,4},{1,5},{2,6},{3,7},{4,0},{5,1},{6,2},{7,3},{8,12},{9,13},{10,... | collective-permute-start | bytes 688136 | tf_op jit(solution)/shard_map/ppermute | solution.py:454
  71.4 17.3 %collective-permute-start.18 = (bf16[448,256]{1,0:T(8,128)(2,1)S(1)}, bf16[448,256]{1,0:T(8,128)(2,1)S(1)}, u32[]{:S(2)}, u32[]{:S(2)}) collective-permute-start(bf16[448,256]{1,0:T(8,128)(2,1)S(1)} %collective-permute-done.10), channel_id=1, source_target_pairs={{0,1},{4,5},{1,2},{5,6},{2,3},{6,7},{3,11},{7,15},{11,10},{15,14},... | collective-permute-start | bytes 688136 | tf_op jit(solution)/shard_map/ppermute | solution.py:567
  72.8 0.7 copy-start.1
  75.4 6.3 %collective-permute-start.13 = (bf16[256,256]{1,0:T(8,128)(2,1)}, bf16[256,256]{1,0:T(8,128)(2,1)S(1)}, u32[]{:S(2)}, u32[]{:S(2)}) collective-permute-start(bf16[256,256]{1,0:T(8,128)(2,1)} %get-tuple-element.63.mine), channel_id=1, source_target_pairs={{0,8},{1,9},{2,10},{3,11},{4,12},{5,13},{6,14},{7,15},{8,0},{9,1},... | collective-permute-start | bytes 393224 | tf_op jit(solution)/shard_map/ppermute | solution.py:454
  81.7 0.7 copy-start.19
  84.2 5.0 %collective-permute-start.14 = (bf16[160,256]{1,0:T(8,128)(2,1)}, bf16[160,256]{1,0:T(8,128)(2,1)S(1)}, u32[]{:S(2)}, u32[]{:S(2)}) collective-permute-start(bf16[160,256]{1,0:T(8,128)(2,1)} %get-tuple-element.65.mine), channel_id=1, source_target_pairs={{0,1},{1,0},{2,3},{3,2},{4,5},{5,4},{6,7},{7,6},{8,9},{9,8},{10,11... | collective-permute-start | bytes 245768 | tf_op jit(solution)/shard_map/ppermute | solution.py:454
  84.2 9.9 %collective-permute-start.15 = (bf16[160,256]{1,0:T(8,128)(2,1)}, bf16[160,256]{1,0:T(8,128)(2,1)S(1)}, u32[]{:S(2)}, u32[]{:S(2)}) collective-permute-start(bf16[160,256]{1,0:T(8,128)(2,1)} %get-tuple-element.67), channel_id=1, source_target_pairs={{0,2},{1,3},{2,0},{3,1},{4,6},{5,7},{6,4},{7,5},{8,10},{9,11},{10,... | collective-permute-start | bytes 245768 | tf_op jit(solution)/shard_map/ppermute | solution.py:454
  84.7 9.3 %collective-permute-start.16 = (bf16[160,256]{1,0:T(8,128)(2,1)}, bf16[160,256]{1,0:T(8,128)(2,1)S(1)}, u32[]{:S(2)}, u32[]{:S(2)}) collective-permute-start(bf16[160,256]{1,0:T(8,128)(2,1)} %get-tuple-element.68), channel_id=1, source_target_pairs={{0,3},{1,2},{2,1},{3,0},{4,7},{5,6},{6,5},{7,4},{8,11},{9,10},{10,... | collective-permute-start | bytes 245768 | tf_op jit(solution)/shard_map/ppermute | solution.py:454
  88.6 15.3 %copy-start.7 = (bf16[448,256]{1,0:T(8,128)(2,1)}, bf16[448,256]{1,0:T(8,128)(2,1)S(1)}, u32[]{:S(2)}) copy-start(bf16[448,256]{1,0:T(8,128)(2,1)S(1)} %collective-permute-done.21) | copy-start | bytes 688132
  88.6 10.3 %collective-permute-start.22 = (bf16[448,256]{1,0:T(8,128)(2,1)S(1)}, bf16[448,256]{1,0:T(8,128)(2,1)S(1)}, u32[]{:S(2)}, u32[]{:S(2)}) collective-permute-start(bf16[448,256]{1,0:T(8,128)(2,1)S(1)} %collective-permute-done.8), channel_id=1, source_target_pairs={{0,4},{1,5},{2,6},{3,7},{4,0},{5,1},{6,2},{7,3},{8,12},{9,13},{10,... | collective-permute-start | bytes 688136 | tf_op jit(solution)/shard_map/ppermute | solution.py:454
  88.6 15.2 %copy-start.8 = (bf16[448,256]{1,0:T(8,128)(2,1)}, bf16[448,256]{1,0:T(8,128)(2,1)S(1)}, u32[]{:S(2)}) copy-start(bf16[448,256]{1,0:T(8,128)(2,1)S(1)} %collective-permute-done.18) | copy-start | bytes 688132
  88.7 10.2 %collective-permute-start.23 = (bf16[448,256]{1,0:T(8,128)(2,1)S(1)}, bf16[448,256]{1,0:T(8,128)(2,1)S(1)}, u32[]{:S(2)}, u32[]{:S(2)}) collective-permute-start(bf16[448,256]{1,0:T(8,128)(2,1)S(1)} %collective-permute-done.9), channel_id=1, source_target_pairs={{0,4},{1,5},{2,6},{3,7},{4,0},{5,1},{6,2},{7,3},{8,12},{9,13},{10,... | collective-permute-start | bytes 688136 | tf_op jit(solution)/shard_map/ppermute | solution.py:454
  89.2 7.9 %copy-start.23 = (bf16[160,256]{1,0:T(8,128)(2,1)}, bf16[160,256]{1,0:T(8,128)(2,1)S(1)}, u32[]{:S(2)}) copy-start(bf16[160,256]{1,0:T(8,128)(2,1)S(1)} %collective-permute-done.14.one) | copy-start | bytes 245764
  89.2 11.4 %collective-permute-start.24 = (bf16[448,256]{1,0:T(8,128)(2,1)S(1)}, bf16[448,256]{1,0:T(8,128)(2,1)S(1)}, u32[]{:S(2)}, u32[]{:S(2)}) collective-permute-start(bf16[448,256]{1,0:T(8,128)(2,1)S(1)} %collective-permute-done.10), channel_id=1, source_target_pairs={{0,4},{1,5},{2,6},{3,7},{4,0},{5,1},{6,2},{7,3},{8,12},{9,13},{10,... | collective-permute-start | bytes 688136 | tf_op jit(solution)/shard_map/ppermute | solution.py:454
  94.0 3.1 %copy-start.24 = (bf16[160,256]{1,0:T(8,128)(2,1)}, bf16[160,256]{1,0:T(8,128)(2,1)S(1)}, u32[]{:S(2)}) copy-start(bf16[160,256]{1,0:T(8,128)(2,1)S(1)} %collective-permute-done.15.two) | copy-start | bytes 245764
  94.0 6.0 %collective-permute-start.19 = (bf16[448,256]{1,0:T(8,128)(2,1)S(1)}, bf16[448,256]{1,0:T(8,128)(2,1)S(1)}, u32[]{:S(2)}, u32[]{:S(2)}) collective-permute-start(bf16[448,256]{1,0:T(8,128)(2,1)S(1)} %collective-permute-done.11), channel_id=1, source_target_pairs={{0,8},{4,12},{1,0},{5,4},{2,1},{6,5},{3,2},{7,6},{11,3},{15,7},{10... | collective-permute-start | bytes 688136 | tf_op jit(solution)/shard_map/ppermute | solution.py:567
  94.0 3.0 %copy-start.25 = (bf16[160,256]{1,0:T(8,128)(2,1)}, bf16[160,256]{1,0:T(8,128)(2,1)S(1)}, u32[]{:S(2)}) copy-start(bf16[160,256]{1,0:T(8,128)(2,1)S(1)} %collective-permute-done.16.three) | copy-start | bytes 245764
  94.1 6.1 %collective-permute-start.20 = (bf16[448,256]{1,0:T(8,128)(2,1)S(1)}, bf16[448,256]{1,0:T(8,128)(2,1)S(1)}, u32[]{:S(2)}, u32[]{:S(2)}) collective-permute-start(bf16[448,256]{1,0:T(8,128)(2,1)S(1)} %collective-permute-done.18), channel_id=1, source_target_pairs={{0,1},{4,5},{1,2},{5,6},{2,3},{6,7},{3,11},{7,15},{11,10},{15,14},... | collective-permute-start | bytes 688136 | tf_op jit(solution)/shard_map/ppermute | solution.py:567
  98.8 5.0 %copy-start.9 = (bf16[448,256]{1,0:T(8,128)(2,1)}, bf16[448,256]{1,0:T(8,128)(2,1)S(1)}, u32[]{:S(2)}) copy-start(bf16[448,256]{1,0:T(8,128)(2,1)S(1)} %collective-permute-done.22) | copy-start | bytes 688132
  98.8 4.9 %collective-permute-start.25 = (bf16[448,256]{1,0:T(8,128)(2,1)S(1)}, bf16[448,256]{1,0:T(8,128)(2,1)S(1)}, u32[]{:S(2)}, u32[]{:S(2)}) collective-permute-start(bf16[448,256]{1,0:T(8,128)(2,1)S(1)} %collective-permute-done.11), channel_id=1, source_target_pairs={{0,4},{1,5},{2,6},{3,7},{4,0},{5,1},{6,2},{7,3},{8,12},{9,13},{10,... | collective-permute-start | bytes 688136 | tf_op jit(solution)/shard_map/ppermute | solution.py:454
  98.9 4.9 %copy-start.10 = (bf16[448,256]{1,0:T(8,128)(2,1)}, bf16[448,256]{1,0:T(8,128)(2,1)S(1)}, u32[]{:S(2)}) copy-start(bf16[448,256]{1,0:T(8,128)(2,1)S(1)} %collective-permute-done.23) | copy-start | bytes 688132
  98.9 4.8 %collective-permute-start.26 = (bf16[448,256]{1,0:T(8,128)(2,1)S(1)}, bf16[448,256]{1,0:T(8,128)(2,1)S(1)}, u32[]{:S(2)}, u32[]{:S(2)}) collective-permute-start(bf16[448,256]{1,0:T(8,128)(2,1)S(1)} %collective-permute-done.18), channel_id=1, source_target_pairs={{0,4},{1,5},{2,6},{3,7},{4,0},{5,1},{6,2},{7,3},{8,12},{9,13},{10,... | collective-permute-start | bytes 688136 | tf_op jit(solution)/shard_map/ppermute | solution.py:454
  100.1 3.8 %copy-start.12 = (bf16[448,256]{1,0:T(8,128)(2,1)}, bf16[448,256]{1,0:T(8,128)(2,1)S(1)}, u32[]{:S(2)}) copy-start(bf16[448,256]{1,0:T(8,128)(2,1)S(1)} %collective-permute-done.19) | copy-start | bytes 688132
  100.1 3.7 %collective-permute-start.27 = (bf16[448,256]{1,0:T(8,128)(2,1)S(1)}, bf16[448,256]{1,0:T(8,128)(2,1)S(1)}, u32[]{:S(2)}, u32[]{:S(2)}) collective-permute-start(bf16[448,256]{1,0:T(8,128)(2,1)S(1)} %collective-permute-done.19), channel_id=1, source_target_pairs={{0,4},{1,5},{2,6},{3,7},{4,0},{5,1},{6,2},{7,3},{8,12},{9,13},{10,... | collective-permute-start | bytes 688136 | tf_op jit(solution)/shard_map/ppermute | solution.py:454
  100.1 3.7 %copy-start.13 = (bf16[448,256]{1,0:T(8,128)(2,1)}, bf16[448,256]{1,0:T(8,128)(2,1)S(1)}, u32[]{:S(2)}) copy-start(bf16[448,256]{1,0:T(8,128)(2,1)S(1)} %collective-permute-done.20) | copy-start | bytes 688132
  100.1 3.6 %collective-permute-start.28 = (bf16[448,256]{1,0:T(8,128)(2,1)S(1)}, bf16[448,256]{1,0:T(8,128)(2,1)S(1)}, u32[]{:S(2)}, u32[]{:S(2)}) collective-permute-start(bf16[448,256]{1,0:T(8,128)(2,1)S(1)} %collective-permute-done.20), channel_id=1, source_target_pairs={{0,4},{1,5},{2,6},{3,7},{4,0},{5,1},{6,2},{7,3},{8,12},{9,13},{10,... | collective-permute-start | bytes 688136 | tf_op jit(solution)/shard_map/ppermute | solution.py:454
  100.6 3.3 %copy-start.11 = (bf16[448,256]{1,0:T(8,128)(2,1)}, bf16[448,256]{1,0:T(8,128)(2,1)S(1)}, u32[]{:S(2)}) copy-start(bf16[448,256]{1,0:T(8,128)(2,1)S(1)} %collective-permute-done.24) | copy-start | bytes 688132
  100.6 3.2 %collective-permute-start.17 = (f32[128,256]{1,0:T(8,128)}, f32[128,256]{1,0:T(8,128)S(1)}, u32[]{:S(2)}, u32[]{:S(2)}) collective-permute-start(f32[128,256]{1,0:T(8,128)} %get-tuple-element.70.own), channel_id=1, source_target_pairs={{0,4},{1,5},{2,6},{3,7},{4,0},{5,1},{6,2},{7,3},{8,12},{9,13},{10,... | collective-permute-start | bytes 393224 | tf_op jit(solution)/shard_map/ppermute | solution.py:454
  103.7 0.7 copy-start.14
  103.7 0.8 copy-start.15
  103.8 0.8 copy-start.16
  103.8 0.9 copy-start.17
  103.8 0.9 copy-start.18

commit v3 on v2

--- a/solution.py
+++ b/solution.py
@@ -15,7 +15,6 @@
 
 F32 = jnp.float32
 BF16 = jnp.bfloat16
-VMEM_BYTES = 58 * 2**20
 offsets = [(x, y, z) for x in (-1, 0, 1) for y in (-1, 0, 1) for z in (-1, 0, 1)]
 
 
@@ -321,14 +320,19 @@
             messages[o - 1][half:] = rows.astype(BF16)
 
 
-def total_kernel(mine, kept, one, two, three, half, closure):
+def step_kernel(nz, place, fields, drag, closure, *refs):
+    step_fields(nz, place, fields, drag, closure[...], refs[:-1], refs[-1])
+
+
+def total_kernel(nz, place, fields, drag, mine, kept, one, two, three, *refs):
+    sources, (half, out) = refs[:-2], refs[-2:]
     pair = mine[0:128].astype(F32) + one[0:128].astype(F32)
     half[...] = pair + (two[0:128].astype(F32) + three[0:128].astype(F32))
-    closure[...] = kept[...] + (one[128:].astype(F32) + two[128:].astype(F32) + three[128:].astype(F32))
-
-
-def step_kernel(nz, place, fields, drag, closure, *refs):
-    sources, out = refs[:-1], refs[-1]
+    closure = kept[...] + (one[128:].astype(F32) + two[128:].astype(F32) + three[128:].astype(F32))
+    step_fields(nz, place, fields, drag, closure, sources, out)
+
+
+def step_fields(nz, place, fields, drag, closure, sources, out):
     state = flat_cells(fields)
     cells = state.shape[1]
     planes, rows = fields.shape[2], fields.shape[3]
@@ -425,8 +429,8 @@
     return pl.CostEstimate(flops=int(flops), bytes_accessed=2**22, transcendentals=0)
 
 
-def params(**more):
-    return pltpu.CompilerParams(vmem_limit_bytes=VMEM_BYTES, **more)
+def params(mebibytes):
+    return pltpu.CompilerParams(vmem_limit_bytes=mebibytes * 2**20)
 
 
 def shards(
@@ -459,7 +463,7 @@
         out_shape=(dense, dense, dense),
         in_specs=[VMEM] * 4 + [SMEM],
         out_specs=(VMEM,) * 3,
-        compiler_params=params(),
+        compiler_params=params(8),
         name="deposit",
     )(drop_mass, jnp.transpose(drop_vel, (1, 0, 2)), drop_cell, cross_list, cross_count)
     from_below = lax.ppermute(up, "slab", [(i, (i + 1) % n_slab) for i in range(n_slab)])
@@ -469,22 +473,9 @@
         out_shape=(shape((16, cells), BF16), shape((3, cells), F32)),
         in_specs=[VMEM] * 5,
         out_specs=(VMEM,) * 2,
-        compiler_params=params(),
+        compiler_params=params(4),
         name="features",
     )(stay, from_below, from_above, fields, cotangent)
-
-    if fast:
-        near_z = [trade(own_feats, mask) for mask in (1, 2, 3)]
-        mine = jnp.stack([own_feats] + near_z)
-        across = trade(mine, 8)
-        sources = [mine, across, trade(mine, 4), trade(across, 4)]
-        slabs = jnp.arange(n_slab, dtype=jnp.int32)
-        group = 2 * ((slabs ^ slab) & 1) + (((slabs ^ slab) >> 1) & 1)
-        place = group * samples
-    else:
-        sources = [lax.all_gather(own_feats, team)]
-        group = jnp.arange(n_slab, dtype=jnp.int32)
-        place = group * samples
 
     rows = 27 * block
     wt, w_back, w_first, wo, wc = pl.pallas_call(
@@ -498,10 +489,26 @@
         ),
         in_specs=[SMEM] + [VMEM] * 3,
         out_specs=(VMEM,) * 5,
-        compiler_params=params(),
+        compiler_params=params(16),
         cost_estimate=cost(1.5e9),
         name="weights",
     )(me[None], jnp.transpose(w_in, (1, 0, 2)), w_mid, w_out.T)
+
+    if fast:
+        near_z = [trade(own_feats, mask) for mask in (1, 2, 3)]
+        wt, w_back, w_first, wo, wc, *near_z = lax.optimization_barrier((wt, w_back, w_first, wo, wc, *near_z))
+        mine = jnp.stack([own_feats] + near_z)
+        across = trade(mine, 8)
+        sources = [mine, across, trade(mine, 4), trade(across, 4)]
+        slabs = jnp.arange(n_slab, dtype=jnp.int32)
+        group = 2 * ((slabs ^ slab) & 1) + (((slabs ^ slab) >> 1) & 1)
+        place = group * samples
+    else:
+        sources = [lax.all_gather(own_feats, team)]
+        group = jnp.arange(n_slab, dtype=jnp.int32)
+        place = group * samples
+
+    near = jnp.take(group, jnp.stack([(slab + n_slab - 1) % n_slab, (slab + 1) % n_slab]))
 
     team_cells = all_planes * lanes
     piece, closure, g2z, fcol = pl.pallas_call(
@@ -530,7 +537,7 @@
             pltpu.VMEM((rows, hid), F32),
             pltpu.VMEM((16, block), F32),
         ],
-        compiler_params=params(),
+        compiler_params=params(30 if all_planes <= 8 else 58),
         cost_estimate=cost(9e9),
         name="closure",
     )(place, w_first, wt, wo, wc, *sources)
@@ -547,7 +554,7 @@
                 pl.BlockSpec((1, 3, block, team_cells), lambda s: (s + lo, 0, 0, 0)),
             ],
             out_specs=whole_spec((256, hid)),
-            compiler_params=params(),
+            compiler_params=params(18 if all_planes <= 8 else 58),
             cost_estimate=cost(7.6e9 * count / samples),
             name="first",
         )(w_first, w_back, fcol, g2z)
@@ -569,9 +576,15 @@
         def tie(*values):
             return lax.optimization_barrier(values)
 
+        position = jnp.where(y == 0, rep, 7 - rep)
+        theirs, their_z = everyone // n_rep, everyone % n_rep
+        apart = (jnp.where(theirs < 2, their_z, 7 - their_z) - position) % 8
+        piece_place = jnp.where(apart < 4, 2 * apart, 2 * (8 - apart) - 1)
+        piece_place = jnp.where(apart == 0, 0, piece_place) + 8 * ((theirs ^ slab) & 1)
+        piece_place = piece_place.astype(jnp.int32)
         f1, b1 = around(piece, 1), around(piece, -1)
         half_one = first_part(0, samples // 2, fcol, g2z)
-        f1, b1, half_one, fcol, g2z = tie(f1, b1, half_one, fcol, g2z)
+        f1, b1, half_one, fcol, g2z, piece_place, near = tie(f1, b1, half_one, fcol, g2z, piece_place, near)
         f2, b2 = around(f1, 1), around(b1, -1)
         half_two = first_part(samples // 2, samples - samples // 2, fcol, g2z)
         f2, b2, half_two = tie(f2, b2, half_two)
@@ -582,7 +595,7 @@
             out_shape=(shape((384, hid), F32), shape((128, hid), F32), shape((256, hid), F32)),
             in_specs=[SMEM] + [VMEM] * 3,
             out_specs=(VMEM,) * 3,
-            compiler_params=params(),
+            compiler_params=params(4),
             name="split",
         )(core[None], half_one, half_two, closure)
         got = trade(message, 4)
@@ -591,37 +604,31 @@
             out_shape=(shape((256, hid), BF16), shape((128, hid), F32)),
             in_specs=[SMEM] + [VMEM] * 3,
             out_specs=(VMEM,) * 2,
-            compiler_params=params(),
+            compiler_params=params(4),
             name="merge",
         )(y[None], got, keep, kept)
-        got = trade(message, 8)
+        got, f3, b3 = tie(trade(message, 8), f3, b3)
+        f4 = around(f3, 1)
         kept, *messages = pl.pallas_call(
             fan_kernel,
             out_shape=(shape((32, hid), F32),) + (shape((160, hid), BF16),) * 3,
             in_specs=[VMEM] * 3,
             out_specs=(VMEM,) * 4,
-            compiler_params=params(),
+            compiler_params=params(4),
             name="fan",
         )(got, message, kept)
         got = [trade(message, mask) for mask, message in zip((1, 2, 3), messages)]
-        f4 = around(f3, 1)
-        own, own_closure = pl.pallas_call(
-            total_kernel,
-            out_shape=(shape((128, hid), F32), shape((32, hid), F32)),
-            in_specs=[VMEM] * 5,
+        own, new_fields = pl.pallas_call(
+            functools.partial(total_kernel, nz),
+            out_shape=(shape((128, hid), F32), shape(fields.shape, F32)),
+            in_specs=[SMEM] + [VMEM] * (7 + len(sources)),
             out_specs=(VMEM,) * 2,
-            compiler_params=params(),
+            compiler_params=params(6),
             name="total",
-        )(messages[0], kept, *got)
+        )(near, fields, drag, messages[0], kept, *got, *sources)
         other = trade(own, 4)
         pieces = [piece, f1, b1, f2, b2, f3, b3, f4]
         pieces = [v[None] for v in pieces + [trade(v, 4) for v in pieces]]
-        position = jnp.where(y == 0, rep, 7 - rep)
-        theirs, their_z = everyone // n_rep, everyone % n_rep
-        apart = (jnp.where(theirs < 2, their_z, 7 - their_z) - position) % 8
-        piece_place = jnp.where(apart < 4, 2 * apart, 2 * (8 - apart) - 1)
-        piece_place = jnp.where(apart == 0, 0, piece_place) + 8 * ((theirs ^ slab) & 1)
-        piece_place = piece_place.astype(jnp.int32)
     else:
         raw_first = first_part(0, samples, fcol, g2z)
         core = jnp.zeros((), jnp.int32)
@@ -640,17 +647,14 @@
         part = closure.reshape(samples, n_slab, planes * 16, lanes // 2)
         part = jnp.swapaxes(part, 0, 1).reshape(size, planes * 16, lanes // 2).astype(F32)
         own_closure = lax.psum_scatter(part, team, scatter_dimension=0)
-
-    near = jnp.take(group, jnp.stack([(slab + n_slab - 1) % n_slab, (slab + 1) % n_slab]))
-    halo = sources if fast else [sources[0].reshape(n_slab, samples, 16, cells)[:, sample]]
-    new_fields = pl.pallas_call(
-        functools.partial(step_kernel, nz),
-        out_shape=shape(fields.shape, F32),
-        in_specs=[SMEM] + [VMEM] * (3 + len(halo)),
-        out_specs=VMEM,
-        compiler_params=params(),
-        name="step",
-    )(near, fields, drag, own_closure, *halo)
+        new_fields = pl.pallas_call(
+            functools.partial(step_kernel, nz),
+            out_shape=shape(fields.shape, F32),
+            in_specs=[SMEM] + [VMEM] * 4,
+            out_specs=VMEM,
+            compiler_params=params(6),
+            name="step",
+        )(near, fields, drag, own_closure, sources[0].reshape(n_slab, samples, 16, cells)[:, sample])
 
     weight_count = w_in.size + w_mid.size + w_out.size
     grad_middle, grad_first, grad_last = pl.pallas_call(
@@ -664,7 +668,7 @@
             pltpu.SemaphoreType.DMA((len(pieces),)),
             pltpu.SemaphoreType.DMA((27,)),
         ],
-        compiler_params=params(),
+        compiler_params=params(20),
         name="finish",
     )(piece_place, core[None], own, other, *pieces)
     return (new_fields, jnp.transpose(grad_first, (1, 0, 2)), grad_middle, grad_last.T)

time: 113 us -> 99 us (0.88); the launches traced: 113 us -> 97.5 us
  Pallas kernels: 58.4 us -> 41.1 us
  local copies, waits for them, and re-layouts: 4.18 us -> 9.09 us
  other arithmetic: 2.53 us -> 0.21 us
    unnamed x56 -> x22, local copies, waits for them, and re-layouts: 3.55 us -> 8.46 us
    pallas_call x2, Pallas kernels: 16.8 us -> 12.1 us  [first_part(): pl.pallas_call(functools.partial(first_kernel, nz, lanes), grid=(count,),...]
    ppermute x7, waiting for transfers between devices: 0.73 us -> 4.24 us  [around(): lax.ppermute(v, team, [(device(at, c), device(at + by, c)) for at in rang...]
    pallas_call x1, Pallas kernels: 3.96 us -> 1.17 us  [shards(): pl.pallas_call(weight_kernel, out_shape=(shape((rows, hid), BF16), shape(...]
    pallas_call x1, Pallas kernels: 8.05 us -> 10.8 us  [shards(): pl.pallas_call(functools.partial(finish_kernel, len(pieces), weight_count...]
    pallas_call x2 -> x1, Pallas kernels: 3.59 us -> 1.26 us  [shards(): pl.pallas_call(functools.partial(total_kernel, nz), out_shape=(shape((128...]
    pallas_call x1, Pallas kernels: 16.4 us -> 14.2 us  [shards(): pl.pallas_call(functools.partial(closure_kernel, nz, lanes, len(sources))...]
    ppermute x20, waiting for transfers between devices: 21.7 us -> 19.6 us  [trade(): return lax.ppermute(v, team, [(d, d ^ mask) for d in range(size)])]
  transfers between devices with their start and end apart: 29 -> 29, of which waited for: 9 -> 10; matrix products, arithmetic and copies ran while one was open for 2% -> 1% of each run, Pallas kernels for 25% -> 15%
where the time goes in v3:
time: 99 us; the launch traced here: 97.5 us
  Pallas kernels  41.1 us (42%)
  waiting for transfers between devices  23.9 us (24%)
  starting transfers between devices  22.4 us (23%)
  local copies, waits for them, and re-layouts  9.09 us (9%)
    ppermute x20, waiting for transfers between devices, trade(): return lax.ppermute(v, team, [(d, d ^ mask) for d in range(size)])  19.6 us
    pallas_call x1, Pallas kernels, shards(): pl.pallas_call(functools.partial(closure_kernel, nz, lanes, len(sources))...  14.2 us
    ppermute x20, starting transfers between devices, trade(): return lax.ppermute(v, team, [(d, d ^ mask) for d in range(size)])  13.7 us
    pallas_call x2, Pallas kernels, first_part(): pl.pallas_call(functools.partial(first_kernel, nz, lanes), grid=(count,),...  12.1 us
    pallas_call x1, Pallas kernels, shards(): pl.pallas_call(functools.partial(finish_kernel, len(pieces), weight_count...  10.8 us
    unnamed x22, local copies, waits for them, and re-layouts  8.46 us
    ppermute x7, starting transfers between devices, around(): lax.ppermute(v, team, [(device(at, c), device(at + by, c)) for at in rang...  6.23 us
    ppermute x7, waiting for transfers between devices, around(): lax.ppermute(v, team, [(device(at, c), device(at + by, c)) for at in rang...  4.24 us
  transfers between devices with their start and end apart: 29, of which 10 were waited for; matrix products, arithmetic and copies ran while one was open for 1% of the time, Pallas kernels for 15%

profile of v3, /device:TPU:0, one launch (start us, length us, event | category | flops | bytes accessed | tf_op | source)
XLA Modules:
  0.0 97.5 jit_solution(3679989211739142400)
XLA Ops:
  0.6 0.7 copy-done.3
  1.3 0.7 copy-done.4
  2.0 0.7 copy-done.5
  2.7 0.7 copy-done.6
  3.4 0.7 copy-done.7
  4.1 1.4 %deposit.1 = (f32[4,1024]{1,0:T(4,128)S(1)}, f32[4,1024]{1,0:T(4,128)S(1)}, f32[4,1024]{1,0:T(4,128)S(1)}) custom-call(f32[1,1024]{1,0:T(1,128)S(1)} %copy-done.4, f32[3,1,1024]{2,1,0:T(1,128)S(1)} %bitcast.51, s32[1,1024]{1,0:T(1,128)S(1)} %copy-done.5, s32[1,256]{1,0:T(1,128)S(1)} %copy-done.6, s32[1,2]{1,0:T(1,128)S(1)} %copy-done.7), custom_call_target="tpu_custom_call" | custom-call | tf_op jit(solution)/shard_map/deposit/pallas_call | solution.py:461
  5.5 0.5 collective-permute-start
  6.0 2.0 %collective-permute-start.1 = (f32[4,1024]{1,0:T(4,128)S(1)}, f32[4,1024]{1,0:T(4,128)S(1)}, u32[]{:S(2)}, u32[]{:S(2)}) collective-permute-start(f32[4,1024]{1,0:T(4,128)S(1)} %get-tuple-element.60), channel_id=1, source_target_pairs={{4,0},{8,4},{12,8},{0,12},{5,1},{9,5},{13,9},{1,13},{6,2},{10,6},{... | collective-permute-start | bytes 49160 | tf_op jit(solution)/shard_map/ppermute | solution.py:470
  8.0 0.1 fusion.3
  8.1 2.0 %copy-done.8 = bf16[27,256,256]{2,1,0:T(8,128)(2,1)S(1)} copy-done((bf16[27,256,256]{2,1,0:T(8,128)(2,1)S(1)}, bf16[27,256,256]{2,1,0:T(8,128)(2,1)}, u32[]{:S(2)}) %copy-start.8) | copy-done | bytes 3538968
  10.1 0.9 copy-done.9
  11.0 0.7 copy-done.10
  11.7 1.2 %weights.1 = (bf16[432,256]{1,0:T(8,128)(2,1)S(1)}, bf16[256,432]{1,0:T(8,128)(2,1)S(1)}, bf16[256,256]{1,0:T(8,128)(2,1)S(1)}, bf16[16,16]{1,0:T(8,128)(2,1)S(1)}, bf16[16,16]{1,0:T(8,128)(2,1)S(1)}) custom-call(s32[1]{0:T(128)} %bitcast.me, bf16[9,27,256]{2,1,0:T(8,128)(2,1)S(1)} %bitcast.52, bf16[27,256,256]{2,1,0:T(8,128)(2,1)S(1)} %copy-done.8, ...), custom_call_target="tpu_custom_call" | custom-call | flops 1500000000 | bytes 4194304 | tf_op jit(solution)/shard_map/weights/pallas_call | solution.py:481
  12.9 0.0 collective-permute-done.below
  12.9 0.0 collective-permute-done.1.above
  12.9 0.0 copy-start
  12.9 0.7 copy-done
  13.6 0.7 copy-done.2
  14.4 2.4 %collective-permute-start.2 = (bf16[16,1024]{1,0:T(8,128)(2,1)S(1)}, bf16[16,1024]{1,0:T(8,128)(2,1)S(1)}, u32[]{:S(2)}, u32[]{:S(2)}) collective-permute-start(bf16[16,1024]{1,0:T(8,128)(2,1)S(1)} %get-tuple-element.61), channel_id=1, source_target_pairs={{0,1},{1,0},{2,3},{3,2},{4,5},{5,4},{6,7},{7,6},{8,9},{9,8},{10,11... | collective-permute-start | bytes 98312 | tf_op jit(solution)/shard_map/ppermute | solution.py:458
  16.7 2.6 %collective-permute-start.3 = (bf16[16,1024]{1,0:T(8,128)(2,1)S(1)}, bf16[16,1024]{1,0:T(8,128)(2,1)S(1)}, u32[]{:S(2)}, u32[]{:S(2)}) collective-permute-start(bf16[16,1024]{1,0:T(8,128)(2,1)S(1)} %get-tuple-element.61), channel_id=1, source_target_pairs={{0,2},{1,3},{2,0},{3,1},{4,6},{5,7},{6,4},{7,5},{8,10},{9,11},{10,... | collective-permute-start | bytes 98312 | tf_op jit(solution)/shard_map/ppermute | solution.py:458
  19.3 0.6 gather_fusion
  20.0 0.0 collective-permute-done.2
  20.0 2.2 %collective-permute-done.3 = bf16[16,1024]{1,0:T(8,128)(2,1)S(1)} collective-permute-done((bf16[16,1024]{1,0:T(8,128)(2,1)S(1)}, bf16[16,1024]{1,0:T(8,128)(2,1)S(1)}, u32[]{:S(2)}, u32[]{:S(2)}) %collective-permute-start.3) | collective-permute-done | bytes 32800 | tf_op jit(solution)/shard_map/ppermute | solution.py:458
  22.2 2.9 %collective-permute-done.4 = bf16[16,1024]{1,0:T(8,128)(2,1)S(1)} collective-permute-done((bf16[16,1024]{1,0:T(8,128)(2,1)S(1)}, bf16[16,1024]{1,0:T(8,128)(2,1)S(1)}, u32[]{:S(2)}, u32[]{:S(2)}) %collective-permute-start.4) | collective-permute-done | bytes 32800 | tf_op jit(solution)/shard_map/ppermute | solution.py:458
  25.1 1.6 %collective-permute-start.5 = (bf16[4,16,1024]{2,1,0:T(8,128)(2,1)S(1)}, bf16[4,16,1024]{2,1,0:T(8,128)(2,1)S(1)}, u32[]{:S(2)}, u32[]{:S(2)}) collective-permute-start(bf16[4,16,1024]{2,1,0:T(8,128)(2,1)S(1)} %pad_maximum_fusion.refs_0_), channel_id=1, source_target_pairs={{0,8},{1,9},{2,10},{3,11},{4,12},{5,13},{6,14},{7,15},{8,0},{9,1},... | collective-permute-start | bytes 393224 | tf_op jit(solution)/shard_map/ppermute | solution.py:458
  26.6 0.1 and_select_fusion.place
  26.7 0.0 collective-permute-start.6
  26.7 3.4 %collective-permute-done.5.refs_1_ = bf16[4,16,1024]{2,1,0:T(8,128)(2,1)S(1)} collective-permute-done((bf16[4,16,1024]{2,1,0:T(8,128)(2,1)S(1)}, bf16[4,16,1024]{2,1,0:T(8,128)(2,1)S(1)}, u32[]{:S(2)}, u32[]{:S(2)}) %collective-permute-start.5) | collective-permute-done | bytes 131104 | tf_op jit(solution)/shard_map/ppermute | solution.py:458
  30.1 0.0 collective-permute-start.7
  30.1 1.3 %collective-permute-done.7.refs_3_ = bf16[4,16,1024]{2,1,0:T(8,128)(2,1)S(1)} collective-permute-done((bf16[4,16,1024]{2,1,0:T(8,128)(2,1)S(1)}, bf16[4,16,1024]{2,1,0:T(8,128)(2,1)S(1)}, u32[]{:S(2)}, u32[]{:S(2)}) %collective-permute-start.7) | collective-permute-done | bytes 131104 | tf_op jit(solution)/shard_map/ppermute | solution.py:458
  31.4 14.2 %closure.1 = (bf16[448,256]{1,0:T(8,128)(2,1)S(1)}, bf16[4,8,16,256]{3,2,1,0:T(8,128)(2,1)S(1)}, bf16[4,3,16,4096]{3,2,1,0:T(8,128)(2,1)S(1)}, bf16[4,256,4096]{2,1,0:T(8,128)(2,1)S(1)}) custom-call(s32[4]{0:T(128)S(1)} %broadcast_multiply_fusion.place, bf16[256,256]{1,0:T(8,128)(2,1)S(1)} %get-tuple-element.62.w_first, ...), custom_call_target="tpu_custom_call" | custom-call | flops 8999999488 | bytes 4194304 | tf_op jit(solution)/shard_map/closure/pallas_call | solution.py:514
  45.7 0.1 collective-permute-start.8
  45.7 2.0 %collective-permute-start.9 = (bf16[448,256]{1,0:T(8,128)(2,1)S(1)}, bf16[448,256]{1,0:T(8,128)(2,1)S(1)}, u32[]{:S(2)}, u32[]{:S(2)}) collective-permute-start(bf16[448,256]{1,0:T(8,128)(2,1)S(1)} %get-tuple-element.69), channel_id=1, source_target_pairs={{0,8},{4,12},{1,0},{5,4},{2,1},{6,5},{3,2},{7,6},{11,3},{15,7},{10... | collective-permute-start | bytes 688136 | tf_op jit(solution)/shard_map/ppermute | solution.py:574
  47.8 6.0 %first.2.one = f32[256,256]{1,0:T(8,128)S(1)} custom-call(bf16[256,256]{1,0:T(8,128)(2,1)S(1)} %get-tuple-element.62.w_first, bf16[256,432]{1,0:T(8,128)(2,1)S(1)} %get-tuple-element.70.w_back, bf16[4,256,4096]{2,1,0:T(8,128)(2,1)S(1)} %get-tuple-element.78.fcol, bf16[4,3,16,4096]{3,2,1,0:T(8,128)(2,1)S(1)} %get-tuple-element.79.g2z), custom_call_target="tpu_custom_call" | custom-call | flops 3800000000 | bytes 4194304 | tf_op jit(solution)/shard_map/first/pallas_call | solution.py:546
  53.8 0.0 copy-start.1
  53.8 0.1 collective-permute-start.10
  53.9 2.0 %collective-permute-start.11 = (bf16[448,256]{1,0:T(8,128)(2,1)S(1)}, bf16[448,256]{1,0:T(8,128)(2,1)S(1)}, u32[]{:S(2)}, u32[]{:S(2)}) collective-permute-start(bf16[448,256]{1,0:T(8,128)(2,1)S(1)} %collective-permute-done.9), channel_id=1, source_target_pairs={{0,8},{4,12},{1,0},{5,4},{2,1},{6,5},{3,2},{7,6},{11,3},{15,7},{10... | collective-permute-start | bytes 688136 | tf_op jit(solution)/shard_map/ppermute | solution.py:574
  55.9 6.0 %first.3.two = f32[256,256]{1,0:T(8,128)S(1)} custom-call(bf16[256,256]{1,0:T(8,128)(2,1)S(1)} %get-tuple-element.62.w_first, bf16[256,432]{1,0:T(8,128)(2,1)S(1)} %get-tuple-element.70.w_back, bf16[4,256,4096]{2,1,0:T(8,128)(2,1)S(1)} %get-tuple-element.78.fcol, bf16[4,3,16,4096]{3,2,1,0:T(8,128)(2,1)S(1)} %get-tuple-element.79.g2z), custom_call_target="tpu_custom_call" | custom-call | flops 3800000000 | bytes 4194304 | tf_op jit(solution)/shard_map/first/pallas_call | solution.py:546
  61.9 0.0 collective-permute-done.10
  62.0 0.1 split.1
  62.0 0.1 collective-permute-start.12
  62.1 0.1 collective-permute-start.14
  62.2 2.0 %collective-permute-start.15 = (bf16[448,256]{1,0:T(8,128)(2,1)S(1)}, bf16[448,256]{1,0:T(8,128)(2,1)S(1)}, u32[]{:S(2)}, u32[]{:S(2)}) collective-permute-start(bf16[448,256]{1,0:T(8,128)(2,1)S(1)} %collective-permute-done.11), channel_id=1, source_target_pairs={{0,8},{4,12},{1,0},{5,4},{2,1},{6,5},{3,2},{7,6},{11,3},{15,7},{10... | collective-permute-start | bytes 688136 | tf_op jit(solution)/shard_map/ppermute | solution.py:574
  64.2 0.1 merge.1
  64.3 1.6 %collective-permute-start.13 = (bf16[256,256]{1,0:T(8,128)(2,1)S(1)}, bf16[256,256]{1,0:T(8,128)(2,1)S(1)}, u32[]{:S(2)}, u32[]{:S(2)}) collective-permute-start(bf16[256,256]{1,0:T(8,128)(2,1)S(1)} %get-tuple-element.85.mine), channel_id=1, source_target_pairs={{0,8},{1,9},{2,10},{3,11},{4,12},{5,13},{6,14},{7,15},{8,0},{9,1},... | collective-permute-start | bytes 393224 | tf_op jit(solution)/shard_map/ppermute | solution.py:458
  65.8 0.5 collective-permute-start.22
  66.3 4.2 %collective-permute-done.14 = bf16[448,256]{1,0:T(8,128)(2,1)S(1)} collective-permute-done((bf16[448,256]{1,0:T(8,128)(2,1)S(1)}, bf16[448,256]{1,0:T(8,128)(2,1)S(1)}, u32[]{:S(2)}, u32[]{:S(2)}) %collective-permute-start.14) | collective-permute-done | bytes 229408 | tf_op jit(solution)/shard_map/ppermute | solution.py:574
  70.6 0.0 collective-permute-start.23
  70.6 2.4 %collective-permute-done.13.got = bf16[256,256]{1,0:T(8,128)(2,1)S(1)} collective-permute-done((bf16[256,256]{1,0:T(8,128)(2,1)S(1)}, bf16[256,256]{1,0:T(8,128)(2,1)S(1)}, u32[]{:S(2)}, u32[]{:S(2)}) %collective-permute-start.13) | collective-permute-done | bytes 131104 | tf_op jit(solution)/shard_map/ppermute | solution.py:458
  72.9 0.0 collective-permute-start.20
  72.9 0.0 collective-permute-start.24
  73.0 0.0 collective-permute-done.21
  73.0 0.1 collective-permute-start.16
  73.1 0.0 collective-permute-done.22
  73.1 2.9 %collective-permute-start.17 = (bf16[160,256]{1,0:T(8,128)(2,1)S(1)}, bf16[160,256]{1,0:T(8,128)(2,1)S(1)}, u32[]{:S(2)}, u32[]{:S(2)}) collective-permute-start(bf16[160,256]{1,0:T(8,128)(2,1)S(1)} %get-tuple-element.92), channel_id=1, source_target_pairs={{0,2},{1,3},{2,0},{3,1},{4,6},{5,7},{6,4},{7,5},{8,10},{9,11},{10,... | collective-permute-start | bytes 245768 | tf_op jit(solution)/shard_map/ppermute | solution.py:458
  76.0 1.4 %collective-permute-start.18 = (bf16[160,256]{1,0:T(8,128)(2,1)S(1)}, bf16[160,256]{1,0:T(8,128)(2,1)S(1)}, u32[]{:S(2)}, u32[]{:S(2)}) collective-permute-start(bf16[160,256]{1,0:T(8,128)(2,1)S(1)} %get-tuple-element.93), channel_id=1, source_target_pairs={{0,3},{1,2},{2,1},{3,0},{4,7},{5,6},{6,5},{7,4},{8,11},{9,10},{10,... | collective-permute-start | bytes 245768 | tf_op jit(solution)/shard_map/ppermute | solution.py:458
  77.4 3.2 %collective-permute-done.16.one = bf16[160,256]{1,0:T(8,128)(2,1)S(1)} collective-permute-done((bf16[160,256]{1,0:T(8,128)(2,1)S(1)}, bf16[160,256]{1,0:T(8,128)(2,1)S(1)}, u32[]{:S(2)}, u32[]{:S(2)}) %collective-permute-start.16) | collective-permute-done | bytes 81952 | tf_op jit(solution)/shard_map/ppermute | solution.py:458
  80.7 1.6 %collective-permute-done.17.two = bf16[160,256]{1,0:T(8,128)(2,1)S(1)} collective-permute-done((bf16[160,256]{1,0:T(8,128)(2,1)S(1)}, bf16[160,256]{1,0:T(8,128)(2,1)S(1)}, u32[]{:S(2)}, u32[]{:S(2)}) %collective-permute-start.17) | collective-permute-done | bytes 81952 | tf_op jit(solution)/shard_map/ppermute | solution.py:458
  82.3 1.3 %collective-permute-done.18.three = bf16[160,256]{1,0:T(8,128)(2,1)S(1)} collective-permute-done((bf16[160,256]{1,0:T(8,128)(2,1)S(1)}, bf16[160,256]{1,0:T(8,128)(2,1)S(1)}, u32[]{:S(2)}, u32[]{:S(2)}) %collective-permute-start.18) | collective-permute-done | bytes 81952 | tf_op jit(solution)/shard_map/ppermute | solution.py:458
  83.6 0.5 collective-permute-start.28
  84.1 1.3 %total.1 = (f32[128,256]{1,0:T(8,128)S(1)}, f32[1,5,2,4,128]{4,3,2,1,0:T(4,128)}) custom-call(s32[2]{0:T(128)S(1)} %and_select_fusion.place, f32[1,5,2,4,128]{4,3,2,1,0:T(4,128)S(1)} %copy-done.1, f32[3,1024]{1,0:T(4,128)S(1)} %get-tuple-element.74.drag, bf16[160,256]{1,0:T(8,128)(2,1)S(1)} %get-tuple-element.90.mine, f32[32,256]{1,0:T(8,128)S(1)} %get-tuple-element.91.kept, ...), custom_call_target="tpu_custom_call" | custom-call | tf_op jit(solution)/shard_map/total/pallas_call | solution.py:621
  85.4 0.0 collective-permute-start.19
  85.4 1.3 %collective-permute-done.19.other = f32[128,256]{1,0:T(8,128)S(1)} collective-permute-done((f32[128,256]{1,0:T(8,128)S(1)}, f32[128,256]{1,0:T(8,128)S(1)}, u32[]{:S(2)}, u32[]{:S(2)}) %collective-permute-start.19) | collective-permute-done | bytes 131104 | tf_op jit(solution)/shard_map/ppermute | solution.py:458
  86.8 10.8 %finish.1 = (f32[27,256,256]{2,1,0:T(8,128)}, f32[9,27,256]{2,1,0:T(8,128)}, f32[5,256]{1,0:T(8,128)}) custom-call(s32[16]{0:T(128)S(1)} %fusion.1.place, s32[1]{0:T(128)} %bitcast.14.core, f32[128,256]{1,0:T(8,128)S(1)} %get-tuple-element.96.own, f32[128,256]{1,0:T(8,128)S(1)} %collective-permute-done.19.other, bf16[1,448,256]{2,1,0:T(8,128)(2,1)S(1)} %bitcast.34, ...), custom_call_target="tpu_custom_call" | custom-call | tf_op jit(solution)/shard_map/finish/pallas_call | solution.py:660
  (35 shorter events, 0.2 us)
Async XLA Ops:
  0.6 0.7 copy-start.3
  1.3 0.7 copy-start.4
  2.0 0.7 copy-start.5
  2.7 0.7 copy-start.6
  3.4 0.7 copy-start.7
  5.5 7.4 %collective-permute-start = (f32[4,1024]{1,0:T(4,128)S(1)}, f32[4,1024]{1,0:T(4,128)S(1)}, u32[]{:S(2)}, u32[]{:S(2)}) collective-permute-start(f32[4,1024]{1,0:T(4,128)S(1)} %get-tuple-element.59), channel_id=1, source_target_pairs={{0,4},{4,8},{8,12},{12,0},{1,5},{5,9},{9,13},{13,1},{2,6},{6,10},{... | collective-permute-start | bytes 49160 | tf_op jit(solution)/shard_map/ppermute | solution.py:469
  6.0 6.9 %collective-permute-start.1 = (f32[4,1024]{1,0:T(4,128)S(1)}, f32[4,1024]{1,0:T(4,128)S(1)}, u32[]{:S(2)}, u32[]{:S(2)}) collective-permute-start(f32[4,1024]{1,0:T(4,128)S(1)} %get-tuple-element.60), channel_id=1, source_target_pairs={{4,0},{8,4},{12,8},{0,12},{5,1},{9,5},{13,9},{1,13},{6,2},{10,6},{... | collective-permute-start | bytes 49160 | tf_op jit(solution)/shard_map/ppermute | solution.py:470
  8.1 2.0 %copy-start.8 = (bf16[27,256,256]{2,1,0:T(8,128)(2,1)S(1)}, bf16[27,256,256]{2,1,0:T(8,128)(2,1)}, u32[]{:S(2)}) copy-start(bf16[27,256,256]{2,1,0:T(8,128)(2,1)} %w_mid.1) | copy-start | bytes 10616836
  10.1 0.9 copy-start.9
  11.0 0.7 copy-start.10
  12.9 0.7 copy-start
  13.6 0.7 copy-start.2
  14.4 5.6 %collective-permute-start.2 = (bf16[16,1024]{1,0:T(8,128)(2,1)S(1)}, bf16[16,1024]{1,0:T(8,128)(2,1)S(1)}, u32[]{:S(2)}, u32[]{:S(2)}) collective-permute-start(bf16[16,1024]{1,0:T(8,128)(2,1)S(1)} %get-tuple-element.61), channel_id=1, source_target_pairs={{0,1},{1,0},{2,3},{3,2},{4,5},{5,4},{6,7},{7,6},{8,9},{9,8},{10,11... | collective-permute-start | bytes 98312 | tf_op jit(solution)/shard_map/ppermute | solution.py:458
  16.7 5.4 %collective-permute-start.3 = (bf16[16,1024]{1,0:T(8,128)(2,1)S(1)}, bf16[16,1024]{1,0:T(8,128)(2,1)S(1)}, u32[]{:S(2)}, u32[]{:S(2)}) collective-permute-start(bf16[16,1024]{1,0:T(8,128)(2,1)S(1)} %get-tuple-element.61), channel_id=1, source_target_pairs={{0,2},{1,3},{2,0},{3,1},{4,6},{5,7},{6,4},{7,5},{8,10},{9,11},{10,... | collective-permute-start | bytes 98312 | tf_op jit(solution)/shard_map/ppermute | solution.py:458
  19.3 5.7 %collective-permute-start.4 = (bf16[16,1024]{1,0:T(8,128)(2,1)S(1)}, bf16[16,1024]{1,0:T(8,128)(2,1)S(1)}, u32[]{:S(2)}, u32[]{:S(2)}) collective-permute-start(bf16[16,1024]{1,0:T(8,128)(2,1)S(1)} %get-tuple-element.61), channel_id=1, source_target_pairs={{0,3},{1,2},{2,1},{3,0},{4,7},{5,6},{6,5},{7,4},{8,11},{9,10},{10,... | collective-permute-start | bytes 98312 | tf_op jit(solution)/shard_map/ppermute | solution.py:458
  25.1 5.0 %collective-permute-start.5 = (bf16[4,16,1024]{2,1,0:T(8,128)(2,1)S(1)}, bf16[4,16,1024]{2,1,0:T(8,128)(2,1)S(1)}, u32[]{:S(2)}, u32[]{:S(2)}) collective-permute-start(bf16[4,16,1024]{2,1,0:T(8,128)(2,1)S(1)} %pad_maximum_fusion.refs_0_), channel_id=1, source_target_pairs={{0,8},{1,9},{2,10},{3,11},{4,12},{5,13},{6,14},{7,15},{8,0},{9,1},... | collective-permute-start | bytes 393224 | tf_op jit(solution)/shard_map/ppermute | solution.py:458
  26.7 3.4 %collective-permute-start.6 = (bf16[4,16,1024]{2,1,0:T(8,128)(2,1)S(1)}, bf16[4,16,1024]{2,1,0:T(8,128)(2,1)S(1)}, u32[]{:S(2)}, u32[]{:S(2)}) collective-permute-start(bf16[4,16,1024]{2,1,0:T(8,128)(2,1)S(1)} %pad_maximum_fusion.refs_0_), channel_id=1, source_target_pairs={{0,4},{1,5},{2,6},{3,7},{4,0},{5,1},{6,2},{7,3},{8,12},{9,13},{10,... | collective-permute-start | bytes 393224 | tf_op jit(solution)/shard_map/ppermute | solution.py:458
  30.1 1.3 %collective-permute-start.7 = (bf16[4,16,1024]{2,1,0:T(8,128)(2,1)S(1)}, bf16[4,16,1024]{2,1,0:T(8,128)(2,1)S(1)}, u32[]{:S(2)}, u32[]{:S(2)}) collective-permute-start(bf16[4,16,1024]{2,1,0:T(8,128)(2,1)S(1)} %collective-permute-done.5.refs_1_), channel_id=1, source_target_pairs={{0,4},{1,5},{2,6},{3,7},{4,0},{5,1},{6,2},{7,3},{8,12},{9,13},{10,... | collective-permute-start | bytes 393224 | tf_op jit(solution)/shard_map/ppermute | solution.py:458
  45.7 8.1 %collective-permute-start.8 = (bf16[448,256]{1,0:T(8,128)(2,1)S(1)}, bf16[448,256]{1,0:T(8,128)(2,1)S(1)}, u32[]{:S(2)}, u32[]{:S(2)}) collective-permute-start(bf16[448,256]{1,0:T(8,128)(2,1)S(1)} %get-tuple-element.69), channel_id=1, source_target_pairs={{0,1},{4,5},{1,2},{5,6},{2,3},{6,7},{3,11},{7,15},{11,10},{15,14},... | collective-permute-start | bytes 688136 | tf_op jit(solution)/shard_map/ppermute | solution.py:574
  45.7 8.1 %collective-permute-start.9 = (bf16[448,256]{1,0:T(8,128)(2,1)S(1)}, bf16[448,256]{1,0:T(8,128)(2,1)S(1)}, u32[]{:S(2)}, u32[]{:S(2)}) collective-permute-start(bf16[448,256]{1,0:T(8,128)(2,1)S(1)} %get-tuple-element.69), channel_id=1, source_target_pairs={{0,8},{4,12},{1,0},{5,4},{2,1},{6,5},{3,2},{7,6},{11,3},{15,7},{10... | collective-permute-start | bytes 688136 | tf_op jit(solution)/shard_map/ppermute | solution.py:574
  53.8 30.4 %copy-start.1 = (f32[1,5,2,4,128]{4,3,2,1,0:T(4,128)S(1)}, f32[1,5,2,4,128]{4,3,2,1,0:T(4,128)}, u32[]{:S(2)}) copy-start(f32[1,5,2,4,128]{4,3,2,1,0:T(4,128)} %fields.3) | copy-start | bytes 61444
  53.8 8.1 %collective-permute-start.10 = (bf16[448,256]{1,0:T(8,128)(2,1)S(1)}, bf16[448,256]{1,0:T(8,128)(2,1)S(1)}, u32[]{:S(2)}, u32[]{:S(2)}) collective-permute-start(bf16[448,256]{1,0:T(8,128)(2,1)S(1)} %collective-permute-done.8), channel_id=1, source_target_pairs={{0,1},{4,5},{1,2},{5,6},{2,3},{6,7},{3,11},{7,15},{11,10},{15,14},... | collective-permute-start | bytes 688136 | tf_op jit(solution)/shard_map/ppermute | solution.py:574
  53.9 8.0 %collective-permute-start.11 = (bf16[448,256]{1,0:T(8,128)(2,1)S(1)}, bf16[448,256]{1,0:T(8,128)(2,1)S(1)}, u32[]{:S(2)}, u32[]{:S(2)}) collective-permute-start(bf16[448,256]{1,0:T(8,128)(2,1)S(1)} %collective-permute-done.9), channel_id=1, source_target_pairs={{0,8},{4,12},{1,0},{5,4},{2,1},{6,5},{3,2},{7,6},{11,3},{15,7},{10... | collective-permute-start | bytes 688136 | tf_op jit(solution)/shard_map/ppermute | solution.py:574
  62.0 2.2 %collective-permute-start.12 = (f32[384,256]{1,0:T(8,128)S(1)}, f32[384,256]{1,0:T(8,128)S(1)}, u32[]{:S(2)}, u32[]{:S(2)}) collective-permute-start(f32[384,256]{1,0:T(8,128)S(1)} %get-tuple-element.82), channel_id=1, source_target_pairs={{0,4},{1,5},{2,6},{3,7},{4,0},{5,1},{6,2},{7,3},{8,12},{9,13},{10,... | collective-permute-start | bytes 1179656 | tf_op jit(solution)/shard_map/ppermute | solution.py:458
  62.1 8.5 %collective-permute-start.14 = (bf16[448,256]{1,0:T(8,128)(2,1)S(1)}, bf16[448,256]{1,0:T(8,128)(2,1)S(1)}, u32[]{:S(2)}, u32[]{:S(2)}) collective-permute-start(bf16[448,256]{1,0:T(8,128)(2,1)S(1)} %collective-permute-done.10), channel_id=1, source_target_pairs={{0,1},{4,5},{1,2},{5,6},{2,3},{6,7},{3,11},{7,15},{11,10},{15,14},... | collective-permute-start | bytes 688136 | tf_op jit(solution)/shard_map/ppermute | solution.py:574
  62.2 8.3 %collective-permute-start.15 = (bf16[448,256]{1,0:T(8,128)(2,1)S(1)}, bf16[448,256]{1,0:T(8,128)(2,1)S(1)}, u32[]{:S(2)}, u32[]{:S(2)}) collective-permute-start(bf16[448,256]{1,0:T(8,128)(2,1)S(1)} %collective-permute-done.11), channel_id=1, source_target_pairs={{0,8},{4,12},{1,0},{5,4},{2,1},{6,5},{3,2},{7,6},{11,3},{15,7},{10... | collective-permute-start | bytes 688136 | tf_op jit(solution)/shard_map/ppermute | solution.py:574
  64.3 8.7 %collective-permute-start.13 = (bf16[256,256]{1,0:T(8,128)(2,1)S(1)}, bf16[256,256]{1,0:T(8,128)(2,1)S(1)}, u32[]{:S(2)}, u32[]{:S(2)}) collective-permute-start(bf16[256,256]{1,0:T(8,128)(2,1)S(1)} %get-tuple-element.85.mine), channel_id=1, source_target_pairs={{0,8},{1,9},{2,10},{3,11},{4,12},{5,13},{6,14},{7,15},{8,0},{9,1},... | collective-permute-start | bytes 393224 | tf_op jit(solution)/shard_map/ppermute | solution.py:458
  65.8 7.1 %collective-permute-start.21 = (bf16[448,256]{1,0:T(8,128)(2,1)S(1)}, bf16[448,256]{1,0:T(8,128)(2,1)S(1)}, u32[]{:S(2)}, u32[]{:S(2)}) collective-permute-start(bf16[448,256]{1,0:T(8,128)(2,1)S(1)} %get-tuple-element.69), channel_id=1, source_target_pairs={{0,4},{1,5},{2,6},{3,7},{4,0},{5,1},{6,2},{7,3},{8,12},{9,13},{10,... | collective-permute-start | bytes 688136 | tf_op jit(solution)/shard_map/ppermute | solution.py:458
  65.8 7.2 %collective-permute-start.22 = (bf16[448,256]{1,0:T(8,128)(2,1)S(1)}, bf16[448,256]{1,0:T(8,128)(2,1)S(1)}, u32[]{:S(2)}, u32[]{:S(2)}) collective-permute-start(bf16[448,256]{1,0:T(8,128)(2,1)S(1)} %collective-permute-done.8), channel_id=1, source_target_pairs={{0,4},{1,5},{2,6},{3,7},{4,0},{5,1},{6,2},{7,3},{8,12},{9,13},{10,... | collective-permute-start | bytes 688136 | tf_op jit(solution)/shard_map/ppermute | solution.py:458
  70.6 5.4 %collective-permute-start.23 = (bf16[448,256]{1,0:T(8,128)(2,1)S(1)}, bf16[448,256]{1,0:T(8,128)(2,1)S(1)}, u32[]{:S(2)}, u32[]{:S(2)}) collective-permute-start(bf16[448,256]{1,0:T(8,128)(2,1)S(1)} %collective-permute-done.9), channel_id=1, source_target_pairs={{0,4},{1,5},{2,6},{3,7},{4,0},{5,1},{6,2},{7,3},{8,12},{9,13},{10,... | collective-permute-start | bytes 688136 | tf_op jit(solution)/shard_map/ppermute | solution.py:458
  72.9 10.7 %collective-permute-start.20 = (bf16[448,256]{1,0:T(8,128)(2,1)S(1)}, bf16[448,256]{1,0:T(8,128)(2,1)S(1)}, u32[]{:S(2)}, u32[]{:S(2)}) collective-permute-start(bf16[448,256]{1,0:T(8,128)(2,1)S(1)} %collective-permute-done.14), channel_id=1, source_target_pairs={{0,1},{4,5},{1,2},{5,6},{2,3},{6,7},{3,11},{7,15},{11,10},{15,14},... | collective-permute-start | bytes 688136 | tf_op jit(solution)/shard_map/ppermute | solution.py:574
  72.9 12.5 %collective-permute-start.24 = (bf16[448,256]{1,0:T(8,128)(2,1)S(1)}, bf16[448,256]{1,0:T(8,128)(2,1)S(1)}, u32[]{:S(2)}, u32[]{:S(2)}) collective-permute-start(bf16[448,256]{1,0:T(8,128)(2,1)S(1)} %collective-permute-done.10), channel_id=1, source_target_pairs={{0,4},{1,5},{2,6},{3,7},{4,0},{5,1},{6,2},{7,3},{8,12},{9,13},{10,... | collective-permute-start | bytes 688136 | tf_op jit(solution)/shard_map/ppermute | solution.py:458
  73.0 7.7 %collective-permute-start.16 = (bf16[160,256]{1,0:T(8,128)(2,1)S(1)}, bf16[160,256]{1,0:T(8,128)(2,1)S(1)}, u32[]{:S(2)}, u32[]{:S(2)}) collective-permute-start(bf16[160,256]{1,0:T(8,128)(2,1)S(1)} %get-tuple-element.90.mine), channel_id=1, source_target_pairs={{0,1},{1,0},{2,3},{3,2},{4,5},{5,4},{6,7},{7,6},{8,9},{9,8},{10,11... | collective-permute-start | bytes 245768 | tf_op jit(solution)/shard_map/ppermute | solution.py:458
  73.1 9.3 %collective-permute-start.17 = (bf16[160,256]{1,0:T(8,128)(2,1)S(1)}, bf16[160,256]{1,0:T(8,128)(2,1)S(1)}, u32[]{:S(2)}, u32[]{:S(2)}) collective-permute-start(bf16[160,256]{1,0:T(8,128)(2,1)S(1)} %get-tuple-element.92), channel_id=1, source_target_pairs={{0,2},{1,3},{2,0},{3,1},{4,6},{5,7},{6,4},{7,5},{8,10},{9,11},{10,... | collective-permute-start | bytes 245768 | tf_op jit(solution)/shard_map/ppermute | solution.py:458
  76.0 7.6 %collective-permute-start.18 = (bf16[160,256]{1,0:T(8,128)(2,1)S(1)}, bf16[160,256]{1,0:T(8,128)(2,1)S(1)}, u32[]{:S(2)}, u32[]{:S(2)}) collective-permute-start(bf16[160,256]{1,0:T(8,128)(2,1)S(1)} %get-tuple-element.93), channel_id=1, source_target_pairs={{0,3},{1,2},{2,1},{3,0},{4,7},{5,6},{6,5},{7,4},{8,11},{9,10},{10,... | collective-permute-start | bytes 245768 | tf_op jit(solution)/shard_map/ppermute | solution.py:458
  80.7 4.7 %collective-permute-start.25 = (bf16[448,256]{1,0:T(8,128)(2,1)S(1)}, bf16[448,256]{1,0:T(8,128)(2,1)S(1)}, u32[]{:S(2)}, u32[]{:S(2)}) collective-permute-start(bf16[448,256]{1,0:T(8,128)(2,1)S(1)} %collective-permute-done.11), channel_id=1, source_target_pairs={{0,4},{1,5},{2,6},{3,7},{4,0},{5,1},{6,2},{7,3},{8,12},{9,13},{10,... | collective-permute-start | bytes 688136 | tf_op jit(solution)/shard_map/ppermute | solution.py:458
  82.3 4.4 %collective-permute-start.26 = (bf16[448,256]{1,0:T(8,128)(2,1)S(1)}, bf16[448,256]{1,0:T(8,128)(2,1)S(1)}, u32[]{:S(2)}, u32[]{:S(2)}) collective-permute-start(bf16[448,256]{1,0:T(8,128)(2,1)S(1)} %collective-permute-done.14), channel_id=1, source_target_pairs={{0,4},{1,5},{2,6},{3,7},{4,0},{5,1},{6,2},{7,3},{8,12},{9,13},{10,... | collective-permute-start | bytes 688136 | tf_op jit(solution)/shard_map/ppermute | solution.py:458
  83.6 3.1 %collective-permute-start.27 = (bf16[448,256]{1,0:T(8,128)(2,1)S(1)}, bf16[448,256]{1,0:T(8,128)(2,1)S(1)}, u32[]{:S(2)}, u32[]{:S(2)}) collective-permute-start(bf16[448,256]{1,0:T(8,128)(2,1)S(1)} %collective-permute-done.15), channel_id=1, source_target_pairs={{0,4},{1,5},{2,6},{3,7},{4,0},{5,1},{6,2},{7,3},{8,12},{9,13},{10,... | collective-permute-start | bytes 688136 | tf_op jit(solution)/shard_map/ppermute | solution.py:458
  83.6 3.1 %collective-permute-start.28 = (bf16[448,256]{1,0:T(8,128)(2,1)S(1)}, bf16[448,256]{1,0:T(8,128)(2,1)S(1)}, u32[]{:S(2)}, u32[]{:S(2)}) collective-permute-start(bf16[448,256]{1,0:T(8,128)(2,1)S(1)} %collective-permute-done.20), channel_id=1, source_target_pairs={{0,4},{1,5},{2,6},{3,7},{4,0},{5,1},{6,2},{7,3},{8,12},{9,13},{10,... | collective-permute-start | bytes 688136 | tf_op jit(solution)/shard_map/ppermute | solution.py:458
  85.4 1.3 %collective-permute-start.19 = (f32[128,256]{1,0:T(8,128)S(1)}, f32[128,256]{1,0:T(8,128)S(1)}, u32[]{:S(2)}, u32[]{:S(2)}) collective-permute-start(f32[128,256]{1,0:T(8,128)S(1)} %get-tuple-element.96.own), channel_id=1, source_target_pairs={{0,4},{1,5},{2,6},{3,7},{4,0},{5,1},{6,2},{7,3},{8,12},{9,13},{10,... | collective-permute-start | bytes 393224 | tf_op jit(solution)/shard_map/ppermute | solution.py:458

commit v4 on v3

--- a/solution.py
+++ b/solution.py
@@ -48,7 +48,20 @@
     return jnp.concatenate([ref[0, :, x, y, :] for x in range(planes) for y in range(rows)], 1)
 
 
-def deposit_kernel(mass, vel, cell, listed, counts, stay, up, down):
+def fetch(pairs, sems):
+    copies = [pltpu.make_async_copy(src, dst, sems.at[i]) for i, (src, dst) in enumerate(pairs)]
+    for copy in copies:
+        copy.start()
+    for copy in copies:
+        copy.wait()
+
+
+def deposit_kernel(mass_in, vel_in, cell_in, listed_in, fields_in, cotangent_in, counts, stay, up, down, state, last_grad, *held):
+    *held, sems = held
+    fetch(list(zip((mass_in, vel_in, cell_in, listed_in, fields_in, cotangent_in), held)), sems)
+    mass, vel, cell, listed, fields, cotangent = held
+    state[...] = flat_cells(fields)
+    last_grad[...] = dt_step * flat_cells(cotangent)
     drops = mass.shape[1]
     slots = listed.shape[1]
     half = slots // 2
@@ -77,15 +90,15 @@
             out[:, start : start + chunk] = got[8 * i : 8 * i + 4] + got[8 * i + 4 : 8 * i + 8]
 
 
-def feature_kernel(stay, below, above, fields, cotangent, feats, drag):
+def feature_kernel(stay, below, above, fields, last_grad, feats, drag):
     deposit = stay[...] + below[...] + above[...]
-    state = flat_cells(fields)
+    state = fields[...]
     force = drag_rate * (deposit[1:4] - deposit[0:1] * state[0:3])
     drag[...] = force
     cells = state.shape[1]
     feats[...] = jnp.concatenate(
         [
-            dt_step * flat_cells(cotangent),
+            last_grad[...],
             force[2:3],
             jnp.zeros((2, cells), F32),
             state,
@@ -107,14 +120,22 @@
     return ((at == k) & (t < 27)).astype(F32).astype(BF16)
 
 
-def weight_kernel(me, w_in, w_mid, w_out, wt, w_back, w_first, wo, wc):
+def weight_kernel(me, in_hbm, mid_hbm, out_hbm, wt, w_back, w_first, wo, wc, w_in, w_mid, w_out, sems):
+    parts = 9
+    share = w_mid.shape[0] // parts
+    copies = []
+    for i in range(parts):
+        at = slice(i * share, (i + 1) * share)
+        copies.append(pltpu.make_async_copy(mid_hbm.at[at], w_mid.at[at], sems.at[i]))
+    small = [pltpu.make_async_copy(in_hbm, w_in, sems.at[parts]), pltpu.make_async_copy(out_hbm, w_out, sems.at[parts + 1])]
+    for copy in small + copies:
+        copy.start()
+    for copy in small:
+        copy.wait()
     block, hid = wo.shape[0], wt.shape[1]
     row = lax.broadcasted_iota(jnp.int32, (block, hid), 0)
     column = lax.broadcasted_iota(jnp.int32, (block, hid), 1)
     chosen = (column == row + me[0] * block).astype(F32).astype(BF16)
-    for t in range(27):
-        wt[t * block : (t + 1) * block] = dot_nt(chosen, w_mid[t]).astype(BF16)
-    w_back[...] = wt[...].astype(F32).T.astype(BF16)
     pad = jnp.zeros((5, hid), F32)
     tall = jnp.concatenate([v for c in range(9) for v in (w_in[c].astype(F32), pad)], 0)
     w_first[...] = (0.5 * dot(tall.T.astype(BF16), tap_rows())).astype(BF16)
@@ -122,6 +143,11 @@
     wide = jnp.concatenate([wide, jnp.zeros((16 - wide.shape[0], hid), F32)], 0).astype(BF16)
     wo[...] = dot_nt(chosen, wide).astype(BF16)
     wc[...] = dot_nt(wide, chosen).astype(BF16)
+    for i, copy in enumerate(copies):
+        copy.wait()
+        for t in range(i * share, (i + 1) * share):
+            wt[t * block : (t + 1) * block] = dot_nt(chosen, w_mid[t]).astype(BF16)
+    w_back[...] = wt[...].astype(F32).T.astype(BF16)
 
 
 def span(x, lanes, count=1):
@@ -333,9 +359,9 @@
 
 
 def step_fields(nz, place, fields, drag, closure, sources, out):
-    state = flat_cells(fields)
+    state = fields[...]
     cells = state.shape[1]
-    planes, rows = fields.shape[2], fields.shape[3]
+    planes, rows = out.shape[2], out.shape[3]
     lanes = cells // planes
     lower, upper = (sources[0][place[i] if len(sources) == 1 else 0].astype(F32) for i in range(2))
     for g in range(1, len(sources)):
@@ -362,26 +388,22 @@
 
 
 def finish_kernel(count, weight_count, place, core, own, other, *refs):
-    pieces, (mid_out, first_out, last_out, held, done, arrive, leave) = refs[:count], refs[count:]
+    pieces, (mid_out, first_out, last_out, held, done, leave) = refs[:count], refs[count:]
     slots = held.shape[0]
     block = done.shape[1] // slots
     rows = held.shape[1] - 16
     width = done.shape[1]
 
-    copies, at = [], 0
-    for i, ref in enumerate(pieces):
-        copies.append(pltpu.make_async_copy(ref, held.at[at : at + ref.shape[0]], arrive.at[i]))
+    at = 0
+    for ref in pieces:
+        held[at : at + ref.shape[0]] = ref[...]
         at += ref.shape[0]
-    for copy in copies:
-        copy.start()
     a, b = own[...], other[...]
     swapped = core[0] == 1
     raw = jnp.concatenate([jnp.where(swapped, b, a), jnp.where(swapped, a, b)], 0)
     squares = jnp.sum(raw * raw, keepdims=True)
     high = raw.astype(BF16)
     ordered = dot(tap_rows(), high) + dot(tap_rows(), (raw - high.astype(F32)).astype(BF16))
-    for copy in copies:
-        copy.wait()
     last = []
     for d in range(slots):
         extra = held[place[d], rows:].astype(F32)
@@ -411,7 +433,7 @@
             leaving(t).start()
         return carry
 
-    lax.fori_loop(0, 9, flip, 0)
+    lax.fori_loop(0, 9, flip, 0, unroll=3)
     for t in range(27):
         leaving(t).wait()
 
@@ -423,6 +445,7 @@
 SMEM = pl.BlockSpec(memory_space=pltpu.SMEM)
 VMEM = pl.BlockSpec(memory_space=pltpu.VMEM)
 ANY = pl.BlockSpec(memory_space=pl.ANY)
+HBM = pl.BlockSpec(memory_space=pltpu.HBM)
 
 
 def cost(flops):
@@ -458,14 +481,16 @@
         return lax.ppermute(v, team, [(d, d ^ mask) for d in range(size)])
 
     dense = shape((4, cells), F32)
-    stay, up, down = pl.pallas_call(
+    flows = (drop_mass, jnp.transpose(drop_vel, (1, 0, 2)), drop_cell, cross_list, fields, cotangent)
+    stay, up, down, state, last_grad = pl.pallas_call(
         deposit_kernel,
-        out_shape=(dense, dense, dense),
-        in_specs=[VMEM] * 4 + [SMEM],
-        out_specs=(VMEM,) * 3,
+        out_shape=(dense, dense, dense, shape((5, cells), F32), shape((5, cells), F32)),
+        in_specs=[HBM] * 6 + [SMEM],
+        out_specs=(VMEM,) * 5,
+        scratch_shapes=[pltpu.VMEM(v.shape, v.dtype) for v in flows] + [pltpu.SemaphoreType.DMA((6,))],
         compiler_params=params(8),
         name="deposit",
-    )(drop_mass, jnp.transpose(drop_vel, (1, 0, 2)), drop_cell, cross_list, cross_count)
+    )(*flows, cross_count)
     from_below = lax.ppermute(up, "slab", [(i, (i + 1) % n_slab) for i in range(n_slab)])
     from_above = lax.ppermute(down, "slab", [((i + 1) % n_slab, i) for i in range(n_slab)])
     own_feats, drag = pl.pallas_call(
@@ -475,7 +500,7 @@
         out_specs=(VMEM,) * 2,
         compiler_params=params(4),
         name="features",
-    )(stay, from_below, from_above, fields, cotangent)
+    )(stay, from_below, from_above, state, last_grad)
 
     rows = 27 * block
     wt, w_back, w_first, wo, wc = pl.pallas_call(
@@ -487,15 +512,22 @@
             shape((block, 16), BF16),
             shape((16, block), BF16),
         ),
-        in_specs=[SMEM] + [VMEM] * 3,
+        in_specs=[SMEM] + [HBM] * 3,
         out_specs=(VMEM,) * 5,
+        scratch_shapes=[
+            pltpu.VMEM((9, 27, hid), BF16),
+            pltpu.VMEM(w_mid.shape, BF16),
+            pltpu.VMEM((cout, hid), BF16),
+            pltpu.SemaphoreType.DMA((11,)),
+        ],
         compiler_params=params(16),
         cost_estimate=cost(1.5e9),
         name="weights",
     )(me[None], jnp.transpose(w_in, (1, 0, 2)), w_mid, w_out.T)
 
     if fast:
-        near_z = [trade(own_feats, mask) for mask in (1, 2, 3)]
+        far, middle, close = (trade(own_feats, mask) for mask in (3, 2, 1))
+        near_z = [close, middle, far]
         wt, w_back, w_first, wo, wc, *near_z = lax.optimization_barrier((wt, w_back, w_first, wo, wc, *near_z))
         mine = jnp.stack([own_feats] + near_z)
         across = trade(mine, 8)
@@ -625,7 +657,7 @@
             out_specs=(VMEM,) * 2,
             compiler_params=params(6),
             name="total",
-        )(near, fields, drag, messages[0], kept, *got, *sources)
+        )(near, state, drag, messages[0], kept, *got, *sources)
         other = trade(own, 4)
         pieces = [piece, f1, b1, f2, b2, f3, b3, f4]
         pieces = [v[None] for v in pieces + [trade(v, 4) for v in pieces]]
@@ -654,21 +686,20 @@
             out_specs=VMEM,
             compiler_params=params(6),
             name="step",
-        )(near, fields, drag, own_closure, sources[0].reshape(n_slab, samples, 16, cells)[:, sample])
+        )(near, state, drag, own_closure, sources[0].reshape(n_slab, samples, 16, cells)[:, sample])
 
     weight_count = w_in.size + w_mid.size + w_out.size
     grad_middle, grad_first, grad_last = pl.pallas_call(
         functools.partial(finish_kernel, len(pieces), weight_count),
         out_shape=(shape((27, hid, hid), F32), shape((9, 27, hid), F32), shape((cout, hid), F32)),
-        in_specs=[SMEM] * 2 + [VMEM] * 2 + [ANY] * len(pieces),
+        in_specs=[SMEM] * 2 + [VMEM] * (2 + len(pieces)),
         out_specs=(ANY, VMEM, VMEM),
         scratch_shapes=[
             pltpu.VMEM((size, rows + 16, hid), BF16),
             pltpu.VMEM((27, hid, hid), F32),
-            pltpu.SemaphoreType.DMA((len(pieces),)),
             pltpu.SemaphoreType.DMA((27,)),
         ],
-        compiler_params=params(20),
+        compiler_params=params(24),
         name="finish",
     )(piece_place, core[None], own, other, *pieces)
     return (new_fields, jnp.transpose(grad_first, (1, 0, 2)), grad_middle, grad_last.T)

time: 99 us -> 97.2 us (0.982)
  Pallas kernels: 41.1 us -> 39.1 us
    pallas_call x1, Pallas kernels: 10.8 us -> 5.21 us  [shards(): pl.pallas_call(functools.partial(finish_kernel, len(pieces), weight_count...]
    pallas_call x1, Pallas kernels: 1.17 us -> 4.64 us  [shards(): pl.pallas_call(weight_kernel, out_shape=(shape((rows, hid), BF16), shape(...]
    unnamed x22 -> x20, local copies, waits for them, and re-layouts: 8.46 us -> 8.46 us
  transfers between devices with their start and end apart: 29 -> 29, of which waited for: 10 -> 10; matrix products, arithmetic and copies ran while one was open for 1% -> 1% of each run, Pallas kernels for 15% -> 19%
where the time goes in v4:
time: 97.2 us; the launch traced here: 95.8 us
  Pallas kernels  39.1 us (40%)
  waiting for transfers between devices  23.9 us (25%)
  starting transfers between devices  22.4 us (23%)
  local copies, waits for them, and re-layouts  9.09 us (9%)
  between operations  1.03 us (1%)
    ppermute x20, waiting for transfers between devices, trade(): return lax.ppermute(v, team, [(d, d ^ mask) for d in range(size)])  19.6 us
    pallas_call x1, Pallas kernels, shards(): pl.pallas_call(functools.partial(closure_kernel, nz, lanes, len(sources))...  14.2 us
    ppermute x20, starting transfers between devices, trade(): return lax.ppermute(v, team, [(d, d ^ mask) for d in range(size)])  13.7 us
    pallas_call x2, Pallas kernels, first_part(): pl.pallas_call(functools.partial(first_kernel, nz, lanes), grid=(count,),...  12.1 us
    unnamed x20, local copies, waits for them, and re-layouts  8.46 us
    ppermute x7, starting transfers between devices, around(): lax.ppermute(v, team, [(device(at, c), device(at + by, c)) for at in rang...  6.23 us
    pallas_call x1, Pallas kernels, shards(): pl.pallas_call(functools.partial(finish_kernel, len(pieces), weight_count...  5.21 us
    pallas_call x1, Pallas kernels, shards(): pl.pallas_call(weight_kernel, out_shape=(shape((rows, hid), BF16), shape(...  4.64 us
  transfers between devices with their start and end apart: 29, of which 10 were waited for; matrix products, arithmetic and copies ran while one was open for 1% of the time, Pallas kernels for 19%

profile of v4, /device:TPU:0, one launch (start us, length us, event | category | flops | bytes accessed | tf_op | source)
XLA Modules:
  0.0 95.8 jit_solution(4858622378349880412)
XLA Ops:
  0.6 0.7 copy-done
  1.4 0.7 copy-done.1
  2.1 0.7 copy-done.2
  2.8 0.7 copy-done.3
  3.5 0.7 copy-done.4
  4.2 0.7 copy-done.5
  4.9 0.7 copy-done.6
  5.5 1.6 %deposit.1 = (f32[4,1024]{1,0:T(4,128)S(1)}, f32[4,1024]{1,0:T(4,128)S(1)}, f32[4,1024]{1,0:T(4,128)S(1)}, f32[5,1024]{1,0:T(8,128)S(1)}, f32[5,1024]{1,0:T(8,128)S(1)}) custom-call(f32[1,1024]{1,0:T(1,128)S(1)} %copy-done.3, f32[3,1,1024]{2,1,0:T(1,128)S(1)} %bitcast.51, s32[1,1024]{1,0:T(1,128)S(1)} %copy-done.4, s32[1,256]{1,0:T(1,128)S(1)} %copy-done.5, ...), custom_call_target="tpu_custom_call" | custom-call | tf_op jit(solution)/shard_map/deposit/pallas_call | solution.py:485
  7.1 0.5 collective-permute-start
  7.6 2.0 %collective-permute-start.1 = (f32[4,1024]{1,0:T(4,128)S(1)}, f32[4,1024]{1,0:T(4,128)S(1)}, u32[]{:S(2)}, u32[]{:S(2)}) collective-permute-start(f32[4,1024]{1,0:T(4,128)S(1)} %get-tuple-element.62), channel_id=1, source_target_pairs={{4,0},{8,4},{12,8},{0,12},{5,1},{9,5},{13,9},{1,13},{6,2},{10,6},{... | collective-permute-start | bytes 49160 | tf_op jit(solution)/shard_map/ppermute | solution.py:495
  9.6 0.1 fusion.3
  9.7 2.0 %copy-done.7 = bf16[27,256,256]{2,1,0:T(8,128)(2,1)S(1)} copy-done((bf16[27,256,256]{2,1,0:T(8,128)(2,1)S(1)}, bf16[27,256,256]{2,1,0:T(8,128)(2,1)}, u32[]{:S(2)}) %copy-start.7) | copy-done | bytes 3538968
  11.7 0.9 copy-done.8
  12.6 0.7 copy-done.9
  13.3 4.6 %weights.1 = (bf16[432,256]{1,0:T(8,128)(2,1)S(1)}, bf16[256,432]{1,0:T(8,128)(2,1)S(1)}, bf16[256,256]{1,0:T(8,128)(2,1)S(1)}, bf16[16,16]{1,0:T(8,128)(2,1)S(1)}, bf16[16,16]{1,0:T(8,128)(2,1)S(1)}) custom-call(s32[1]{0:T(128)} %bitcast.me, bf16[9,27,256]{2,1,0:T(8,128)(2,1)S(1)} %bitcast.52, bf16[27,256,256]{2,1,0:T(8,128)(2,1)S(1)} %copy-done.7, ...), custom_call_target="tpu_custom_call" | custom-call | flops 1500000000 | bytes 4194304 | tf_op jit(solution)/shard_map/weights/pallas_call | solution.py:506
  18.0 0.0 collective-permute-done.1.above
  18.0 2.4 %collective-permute-start.2 = (bf16[16,1024]{1,0:T(8,128)(2,1)S(1)}, bf16[16,1024]{1,0:T(8,128)(2,1)S(1)}, u32[]{:S(2)}, u32[]{:S(2)}) collective-permute-start(bf16[16,1024]{1,0:T(8,128)(2,1)S(1)} %get-tuple-element.65), channel_id=1, source_target_pairs={{0,1},{1,0},{2,3},{3,2},{4,5},{5,4},{6,7},{7,6},{8,9},{9,8},{10,11... | collective-permute-start | bytes 98312 | tf_op jit(solution)/shard_map/ppermute | solution.py:481
  20.4 2.6 %collective-permute-start.3 = (bf16[16,1024]{1,0:T(8,128)(2,1)S(1)}, bf16[16,1024]{1,0:T(8,128)(2,1)S(1)}, u32[]{:S(2)}, u32[]{:S(2)}) collective-permute-start(bf16[16,1024]{1,0:T(8,128)(2,1)S(1)} %get-tuple-element.65), channel_id=1, source_target_pairs={{0,2},{1,3},{2,0},{3,1},{4,6},{5,7},{6,4},{7,5},{8,10},{9,11},{10,... | collective-permute-start | bytes 98312 | tf_op jit(solution)/shard_map/ppermute | solution.py:481
  23.0 0.6 gather_fusion
  23.6 0.0 collective-permute-done.2
  23.6 2.2 %collective-permute-done.3 = bf16[16,1024]{1,0:T(8,128)(2,1)S(1)} collective-permute-done((bf16[16,1024]{1,0:T(8,128)(2,1)S(1)}, bf16[16,1024]{1,0:T(8,128)(2,1)S(1)}, u32[]{:S(2)}, u32[]{:S(2)}) %collective-permute-start.3) | collective-permute-done | bytes 32800 | tf_op jit(solution)/shard_map/ppermute | solution.py:481
  25.8 2.9 %collective-permute-done.4 = bf16[16,1024]{1,0:T(8,128)(2,1)S(1)} collective-permute-done((bf16[16,1024]{1,0:T(8,128)(2,1)S(1)}, bf16[16,1024]{1,0:T(8,128)(2,1)S(1)}, u32[]{:S(2)}, u32[]{:S(2)}) %collective-permute-start.4) | collective-permute-done | bytes 32800 | tf_op jit(solution)/shard_map/ppermute | solution.py:481
  28.7 1.6 %collective-permute-start.5 = (bf16[4,16,1024]{2,1,0:T(8,128)(2,1)S(1)}, bf16[4,16,1024]{2,1,0:T(8,128)(2,1)S(1)}, u32[]{:S(2)}, u32[]{:S(2)}) collective-permute-start(bf16[4,16,1024]{2,1,0:T(8,128)(2,1)S(1)} %pad_maximum_fusion.refs_0_), channel_id=1, source_target_pairs={{0,8},{1,9},{2,10},{3,11},{4,12},{5,13},{6,14},{7,15},{8,0},{9,1},... | collective-permute-start | bytes 393224 | tf_op jit(solution)/shard_map/ppermute | solution.py:481
  30.3 0.1 and_select_fusion.place
  30.4 0.0 collective-permute-start.6
  30.4 3.4 %collective-permute-done.5.refs_1_ = bf16[4,16,1024]{2,1,0:T(8,128)(2,1)S(1)} collective-permute-done((bf16[4,16,1024]{2,1,0:T(8,128)(2,1)S(1)}, bf16[4,16,1024]{2,1,0:T(8,128)(2,1)S(1)}, u32[]{:S(2)}, u32[]{:S(2)}) %collective-permute-start.5) | collective-permute-done | bytes 131104 | tf_op jit(solution)/shard_map/ppermute | solution.py:481
  33.8 0.0 collective-permute-done.6.refs_2_
  33.8 1.3 %collective-permute-done.7.refs_3_ = bf16[4,16,1024]{2,1,0:T(8,128)(2,1)S(1)} collective-permute-done((bf16[4,16,1024]{2,1,0:T(8,128)(2,1)S(1)}, bf16[4,16,1024]{2,1,0:T(8,128)(2,1)S(1)}, u32[]{:S(2)}, u32[]{:S(2)}) %collective-permute-start.7) | collective-permute-done | bytes 131104 | tf_op jit(solution)/shard_map/ppermute | solution.py:481
  35.1 14.2 %closure.1 = (bf16[448,256]{1,0:T(8,128)(2,1)S(1)}, bf16[4,8,16,256]{3,2,1,0:T(8,128)(2,1)S(1)}, bf16[4,3,16,4096]{3,2,1,0:T(8,128)(2,1)S(1)}, bf16[4,256,4096]{2,1,0:T(8,128)(2,1)S(1)}) custom-call(s32[4]{0:T(128)S(1)} %broadcast_multiply_fusion.place, bf16[256,256]{1,0:T(8,128)(2,1)S(1)} %get-tuple-element.66.w_first, ...), custom_call_target="tpu_custom_call" | custom-call | flops 8999999488 | bytes 4194304 | tf_op jit(solution)/shard_map/closure/pallas_call | solution.py:546
  49.3 0.1 collective-permute-start.8
  49.4 2.0 %collective-permute-start.9 = (bf16[448,256]{1,0:T(8,128)(2,1)S(1)}, bf16[448,256]{1,0:T(8,128)(2,1)S(1)}, u32[]{:S(2)}, u32[]{:S(2)}) collective-permute-start(bf16[448,256]{1,0:T(8,128)(2,1)S(1)} %get-tuple-element.73), channel_id=1, source_target_pairs={{0,8},{4,12},{1,0},{5,4},{2,1},{6,5},{3,2},{7,6},{11,3},{15,7},{10... | collective-permute-start | bytes 688136 | tf_op jit(solution)/shard_map/ppermute | solution.py:606
  51.4 6.0 %first.2.one = f32[256,256]{1,0:T(8,128)S(1)} custom-call(bf16[256,256]{1,0:T(8,128)(2,1)S(1)} %get-tuple-element.66.w_first, bf16[256,432]{1,0:T(8,128)(2,1)S(1)} %get-tuple-element.74.w_back, bf16[4,256,4096]{2,1,0:T(8,128)(2,1)S(1)} %get-tuple-element.82.fcol, bf16[4,3,16,4096]{3,2,1,0:T(8,128)(2,1)S(1)} %get-tuple-element.83.g2z), custom_call_target="tpu_custom_call" | custom-call | flops 3800000000 | bytes 4194304 | tf_op jit(solution)/shard_map/first/pallas_call | solution.py:578
  57.4 0.0 collective-permute-done.9
  57.4 0.1 collective-permute-start.10
  57.5 2.0 %collective-permute-start.11 = (bf16[448,256]{1,0:T(8,128)(2,1)S(1)}, bf16[448,256]{1,0:T(8,128)(2,1)S(1)}, u32[]{:S(2)}, u32[]{:S(2)}) collective-permute-start(bf16[448,256]{1,0:T(8,128)(2,1)S(1)} %collective-permute-done.9), channel_id=1, source_target_pairs={{0,8},{4,12},{1,0},{5,4},{2,1},{6,5},{3,2},{7,6},{11,3},{15,7},{10... | collective-permute-start | bytes 688136 | tf_op jit(solution)/shard_map/ppermute | solution.py:606
  59.5 6.0 %first.3.two = f32[256,256]{1,0:T(8,128)S(1)} custom-call(bf16[256,256]{1,0:T(8,128)(2,1)S(1)} %get-tuple-element.66.w_first, bf16[256,432]{1,0:T(8,128)(2,1)S(1)} %get-tuple-element.74.w_back, bf16[4,256,4096]{2,1,0:T(8,128)(2,1)S(1)} %get-tuple-element.82.fcol, bf16[4,3,16,4096]{3,2,1,0:T(8,128)(2,1)S(1)} %get-tuple-element.83.g2z), custom_call_target="tpu_custom_call" | custom-call | flops 3800000000 | bytes 4194304 | tf_op jit(solution)/shard_map/first/pallas_call | solution.py:578
  65.5 0.0 collective-permute-done.10
  65.6 0.1 split.1
  65.6 0.1 collective-permute-start.12
  65.7 0.3 collective-permute-start.14
  66.0 1.8 %collective-permute-start.15 = (bf16[448,256]{1,0:T(8,128)(2,1)S(1)}, bf16[448,256]{1,0:T(8,128)(2,1)S(1)}, u32[]{:S(2)}, u32[]{:S(2)}) collective-permute-start(bf16[448,256]{1,0:T(8,128)(2,1)S(1)} %collective-permute-done.11), channel_id=1, source_target_pairs={{0,8},{4,12},{1,0},{5,4},{2,1},{6,5},{3,2},{7,6},{11,3},{15,7},{10... | collective-permute-start | bytes 688136 | tf_op jit(solution)/shard_map/ppermute | solution.py:606
  67.8 0.0 collective-permute-done.12.got
  67.8 0.1 merge.1
  67.9 1.6 %collective-permute-start.13 = (bf16[256,256]{1,0:T(8,128)(2,1)S(1)}, bf16[256,256]{1,0:T(8,128)(2,1)S(1)}, u32[]{:S(2)}, u32[]{:S(2)}) collective-permute-start(bf16[256,256]{1,0:T(8,128)(2,1)S(1)} %get-tuple-element.89.mine), channel_id=1, source_target_pairs={{0,8},{1,9},{2,10},{3,11},{4,12},{5,13},{6,14},{7,15},{8,0},{9,1},... | collective-permute-start | bytes 393224 | tf_op jit(solution)/shard_map/ppermute | solution.py:481
  69.4 0.5 collective-permute-start.22
  70.0 4.2 %collective-permute-done.14 = bf16[448,256]{1,0:T(8,128)(2,1)S(1)} collective-permute-done((bf16[448,256]{1,0:T(8,128)(2,1)S(1)}, bf16[448,256]{1,0:T(8,128)(2,1)S(1)}, u32[]{:S(2)}, u32[]{:S(2)}) %collective-permute-start.14) | collective-permute-done | bytes 229408 | tf_op jit(solution)/shard_map/ppermute | solution.py:606
  74.2 2.4 %collective-permute-done.13.got = bf16[256,256]{1,0:T(8,128)(2,1)S(1)} collective-permute-done((bf16[256,256]{1,0:T(8,128)(2,1)S(1)}, bf16[256,256]{1,0:T(8,128)(2,1)S(1)}, u32[]{:S(2)}, u32[]{:S(2)}) %collective-permute-start.13) | collective-permute-done | bytes 131104 | tf_op jit(solution)/shard_map/ppermute | solution.py:481
  76.5 0.0 collective-permute-start.20
  76.5 0.0 collective-permute-start.24
  76.6 0.1 collective-permute-start.16
  76.7 3.0 %collective-permute-start.17 = (bf16[160,256]{1,0:T(8,128)(2,1)S(1)}, bf16[160,256]{1,0:T(8,128)(2,1)S(1)}, u32[]{:S(2)}, u32[]{:S(2)}) collective-permute-start(bf16[160,256]{1,0:T(8,128)(2,1)S(1)} %get-tuple-element.96), channel_id=1, source_target_pairs={{0,2},{1,3},{2,0},{3,1},{4,6},{5,7},{6,4},{7,5},{8,10},{9,11},{10,... | collective-permute-start | bytes 245768 | tf_op jit(solution)/shard_map/ppermute | solution.py:481
  79.6 0.0 collective-permute-done.23
  79.6 1.4 %collective-permute-start.18 = (bf16[160,256]{1,0:T(8,128)(2,1)S(1)}, bf16[160,256]{1,0:T(8,128)(2,1)S(1)}, u32[]{:S(2)}, u32[]{:S(2)}) collective-permute-start(bf16[160,256]{1,0:T(8,128)(2,1)S(1)} %get-tuple-element.97), channel_id=1, source_target_pairs={{0,3},{1,2},{2,1},{3,0},{4,7},{5,6},{6,5},{7,4},{8,11},{9,10},{10,... | collective-permute-start | bytes 245768 | tf_op jit(solution)/shard_map/ppermute | solution.py:481
  81.0 3.2 %collective-permute-done.16.one = bf16[160,256]{1,0:T(8,128)(2,1)S(1)} collective-permute-done((bf16[160,256]{1,0:T(8,128)(2,1)S(1)}, bf16[160,256]{1,0:T(8,128)(2,1)S(1)}, u32[]{:S(2)}, u32[]{:S(2)}) %collective-permute-start.16) | collective-permute-done | bytes 81952 | tf_op jit(solution)/shard_map/ppermute | solution.py:481
  84.3 0.0 collective-permute-start.25
  84.3 1.6 %collective-permute-done.17.two = bf16[160,256]{1,0:T(8,128)(2,1)S(1)} collective-permute-done((bf16[160,256]{1,0:T(8,128)(2,1)S(1)}, bf16[160,256]{1,0:T(8,128)(2,1)S(1)}, u32[]{:S(2)}, u32[]{:S(2)}) %collective-permute-start.17) | collective-permute-done | bytes 81952 | tf_op jit(solution)/shard_map/ppermute | solution.py:481
  85.9 1.3 %collective-permute-done.18.three = bf16[160,256]{1,0:T(8,128)(2,1)S(1)} collective-permute-done((bf16[160,256]{1,0:T(8,128)(2,1)S(1)}, bf16[160,256]{1,0:T(8,128)(2,1)S(1)}, u32[]{:S(2)}, u32[]{:S(2)}) %collective-permute-start.18) | collective-permute-done | bytes 81952 | tf_op jit(solution)/shard_map/ppermute | solution.py:481
  87.3 0.0 collective-permute-start.27
  87.3 0.0 collective-permute-done.20
  87.3 0.5 collective-permute-start.28
  87.8 1.3 %total.1 = (f32[128,256]{1,0:T(8,128)S(1)}, f32[1,5,2,4,128]{4,3,2,1,0:T(4,128)}) custom-call(s32[2]{0:T(128)S(1)} %and_select_fusion.place, f32[5,1024]{1,0:T(8,128)S(1)} %get-tuple-element.63.fields, f32[3,1024]{1,0:T(4,128)S(1)} %get-tuple-element.78.drag, bf16[160,256]{1,0:T(8,128)(2,1)S(1)} %get-tuple-element.94.mine, ...), custom_call_target="tpu_custom_call" | custom-call | tf_op jit(solution)/shard_map/total/pallas_call | solution.py:653
  89.0 0.0 collective-permute-start.19
  89.0 1.3 %collective-permute-done.19.other = f32[128,256]{1,0:T(8,128)S(1)} collective-permute-done((f32[128,256]{1,0:T(8,128)S(1)}, f32[128,256]{1,0:T(8,128)S(1)}, u32[]{:S(2)}, u32[]{:S(2)}) %collective-permute-start.19) | collective-permute-done | bytes 131104 | tf_op jit(solution)/shard_map/ppermute | solution.py:481
  90.4 5.2 %finish.1 = (f32[27,256,256]{2,1,0:T(8,128)}, f32[9,27,256]{2,1,0:T(8,128)}, f32[5,256]{1,0:T(8,128)}) custom-call(s32[16]{0:T(128)S(1)} %fusion.1.place, s32[1]{0:T(128)} %bitcast.14.core, f32[128,256]{1,0:T(8,128)S(1)} %get-tuple-element.100.own, f32[128,256]{1,0:T(8,128)S(1)} %collective-permute-done.19.other, bf16[1,448,256]{2,1,0:T(8,128)(2,1)S(1)} %bitcast.34, ...), custom_call_target="tpu_custom_call" | custom-call | tf_op jit(solution)/shard_map/finish/pallas_call | solution.py:692
  (33 shorter events, 0.2 us)
Async XLA Ops:
  0.6 0.7 copy-start
  1.4 0.7 copy-start.1
  2.1 0.7 copy-start.2
  2.8 0.7 copy-start.3
  3.5 0.7 copy-start.4
  4.2 0.7 copy-start.5
  4.9 0.7 copy-start.6
  7.1 10.9 %collective-permute-start = (f32[4,1024]{1,0:T(4,128)S(1)}, f32[4,1024]{1,0:T(4,128)S(1)}, u32[]{:S(2)}, u32[]{:S(2)}) collective-permute-start(f32[4,1024]{1,0:T(4,128)S(1)} %get-tuple-element.61), channel_id=1, source_target_pairs={{0,4},{4,8},{8,12},{12,0},{1,5},{5,9},{9,13},{13,1},{2,6},{6,10},{... | collective-permute-start | bytes 49160 | tf_op jit(solution)/shard_map/ppermute | solution.py:494
  7.6 10.4 %collective-permute-start.1 = (f32[4,1024]{1,0:T(4,128)S(1)}, f32[4,1024]{1,0:T(4,128)S(1)}, u32[]{:S(2)}, u32[]{:S(2)}) collective-permute-start(f32[4,1024]{1,0:T(4,128)S(1)} %get-tuple-element.62), channel_id=1, source_target_pairs={{4,0},{8,4},{12,8},{0,12},{5,1},{9,5},{13,9},{1,13},{6,2},{10,6},{... | collective-permute-start | bytes 49160 | tf_op jit(solution)/shard_map/ppermute | solution.py:495
  9.7 2.0 %copy-start.7 = (bf16[27,256,256]{2,1,0:T(8,128)(2,1)S(1)}, bf16[27,256,256]{2,1,0:T(8,128)(2,1)}, u32[]{:S(2)}) copy-start(bf16[27,256,256]{2,1,0:T(8,128)(2,1)} %mid_hbm.1) | copy-start | bytes 10616836
  11.7 0.9 copy-start.8
  12.6 0.7 copy-start.9
  18.0 5.6 %collective-permute-start.2 = (bf16[16,1024]{1,0:T(8,128)(2,1)S(1)}, bf16[16,1024]{1,0:T(8,128)(2,1)S(1)}, u32[]{:S(2)}, u32[]{:S(2)}) collective-permute-start(bf16[16,1024]{1,0:T(8,128)(2,1)S(1)} %get-tuple-element.65), channel_id=1, source_target_pairs={{0,1},{1,0},{2,3},{3,2},{4,5},{5,4},{6,7},{7,6},{8,9},{9,8},{10,11... | collective-permute-start | bytes 98312 | tf_op jit(solution)/shard_map/ppermute | solution.py:481
  20.4 5.4 %collective-permute-start.3 = (bf16[16,1024]{1,0:T(8,128)(2,1)S(1)}, bf16[16,1024]{1,0:T(8,128)(2,1)S(1)}, u32[]{:S(2)}, u32[]{:S(2)}) collective-permute-start(bf16[16,1024]{1,0:T(8,128)(2,1)S(1)} %get-tuple-element.65), channel_id=1, source_target_pairs={{0,2},{1,3},{2,0},{3,1},{4,6},{5,7},{6,4},{7,5},{8,10},{9,11},{10,... | collective-permute-start | bytes 98312 | tf_op jit(solution)/shard_map/ppermute | solution.py:481
  23.0 5.7 %collective-permute-start.4 = (bf16[16,1024]{1,0:T(8,128)(2,1)S(1)}, bf16[16,1024]{1,0:T(8,128)(2,1)S(1)}, u32[]{:S(2)}, u32[]{:S(2)}) collective-permute-start(bf16[16,1024]{1,0:T(8,128)(2,1)S(1)} %get-tuple-element.65), channel_id=1, source_target_pairs={{0,3},{1,2},{2,1},{3,0},{4,7},{5,6},{6,5},{7,4},{8,11},{9,10},{10,... | collective-permute-start | bytes 98312 | tf_op jit(solution)/shard_map/ppermute | solution.py:481
  28.7 5.0 %collective-permute-start.5 = (bf16[4,16,1024]{2,1,0:T(8,128)(2,1)S(1)}, bf16[4,16,1024]{2,1,0:T(8,128)(2,1)S(1)}, u32[]{:S(2)}, u32[]{:S(2)}) collective-permute-start(bf16[4,16,1024]{2,1,0:T(8,128)(2,1)S(1)} %pad_maximum_fusion.refs_0_), channel_id=1, source_target_pairs={{0,8},{1,9},{2,10},{3,11},{4,12},{5,13},{6,14},{7,15},{8,0},{9,1},... | collective-permute-start | bytes 393224 | tf_op jit(solution)/shard_map/ppermute | solution.py:481
  30.4 3.4 %collective-permute-start.6 = (bf16[4,16,1024]{2,1,0:T(8,128)(2,1)S(1)}, bf16[4,16,1024]{2,1,0:T(8,128)(2,1)S(1)}, u32[]{:S(2)}, u32[]{:S(2)}) collective-permute-start(bf16[4,16,1024]{2,1,0:T(8,128)(2,1)S(1)} %pad_maximum_fusion.refs_0_), channel_id=1, source_target_pairs={{0,4},{1,5},{2,6},{3,7},{4,0},{5,1},{6,2},{7,3},{8,12},{9,13},{10,... | collective-permute-start | bytes 393224 | tf_op jit(solution)/shard_map/ppermute | solution.py:481
  33.7 1.3 %collective-permute-start.7 = (bf16[4,16,1024]{2,1,0:T(8,128)(2,1)S(1)}, bf16[4,16,1024]{2,1,0:T(8,128)(2,1)S(1)}, u32[]{:S(2)}, u32[]{:S(2)}) collective-permute-start(bf16[4,16,1024]{2,1,0:T(8,128)(2,1)S(1)} %collective-permute-done.5.refs_1_), channel_id=1, source_target_pairs={{0,4},{1,5},{2,6},{3,7},{4,0},{5,1},{6,2},{7,3},{8,12},{9,13},{10,... | collective-permute-start | bytes 393224 | tf_op jit(solution)/shard_map/ppermute | solution.py:481
  49.3 8.1 %collective-permute-start.8 = (bf16[448,256]{1,0:T(8,128)(2,1)S(1)}, bf16[448,256]{1,0:T(8,128)(2,1)S(1)}, u32[]{:S(2)}, u32[]{:S(2)}) collective-permute-start(bf16[448,256]{1,0:T(8,128)(2,1)S(1)} %get-tuple-element.73), channel_id=1, source_target_pairs={{0,1},{4,5},{1,2},{5,6},{2,3},{6,7},{3,11},{7,15},{11,10},{15,14},... | collective-permute-start | bytes 688136 | tf_op jit(solution)/shard_map/ppermute | solution.py:606
  49.4 8.1 %collective-permute-start.9 = (bf16[448,256]{1,0:T(8,128)(2,1)S(1)}, bf16[448,256]{1,0:T(8,128)(2,1)S(1)}, u32[]{:S(2)}, u32[]{:S(2)}) collective-permute-start(bf16[448,256]{1,0:T(8,128)(2,1)S(1)} %get-tuple-element.73), channel_id=1, source_target_pairs={{0,8},{4,12},{1,0},{5,4},{2,1},{6,5},{3,2},{7,6},{11,3},{15,7},{10... | collective-permute-start | bytes 688136 | tf_op jit(solution)/shard_map/ppermute | solution.py:606
  57.4 8.1 %collective-permute-start.10 = (bf16[448,256]{1,0:T(8,128)(2,1)S(1)}, bf16[448,256]{1,0:T(8,128)(2,1)S(1)}, u32[]{:S(2)}, u32[]{:S(2)}) collective-permute-start(bf16[448,256]{1,0:T(8,128)(2,1)S(1)} %collective-permute-done.8), channel_id=1, source_target_pairs={{0,1},{4,5},{1,2},{5,6},{2,3},{6,7},{3,11},{7,15},{11,10},{15,14},... | collective-permute-start | bytes 688136 | tf_op jit(solution)/shard_map/ppermute | solution.py:606
  57.5 8.0 %collective-permute-start.11 = (bf16[448,256]{1,0:T(8,128)(2,1)S(1)}, bf16[448,256]{1,0:T(8,128)(2,1)S(1)}, u32[]{:S(2)}, u32[]{:S(2)}) collective-permute-start(bf16[448,256]{1,0:T(8,128)(2,1)S(1)} %collective-permute-done.9), channel_id=1, source_target_pairs={{0,8},{4,12},{1,0},{5,4},{2,1},{6,5},{3,2},{7,6},{11,3},{15,7},{10... | collective-permute-start | bytes 688136 | tf_op jit(solution)/shard_map/ppermute | solution.py:606
  65.6 2.2 %collective-permute-start.12 = (f32[384,256]{1,0:T(8,128)S(1)}, f32[384,256]{1,0:T(8,128)S(1)}, u32[]{:S(2)}, u32[]{:S(2)}) collective-permute-start(f32[384,256]{1,0:T(8,128)S(1)} %get-tuple-element.86), channel_id=1, source_target_pairs={{0,4},{1,5},{2,6},{3,7},{4,0},{5,1},{6,2},{7,3},{8,12},{9,13},{10,... | collective-permute-start | bytes 1179656 | tf_op jit(solution)/shard_map/ppermute | solution.py:481
  65.7 8.5 %collective-permute-start.14 = (bf16[448,256]{1,0:T(8,128)(2,1)S(1)}, bf16[448,256]{1,0:T(8,128)(2,1)S(1)}, u32[]{:S(2)}, u32[]{:S(2)}) collective-permute-start(bf16[448,256]{1,0:T(8,128)(2,1)S(1)} %collective-permute-done.10), channel_id=1, source_target_pairs={{0,1},{4,5},{1,2},{5,6},{2,3},{6,7},{3,11},{7,15},{11,10},{15,14},... | collective-permute-start | bytes 688136 | tf_op jit(solution)/shard_map/ppermute | solution.py:606
  66.0 8.2 %collective-permute-start.15 = (bf16[448,256]{1,0:T(8,128)(2,1)S(1)}, bf16[448,256]{1,0:T(8,128)(2,1)S(1)}, u32[]{:S(2)}, u32[]{:S(2)}) collective-permute-start(bf16[448,256]{1,0:T(8,128)(2,1)S(1)} %collective-permute-done.11), channel_id=1, source_target_pairs={{0,8},{4,12},{1,0},{5,4},{2,1},{6,5},{3,2},{7,6},{11,3},{15,7},{10... | collective-permute-start | bytes 688136 | tf_op jit(solution)/shard_map/ppermute | solution.py:606
  67.9 8.7 %collective-permute-start.13 = (bf16[256,256]{1,0:T(8,128)(2,1)S(1)}, bf16[256,256]{1,0:T(8,128)(2,1)S(1)}, u32[]{:S(2)}, u32[]{:S(2)}) collective-permute-start(bf16[256,256]{1,0:T(8,128)(2,1)S(1)} %get-tuple-element.89.mine), channel_id=1, source_target_pairs={{0,8},{1,9},{2,10},{3,11},{4,12},{5,13},{6,14},{7,15},{8,0},{9,1},... | collective-permute-start | bytes 393224 | tf_op jit(solution)/shard_map/ppermute | solution.py:481
  69.4 7.1 %collective-permute-start.21 = (bf16[448,256]{1,0:T(8,128)(2,1)S(1)}, bf16[448,256]{1,0:T(8,128)(2,1)S(1)}, u32[]{:S(2)}, u32[]{:S(2)}) collective-permute-start(bf16[448,256]{1,0:T(8,128)(2,1)S(1)} %get-tuple-element.73), channel_id=1, source_target_pairs={{0,4},{1,5},{2,6},{3,7},{4,0},{5,1},{6,2},{7,3},{8,12},{9,13},{10,... | collective-permute-start | bytes 688136 | tf_op jit(solution)/shard_map/ppermute | solution.py:481
  69.4 7.2 %collective-permute-start.22 = (bf16[448,256]{1,0:T(8,128)(2,1)S(1)}, bf16[448,256]{1,0:T(8,128)(2,1)S(1)}, u32[]{:S(2)}, u32[]{:S(2)}) collective-permute-start(bf16[448,256]{1,0:T(8,128)(2,1)S(1)} %collective-permute-done.8), channel_id=1, source_target_pairs={{0,4},{1,5},{2,6},{3,7},{4,0},{5,1},{6,2},{7,3},{8,12},{9,13},{10,... | collective-permute-start | bytes 688136 | tf_op jit(solution)/shard_map/ppermute | solution.py:481
  74.2 5.5 %collective-permute-start.23 = (bf16[448,256]{1,0:T(8,128)(2,1)S(1)}, bf16[448,256]{1,0:T(8,128)(2,1)S(1)}, u32[]{:S(2)}, u32[]{:S(2)}) collective-permute-start(bf16[448,256]{1,0:T(8,128)(2,1)S(1)} %collective-permute-done.9), channel_id=1, source_target_pairs={{0,4},{1,5},{2,6},{3,7},{4,0},{5,1},{6,2},{7,3},{8,12},{9,13},{10,... | collective-permute-start | bytes 688136 | tf_op jit(solution)/shard_map/ppermute | solution.py:481
  76.5 10.7 %collective-permute-start.20 = (bf16[448,256]{1,0:T(8,128)(2,1)S(1)}, bf16[448,256]{1,0:T(8,128)(2,1)S(1)}, u32[]{:S(2)}, u32[]{:S(2)}) collective-permute-start(bf16[448,256]{1,0:T(8,128)(2,1)S(1)} %collective-permute-done.14), channel_id=1, source_target_pairs={{0,1},{4,5},{1,2},{5,6},{2,3},{6,7},{3,11},{7,15},{11,10},{15,14},... | collective-permute-start | bytes 688136 | tf_op jit(solution)/shard_map/ppermute | solution.py:606
  76.5 12.5 %collective-permute-start.24 = (bf16[448,256]{1,0:T(8,128)(2,1)S(1)}, bf16[448,256]{1,0:T(8,128)(2,1)S(1)}, u32[]{:S(2)}, u32[]{:S(2)}) collective-permute-start(bf16[448,256]{1,0:T(8,128)(2,1)S(1)} %collective-permute-done.10), channel_id=1, source_target_pairs={{0,4},{1,5},{2,6},{3,7},{4,0},{5,1},{6,2},{7,3},{8,12},{9,13},{10,... | collective-permute-start | bytes 688136 | tf_op jit(solution)/shard_map/ppermute | solution.py:481
  76.6 7.7 %collective-permute-start.16 = (bf16[160,256]{1,0:T(8,128)(2,1)S(1)}, bf16[160,256]{1,0:T(8,128)(2,1)S(1)}, u32[]{:S(2)}, u32[]{:S(2)}) collective-permute-start(bf16[160,256]{1,0:T(8,128)(2,1)S(1)} %get-tuple-element.94.mine), channel_id=1, source_target_pairs={{0,1},{1,0},{2,3},{3,2},{4,5},{5,4},{6,7},{7,6},{8,9},{9,8},{10,11... | collective-permute-start | bytes 245768 | tf_op jit(solution)/shard_map/ppermute | solution.py:481
  76.7 9.3 %collective-permute-start.17 = (bf16[160,256]{1,0:T(8,128)(2,1)S(1)}, bf16[160,256]{1,0:T(8,128)(2,1)S(1)}, u32[]{:S(2)}, u32[]{:S(2)}) collective-permute-start(bf16[160,256]{1,0:T(8,128)(2,1)S(1)} %get-tuple-element.96), channel_id=1, source_target_pairs={{0,2},{1,3},{2,0},{3,1},{4,6},{5,7},{6,4},{7,5},{8,10},{9,11},{10,... | collective-permute-start | bytes 245768 | tf_op jit(solution)/shard_map/ppermute | solution.py:481
  79.6 7.6 %collective-permute-start.18 = (bf16[160,256]{1,0:T(8,128)(2,1)S(1)}, bf16[160,256]{1,0:T(8,128)(2,1)S(1)}, u32[]{:S(2)}, u32[]{:S(2)}) collective-permute-start(bf16[160,256]{1,0:T(8,128)(2,1)S(1)} %get-tuple-element.97), channel_id=1, source_target_pairs={{0,3},{1,2},{2,1},{3,0},{4,7},{5,6},{6,5},{7,4},{8,11},{9,10},{10,... | collective-permute-start | bytes 245768 | tf_op jit(solution)/shard_map/ppermute | solution.py:481
  84.3 4.8 %collective-permute-start.25 = (bf16[448,256]{1,0:T(8,128)(2,1)S(1)}, bf16[448,256]{1,0:T(8,128)(2,1)S(1)}, u32[]{:S(2)}, u32[]{:S(2)}) collective-permute-start(bf16[448,256]{1,0:T(8,128)(2,1)S(1)} %collective-permute-done.11), channel_id=1, source_target_pairs={{0,4},{1,5},{2,6},{3,7},{4,0},{5,1},{6,2},{7,3},{8,12},{9,13},{10,... | collective-permute-start | bytes 688136 | tf_op jit(solution)/shard_map/ppermute | solution.py:481
  85.9 4.4 %collective-permute-start.26 = (bf16[448,256]{1,0:T(8,128)(2,1)S(1)}, bf16[448,256]{1,0:T(8,128)(2,1)S(1)}, u32[]{:S(2)}, u32[]{:S(2)}) collective-permute-start(bf16[448,256]{1,0:T(8,128)(2,1)S(1)} %collective-permute-done.14), channel_id=1, source_target_pairs={{0,4},{1,5},{2,6},{3,7},{4,0},{5,1},{6,2},{7,3},{8,12},{9,13},{10,... | collective-permute-start | bytes 688136 | tf_op jit(solution)/shard_map/ppermute | solution.py:481
  87.3 3.1 %collective-permute-start.27 = (bf16[448,256]{1,0:T(8,128)(2,1)S(1)}, bf16[448,256]{1,0:T(8,128)(2,1)S(1)}, u32[]{:S(2)}, u32[]{:S(2)}) collective-permute-start(bf16[448,256]{1,0:T(8,128)(2,1)S(1)} %collective-permute-done.15), channel_id=1, source_target_pairs={{0,4},{1,5},{2,6},{3,7},{4,0},{5,1},{6,2},{7,3},{8,12},{9,13},{10,... | collective-permute-start | bytes 688136 | tf_op jit(solution)/shard_map/ppermute | solution.py:481
  87.3 3.1 %collective-permute-start.28 = (bf16[448,256]{1,0:T(8,128)(2,1)S(1)}, bf16[448,256]{1,0:T(8,128)(2,1)S(1)}, u32[]{:S(2)}, u32[]{:S(2)}) collective-permute-start(bf16[448,256]{1,0:T(8,128)(2,1)S(1)} %collective-permute-done.20), channel_id=1, source_target_pairs={{0,4},{1,5},{2,6},{3,7},{4,0},{5,1},{6,2},{7,3},{8,12},{9,13},{10,... | collective-permute-start | bytes 688136 | tf_op jit(solution)/shard_map/ppermute | solution.py:481
  89.0 1.3 %collective-permute-start.19 = (f32[128,256]{1,0:T(8,128)S(1)}, f32[128,256]{1,0:T(8,128)S(1)}, u32[]{:S(2)}, u32[]{:S(2)}) collective-permute-start(f32[128,256]{1,0:T(8,128)S(1)} %get-tuple-element.100.own), channel_id=1, source_target_pairs={{0,4},{1,5},{2,6},{3,7},{4,0},{5,1},{6,2},{7,3},{8,12},{9,13},{10,... | collective-permute-start | bytes 393224 | tf_op jit(solution)/shard_map/ppermute | solution.py:481

commit v5 on v4

--- a/solution.py
+++ b/solution.py
@@ -56,12 +56,13 @@
         copy.wait()
 
 
-def deposit_kernel(mass_in, vel_in, cell_in, listed_in, fields_in, cotangent_in, counts, stay, up, down, state, last_grad, *held):
+def deposit_kernel(mass_in, vel_in, cell_in, listed_in, fields_in, cotangent_in, counts, stay, up, down, *held):
     *held, sems = held
     fetch(list(zip((mass_in, vel_in, cell_in, listed_in, fields_in, cotangent_in), held)), sems)
     mass, vel, cell, listed, fields, cotangent = held
-    state[...] = flat_cells(fields)
-    last_grad[...] = dt_step * flat_cells(cotangent)
+    stay[4:9] = flat_cells(fields)
+    stay[9:14] = dt_step * flat_cells(cotangent)
+    stay[14:] = jnp.zeros((2, stay.shape[1]), F32)
     drops = mass.shape[1]
     slots = listed.shape[1]
     half = slots // 2
@@ -87,18 +88,18 @@
         onehot = (here == cell[...]).astype(F32).astype(BF16)
         got = dot_nt(rows, onehot)
         for i, out in enumerate((stay, up, down)):
-            out[:, start : start + chunk] = got[8 * i : 8 * i + 4] + got[8 * i + 4 : 8 * i + 8]
-
-
-def feature_kernel(stay, below, above, fields, last_grad, feats, drag):
-    deposit = stay[...] + below[...] + above[...]
-    state = fields[...]
+            out[0:4, start : start + chunk] = got[8 * i : 8 * i + 4] + got[8 * i + 4 : 8 * i + 8]
+
+
+def feature_kernel(stay, below, above, feats, own):
+    deposit = stay[0:4] + below[...] + above[...]
+    state = stay[4:9]
     force = drag_rate * (deposit[1:4] - deposit[0:1] * state[0:3])
-    drag[...] = force
+    own[...] = jnp.concatenate([state, force], 0)
     cells = state.shape[1]
     feats[...] = jnp.concatenate(
         [
-            last_grad[...],
+            stay[9:14],
             force[2:3],
             jnp.zeros((2, cells), F32),
             state,
@@ -120,7 +121,7 @@
     return ((at == k) & (t < 27)).astype(F32).astype(BF16)
 
 
-def weight_kernel(me, in_hbm, mid_hbm, out_hbm, wt, w_back, w_first, wo, wc, w_in, w_mid, w_out, sems):
+def weight_kernel(me, in_hbm, mid_hbm, out_hbm, packed, w_back, w_in, w_mid, w_out, sems):
     parts = 9
     share = w_mid.shape[0] // parts
     copies = []
@@ -132,22 +133,23 @@
         copy.start()
     for copy in small:
         copy.wait()
-    block, hid = wo.shape[0], wt.shape[1]
+    hid, rows = w_back.shape
+    block = rows // 27
     row = lax.broadcasted_iota(jnp.int32, (block, hid), 0)
     column = lax.broadcasted_iota(jnp.int32, (block, hid), 1)
     chosen = (column == row + me[0] * block).astype(F32).astype(BF16)
     pad = jnp.zeros((5, hid), F32)
     tall = jnp.concatenate([v for c in range(9) for v in (w_in[c].astype(F32), pad)], 0)
-    w_first[...] = (0.5 * dot(tall.T.astype(BF16), tap_rows())).astype(BF16)
+    packed[rows : rows + hid] = (0.5 * dot(tall.T.astype(BF16), tap_rows())).astype(BF16)
     wide = w_out[...].astype(F32)
     wide = jnp.concatenate([wide, jnp.zeros((16 - wide.shape[0], hid), F32)], 0).astype(BF16)
-    wo[...] = dot_nt(chosen, wide).astype(BF16)
-    wc[...] = dot_nt(wide, chosen).astype(BF16)
+    both = jnp.concatenate([dot_nt(chosen, wide), dot_nt(wide, chosen)], 0)
+    packed[rows + hid :] = jnp.concatenate([both, jnp.zeros((32, hid - 16), F32)], 1).astype(BF16)
     for i, copy in enumerate(copies):
         copy.wait()
         for t in range(i * share, (i + 1) * share):
-            wt[t * block : (t + 1) * block] = dot_nt(chosen, w_mid[t]).astype(BF16)
-    w_back[...] = wt[...].astype(F32).T.astype(BF16)
+            packed[t * block : (t + 1) * block] = dot_nt(chosen, w_mid[t]).astype(BF16)
+    w_back[...] = packed[0:rows].astype(F32).T.astype(BF16)
 
 
 def span(x, lanes, count=1):
@@ -161,7 +163,7 @@
     return jnp.concatenate(parts, 0)
 
 
-def closure_kernel(nz, lanes, sources, place, w_first, wt, wo, wc, *refs):
+def closure_kernel(nz, lanes, sources, place, packed, *refs):
     arrived, refs = refs[:sources], refs[sources:]
     piece, closure, g2z, fcol, feats, fz, eighth, ninth, hidden, sums, mid, last = refs
     s = pl.program_id(0)
@@ -170,8 +172,12 @@
     cells = hidden.shape[1]
     planes = cells // lanes
     per = planes // slabs
-    block = wo.shape[0]
+    rows, hid = mid.shape
+    block = last.shape[1]
     group = 4
+    wt, w_first = packed.at[0:rows], packed.at[rows : rows + hid]
+    wo = packed[rows + hid : rows + hid + 16, 0:16]
+    wc = packed[rows + hid + 16 :, 0:16]
 
     @pl.when(s == 0)
     def _():
@@ -250,14 +256,14 @@
         at = span(j, per * lanes)
         pre = sums[1, :, at] + roll_z(sums[0, :, at], 1, nz) + roll_z(sums[2, :, at], -1, nz)
         sig = logistic(pre)
-        hid = (pre * sig).astype(BF16)
-        out = dot(wc[...], hid)
+        active = (pre * sig).astype(BF16)
+        out = dot(wc, active)
         for h in range(per):
             for k in range(2):
                 start = h * lanes + k * (lanes // 2)
                 closure[0, j * per + h, 8 * k : 8 * k + 8] = out[0:8, start : start + lanes // 2].astype(BF16)
-        grad = dot(wo[...], here) * (sig * (1.0 + pre * (1.0 - sig)))
-        last[...] += dot_nt(here, hid)
+        grad = dot(wo, here) * (sig * (1.0 + pre * (1.0 - sig)))
+        last[...] += dot_nt(here, active)
         rounded = grad.astype(BF16)
         grad = rounded.astype(F32)
         g2z[0, 0, :, at] = roll_z(grad, -1, nz).astype(BF16)
@@ -290,13 +296,15 @@
         piece[taps:] = extra.astype(BF16)
 
 
-def first_kernel(nz, lanes, w_first, w_back, fcol, g2z, out):
+def first_kernel(nz, lanes, packed, w_back, fcol, g2z, out):
     @pl.when(pl.program_id(0) == 0)
     def _():
         out[...] = jnp.zeros_like(out)
 
     planes = fcol.shape[2] // lanes
     group = 2
+    hid, rows = w_back.shape
+    w_first = packed.at[rows : rows + hid]
     for x in range(0, planes, group):
         at = span(x, lanes, group)
         columns = [plane_taps(g2z, x + h, planes, nz, lanes) for h in range(group)]
@@ -346,20 +354,20 @@
             messages[o - 1][half:] = rows.astype(BF16)
 
 
-def step_kernel(nz, place, fields, drag, closure, *refs):
-    step_fields(nz, place, fields, drag, closure[...], refs[:-1], refs[-1])
-
-
-def total_kernel(nz, place, fields, drag, mine, kept, one, two, three, *refs):
+def step_kernel(nz, place, own, closure, *refs):
+    step_fields(nz, place, own, closure[...], refs[:-1], refs[-1])
+
+
+def total_kernel(nz, place, own, mine, kept, one, two, three, *refs):
     sources, (half, out) = refs[:-2], refs[-2:]
     pair = mine[0:128].astype(F32) + one[0:128].astype(F32)
     half[...] = pair + (two[0:128].astype(F32) + three[0:128].astype(F32))
     closure = kept[...] + (one[128:].astype(F32) + two[128:].astype(F32) + three[128:].astype(F32))
-    step_fields(nz, place, fields, drag, closure, sources, out)
-
-
-def step_fields(nz, place, fields, drag, closure, sources, out):
-    state = fields[...]
+    step_fields(nz, place, own, closure, sources, out)
+
+
+def step_fields(nz, place, own, closure, sources, out):
+    state = own[0:5]
     cells = state.shape[1]
     planes, rows = out.shape[2], out.shape[3]
     lanes = cells // planes
@@ -378,7 +386,7 @@
     advect = -0.5 * (
         state[0:1] * (next_x - last_x) + state[1:2] * (next_y - last_y) + state[2:3] * (next_z - last_z)
     )
-    momentum = jnp.concatenate([drag[...], jnp.zeros((2, cells), F32)], 0)
+    momentum = jnp.concatenate([own[5:8], jnp.zeros((2, cells), F32)], 0)
     closed = jnp.concatenate([closure[k : k + 5] for k in range(0, closure.shape[0], 8)], 1)
     new = state + dt_step * (viscosity * laplace + advect + closed + momentum)
     for x in range(planes):
@@ -482,45 +490,39 @@
 
     dense = shape((4, cells), F32)
     flows = (drop_mass, jnp.transpose(drop_vel, (1, 0, 2)), drop_cell, cross_list, fields, cotangent)
-    stay, up, down, state, last_grad = pl.pallas_call(
+    stay, up, down = pl.pallas_call(
         deposit_kernel,
-        out_shape=(dense, dense, dense, shape((5, cells), F32), shape((5, cells), F32)),
+        out_shape=(shape((16, cells), F32), dense, dense),
         in_specs=[HBM] * 6 + [SMEM],
-        out_specs=(VMEM,) * 5,
+        out_specs=(VMEM,) * 3,
         scratch_shapes=[pltpu.VMEM(v.shape, v.dtype) for v in flows] + [pltpu.SemaphoreType.DMA((6,))],
-        compiler_params=params(8),
+        compiler_params=params(60),
         name="deposit",
     )(*flows, cross_count)
     from_below = lax.ppermute(up, "slab", [(i, (i + 1) % n_slab) for i in range(n_slab)])
     from_above = lax.ppermute(down, "slab", [((i + 1) % n_slab, i) for i in range(n_slab)])
-    own_feats, drag = pl.pallas_call(
+    own_feats, own_state = pl.pallas_call(
         feature_kernel,
-        out_shape=(shape((16, cells), BF16), shape((3, cells), F32)),
-        in_specs=[VMEM] * 5,
+        out_shape=(shape((16, cells), BF16), shape((8, cells), F32)),
+        in_specs=[VMEM] * 3,
         out_specs=(VMEM,) * 2,
         compiler_params=params(4),
         name="features",
-    )(stay, from_below, from_above, state, last_grad)
+    )(stay, from_below, from_above)
 
     rows = 27 * block
-    wt, w_back, w_first, wo, wc = pl.pallas_call(
+    packed, w_back = pl.pallas_call(
         weight_kernel,
-        out_shape=(
-            shape((rows, hid), BF16),
-            shape((hid, rows), BF16),
-            shape((hid, 256), BF16),
-            shape((block, 16), BF16),
-            shape((16, block), BF16),
-        ),
+        out_shape=(shape((rows + hid + 32, hid), BF16), shape((hid, rows), BF16)),
         in_specs=[SMEM] + [HBM] * 3,
-        out_specs=(VMEM,) * 5,
+        out_specs=(VMEM,) * 2,
         scratch_shapes=[
             pltpu.VMEM((9, 27, hid), BF16),
             pltpu.VMEM(w_mid.shape, BF16),
             pltpu.VMEM((cout, hid), BF16),
             pltpu.SemaphoreType.DMA((11,)),
         ],
-        compiler_params=params(16),
+        compiler_params=params(60),
         cost_estimate=cost(1.5e9),
         name="weights",
     )(me[None], jnp.transpose(w_in, (1, 0, 2)), w_mid, w_out.T)
@@ -528,7 +530,7 @@
     if fast:
         far, middle, close = (trade(own_feats, mask) for mask in (3, 2, 1))
         near_z = [close, middle, far]
-        wt, w_back, w_first, wo, wc, *near_z = lax.optimization_barrier((wt, w_back, w_first, wo, wc, *near_z))
+        packed, w_back, *near_z = lax.optimization_barrier((packed, w_back, *near_z))
         mine = jnp.stack([own_feats] + near_z)
         across = trade(mine, 8)
         sources = [mine, across, trade(mine, 4), trade(across, 4)]
@@ -552,7 +554,7 @@
             shape((samples, 3, block, team_cells), BF16),
             shape((samples, 256, team_cells), BF16),
         ),
-        in_specs=[SMEM] + [VMEM] * (4 + len(sources)),
+        in_specs=[SMEM] + [VMEM] * (1 + len(sources)),
         out_specs=(
             whole_spec((rows + 16, hid)),
             pl.BlockSpec((1, all_planes, 16, lanes // 2), lambda s: (s, 0, 0, 0)),
@@ -572,7 +574,7 @@
         compiler_params=params(30 if all_planes <= 8 else 58),
         cost_estimate=cost(9e9),
         name="closure",
-    )(place, w_first, wt, wo, wc, *sources)
+    )(place, packed, *sources)
 
     def first_part(lo, count, fcol, g2z):
         return pl.pallas_call(
@@ -580,7 +582,7 @@
             grid=(count,),
             out_shape=shape((256, hid), F32),
             in_specs=[
-                whole_spec((hid, 256)),
+                whole_spec(packed.shape),
                 whole_spec((hid, rows)),
                 pl.BlockSpec((1, 256, team_cells), lambda s: (s + lo, 0, 0)),
                 pl.BlockSpec((1, 3, block, team_cells), lambda s: (s + lo, 0, 0, 0)),
@@ -589,7 +591,7 @@
             compiler_params=params(18 if all_planes <= 8 else 58),
             cost_estimate=cost(7.6e9 * count / samples),
             name="first",
-        )(w_first, w_back, fcol, g2z)
+        )(packed, w_back, fcol, g2z)
 
     if fast:
         core, y = slab & 1, slab >> 1
@@ -653,11 +655,11 @@
         own, new_fields = pl.pallas_call(
             functools.partial(total_kernel, nz),
             out_shape=(shape((128, hid), F32), shape(fields.shape, F32)),
-            in_specs=[SMEM] + [VMEM] * (7 + len(sources)),
+            in_specs=[SMEM] + [VMEM] * (6 + len(sources)),
             out_specs=(VMEM,) * 2,
             compiler_params=params(6),
             name="total",
-        )(near, state, drag, messages[0], kept, *got, *sources)
+        )(near, own_state, messages[0], kept, *got, *sources)
         other = trade(own, 4)
         pieces = [piece, f1, b1, f2, b2, f3, b3, f4]
         pieces = [v[None] for v in pieces + [trade(v, 4) for v in pieces]]
@@ -682,11 +684,11 @@
         new_fields = pl.pallas_call(
             functools.partial(step_kernel, nz),
             out_shape=shape(fields.shape, F32),
-            in_specs=[SMEM] + [VMEM] * 4,
+            in_specs=[SMEM] + [VMEM] * 3,
             out_specs=VMEM,
             compiler_params=params(6),
             name="step",
-        )(near, state, drag, own_closure, sources[0].reshape(n_slab, samples, 16, cells)[:, sample])
+        )(near, own_state, own_closure, sources[0].reshape(n_slab, samples, 16, cells)[:, sample])
 
     weight_count = w_in.size + w_mid.size + w_out.size
     grad_middle, grad_first, grad_last = pl.pallas_call(

time: 97.2 us -> 91.5 us (0.941)
  local copies, waits for them, and re-layouts: 9.09 us -> 2.46 us
  Pallas kernels: 39.1 us -> 40.2 us
    unnamed x20 -> x6, local copies, waits for them, and re-layouts: 8.46 us -> 1.82 us
    pallas_call x2, Pallas kernels: 6.22 us -> 7.46 us  [the longest x1 4.45 us: shards(): pl.pallas_call(weight_kernel, out_shape=(shape((rows + hid + 32, hid), BF...]
  transfers between devices with their start and end apart: 29 -> 29, of which waited for: 10 -> 10; matrix products, arithmetic and copies ran while one was open for 1% -> 1% of each run, Pallas kernels for 19% -> 20%
where the time goes in v5:
time: 91.5 us; the launch traced here: 90.2 us
  Pallas kernels  40.2 us (44%)
  waiting for transfers between devices  23.9 us (26%)
  starting transfers between devices  22.4 us (24%)
  local copies, waits for them, and re-layouts  2.46 us (3%)
  between operations  1.02 us (1%)
    ppermute x20, waiting for transfers between devices, trade(): return lax.ppermute(v, team, [(d, d ^ mask) for d in range(size)])  19.6 us
    pallas_call x1, Pallas kernels, shards(): pl.pallas_call(functools.partial(closure_kernel, nz, lanes, len(sources))...  14 us
    ppermute x20, starting transfers between devices, trade(): return lax.ppermute(v, team, [(d, d ^ mask) for d in range(size)])  13.7 us
    pallas_call x2, Pallas kernels, first_part(): pl.pallas_call(functools.partial(first_kernel, nz, lanes), grid=(count,),...  12.1 us
    ppermute x7, starting transfers between devices, around(): lax.ppermute(v, team, [(device(at, c), device(at + by, c)) for at in rang...  6.23 us
    pallas_call x1, Pallas kernels, shards(): pl.pallas_call(functools.partial(finish_kernel, len(pieces), weight_count...  5.21 us
    pallas_call x1, Pallas kernels, shards(): pl.pallas_call(weight_kernel, out_shape=(shape((rows + hid + 32, hid), BF...  4.45 us
    ppermute x7, waiting for transfers between devices, around(): lax.ppermute(v, team, [(device(at, c), device(at + by, c)) for at in rang...  4.23 us
  transfers between devices with their start and end apart: 29, of which 10 were waited for; matrix products, arithmetic and copies ran while one was open for 1% of the time, Pallas kernels for 20%

profile of v5, /device:TPU:0, one launch (start us, length us, event | category | flops | bytes accessed | tf_op | source)
XLA Modules:
  0.0 90.2 jit_solution(7262942235718388876)
XLA Ops:
  0.6 3.0 %deposit.1 = (f32[16,1024]{1,0:T(8,128)}, f32[4,1024]{1,0:T(4,128)}, f32[4,1024]{1,0:T(4,128)}) custom-call(f32[1,1024]{1,0:T(1,128)} %mass_in.1, f32[3,1,1024]{2,1,0:T(1,128)} %bitcast.54, s32[1,1024]{1,0:T(1,128)} %cell_in.1, s32[1,256]{1,0:T(1,128)} %listed_in.1, f32[1,5,2,4,128]{4,3,2,1,0:T(4,128)} %fields_in.1, f32[1,5,2,4,128]{4,3,2,1,0:T(4,128)} %cotangent_in.1, ...), custom_call_target="tpu_custom_call" | custom-call | tf_op jit(solution)/shard_map/deposit/pallas_call | solution.py:493
  3.7 0.5 collective-permute-start
  4.2 2.0 %collective-permute-start.1 = (f32[4,1024]{1,0:T(4,128)}, f32[4,1024]{1,0:T(4,128)S(1)}, u32[]{:S(2)}, u32[]{:S(2)}) collective-permute-start(f32[4,1024]{1,0:T(4,128)} %get-tuple-element.51), channel_id=1, source_target_pairs={{4,0},{8,4},{12,8},{0,12},{5,1},{9,5},{13,9},{1,13},{6,2},{10,6},{... | collective-permute-start | bytes 49160 | tf_op jit(solution)/shard_map/ppermute | solution.py:503
  6.2 0.1 fusion.3
  6.3 4.4 %weights.1 = (bf16[720,256]{1,0:T(8,128)(2,1)}, bf16[256,432]{1,0:T(8,128)(2,1)}) custom-call(s32[1]{0:T(128)} %bitcast.me, bf16[9,27,256]{2,1,0:T(8,128)(2,1)} %bitcast.56, bf16[27,256,256]{2,1,0:T(8,128)(2,1)} %mid_hbm.1, bf16[5,256]{1,0:T(8,128)(2,1)} %bitcast.58), custom_call_target="tpu_custom_call" | custom-call | flops 1500000000 | bytes 4194304 | tf_op jit(solution)/shard_map/weights/pallas_call | solution.py:514
  10.7 0.0 collective-permute-done.below
  10.7 0.0 collective-permute-done.1.above
  10.8 0.8 copy-done
  11.6 2.4 %collective-permute-start.2 = (bf16[16,1024]{1,0:T(8,128)(2,1)S(1)}, bf16[16,1024]{1,0:T(8,128)(2,1)S(1)}, u32[]{:S(2)}, u32[]{:S(2)}) collective-permute-start(bf16[16,1024]{1,0:T(8,128)(2,1)S(1)} %get-tuple-element.52), channel_id=1, source_target_pairs={{0,1},{1,0},{2,3},{3,2},{4,5},{5,4},{6,7},{7,6},{8,9},{9,8},{10,11... | collective-permute-start | bytes 98312 | tf_op jit(solution)/shard_map/ppermute | solution.py:489
  14.0 2.6 %collective-permute-start.3 = (bf16[16,1024]{1,0:T(8,128)(2,1)S(1)}, bf16[16,1024]{1,0:T(8,128)(2,1)S(1)}, u32[]{:S(2)}, u32[]{:S(2)}) collective-permute-start(bf16[16,1024]{1,0:T(8,128)(2,1)S(1)} %get-tuple-element.52), channel_id=1, source_target_pairs={{0,2},{1,3},{2,0},{3,1},{4,6},{5,7},{6,4},{7,5},{8,10},{9,11},{10,... | collective-permute-start | bytes 98312 | tf_op jit(solution)/shard_map/ppermute | solution.py:489
  16.6 0.0 collective-permute-start.4
  16.6 0.6 gather_fusion
  17.2 0.0 collective-permute-done.2
  17.2 2.2 %collective-permute-done.3 = bf16[16,1024]{1,0:T(8,128)(2,1)S(1)} collective-permute-done((bf16[16,1024]{1,0:T(8,128)(2,1)S(1)}, bf16[16,1024]{1,0:T(8,128)(2,1)S(1)}, u32[]{:S(2)}, u32[]{:S(2)}) %collective-permute-start.3) | collective-permute-done | bytes 32800 | tf_op jit(solution)/shard_map/ppermute | solution.py:489
  19.4 2.9 %collective-permute-done.4 = bf16[16,1024]{1,0:T(8,128)(2,1)S(1)} collective-permute-done((bf16[16,1024]{1,0:T(8,128)(2,1)S(1)}, bf16[16,1024]{1,0:T(8,128)(2,1)S(1)}, u32[]{:S(2)}, u32[]{:S(2)}) %collective-permute-start.4) | collective-permute-done | bytes 32800 | tf_op jit(solution)/shard_map/ppermute | solution.py:489
  22.3 1.6 %collective-permute-start.5 = (bf16[4,16,1024]{2,1,0:T(8,128)(2,1)S(1)}, bf16[4,16,1024]{2,1,0:T(8,128)(2,1)S(1)}, u32[]{:S(2)}, u32[]{:S(2)}) collective-permute-start(bf16[4,16,1024]{2,1,0:T(8,128)(2,1)S(1)} %pad_maximum_fusion.refs_0_), channel_id=1, source_target_pairs={{0,8},{1,9},{2,10},{3,11},{4,12},{5,13},{6,14},{7,15},{8,0},{9,1},... | collective-permute-start | bytes 393224 | tf_op jit(solution)/shard_map/ppermute | solution.py:489
  23.9 0.1 and_select_fusion.place
  24.0 0.0 collective-permute-start.6
  24.0 3.4 %collective-permute-done.5.refs_1_ = bf16[4,16,1024]{2,1,0:T(8,128)(2,1)S(1)} collective-permute-done((bf16[4,16,1024]{2,1,0:T(8,128)(2,1)S(1)}, bf16[4,16,1024]{2,1,0:T(8,128)(2,1)S(1)}, u32[]{:S(2)}, u32[]{:S(2)}) %collective-permute-start.5) | collective-permute-done | bytes 131104 | tf_op jit(solution)/shard_map/ppermute | solution.py:489
  27.3 0.0 collective-permute-start.7
  27.4 0.0 collective-permute-done.6.refs_2_
  27.4 1.3 %collective-permute-done.7.refs_3_ = bf16[4,16,1024]{2,1,0:T(8,128)(2,1)S(1)} collective-permute-done((bf16[4,16,1024]{2,1,0:T(8,128)(2,1)S(1)}, bf16[4,16,1024]{2,1,0:T(8,128)(2,1)S(1)}, u32[]{:S(2)}, u32[]{:S(2)}) %collective-permute-start.7) | collective-permute-done | bytes 131104 | tf_op jit(solution)/shard_map/ppermute | solution.py:489
  28.7 1.0 %copy-done.1 = bf16[720,256]{1,0:T(8,128)(2,1)S(1)} copy-done((bf16[720,256]{1,0:T(8,128)(2,1)S(1)}, bf16[720,256]{1,0:T(8,128)(2,1)}, u32[]{:S(2)}) %copy-start.1) | copy-done | bytes 368664
  29.7 14.0 %closure.1 = (bf16[448,256]{1,0:T(8,128)(2,1)S(1)}, bf16[4,8,16,256]{3,2,1,0:T(8,128)(2,1)S(1)}, bf16[4,3,16,4096]{3,2,1,0:T(8,128)(2,1)S(1)}, bf16[4,256,4096]{2,1,0:T(8,128)(2,1)S(1)}) custom-call(s32[4]{0:T(128)S(1)} %broadcast_multiply_fusion.place, bf16[720,256]{1,0:T(8,128)(2,1)S(1)} %copy-done.1, bf16[4,16,1024]{2,1,0:T(8,128)(2,1)S(1)} %pad_maximum_fusion.refs_0_, ...), custom_call_target="tpu_custom_call" | custom-call | flops 8999999488 | bytes 4194304 | tf_op jit(solution)/shard_map/closure/pallas_call | solution.py:548
  43.7 0.1 collective-permute-start.8
  43.8 2.0 %collective-permute-start.9 = (bf16[448,256]{1,0:T(8,128)(2,1)S(1)}, bf16[448,256]{1,0:T(8,128)(2,1)S(1)}, u32[]{:S(2)}, u32[]{:S(2)}) collective-permute-start(bf16[448,256]{1,0:T(8,128)(2,1)S(1)} %get-tuple-element.57), channel_id=1, source_target_pairs={{0,8},{4,12},{1,0},{5,4},{2,1},{6,5},{3,2},{7,6},{11,3},{15,7},{10... | collective-permute-start | bytes 688136 | tf_op jit(solution)/shard_map/ppermute | solution.py:608
  45.8 6.0 %first.2.one = f32[256,256]{1,0:T(8,128)S(1)} custom-call(bf16[720,256]{1,0:T(8,128)(2,1)S(1)} %copy-done.1, bf16[256,432]{1,0:T(8,128)(2,1)S(1)} %copy-done.2, bf16[4,256,4096]{2,1,0:T(8,128)(2,1)S(1)} %get-tuple-element.66.fcol, bf16[4,3,16,4096]{3,2,1,0:T(8,128)(2,1)S(1)} %get-tuple-element.67.g2z), custom_call_target="tpu_custom_call" | custom-call | flops 3800000000 | bytes 4194304 | tf_op jit(solution)/shard_map/first/pallas_call | solution.py:580
  51.9 0.0 collective-permute-done.8
  51.9 0.0 collective-permute-done.9
  51.9 0.1 collective-permute-start.10
  52.0 2.0 %collective-permute-start.11 = (bf16[448,256]{1,0:T(8,128)(2,1)S(1)}, bf16[448,256]{1,0:T(8,128)(2,1)S(1)}, u32[]{:S(2)}, u32[]{:S(2)}) collective-permute-start(bf16[448,256]{1,0:T(8,128)(2,1)S(1)} %collective-permute-done.9), channel_id=1, source_target_pairs={{0,8},{4,12},{1,0},{5,4},{2,1},{6,5},{3,2},{7,6},{11,3},{15,7},{10... | collective-permute-start | bytes 688136 | tf_op jit(solution)/shard_map/ppermute | solution.py:608
  54.0 6.0 %first.3.two = f32[256,256]{1,0:T(8,128)S(1)} custom-call(bf16[720,256]{1,0:T(8,128)(2,1)S(1)} %copy-done.1, bf16[256,432]{1,0:T(8,128)(2,1)S(1)} %copy-done.2, bf16[4,256,4096]{2,1,0:T(8,128)(2,1)S(1)} %get-tuple-element.66.fcol, bf16[4,3,16,4096]{3,2,1,0:T(8,128)(2,1)S(1)} %get-tuple-element.67.g2z), custom_call_target="tpu_custom_call" | custom-call | flops 3800000000 | bytes 4194304 | tf_op jit(solution)/shard_map/first/pallas_call | solution.py:580
  60.0 0.0 collective-permute-done.10
  60.0 0.0 collective-permute-done.11
  60.0 0.1 split.1
  60.1 0.1 collective-permute-start.12
  60.2 0.1 collective-permute-start.14
  60.3 2.0 %collective-permute-start.15 = (bf16[448,256]{1,0:T(8,128)(2,1)S(1)}, bf16[448,256]{1,0:T(8,128)(2,1)S(1)}, u32[]{:S(2)}, u32[]{:S(2)}) collective-permute-start(bf16[448,256]{1,0:T(8,128)(2,1)S(1)} %collective-permute-done.11), channel_id=1, source_target_pairs={{0,8},{4,12},{1,0},{5,4},{2,1},{6,5},{3,2},{7,6},{11,3},{15,7},{10... | collective-permute-start | bytes 688136 | tf_op jit(solution)/shard_map/ppermute | solution.py:608
  62.3 0.1 merge.1
  62.3 1.6 %collective-permute-start.13 = (bf16[256,256]{1,0:T(8,128)(2,1)S(1)}, bf16[256,256]{1,0:T(8,128)(2,1)S(1)}, u32[]{:S(2)}, u32[]{:S(2)}) collective-permute-start(bf16[256,256]{1,0:T(8,128)(2,1)S(1)} %get-tuple-element.73.mine), channel_id=1, source_target_pairs={{0,8},{1,9},{2,10},{3,11},{4,12},{5,13},{6,14},{7,15},{8,0},{9,1},... | collective-permute-start | bytes 393224 | tf_op jit(solution)/shard_map/ppermute | solution.py:489
  63.9 0.5 collective-permute-start.22
  64.4 4.2 %collective-permute-done.14 = bf16[448,256]{1,0:T(8,128)(2,1)S(1)} collective-permute-done((bf16[448,256]{1,0:T(8,128)(2,1)S(1)}, bf16[448,256]{1,0:T(8,128)(2,1)S(1)}, u32[]{:S(2)}, u32[]{:S(2)}) %collective-permute-start.14) | collective-permute-done | bytes 229408 | tf_op jit(solution)/shard_map/ppermute | solution.py:608
  68.6 2.4 %collective-permute-done.13.got = bf16[256,256]{1,0:T(8,128)(2,1)S(1)} collective-permute-done((bf16[256,256]{1,0:T(8,128)(2,1)S(1)}, bf16[256,256]{1,0:T(8,128)(2,1)S(1)}, u32[]{:S(2)}, u32[]{:S(2)}) %collective-permute-start.13) | collective-permute-done | bytes 131104 | tf_op jit(solution)/shard_map/ppermute | solution.py:489
  71.0 0.0 collective-permute-start.20
  71.0 0.0 collective-permute-start.24
  71.0 0.1 collective-permute-start.16
  71.1 0.0 collective-permute-done.22
  71.1 2.9 %collective-permute-start.17 = (bf16[160,256]{1,0:T(8,128)(2,1)S(1)}, bf16[160,256]{1,0:T(8,128)(2,1)S(1)}, u32[]{:S(2)}, u32[]{:S(2)}) collective-permute-start(bf16[160,256]{1,0:T(8,128)(2,1)S(1)} %get-tuple-element.80), channel_id=1, source_target_pairs={{0,2},{1,3},{2,0},{3,1},{4,6},{5,7},{6,4},{7,5},{8,10},{9,11},{10,... | collective-permute-start | bytes 245768 | tf_op jit(solution)/shard_map/ppermute | solution.py:489
  74.1 0.0 collective-permute-done.23
  74.1 1.4 %collective-permute-start.18 = (bf16[160,256]{1,0:T(8,128)(2,1)S(1)}, bf16[160,256]{1,0:T(8,128)(2,1)S(1)}, u32[]{:S(2)}, u32[]{:S(2)}) collective-permute-start(bf16[160,256]{1,0:T(8,128)(2,1)S(1)} %get-tuple-element.81), channel_id=1, source_target_pairs={{0,3},{1,2},{2,1},{3,0},{4,7},{5,6},{6,5},{7,4},{8,11},{9,10},{10,... | collective-permute-start | bytes 245768 | tf_op jit(solution)/shard_map/ppermute | solution.py:489
  75.5 3.2 %collective-permute-done.16.one = bf16[160,256]{1,0:T(8,128)(2,1)S(1)} collective-permute-done((bf16[160,256]{1,0:T(8,128)(2,1)S(1)}, bf16[160,256]{1,0:T(8,128)(2,1)S(1)}, u32[]{:S(2)}, u32[]{:S(2)}) %collective-permute-start.16) | collective-permute-done | bytes 81952 | tf_op jit(solution)/shard_map/ppermute | solution.py:489
  78.7 0.0 collective-permute-start.25
  78.7 1.6 %collective-permute-done.17.two = bf16[160,256]{1,0:T(8,128)(2,1)S(1)} collective-permute-done((bf16[160,256]{1,0:T(8,128)(2,1)S(1)}, bf16[160,256]{1,0:T(8,128)(2,1)S(1)}, u32[]{:S(2)}, u32[]{:S(2)}) %collective-permute-start.17) | collective-permute-done | bytes 81952 | tf_op jit(solution)/shard_map/ppermute | solution.py:489
  80.4 1.3 %collective-permute-done.18.three = bf16[160,256]{1,0:T(8,128)(2,1)S(1)} collective-permute-done((bf16[160,256]{1,0:T(8,128)(2,1)S(1)}, bf16[160,256]{1,0:T(8,128)(2,1)S(1)}, u32[]{:S(2)}, u32[]{:S(2)}) %collective-permute-start.18) | collective-permute-done | bytes 81952 | tf_op jit(solution)/shard_map/ppermute | solution.py:489
  81.7 0.0 collective-permute-start.27
  81.7 0.0 collective-permute-done.20
  81.7 0.5 collective-permute-start.28
  82.2 1.3 %total.1 = (f32[128,256]{1,0:T(8,128)S(1)}, f32[1,5,2,4,128]{4,3,2,1,0:T(4,128)}) custom-call(s32[2]{0:T(128)S(1)} %and_select_fusion.place, f32[8,1024]{1,0:T(8,128)S(1)} %get-tuple-element.62.own, bf16[160,256]{1,0:T(8,128)(2,1)S(1)} %get-tuple-element.78.mine, f32[32,256]{1,0:T(8,128)S(1)} %get-tuple-element.79.kept, ...), custom_call_target="tpu_custom_call" | custom-call | tf_op jit(solution)/shard_map/total/pallas_call | solution.py:655
  83.5 0.0 collective-permute-start.19
  83.5 1.3 %collective-permute-done.19.other = f32[128,256]{1,0:T(8,128)S(1)} collective-permute-done((f32[128,256]{1,0:T(8,128)S(1)}, f32[128,256]{1,0:T(8,128)S(1)}, u32[]{:S(2)}, u32[]{:S(2)}) %collective-permute-start.19) | collective-permute-done | bytes 131104 | tf_op jit(solution)/shard_map/ppermute | solution.py:489
  84.8 0.0 collective-permute-done.26
  84.8 0.0 collective-permute-done.27
  84.8 0.0 collective-permute-done.28
  84.8 5.2 %finish.1 = (f32[27,256,256]{2,1,0:T(8,128)}, f32[9,27,256]{2,1,0:T(8,128)}, f32[5,256]{1,0:T(8,128)}) custom-call(s32[16]{0:T(128)S(1)} %fusion.1.place, s32[1]{0:T(128)} %bitcast.14.core, f32[128,256]{1,0:T(8,128)S(1)} %get-tuple-element.84.own, f32[128,256]{1,0:T(8,128)S(1)} %collective-permute-done.19.other, bf16[1,448,256]{2,1,0:T(8,128)(2,1)S(1)} %bitcast.34, ...), custom_call_target="tpu_custom_call" | custom-call | tf_op jit(solution)/shard_map/finish/pallas_call | solution.py:694
  (19 shorter events, 0.1 us)
Async XLA Ops:
  3.7 7.1 %collective-permute-start = (f32[4,1024]{1,0:T(4,128)}, f32[4,1024]{1,0:T(4,128)S(1)}, u32[]{:S(2)}, u32[]{:S(2)}) collective-permute-start(f32[4,1024]{1,0:T(4,128)} %get-tuple-element.50), channel_id=1, source_target_pairs={{0,4},{4,8},{8,12},{12,0},{1,5},{5,9},{9,13},{13,1},{2,6},{6,10},{... | collective-permute-start | bytes 49160 | tf_op jit(solution)/shard_map/ppermute | solution.py:502
  4.2 6.6 %collective-permute-start.1 = (f32[4,1024]{1,0:T(4,128)}, f32[4,1024]{1,0:T(4,128)S(1)}, u32[]{:S(2)}, u32[]{:S(2)}) collective-permute-start(f32[4,1024]{1,0:T(4,128)} %get-tuple-element.51), channel_id=1, source_target_pairs={{4,0},{8,4},{12,8},{0,12},{5,1},{9,5},{13,9},{1,13},{6,2},{10,6},{... | collective-permute-start | bytes 49160 | tf_op jit(solution)/shard_map/ppermute | solution.py:503
  10.7 0.8 copy-start
  11.6 5.6 %collective-permute-start.2 = (bf16[16,1024]{1,0:T(8,128)(2,1)S(1)}, bf16[16,1024]{1,0:T(8,128)(2,1)S(1)}, u32[]{:S(2)}, u32[]{:S(2)}) collective-permute-start(bf16[16,1024]{1,0:T(8,128)(2,1)S(1)} %get-tuple-element.52), channel_id=1, source_target_pairs={{0,1},{1,0},{2,3},{3,2},{4,5},{5,4},{6,7},{7,6},{8,9},{9,8},{10,11... | collective-permute-start | bytes 98312 | tf_op jit(solution)/shard_map/ppermute | solution.py:489
  14.0 5.4 %collective-permute-start.3 = (bf16[16,1024]{1,0:T(8,128)(2,1)S(1)}, bf16[16,1024]{1,0:T(8,128)(2,1)S(1)}, u32[]{:S(2)}, u32[]{:S(2)}) collective-permute-start(bf16[16,1024]{1,0:T(8,128)(2,1)S(1)} %get-tuple-element.52), channel_id=1, source_target_pairs={{0,2},{1,3},{2,0},{3,1},{4,6},{5,7},{6,4},{7,5},{8,10},{9,11},{10,... | collective-permute-start | bytes 98312 | tf_op jit(solution)/shard_map/ppermute | solution.py:489
  16.6 5.7 %collective-permute-start.4 = (bf16[16,1024]{1,0:T(8,128)(2,1)S(1)}, bf16[16,1024]{1,0:T(8,128)(2,1)S(1)}, u32[]{:S(2)}, u32[]{:S(2)}) collective-permute-start(bf16[16,1024]{1,0:T(8,128)(2,1)S(1)} %get-tuple-element.52), channel_id=1, source_target_pairs={{0,3},{1,2},{2,1},{3,0},{4,7},{5,6},{6,5},{7,4},{8,11},{9,10},{10,... | collective-permute-start | bytes 98312 | tf_op jit(solution)/shard_map/ppermute | solution.py:489
  22.3 5.0 %collective-permute-start.5 = (bf16[4,16,1024]{2,1,0:T(8,128)(2,1)S(1)}, bf16[4,16,1024]{2,1,0:T(8,128)(2,1)S(1)}, u32[]{:S(2)}, u32[]{:S(2)}) collective-permute-start(bf16[4,16,1024]{2,1,0:T(8,128)(2,1)S(1)} %pad_maximum_fusion.refs_0_), channel_id=1, source_target_pairs={{0,8},{1,9},{2,10},{3,11},{4,12},{5,13},{6,14},{7,15},{8,0},{9,1},... | collective-permute-start | bytes 393224 | tf_op jit(solution)/shard_map/ppermute | solution.py:489
  24.0 3.4 %collective-permute-start.6 = (bf16[4,16,1024]{2,1,0:T(8,128)(2,1)S(1)}, bf16[4,16,1024]{2,1,0:T(8,128)(2,1)S(1)}, u32[]{:S(2)}, u32[]{:S(2)}) collective-permute-start(bf16[4,16,1024]{2,1,0:T(8,128)(2,1)S(1)} %pad_maximum_fusion.refs_0_), channel_id=1, source_target_pairs={{0,4},{1,5},{2,6},{3,7},{4,0},{5,1},{6,2},{7,3},{8,12},{9,13},{10,... | collective-permute-start | bytes 393224 | tf_op jit(solution)/shard_map/ppermute | solution.py:489
  27.3 1.3 %collective-permute-start.7 = (bf16[4,16,1024]{2,1,0:T(8,128)(2,1)S(1)}, bf16[4,16,1024]{2,1,0:T(8,128)(2,1)S(1)}, u32[]{:S(2)}, u32[]{:S(2)}) collective-permute-start(bf16[4,16,1024]{2,1,0:T(8,128)(2,1)S(1)} %collective-permute-done.5.refs_1_), channel_id=1, source_target_pairs={{0,4},{1,5},{2,6},{3,7},{4,0},{5,1},{6,2},{7,3},{8,12},{9,13},{10,... | collective-permute-start | bytes 393224 | tf_op jit(solution)/shard_map/ppermute | solution.py:489
  28.7 1.0 %copy-start.1 = (bf16[720,256]{1,0:T(8,128)(2,1)S(1)}, bf16[720,256]{1,0:T(8,128)(2,1)}, u32[]{:S(2)}) copy-start(bf16[720,256]{1,0:T(8,128)(2,1)} %get-tuple-element.53.packed) | copy-start | bytes 1105924
  29.7 16.1 %copy-start.2 = (bf16[256,432]{1,0:T(8,128)(2,1)S(1)}, bf16[256,432]{1,0:T(8,128)(2,1)}, u32[]{:S(2)}) copy-start(bf16[256,432]{1,0:T(8,128)(2,1)} %get-tuple-element.58.w_back) | copy-start | bytes 663556
  43.7 8.1 %collective-permute-start.8 = (bf16[448,256]{1,0:T(8,128)(2,1)S(1)}, bf16[448,256]{1,0:T(8,128)(2,1)S(1)}, u32[]{:S(2)}, u32[]{:S(2)}) collective-permute-start(bf16[448,256]{1,0:T(8,128)(2,1)S(1)} %get-tuple-element.57), channel_id=1, source_target_pairs={{0,1},{4,5},{1,2},{5,6},{2,3},{6,7},{3,11},{7,15},{11,10},{15,14},... | collective-permute-start | bytes 688136 | tf_op jit(solution)/shard_map/ppermute | solution.py:608
  43.8 8.1 %collective-permute-start.9 = (bf16[448,256]{1,0:T(8,128)(2,1)S(1)}, bf16[448,256]{1,0:T(8,128)(2,1)S(1)}, u32[]{:S(2)}, u32[]{:S(2)}) collective-permute-start(bf16[448,256]{1,0:T(8,128)(2,1)S(1)} %get-tuple-element.57), channel_id=1, source_target_pairs={{0,8},{4,12},{1,0},{5,4},{2,1},{6,5},{3,2},{7,6},{11,3},{15,7},{10... | collective-permute-start | bytes 688136 | tf_op jit(solution)/shard_map/ppermute | solution.py:608
  51.9 8.1 %collective-permute-start.10 = (bf16[448,256]{1,0:T(8,128)(2,1)S(1)}, bf16[448,256]{1,0:T(8,128)(2,1)S(1)}, u32[]{:S(2)}, u32[]{:S(2)}) collective-permute-start(bf16[448,256]{1,0:T(8,128)(2,1)S(1)} %collective-permute-done.8), channel_id=1, source_target_pairs={{0,1},{4,5},{1,2},{5,6},{2,3},{6,7},{3,11},{7,15},{11,10},{15,14},... | collective-permute-start | bytes 688136 | tf_op jit(solution)/shard_map/ppermute | solution.py:608
  52.0 8.0 %collective-permute-start.11 = (bf16[448,256]{1,0:T(8,128)(2,1)S(1)}, bf16[448,256]{1,0:T(8,128)(2,1)S(1)}, u32[]{:S(2)}, u32[]{:S(2)}) collective-permute-start(bf16[448,256]{1,0:T(8,128)(2,1)S(1)} %collective-permute-done.9), channel_id=1, source_target_pairs={{0,8},{4,12},{1,0},{5,4},{2,1},{6,5},{3,2},{7,6},{11,3},{15,7},{10... | collective-permute-start | bytes 688136 | tf_op jit(solution)/shard_map/ppermute | solution.py:608
  60.1 2.2 %collective-permute-start.12 = (f32[384,256]{1,0:T(8,128)S(1)}, f32[384,256]{1,0:T(8,128)S(1)}, u32[]{:S(2)}, u32[]{:S(2)}) collective-permute-start(f32[384,256]{1,0:T(8,128)S(1)} %get-tuple-element.70), channel_id=1, source_target_pairs={{0,4},{1,5},{2,6},{3,7},{4,0},{5,1},{6,2},{7,3},{8,12},{9,13},{10,... | collective-permute-start | bytes 1179656 | tf_op jit(solution)/shard_map/ppermute | solution.py:489
  60.2 8.5 %collective-permute-start.14 = (bf16[448,256]{1,0:T(8,128)(2,1)S(1)}, bf16[448,256]{1,0:T(8,128)(2,1)S(1)}, u32[]{:S(2)}, u32[]{:S(2)}) collective-permute-start(bf16[448,256]{1,0:T(8,128)(2,1)S(1)} %collective-permute-done.10), channel_id=1, source_target_pairs={{0,1},{4,5},{1,2},{5,6},{2,3},{6,7},{3,11},{7,15},{11,10},{15,14},... | collective-permute-start | bytes 688136 | tf_op jit(solution)/shard_map/ppermute | solution.py:608
  60.3 8.3 %collective-permute-start.15 = (bf16[448,256]{1,0:T(8,128)(2,1)S(1)}, bf16[448,256]{1,0:T(8,128)(2,1)S(1)}, u32[]{:S(2)}, u32[]{:S(2)}) collective-permute-start(bf16[448,256]{1,0:T(8,128)(2,1)S(1)} %collective-permute-done.11), channel_id=1, source_target_pairs={{0,8},{4,12},{1,0},{5,4},{2,1},{6,5},{3,2},{7,6},{11,3},{15,7},{10... | collective-permute-start | bytes 688136 | tf_op jit(solution)/shard_map/ppermute | solution.py:608
  62.3 8.7 %collective-permute-start.13 = (bf16[256,256]{1,0:T(8,128)(2,1)S(1)}, bf16[256,256]{1,0:T(8,128)(2,1)S(1)}, u32[]{:S(2)}, u32[]{:S(2)}) collective-permute-start(bf16[256,256]{1,0:T(8,128)(2,1)S(1)} %get-tuple-element.73.mine), channel_id=1, source_target_pairs={{0,8},{1,9},{2,10},{3,11},{4,12},{5,13},{6,14},{7,15},{8,0},{9,1},... | collective-permute-start | bytes 393224 | tf_op jit(solution)/shard_map/ppermute | solution.py:489
  63.9 7.1 %collective-permute-start.21 = (bf16[448,256]{1,0:T(8,128)(2,1)S(1)}, bf16[448,256]{1,0:T(8,128)(2,1)S(1)}, u32[]{:S(2)}, u32[]{:S(2)}) collective-permute-start(bf16[448,256]{1,0:T(8,128)(2,1)S(1)} %get-tuple-element.57), channel_id=1, source_target_pairs={{0,4},{1,5},{2,6},{3,7},{4,0},{5,1},{6,2},{7,3},{8,12},{9,13},{10,... | collective-permute-start | bytes 688136 | tf_op jit(solution)/shard_map/ppermute | solution.py:489
  63.9 7.2 %collective-permute-start.22 = (bf16[448,256]{1,0:T(8,128)(2,1)S(1)}, bf16[448,256]{1,0:T(8,128)(2,1)S(1)}, u32[]{:S(2)}, u32[]{:S(2)}) collective-permute-start(bf16[448,256]{1,0:T(8,128)(2,1)S(1)} %collective-permute-done.8), channel_id=1, source_target_pairs={{0,4},{1,5},{2,6},{3,7},{4,0},{5,1},{6,2},{7,3},{8,12},{9,13},{10,... | collective-permute-start | bytes 688136 | tf_op jit(solution)/shard_map/ppermute | solution.py:489
  68.6 5.4 %collective-permute-start.23 = (bf16[448,256]{1,0:T(8,128)(2,1)S(1)}, bf16[448,256]{1,0:T(8,128)(2,1)S(1)}, u32[]{:S(2)}, u32[]{:S(2)}) collective-permute-start(bf16[448,256]{1,0:T(8,128)(2,1)S(1)} %collective-permute-done.9), channel_id=1, source_target_pairs={{0,4},{1,5},{2,6},{3,7},{4,0},{5,1},{6,2},{7,3},{8,12},{9,13},{10,... | collective-permute-start | bytes 688136 | tf_op jit(solution)/shard_map/ppermute | solution.py:489
  71.0 10.7 %collective-permute-start.20 = (bf16[448,256]{1,0:T(8,128)(2,1)S(1)}, bf16[448,256]{1,0:T(8,128)(2,1)S(1)}, u32[]{:S(2)}, u32[]{:S(2)}) collective-permute-start(bf16[448,256]{1,0:T(8,128)(2,1)S(1)} %collective-permute-done.14), channel_id=1, source_target_pairs={{0,1},{4,5},{1,2},{5,6},{2,3},{6,7},{3,11},{7,15},{11,10},{15,14},... | collective-permute-start | bytes 688136 | tf_op jit(solution)/shard_map/ppermute | solution.py:608
  71.0 12.5 %collective-permute-start.24 = (bf16[448,256]{1,0:T(8,128)(2,1)S(1)}, bf16[448,256]{1,0:T(8,128)(2,1)S(1)}, u32[]{:S(2)}, u32[]{:S(2)}) collective-permute-start(bf16[448,256]{1,0:T(8,128)(2,1)S(1)} %collective-permute-done.10), channel_id=1, source_target_pairs={{0,4},{1,5},{2,6},{3,7},{4,0},{5,1},{6,2},{7,3},{8,12},{9,13},{10,... | collective-permute-start | bytes 688136 | tf_op jit(solution)/shard_map/ppermute | solution.py:489
  71.0 7.7 %collective-permute-start.16 = (bf16[160,256]{1,0:T(8,128)(2,1)S(1)}, bf16[160,256]{1,0:T(8,128)(2,1)S(1)}, u32[]{:S(2)}, u32[]{:S(2)}) collective-permute-start(bf16[160,256]{1,0:T(8,128)(2,1)S(1)} %get-tuple-element.78.mine), channel_id=1, source_target_pairs={{0,1},{1,0},{2,3},{3,2},{4,5},{5,4},{6,7},{7,6},{8,9},{9,8},{10,11... | collective-permute-start | bytes 245768 | tf_op jit(solution)/shard_map/ppermute | solution.py:489
  71.1 9.3 %collective-permute-start.17 = (bf16[160,256]{1,0:T(8,128)(2,1)S(1)}, bf16[160,256]{1,0:T(8,128)(2,1)S(1)}, u32[]{:S(2)}, u32[]{:S(2)}) collective-permute-start(bf16[160,256]{1,0:T(8,128)(2,1)S(1)} %get-tuple-element.80), channel_id=1, source_target_pairs={{0,2},{1,3},{2,0},{3,1},{4,6},{5,7},{6,4},{7,5},{8,10},{9,11},{10,... | collective-permute-start | bytes 245768 | tf_op jit(solution)/shard_map/ppermute | solution.py:489
  74.1 7.6 %collective-permute-start.18 = (bf16[160,256]{1,0:T(8,128)(2,1)S(1)}, bf16[160,256]{1,0:T(8,128)(2,1)S(1)}, u32[]{:S(2)}, u32[]{:S(2)}) collective-permute-start(bf16[160,256]{1,0:T(8,128)(2,1)S(1)} %get-tuple-element.81), channel_id=1, source_target_pairs={{0,3},{1,2},{2,1},{3,0},{4,7},{5,6},{6,5},{7,4},{8,11},{9,10},{10,... | collective-permute-start | bytes 245768 | tf_op jit(solution)/shard_map/ppermute | solution.py:489
  78.7 4.7 %collective-permute-start.25 = (bf16[448,256]{1,0:T(8,128)(2,1)S(1)}, bf16[448,256]{1,0:T(8,128)(2,1)S(1)}, u32[]{:S(2)}, u32[]{:S(2)}) collective-permute-start(bf16[448,256]{1,0:T(8,128)(2,1)S(1)} %collective-permute-done.11), channel_id=1, source_target_pairs={{0,4},{1,5},{2,6},{3,7},{4,0},{5,1},{6,2},{7,3},{8,12},{9,13},{10,... | collective-permute-start | bytes 688136 | tf_op jit(solution)/shard_map/ppermute | solution.py:489
  80.4 4.4 %collective-permute-start.26 = (bf16[448,256]{1,0:T(8,128)(2,1)S(1)}, bf16[448,256]{1,0:T(8,128)(2,1)S(1)}, u32[]{:S(2)}, u32[]{:S(2)}) collective-permute-start(bf16[448,256]{1,0:T(8,128)(2,1)S(1)} %collective-permute-done.14), channel_id=1, source_target_pairs={{0,4},{1,5},{2,6},{3,7},{4,0},{5,1},{6,2},{7,3},{8,12},{9,13},{10,... | collective-permute-start | bytes 688136 | tf_op jit(solution)/shard_map/ppermute | solution.py:489
  81.7 3.1 %collective-permute-start.27 = (bf16[448,256]{1,0:T(8,128)(2,1)S(1)}, bf16[448,256]{1,0:T(8,128)(2,1)S(1)}, u32[]{:S(2)}, u32[]{:S(2)}) collective-permute-start(bf16[448,256]{1,0:T(8,128)(2,1)S(1)} %collective-permute-done.15), channel_id=1, source_target_pairs={{0,4},{1,5},{2,6},{3,7},{4,0},{5,1},{6,2},{7,3},{8,12},{9,13},{10,... | collective-permute-start | bytes 688136 | tf_op jit(solution)/shard_map/ppermute | solution.py:489
  81.7 3.1 %collective-permute-start.28 = (bf16[448,256]{1,0:T(8,128)(2,1)S(1)}, bf16[448,256]{1,0:T(8,128)(2,1)S(1)}, u32[]{:S(2)}, u32[]{:S(2)}) collective-permute-start(bf16[448,256]{1,0:T(8,128)(2,1)S(1)} %collective-permute-done.20), channel_id=1, source_target_pairs={{0,4},{1,5},{2,6},{3,7},{4,0},{5,1},{6,2},{7,3},{8,12},{9,13},{10,... | collective-permute-start | bytes 688136 | tf_op jit(solution)/shard_map/ppermute | solution.py:489
  83.5 1.3 %collective-permute-start.19 = (f32[128,256]{1,0:T(8,128)S(1)}, f32[128,256]{1,0:T(8,128)S(1)}, u32[]{:S(2)}, u32[]{:S(2)}) collective-permute-start(f32[128,256]{1,0:T(8,128)S(1)} %get-tuple-element.84.own), channel_id=1, source_target_pairs={{0,4},{1,5},{2,6},{3,7},{4,0},{5,1},{6,2},{7,3},{8,12},{9,13},{10,... | collective-permute-start | bytes 393224 | tf_op jit(solution)/shard_map/ppermute | solution.py:489

commit v6 on v5

--- a/solution.py
+++ b/solution.py
@@ -121,18 +121,7 @@
     return ((at == k) & (t < 27)).astype(F32).astype(BF16)
 
 
-def weight_kernel(me, in_hbm, mid_hbm, out_hbm, packed, w_back, w_in, w_mid, w_out, sems):
-    parts = 9
-    share = w_mid.shape[0] // parts
-    copies = []
-    for i in range(parts):
-        at = slice(i * share, (i + 1) * share)
-        copies.append(pltpu.make_async_copy(mid_hbm.at[at], w_mid.at[at], sems.at[i]))
-    small = [pltpu.make_async_copy(in_hbm, w_in, sems.at[parts]), pltpu.make_async_copy(out_hbm, w_out, sems.at[parts + 1])]
-    for copy in small + copies:
-        copy.start()
-    for copy in small:
-        copy.wait()
+def weight_kernel(me, w_in, w_mid, w_out, packed, w_back):
     hid, rows = w_back.shape
     block = rows // 27
     row = lax.broadcasted_iota(jnp.int32, (block, hid), 0)
@@ -145,10 +134,8 @@
     wide = jnp.concatenate([wide, jnp.zeros((16 - wide.shape[0], hid), F32)], 0).astype(BF16)
     both = jnp.concatenate([dot_nt(chosen, wide), dot_nt(wide, chosen)], 0)
     packed[rows + hid :] = jnp.concatenate([both, jnp.zeros((32, hid - 16), F32)], 1).astype(BF16)
-    for i, copy in enumerate(copies):
-        copy.wait()
-        for t in range(i * share, (i + 1) * share):
-            packed[t * block : (t + 1) * block] = dot_nt(chosen, w_mid[t]).astype(BF16)
+    for t in range(27):
+        packed[t * block : (t + 1) * block] = dot_nt(chosen, w_mid[t]).astype(BF16)
     w_back[...] = packed[0:rows].astype(F32).T.astype(BF16)
 
 
@@ -358,12 +345,10 @@
     step_fields(nz, place, own, closure[...], refs[:-1], refs[-1])
 
 
-def total_kernel(nz, place, own, mine, kept, one, two, three, *refs):
-    sources, (half, out) = refs[:-2], refs[-2:]
+def total_kernel(mine, kept, one, two, three, half, closure):
     pair = mine[0:128].astype(F32) + one[0:128].astype(F32)
     half[...] = pair + (two[0:128].astype(F32) + three[0:128].astype(F32))
-    closure = kept[...] + (one[128:].astype(F32) + two[128:].astype(F32) + three[128:].astype(F32))
-    step_fields(nz, place, own, closure, sources, out)
+    closure[...] = kept[...] + (one[128:].astype(F32) + two[128:].astype(F32) + three[128:].astype(F32))
 
 
 def step_fields(nz, place, own, closure, sources, out):
@@ -511,21 +496,16 @@
     )(stay, from_below, from_above)
 
     rows = 27 * block
+    own_feats, late_me, late_in, late_mid, late_out = lax.optimization_barrier((own_feats, me, w_in, w_mid, w_out))
     packed, w_back = pl.pallas_call(
         weight_kernel,
         out_shape=(shape((rows + hid + 32, hid), BF16), shape((hid, rows), BF16)),
-        in_specs=[SMEM] + [HBM] * 3,
+        in_specs=[SMEM] + [VMEM] * 3,
         out_specs=(VMEM,) * 2,
-        scratch_shapes=[
-            pltpu.VMEM((9, 27, hid), BF16),
-            pltpu.VMEM(w_mid.shape, BF16),
-            pltpu.VMEM((cout, hid), BF16),
-            pltpu.SemaphoreType.DMA((11,)),
-        ],
-        compiler_params=params(60),
+        compiler_params=params(16),
         cost_estimate=cost(1.5e9),
         name="weights",
-    )(me[None], jnp.transpose(w_in, (1, 0, 2)), w_mid, w_out.T)
+    )(late_me[None], jnp.transpose(late_in, (1, 0, 2)), late_mid, late_out.T)
 
     if fast:
         far, middle, close = (trade(own_feats, mask) for mask in (3, 2, 1))
@@ -534,15 +514,17 @@
         mine = jnp.stack([own_feats] + near_z)
         across = trade(mine, 8)
         sources = [mine, across, trade(mine, 4), trade(across, 4)]
-        slabs = jnp.arange(n_slab, dtype=jnp.int32)
-        group = 2 * ((slabs ^ slab) & 1) + (((slabs ^ slab) >> 1) & 1)
-        place = group * samples
+
+        def held_at(slabs):
+            return 2 * ((slabs ^ slab) & 1) + (((slabs ^ slab) >> 1) & 1)
     else:
         sources = [lax.all_gather(own_feats, team)]
-        group = jnp.arange(n_slab, dtype=jnp.int32)
-        place = group * samples
-
-    near = jnp.take(group, jnp.stack([(slab + n_slab - 1) % n_slab, (slab + 1) % n_slab]))
+
+        def held_at(slabs):
+            return slabs
+
+    place = held_at(jnp.arange(n_slab, dtype=jnp.int32)) * samples
+    near = held_at((slab + jnp.array([n_slab - 1, 1], jnp.int32)) % n_slab)
 
     team_cells = all_planes * lanes
     piece, closure, g2z, fcol = pl.pallas_call(
@@ -641,7 +623,7 @@
             compiler_params=params(4),
             name="merge",
         )(y[None], got, keep, kept)
-        got, f3, b3 = tie(trade(message, 8), f3, b3)
+        got = trade(message, 8)
         f4 = around(f3, 1)
         kept, *messages = pl.pallas_call(
             fan_kernel,
@@ -652,15 +634,16 @@
             name="fan",
         )(got, message, kept)
         got = [trade(message, mask) for mask, message in zip((1, 2, 3), messages)]
-        own, new_fields = pl.pallas_call(
-            functools.partial(total_kernel, nz),
-            out_shape=(shape((128, hid), F32), shape(fields.shape, F32)),
-            in_specs=[SMEM] + [VMEM] * (6 + len(sources)),
+        own, own_closure = pl.pallas_call(
+            total_kernel,
+            out_shape=(shape((128, hid), F32), shape((32, hid), F32)),
+            in_specs=[VMEM] * 5,
             out_specs=(VMEM,) * 2,
-            compiler_params=params(6),
+            compiler_params=params(4),
             name="total",
-        )(near, own_state, messages[0], kept, *got, *sources)
+        )(messages[0], kept, *got)
         other = trade(own, 4)
+        halo = sources
         pieces = [piece, f1, b1, f2, b2, f3, b3, f4]
         pieces = [v[None] for v in pieces + [trade(v, 4) for v in pieces]]
     else:
@@ -681,14 +664,15 @@
         part = closure.reshape(samples, n_slab, planes * 16, lanes // 2)
         part = jnp.swapaxes(part, 0, 1).reshape(size, planes * 16, lanes // 2).astype(F32)
         own_closure = lax.psum_scatter(part, team, scatter_dimension=0)
-        new_fields = pl.pallas_call(
-            functools.partial(step_kernel, nz),
-            out_shape=shape(fields.shape, F32),
-            in_specs=[SMEM] + [VMEM] * 3,
-            out_specs=VMEM,
-            compiler_params=params(6),
-            name="step",
-        )(near, own_state, own_closure, sources[0].reshape(n_slab, samples, 16, cells)[:, sample])
+        halo = [sources[0].reshape(n_slab, samples, 16, cells)[:, sample]]
+    new_fields = pl.pallas_call(
+        functools.partial(step_kernel, nz),
+        out_shape=shape(fields.shape, F32),
+        in_specs=[SMEM] + [VMEM] * (2 + len(halo)),
+        out_specs=VMEM,
+        compiler_params=params(6),
+        name="step",
+    )(near, own_state, own_closure, *halo)
 
     weight_count = w_in.size + w_mid.size + w_out.size
     grad_middle, grad_first, grad_last = pl.pallas_call(

time: 91.5 us -> 87.8 us (0.960); the launches traced: 90.2 us -> 87.5 us
  Pallas kernels: 40.2 us -> 37.2 us
  waiting for transfers between devices: 23.9 us -> 21.4 us
  local copies, waits for them, and re-layouts: 2.46 us -> 4.44 us
    ppermute x20, waiting for transfers between devices: 19.6 us -> 14.4 us  [trade(): return lax.ppermute(v, team, [(d, d ^ mask) for d in range(size)])]
    pallas_call x1, Pallas kernels: 4.45 us -> 1.25 us  [shards(): pl.pallas_call(weight_kernel, out_shape=(shape((rows + hid + 32, hid), BF...]
    unnamed x6 -> x8, local copies, waits for them, and re-layouts: 1.82 us -> 4.44 us
    ppermute x1, waiting for transfers between devices: 0.01 us -> 1.57 us  [shards(): lax.ppermute(up, 'slab', [(i, (i + 1) % n_slab) for i in range(n_slab)])]
    ppermute x7, waiting for transfers between devices: 4.23 us -> 5.35 us  [around(): lax.ppermute(v, team, [(device(at, c), device(at + by, c)) for at in rang...]
  transfers between devices with their start and end apart: 29 -> 29, of which waited for: 10 -> 11; matrix products, arithmetic and copies ran while one was open for 1% -> 1% of each run, Pallas kernels for 20% -> 17%
where the time goes in v6:
time: 87.8 us; the launch traced here: 87.5 us
  Pallas kernels  37.2 us (42%)
  starting transfers between devices  22.8 us (26%)
  waiting for transfers between devices  21.4 us (24%)
  local copies, waits for them, and re-layouts  4.44 us (5%)
    ppermute x20, waiting for transfers between devices, trade(): return lax.ppermute(v, team, [(d, d ^ mask) for d in range(size)])  14.4 us
    pallas_call x1, Pallas kernels, shards(): pl.pallas_call(functools.partial(closure_kernel, nz, lanes, len(sources))...  14.2 us
    ppermute x20, starting transfers between devices, trade(): return lax.ppermute(v, team, [(d, d ^ mask) for d in range(size)])  13.4 us
    pallas_call x2, Pallas kernels, first_part(): pl.pallas_call(functools.partial(first_kernel, nz, lanes), grid=(count,),...  12.2 us
    ppermute x7, starting transfers between devices, around(): lax.ppermute(v, team, [(device(at, c), device(at + by, c)) for at in rang...  6.9 us
    ppermute x7, waiting for transfers between devices, around(): lax.ppermute(v, team, [(device(at, c), device(at + by, c)) for at in rang...  5.35 us
    pallas_call x1, Pallas kernels, shards(): pl.pallas_call(functools.partial(finish_kernel, len(pieces), weight_count...  5.19 us
    unnamed x8, local copies, waits for them, and re-layouts  4.44 us
  transfers between devices with their start and end apart: 29, of which 11 were waited for; matrix products, arithmetic and copies ran while one was open for 1% of the time, Pallas kernels for 17%

profile of v6, /device:TPU:0, one launch (start us, length us, event | category | flops | bytes accessed | tf_op | source)
XLA Modules:
  0.0 87.5 jit_solution(2444366971222836689)
XLA Ops:
  0.6 3.0 %deposit.1 = (f32[16,1024]{1,0:T(8,128)}, f32[4,1024]{1,0:T(4,128)}, f32[4,1024]{1,0:T(4,128)}) custom-call(f32[1,1024]{1,0:T(1,128)} %mass_in.1, f32[3,1,1024]{2,1,0:T(1,128)} %bitcast.50, s32[1,1024]{1,0:T(1,128)} %cell_in.1, s32[1,256]{1,0:T(1,128)} %listed_in.1, f32[1,5,2,4,128]{4,3,2,1,0:T(4,128)} %fields_in.1, f32[1,5,2,4,128]{4,3,2,1,0:T(4,128)} %cotangent_in.1, ...), custom_call_target="tpu_custom_call" | custom-call | tf_op jit(solution)/shard_map/deposit/pallas_call | solution.py:478
  3.7 0.5 collective-permute-start
  4.2 2.0 %collective-permute-start.1 = (f32[4,1024]{1,0:T(4,128)}, f32[4,1024]{1,0:T(4,128)S(1)}, u32[]{:S(2)}, u32[]{:S(2)}) collective-permute-start(f32[4,1024]{1,0:T(4,128)} %get-tuple-element.51), channel_id=1, source_target_pairs={{4,0},{8,4},{12,8},{0,12},{5,1},{9,5},{13,9},{1,13},{6,2},{10,6},{... | collective-permute-start | bytes 49160 | tf_op jit(solution)/shard_map/ppermute | solution.py:488
  6.2 1.6 %collective-permute-done.below = f32[4,1024]{1,0:T(4,128)S(1)} collective-permute-done((f32[4,1024]{1,0:T(4,128)}, f32[4,1024]{1,0:T(4,128)S(1)}, u32[]{:S(2)}, u32[]{:S(2)}) %collective-permute-start) | collective-permute-done | bytes 16416 | tf_op jit(solution)/shard_map/ppermute | solution.py:487
  7.8 0.1 collective-permute-done.1.above
  7.8 0.8 copy-done
  8.7 2.4 %collective-permute-start.2 = (bf16[16,1024]{1,0:T(8,128)(2,1)S(1)}, bf16[16,1024]{1,0:T(8,128)(2,1)S(1)}, u32[]{:S(2)}, u32[]{:S(2)}) collective-permute-start(bf16[16,1024]{1,0:T(8,128)(2,1)S(1)} %get-tuple-element.59), channel_id=1, source_target_pairs={{0,1},{1,0},{2,3},{3,2},{4,5},{5,4},{6,7},{7,6},{8,9},{9,8},{10,11... | collective-permute-start | bytes 98312 | tf_op jit(solution)/shard_map/ppermute | solution.py:474
  11.1 2.6 %collective-permute-start.3 = (bf16[16,1024]{1,0:T(8,128)(2,1)S(1)}, bf16[16,1024]{1,0:T(8,128)(2,1)S(1)}, u32[]{:S(2)}, u32[]{:S(2)}) collective-permute-start(bf16[16,1024]{1,0:T(8,128)(2,1)S(1)} %get-tuple-element.59), channel_id=1, source_target_pairs={{0,2},{1,3},{2,0},{3,1},{4,6},{5,7},{6,4},{7,5},{8,10},{9,11},{10,... | collective-permute-start | bytes 98312 | tf_op jit(solution)/shard_map/ppermute | solution.py:474
  13.7 0.0 collective-permute-start.4
  13.7 2.0 %copy-done.1 = bf16[27,256,256]{2,1,0:T(8,128)(2,1)S(1)} copy-done((bf16[27,256,256]{2,1,0:T(8,128)(2,1)S(1)}, bf16[27,256,256]{2,1,0:T(8,128)(2,1)}, u32[]{:S(2)}) %copy-start.1) | copy-done | bytes 3538968
  15.7 0.9 %copy-done.2 = bf16[27,9,256]{2,0,1:T(8,128)(2,1)S(1)} copy-done((bf16[27,9,256]{2,0,1:T(8,128)(2,1)S(1)}, bf16[27,9,256]{2,0,1:T(8,128)(2,1)}, u32[]{:S(2)}) %copy-start.2) | copy-done | bytes 124440
  16.6 0.7 copy-done.3
  17.3 1.2 %weights.1 = (bf16[720,256]{1,0:T(8,128)(2,1)S(1)}, bf16[256,432]{1,0:T(8,128)(2,1)S(1)}) custom-call(s32[1]{0:T(128)} %bitcast.1.me, bf16[9,27,256]{2,1,0:T(8,128)(2,1)S(1)} %bitcast.45, bf16[27,256,256]{2,1,0:T(8,128)(2,1)S(1)} %copy-done.1, bf16[5,256]{1,0:T(8,128)(2,1)S(1)} %bitcast.46), custom_call_target="tpu_custom_call" | custom-call | flops 1500000000 | bytes 4194304 | tf_op jit(solution)/shard_map/weights/pallas_call | solution.py:500
  18.5 0.0 collective-permute-done.2
  18.5 0.0 collective-permute-done.3
  18.5 1.1 %collective-permute-done.4 = bf16[16,1024]{1,0:T(8,128)(2,1)S(1)} collective-permute-done((bf16[16,1024]{1,0:T(8,128)(2,1)S(1)}, bf16[16,1024]{1,0:T(8,128)(2,1)S(1)}, u32[]{:S(2)}, u32[]{:S(2)}) %collective-permute-start.4) | collective-permute-done | bytes 32800 | tf_op jit(solution)/shard_map/ppermute | solution.py:474
  19.7 1.3 %collective-permute-start.5 = (bf16[4,16,1024]{2,1,0:T(8,128)(2,1)S(1)}, bf16[4,16,1024]{2,1,0:T(8,128)(2,1)S(1)}, u32[]{:S(2)}, u32[]{:S(2)}) collective-permute-start(bf16[4,16,1024]{2,1,0:T(8,128)(2,1)S(1)} %pad_maximum_fusion.refs_0_), channel_id=1, source_target_pairs={{0,8},{1,9},{2,10},{3,11},{4,12},{5,13},{6,14},{7,15},{8,0},{9,1},... | collective-permute-start | bytes 393224 | tf_op jit(solution)/shard_map/ppermute | solution.py:474
  21.0 0.7 and_add_fusion.place
  21.7 0.0 collective-permute-start.6
  21.7 3.6 %collective-permute-done.5.refs_1_ = bf16[4,16,1024]{2,1,0:T(8,128)(2,1)S(1)} collective-permute-done((bf16[4,16,1024]{2,1,0:T(8,128)(2,1)S(1)}, bf16[4,16,1024]{2,1,0:T(8,128)(2,1)S(1)}, u32[]{:S(2)}, u32[]{:S(2)}) %collective-permute-start.5) | collective-permute-done | bytes 131104 | tf_op jit(solution)/shard_map/ppermute | solution.py:474
  25.3 0.0 collective-permute-start.7
  25.3 1.3 %collective-permute-done.7.refs_3_ = bf16[4,16,1024]{2,1,0:T(8,128)(2,1)S(1)} collective-permute-done((bf16[4,16,1024]{2,1,0:T(8,128)(2,1)S(1)}, bf16[4,16,1024]{2,1,0:T(8,128)(2,1)S(1)}, u32[]{:S(2)}, u32[]{:S(2)}) %collective-permute-start.7) | collective-permute-done | bytes 131104 | tf_op jit(solution)/shard_map/ppermute | solution.py:474
  26.6 14.2 %closure.1 = (bf16[448,256]{1,0:T(8,128)(2,1)S(1)}, bf16[4,8,16,256]{3,2,1,0:T(8,128)(2,1)S(1)}, bf16[4,3,16,4096]{3,2,1,0:T(8,128)(2,1)S(1)}, bf16[4,256,4096]{2,1,0:T(8,128)(2,1)S(1)}) custom-call(s32[4]{0:T(128)S(1)} %add_multiply_fusion.place, bf16[720,256]{1,0:T(8,128)(2,1)S(1)} %get-tuple-element.60.packed, ...), custom_call_target="tpu_custom_call" | custom-call | flops 8999999488 | bytes 4194304 | tf_op jit(solution)/shard_map/closure/pallas_call | solution.py:530
  40.8 0.5 collective-permute-start.8
  41.3 1.6 %collective-permute-start.9 = (bf16[448,256]{1,0:T(8,128)(2,1)S(1)}, bf16[448,256]{1,0:T(8,128)(2,1)S(1)}, u32[]{:S(2)}, u32[]{:S(2)}) collective-permute-start(bf16[448,256]{1,0:T(8,128)(2,1)S(1)} %get-tuple-element.64), channel_id=1, source_target_pairs={{0,8},{4,12},{1,0},{5,4},{2,1},{6,5},{3,2},{7,6},{11,3},{15,7},{10... | collective-permute-start | bytes 688136 | tf_op jit(solution)/shard_map/ppermute | solution.py:590
  42.9 6.1 %first.2.one = f32[256,256]{1,0:T(8,128)S(1)} custom-call(bf16[720,256]{1,0:T(8,128)(2,1)S(1)} %get-tuple-element.60.packed, bf16[256,432]{1,0:T(8,128)(2,1)S(1)} %get-tuple-element.65.w_back, bf16[4,256,4096]{2,1,0:T(8,128)(2,1)S(1)} %get-tuple-element.73.fcol, bf16[4,3,16,4096]{3,2,1,0:T(8,128)(2,1)S(1)} %get-tuple-element.74.g2z), custom_call_target="tpu_custom_call" | custom-call | flops 3800000000 | bytes 4194304 | tf_op jit(solution)/shard_map/first/pallas_call | solution.py:562
  49.0 2.0 %collective-permute-start.10 = (bf16[448,256]{1,0:T(8,128)(2,1)S(1)}, bf16[448,256]{1,0:T(8,128)(2,1)S(1)}, u32[]{:S(2)}, u32[]{:S(2)}) collective-permute-start(bf16[448,256]{1,0:T(8,128)(2,1)S(1)} %collective-permute-done.8), channel_id=1, source_target_pairs={{0,1},{4,5},{1,2},{5,6},{2,3},{6,7},{3,11},{7,15},{11,10},{15,14},... | collective-permute-start | bytes 688136 | tf_op jit(solution)/shard_map/ppermute | solution.py:590
  51.0 0.1 collective-permute-start.11
  51.0 6.1 %first.3.two = f32[256,256]{1,0:T(8,128)S(1)} custom-call(bf16[720,256]{1,0:T(8,128)(2,1)S(1)} %get-tuple-element.60.packed, bf16[256,432]{1,0:T(8,128)(2,1)S(1)} %get-tuple-element.65.w_back, bf16[4,256,4096]{2,1,0:T(8,128)(2,1)S(1)} %get-tuple-element.73.fcol, bf16[4,3,16,4096]{3,2,1,0:T(8,128)(2,1)S(1)} %get-tuple-element.74.g2z), custom_call_target="tpu_custom_call" | custom-call | flops 3800000000 | bytes 4194304 | tf_op jit(solution)/shard_map/first/pallas_call | solution.py:562
  57.1 0.0 collective-permute-done.10
  57.1 0.4 collective-permute-done.11
  57.5 0.1 split.1
  57.6 0.1 collective-permute-start.12
  57.7 0.5 collective-permute-start.21
  58.2 1.6 %collective-permute-start.18 = (bf16[448,256]{1,0:T(8,128)(2,1)S(1)}, bf16[448,256]{1,0:T(8,128)(2,1)S(1)}, u32[]{:S(2)}, u32[]{:S(2)}) collective-permute-start(bf16[448,256]{1,0:T(8,128)(2,1)S(1)} %collective-permute-done.10), channel_id=1, source_target_pairs={{0,1},{4,5},{1,2},{5,6},{2,3},{6,7},{3,11},{7,15},{11,10},{15,14},... | collective-permute-start | bytes 688136 | tf_op jit(solution)/shard_map/ppermute | solution.py:590
  59.8 0.0 collective-permute-start.22
  59.8 0.5 collective-permute-start.23
  60.3 0.0 collective-permute-done.12.got
  60.3 0.4 collective-permute-start.19
  60.7 0.1 merge.1
  60.8 0.0 collective-permute-done.21
  60.8 0.9 %collective-permute-start.13 = (bf16[256,256]{1,0:T(8,128)(2,1)S(1)}, bf16[256,256]{1,0:T(8,128)(2,1)S(1)}, u32[]{:S(2)}, u32[]{:S(2)}) collective-permute-start(bf16[256,256]{1,0:T(8,128)(2,1)S(1)} %get-tuple-element.80.mine), channel_id=1, source_target_pairs={{0,8},{1,9},{2,10},{3,11},{4,12},{5,13},{6,14},{7,15},{8,0},{9,1},... | collective-permute-start | bytes 393224 | tf_op jit(solution)/shard_map/ppermute | solution.py:474
  61.7 4.9 %collective-permute-done.18 = bf16[448,256]{1,0:T(8,128)(2,1)S(1)} collective-permute-done((bf16[448,256]{1,0:T(8,128)(2,1)S(1)}, bf16[448,256]{1,0:T(8,128)(2,1)S(1)}, u32[]{:S(2)}, u32[]{:S(2)}) %collective-permute-start.18) | collective-permute-done | bytes 229408 | tf_op jit(solution)/shard_map/ppermute | solution.py:590
  66.6 0.7 collective-permute-start.20
  67.4 2.1 %collective-permute-done.13.got = bf16[256,256]{1,0:T(8,128)(2,1)S(1)} collective-permute-done((bf16[256,256]{1,0:T(8,128)(2,1)S(1)}, bf16[256,256]{1,0:T(8,128)(2,1)S(1)}, u32[]{:S(2)}, u32[]{:S(2)}) %collective-permute-start.13) | collective-permute-done | bytes 131104 | tf_op jit(solution)/shard_map/ppermute | solution.py:474
  69.5 0.0 collective-permute-done.22
  69.5 0.1 collective-permute-start.14
  69.6 4.0 %collective-permute-start.15 = (bf16[160,256]{1,0:T(8,128)(2,1)S(1)}, bf16[160,256]{1,0:T(8,128)(2,1)S(1)}, u32[]{:S(2)}, u32[]{:S(2)}) collective-permute-start(bf16[160,256]{1,0:T(8,128)(2,1)S(1)} %get-tuple-element.84), channel_id=1, source_target_pairs={{0,2},{1,3},{2,0},{3,1},{4,6},{5,7},{6,4},{7,5},{8,10},{9,11},{10,... | collective-permute-start | bytes 245768 | tf_op jit(solution)/shard_map/ppermute | solution.py:474
  73.5 0.0 collective-permute-done.19
  73.5 0.4 collective-permute-start.16
  74.0 0.0 collective-permute-done.20
  74.0 0.0 collective-permute-start.25
  74.0 0.5 collective-permute-done.14.one
  74.4 0.1 collective-permute-start.26
  74.5 5.8 %collective-permute-done.15.two = bf16[160,256]{1,0:T(8,128)(2,1)S(1)} collective-permute-done((bf16[160,256]{1,0:T(8,128)(2,1)S(1)}, bf16[160,256]{1,0:T(8,128)(2,1)S(1)}, u32[]{:S(2)}, u32[]{:S(2)}) %collective-permute-start.15) | collective-permute-done | bytes 81952 | tf_op jit(solution)/shard_map/ppermute | solution.py:474
  80.3 0.0 collective-permute-start.27
  80.3 0.5 collective-permute-start.28
  80.8 0.1 collective-permute-start.17
  80.9 1.3 %step.1 = f32[1,5,2,4,128]{4,3,2,1,0:T(4,128)} custom-call(s32[2]{0:T(128)S(1)} %and_add_fusion.place, f32[8,1024]{1,0:T(8,128)S(1)} %get-tuple-element.69.own, f32[32,256]{1,0:T(8,128)S(1)} %get-tuple-element.86.closure, bf16[4,16,1024]{2,1,0:T(8,128)(2,1)S(1)} %pad_maximum_fusion.refs_0_, bf16[4,16,1024]{2,1,0:T(8,128)(2,1)S(1)} %collective-permute-done.5.refs_1_, ...), custom_call_target="tpu_custom_call" | custom-call | tf_op jit(solution)/shard_map/step/pallas_call | solution.py:668
  82.2 0.0 collective-permute-done.25
  82.2 0.0 collective-permute-done.26
  82.2 0.0 collective-permute-done.27
  82.2 0.1 collective-permute-done.17.other
  82.3 5.2 %finish.1 = (f32[27,256,256]{2,1,0:T(8,128)}, f32[9,27,256]{2,1,0:T(8,128)}, f32[5,256]{1,0:T(8,128)}) custom-call(s32[16]{0:T(128)S(1)} %fusion.3.place, s32[1]{0:T(128)} %bitcast.9.core, f32[128,256]{1,0:T(8,128)S(1)} %get-tuple-element.88.own, f32[128,256]{1,0:T(8,128)S(1)} %collective-permute-done.17.other, bf16[1,448,256]{2,1,0:T(8,128)(2,1)S(1)} %bitcast.28, ...), custom_call_target="tpu_custom_call" | custom-call | tf_op jit(solution)/shard_map/finish/pallas_call | solution.py:678
  (18 shorter events, 0.2 us)
Async XLA Ops:
  3.7 4.1 %collective-permute-start = (f32[4,1024]{1,0:T(4,128)}, f32[4,1024]{1,0:T(4,128)S(1)}, u32[]{:S(2)}, u32[]{:S(2)}) collective-permute-start(f32[4,1024]{1,0:T(4,128)} %get-tuple-element.50), channel_id=1, source_target_pairs={{0,4},{4,8},{8,12},{12,0},{1,5},{5,9},{9,13},{13,1},{2,6},{6,10},{... | collective-permute-start | bytes 49160 | tf_op jit(solution)/shard_map/ppermute | solution.py:487
  4.2 3.7 %collective-permute-start.1 = (f32[4,1024]{1,0:T(4,128)}, f32[4,1024]{1,0:T(4,128)S(1)}, u32[]{:S(2)}, u32[]{:S(2)}) collective-permute-start(f32[4,1024]{1,0:T(4,128)} %get-tuple-element.51), channel_id=1, source_target_pairs={{4,0},{8,4},{12,8},{0,12},{5,1},{9,5},{13,9},{1,13},{6,2},{10,6},{... | collective-permute-start | bytes 49160 | tf_op jit(solution)/shard_map/ppermute | solution.py:488
  7.8 0.8 copy-start
  8.7 9.8 %collective-permute-start.2 = (bf16[16,1024]{1,0:T(8,128)(2,1)S(1)}, bf16[16,1024]{1,0:T(8,128)(2,1)S(1)}, u32[]{:S(2)}, u32[]{:S(2)}) collective-permute-start(bf16[16,1024]{1,0:T(8,128)(2,1)S(1)} %get-tuple-element.59), channel_id=1, source_target_pairs={{0,1},{1,0},{2,3},{3,2},{4,5},{5,4},{6,7},{7,6},{8,9},{9,8},{10,11... | collective-permute-start | bytes 98312 | tf_op jit(solution)/shard_map/ppermute | solution.py:474
  11.1 7.5 %collective-permute-start.3 = (bf16[16,1024]{1,0:T(8,128)(2,1)S(1)}, bf16[16,1024]{1,0:T(8,128)(2,1)S(1)}, u32[]{:S(2)}, u32[]{:S(2)}) collective-permute-start(bf16[16,1024]{1,0:T(8,128)(2,1)S(1)} %get-tuple-element.59), channel_id=1, source_target_pairs={{0,2},{1,3},{2,0},{3,1},{4,6},{5,7},{6,4},{7,5},{8,10},{9,11},{10,... | collective-permute-start | bytes 98312 | tf_op jit(solution)/shard_map/ppermute | solution.py:474
  13.7 6.0 %collective-permute-start.4 = (bf16[16,1024]{1,0:T(8,128)(2,1)S(1)}, bf16[16,1024]{1,0:T(8,128)(2,1)S(1)}, u32[]{:S(2)}, u32[]{:S(2)}) collective-permute-start(bf16[16,1024]{1,0:T(8,128)(2,1)S(1)} %get-tuple-element.59), channel_id=1, source_target_pairs={{0,3},{1,2},{2,1},{3,0},{4,7},{5,6},{6,5},{7,4},{8,11},{9,10},{10,... | collective-permute-start | bytes 98312 | tf_op jit(solution)/shard_map/ppermute | solution.py:474
  13.7 2.0 %copy-start.1 = (bf16[27,256,256]{2,1,0:T(8,128)(2,1)S(1)}, bf16[27,256,256]{2,1,0:T(8,128)(2,1)}, u32[]{:S(2)}) copy-start(bf16[27,256,256]{2,1,0:T(8,128)(2,1)} %w_mid) | copy-start | bytes 10616836
  15.7 0.9 %copy-start.2 = (bf16[27,9,256]{2,0,1:T(8,128)(2,1)S(1)}, bf16[27,9,256]{2,0,1:T(8,128)(2,1)}, u32[]{:S(2)}) copy-start(bf16[27,9,256]{2,0,1:T(8,128)(2,1)} %param.17) | copy-start | bytes 373252
  16.6 0.7 copy-start.3
  19.7 5.6 %collective-permute-start.5 = (bf16[4,16,1024]{2,1,0:T(8,128)(2,1)S(1)}, bf16[4,16,1024]{2,1,0:T(8,128)(2,1)S(1)}, u32[]{:S(2)}, u32[]{:S(2)}) collective-permute-start(bf16[4,16,1024]{2,1,0:T(8,128)(2,1)S(1)} %pad_maximum_fusion.refs_0_), channel_id=1, source_target_pairs={{0,8},{1,9},{2,10},{3,11},{4,12},{5,13},{6,14},{7,15},{8,0},{9,1},... | collective-permute-start | bytes 393224 | tf_op jit(solution)/shard_map/ppermute | solution.py:474
  21.7 3.6 %collective-permute-start.6 = (bf16[4,16,1024]{2,1,0:T(8,128)(2,1)S(1)}, bf16[4,16,1024]{2,1,0:T(8,128)(2,1)S(1)}, u32[]{:S(2)}, u32[]{:S(2)}) collective-permute-start(bf16[4,16,1024]{2,1,0:T(8,128)(2,1)S(1)} %pad_maximum_fusion.refs_0_), channel_id=1, source_target_pairs={{0,4},{1,5},{2,6},{3,7},{4,0},{5,1},{6,2},{7,3},{8,12},{9,13},{10,... | collective-permute-start | bytes 393224 | tf_op jit(solution)/shard_map/ppermute | solution.py:474
  25.3 1.3 %collective-permute-start.7 = (bf16[4,16,1024]{2,1,0:T(8,128)(2,1)S(1)}, bf16[4,16,1024]{2,1,0:T(8,128)(2,1)S(1)}, u32[]{:S(2)}, u32[]{:S(2)}) collective-permute-start(bf16[4,16,1024]{2,1,0:T(8,128)(2,1)S(1)} %collective-permute-done.5.refs_1_), channel_id=1, source_target_pairs={{0,4},{1,5},{2,6},{3,7},{4,0},{5,1},{6,2},{7,3},{8,12},{9,13},{10,... | collective-permute-start | bytes 393224 | tf_op jit(solution)/shard_map/ppermute | solution.py:474
  40.8 8.2 %collective-permute-start.8 = (bf16[448,256]{1,0:T(8,128)(2,1)S(1)}, bf16[448,256]{1,0:T(8,128)(2,1)S(1)}, u32[]{:S(2)}, u32[]{:S(2)}) collective-permute-start(bf16[448,256]{1,0:T(8,128)(2,1)S(1)} %get-tuple-element.64), channel_id=1, source_target_pairs={{0,1},{4,5},{1,2},{5,6},{2,3},{6,7},{3,11},{7,15},{11,10},{15,14},... | collective-permute-start | bytes 688136 | tf_op jit(solution)/shard_map/ppermute | solution.py:590
  41.3 7.7 %collective-permute-start.9 = (bf16[448,256]{1,0:T(8,128)(2,1)S(1)}, bf16[448,256]{1,0:T(8,128)(2,1)S(1)}, u32[]{:S(2)}, u32[]{:S(2)}) collective-permute-start(bf16[448,256]{1,0:T(8,128)(2,1)S(1)} %get-tuple-element.64), channel_id=1, source_target_pairs={{0,8},{4,12},{1,0},{5,4},{2,1},{6,5},{3,2},{7,6},{11,3},{15,7},{10... | collective-permute-start | bytes 688136 | tf_op jit(solution)/shard_map/ppermute | solution.py:590
  49.0 8.2 %collective-permute-start.10 = (bf16[448,256]{1,0:T(8,128)(2,1)S(1)}, bf16[448,256]{1,0:T(8,128)(2,1)S(1)}, u32[]{:S(2)}, u32[]{:S(2)}) collective-permute-start(bf16[448,256]{1,0:T(8,128)(2,1)S(1)} %collective-permute-done.8), channel_id=1, source_target_pairs={{0,1},{4,5},{1,2},{5,6},{2,3},{6,7},{3,11},{7,15},{11,10},{15,14},... | collective-permute-start | bytes 688136 | tf_op jit(solution)/shard_map/ppermute | solution.py:590
  51.0 6.5 %collective-permute-start.11 = (bf16[448,256]{1,0:T(8,128)(2,1)S(1)}, bf16[448,256]{1,0:T(8,128)(2,1)S(1)}, u32[]{:S(2)}, u32[]{:S(2)}) collective-permute-start(bf16[448,256]{1,0:T(8,128)(2,1)S(1)} %collective-permute-done.9), channel_id=1, source_target_pairs={{0,8},{4,12},{1,0},{5,4},{2,1},{6,5},{3,2},{7,6},{11,3},{15,7},{10... | collective-permute-start | bytes 688136 | tf_op jit(solution)/shard_map/ppermute | solution.py:590
  57.6 2.7 %collective-permute-start.12 = (f32[384,256]{1,0:T(8,128)S(1)}, f32[384,256]{1,0:T(8,128)S(1)}, u32[]{:S(2)}, u32[]{:S(2)}) collective-permute-start(f32[384,256]{1,0:T(8,128)S(1)} %get-tuple-element.77), channel_id=1, source_target_pairs={{0,4},{1,5},{2,6},{3,7},{4,0},{5,1},{6,2},{7,3},{8,12},{9,13},{10,... | collective-permute-start | bytes 1179656 | tf_op jit(solution)/shard_map/ppermute | solution.py:474
  57.7 3.1 %collective-permute-start.21 = (bf16[448,256]{1,0:T(8,128)(2,1)S(1)}, bf16[448,256]{1,0:T(8,128)(2,1)S(1)}, u32[]{:S(2)}, u32[]{:S(2)}) collective-permute-start(bf16[448,256]{1,0:T(8,128)(2,1)S(1)} %get-tuple-element.64), channel_id=1, source_target_pairs={{0,4},{1,5},{2,6},{3,7},{4,0},{5,1},{6,2},{7,3},{8,12},{9,13},{10,... | collective-permute-start | bytes 688136 | tf_op jit(solution)/shard_map/ppermute | solution.py:474
  58.2 8.5 %collective-permute-start.18 = (bf16[448,256]{1,0:T(8,128)(2,1)S(1)}, bf16[448,256]{1,0:T(8,128)(2,1)S(1)}, u32[]{:S(2)}, u32[]{:S(2)}) collective-permute-start(bf16[448,256]{1,0:T(8,128)(2,1)S(1)} %collective-permute-done.10), channel_id=1, source_target_pairs={{0,1},{4,5},{1,2},{5,6},{2,3},{6,7},{3,11},{7,15},{11,10},{15,14},... | collective-permute-start | bytes 688136 | tf_op jit(solution)/shard_map/ppermute | solution.py:590
  59.8 9.7 %collective-permute-start.22 = (bf16[448,256]{1,0:T(8,128)(2,1)S(1)}, bf16[448,256]{1,0:T(8,128)(2,1)S(1)}, u32[]{:S(2)}, u32[]{:S(2)}) collective-permute-start(bf16[448,256]{1,0:T(8,128)(2,1)S(1)} %collective-permute-done.8), channel_id=1, source_target_pairs={{0,4},{1,5},{2,6},{3,7},{4,0},{5,1},{6,2},{7,3},{8,12},{9,13},{10,... | collective-permute-start | bytes 688136 | tf_op jit(solution)/shard_map/ppermute | solution.py:474
  59.8 9.8 %collective-permute-start.23 = (bf16[448,256]{1,0:T(8,128)(2,1)S(1)}, bf16[448,256]{1,0:T(8,128)(2,1)S(1)}, u32[]{:S(2)}, u32[]{:S(2)}) collective-permute-start(bf16[448,256]{1,0:T(8,128)(2,1)S(1)} %collective-permute-done.9), channel_id=1, source_target_pairs={{0,4},{1,5},{2,6},{3,7},{4,0},{5,1},{6,2},{7,3},{8,12},{9,13},{10,... | collective-permute-start | bytes 688136 | tf_op jit(solution)/shard_map/ppermute | solution.py:474
  60.3 13.3 %collective-permute-start.19 = (bf16[448,256]{1,0:T(8,128)(2,1)S(1)}, bf16[448,256]{1,0:T(8,128)(2,1)S(1)}, u32[]{:S(2)}, u32[]{:S(2)}) collective-permute-start(bf16[448,256]{1,0:T(8,128)(2,1)S(1)} %collective-permute-done.11), channel_id=1, source_target_pairs={{0,8},{4,12},{1,0},{5,4},{2,1},{6,5},{3,2},{7,6},{11,3},{15,7},{10... | collective-permute-start | bytes 688136 | tf_op jit(solution)/shard_map/ppermute | solution.py:590
  60.8 8.7 %collective-permute-start.13 = (bf16[256,256]{1,0:T(8,128)(2,1)S(1)}, bf16[256,256]{1,0:T(8,128)(2,1)S(1)}, u32[]{:S(2)}, u32[]{:S(2)}) collective-permute-start(bf16[256,256]{1,0:T(8,128)(2,1)S(1)} %get-tuple-element.80.mine), channel_id=1, source_target_pairs={{0,8},{1,9},{2,10},{3,11},{4,12},{5,13},{6,14},{7,15},{8,0},{9,1},... | collective-permute-start | bytes 393224 | tf_op jit(solution)/shard_map/ppermute | solution.py:474
  66.6 7.3 %collective-permute-start.20 = (bf16[448,256]{1,0:T(8,128)(2,1)S(1)}, bf16[448,256]{1,0:T(8,128)(2,1)S(1)}, u32[]{:S(2)}, u32[]{:S(2)}) collective-permute-start(bf16[448,256]{1,0:T(8,128)(2,1)S(1)} %collective-permute-done.18), channel_id=1, source_target_pairs={{0,1},{4,5},{1,2},{5,6},{2,3},{6,7},{3,11},{7,15},{11,10},{15,14},... | collective-permute-start | bytes 688136 | tf_op jit(solution)/shard_map/ppermute | solution.py:590
  69.4 11.4 %collective-permute-start.24 = (bf16[448,256]{1,0:T(8,128)(2,1)S(1)}, bf16[448,256]{1,0:T(8,128)(2,1)S(1)}, u32[]{:S(2)}, u32[]{:S(2)}) collective-permute-start(bf16[448,256]{1,0:T(8,128)(2,1)S(1)} %collective-permute-done.10), channel_id=1, source_target_pairs={{0,4},{1,5},{2,6},{3,7},{4,0},{5,1},{6,2},{7,3},{8,12},{9,13},{10,... | collective-permute-start | bytes 688136 | tf_op jit(solution)/shard_map/ppermute | solution.py:474
  69.5 4.9 %collective-permute-start.14 = (bf16[160,256]{1,0:T(8,128)(2,1)S(1)}, bf16[160,256]{1,0:T(8,128)(2,1)S(1)}, u32[]{:S(2)}, u32[]{:S(2)}) collective-permute-start(bf16[160,256]{1,0:T(8,128)(2,1)S(1)} %get-tuple-element.82.mine), channel_id=1, source_target_pairs={{0,1},{1,0},{2,3},{3,2},{4,5},{5,4},{6,7},{7,6},{8,9},{9,8},{10,11... | collective-permute-start | bytes 245768 | tf_op jit(solution)/shard_map/ppermute | solution.py:474
  69.6 10.7 %collective-permute-start.15 = (bf16[160,256]{1,0:T(8,128)(2,1)S(1)}, bf16[160,256]{1,0:T(8,128)(2,1)S(1)}, u32[]{:S(2)}, u32[]{:S(2)}) collective-permute-start(bf16[160,256]{1,0:T(8,128)(2,1)S(1)} %get-tuple-element.84), channel_id=1, source_target_pairs={{0,2},{1,3},{2,0},{3,1},{4,6},{5,7},{6,4},{7,5},{8,10},{9,11},{10,... | collective-permute-start | bytes 245768 | tf_op jit(solution)/shard_map/ppermute | solution.py:474
  73.5 6.7 %collective-permute-start.16 = (bf16[160,256]{1,0:T(8,128)(2,1)S(1)}, bf16[160,256]{1,0:T(8,128)(2,1)S(1)}, u32[]{:S(2)}, u32[]{:S(2)}) collective-permute-start(bf16[160,256]{1,0:T(8,128)(2,1)S(1)} %get-tuple-element.85), channel_id=1, source_target_pairs={{0,3},{1,2},{2,1},{3,0},{4,7},{5,6},{6,5},{7,4},{8,11},{9,10},{10,... | collective-permute-start | bytes 245768 | tf_op jit(solution)/shard_map/ppermute | solution.py:474
  74.0 8.2 %collective-permute-start.25 = (bf16[448,256]{1,0:T(8,128)(2,1)S(1)}, bf16[448,256]{1,0:T(8,128)(2,1)S(1)}, u32[]{:S(2)}, u32[]{:S(2)}) collective-permute-start(bf16[448,256]{1,0:T(8,128)(2,1)S(1)} %collective-permute-done.11), channel_id=1, source_target_pairs={{0,4},{1,5},{2,6},{3,7},{4,0},{5,1},{6,2},{7,3},{8,12},{9,13},{10,... | collective-permute-start | bytes 688136 | tf_op jit(solution)/shard_map/ppermute | solution.py:474
  74.4 7.8 %collective-permute-start.26 = (bf16[448,256]{1,0:T(8,128)(2,1)S(1)}, bf16[448,256]{1,0:T(8,128)(2,1)S(1)}, u32[]{:S(2)}, u32[]{:S(2)}) collective-permute-start(bf16[448,256]{1,0:T(8,128)(2,1)S(1)} %collective-permute-done.18), channel_id=1, source_target_pairs={{0,4},{1,5},{2,6},{3,7},{4,0},{5,1},{6,2},{7,3},{8,12},{9,13},{10,... | collective-permute-start | bytes 688136 | tf_op jit(solution)/shard_map/ppermute | solution.py:474
  80.3 1.9 %collective-permute-start.27 = (bf16[448,256]{1,0:T(8,128)(2,1)S(1)}, bf16[448,256]{1,0:T(8,128)(2,1)S(1)}, u32[]{:S(2)}, u32[]{:S(2)}) collective-permute-start(bf16[448,256]{1,0:T(8,128)(2,1)S(1)} %collective-permute-done.19), channel_id=1, source_target_pairs={{0,4},{1,5},{2,6},{3,7},{4,0},{5,1},{6,2},{7,3},{8,12},{9,13},{10,... | collective-permute-start | bytes 688136 | tf_op jit(solution)/shard_map/ppermute | solution.py:474
  80.3 1.9 %collective-permute-start.28 = (bf16[448,256]{1,0:T(8,128)(2,1)S(1)}, bf16[448,256]{1,0:T(8,128)(2,1)S(1)}, u32[]{:S(2)}, u32[]{:S(2)}) collective-permute-start(bf16[448,256]{1,0:T(8,128)(2,1)S(1)} %collective-permute-done.20), channel_id=1, source_target_pairs={{0,4},{1,5},{2,6},{3,7},{4,0},{5,1},{6,2},{7,3},{8,12},{9,13},{10,... | collective-permute-start | bytes 688136 | tf_op jit(solution)/shard_map/ppermute | solution.py:474
  80.8 1.4 %collective-permute-start.17 = (f32[128,256]{1,0:T(8,128)S(1)}, f32[128,256]{1,0:T(8,128)S(1)}, u32[]{:S(2)}, u32[]{:S(2)}) collective-permute-start(f32[128,256]{1,0:T(8,128)S(1)} %get-tuple-element.88.own), channel_id=1, source_target_pairs={{0,4},{1,5},{2,6},{3,7},{4,0},{5,1},{6,2},{7,3},{8,12},{9,13},{10,... | collective-permute-start | bytes 393224 | tf_op jit(solution)/shard_map/ppermute | solution.py:474

commit v7 on v6

--- a/solution.py
+++ b/solution.py
@@ -48,21 +48,15 @@
     return jnp.concatenate([ref[0, :, x, y, :] for x in range(planes) for y in range(rows)], 1)
 
 
-def fetch(pairs, sems):
-    copies = [pltpu.make_async_copy(src, dst, sems.at[i]) for i, (src, dst) in enumerate(pairs)]
+def deposit_kernel(mass_in, vel_in, cell_in, listed_in, fields_in, cotangent_in, counts, stay, up, down, *held):
+    *held, sems = held
+    sources = (mass_in, vel_in, cell_in, listed_in, fields_in, cotangent_in)
+    copies = [pltpu.make_async_copy(src, dst, sems.at[i]) for i, (src, dst) in enumerate(zip(sources, held))]
     for copy in copies:
         copy.start()
-    for copy in copies:
+    mass, vel, cell, listed, fields, cotangent = held
+    for copy in copies[:4]:
         copy.wait()
-
-
-def deposit_kernel(mass_in, vel_in, cell_in, listed_in, fields_in, cotangent_in, counts, stay, up, down, *held):
-    *held, sems = held
-    fetch(list(zip((mass_in, vel_in, cell_in, listed_in, fields_in, cotangent_in), held)), sems)
-    mass, vel, cell, listed, fields, cotangent = held
-    stay[4:9] = flat_cells(fields)
-    stay[9:14] = dt_step * flat_cells(cotangent)
-    stay[14:] = jnp.zeros((2, stay.shape[1]), F32)
     drops = mass.shape[1]
     slots = listed.shape[1]
     half = slots // 2
@@ -89,6 +83,15 @@
         got = dot_nt(rows, onehot)
         for i, out in enumerate((stay, up, down)):
             out[0:4, start : start + chunk] = got[8 * i : 8 * i + 4] + got[8 * i + 4 : 8 * i + 8]
+    for copy in copies[4:]:
+        copy.wait()
+    stay[4:9] = flat_cells(fields)
+    stay[9:14] = dt_step * flat_cells(cotangent)
+    stay[14:] = jnp.zeros((2, stay.shape[1]), F32)
+
+
+def hold_kernel(values, out):
+    out[...] = values[...]
 
 
 def feature_kernel(stay, below, above, feats, own):
@@ -121,22 +124,31 @@
     return ((at == k) & (t < 27)).astype(F32).astype(BF16)
 
 
-def weight_kernel(me, w_in, w_mid, w_out, packed, w_back):
-    hid, rows = w_back.shape
-    block = rows // 27
+def chosen_columns(me, block, hid):
     row = lax.broadcasted_iota(jnp.int32, (block, hid), 0)
     column = lax.broadcasted_iota(jnp.int32, (block, hid), 1)
-    chosen = (column == row + me[0] * block).astype(F32).astype(BF16)
+    return (column == row + me[0] * block).astype(F32).astype(BF16)
+
+
+def outer_weight_kernel(me, w_in, w_out, packed):
+    hid = packed.shape[1]
     pad = jnp.zeros((5, hid), F32)
     tall = jnp.concatenate([v for c in range(9) for v in (w_in[c].astype(F32), pad)], 0)
-    packed[rows : rows + hid] = (0.5 * dot(tall.T.astype(BF16), tap_rows())).astype(BF16)
+    packed[0:hid] = (0.5 * dot(tall.T.astype(BF16), tap_rows())).astype(BF16)
     wide = w_out[...].astype(F32)
     wide = jnp.concatenate([wide, jnp.zeros((16 - wide.shape[0], hid), F32)], 0).astype(BF16)
+    chosen = chosen_columns(me, 16, hid)
     both = jnp.concatenate([dot_nt(chosen, wide), dot_nt(wide, chosen)], 0)
-    packed[rows + hid :] = jnp.concatenate([both, jnp.zeros((32, hid - 16), F32)], 1).astype(BF16)
+    packed[hid:] = jnp.concatenate([both, jnp.zeros((32, hid - 16), F32)], 1).astype(BF16)
+
+
+def middle_weight_kernel(me, w_mid, wt, w_back):
+    rows, hid = wt.shape
+    block = rows // 27
+    chosen = chosen_columns(me, block, hid)
     for t in range(27):
-        packed[t * block : (t + 1) * block] = dot_nt(chosen, w_mid[t]).astype(BF16)
-    w_back[...] = packed[0:rows].astype(F32).T.astype(BF16)
+        wt[t * block : (t + 1) * block] = dot_nt(chosen, w_mid[t]).astype(BF16)
+    w_back[...] = wt[...].astype(F32).T.astype(BF16)
 
 
 def span(x, lanes, count=1):
@@ -150,7 +162,7 @@
     return jnp.concatenate(parts, 0)
 
 
-def closure_kernel(nz, lanes, sources, place, packed, *refs):
+def closure_kernel(nz, lanes, sources, place, wt, packed, *refs):
     arrived, refs = refs[:sources], refs[sources:]
     piece, closure, g2z, fcol, feats, fz, eighth, ninth, hidden, sums, mid, last = refs
     s = pl.program_id(0)
@@ -159,12 +171,12 @@
     cells = hidden.shape[1]
     planes = cells // lanes
     per = planes // slabs
-    rows, hid = mid.shape
     block = last.shape[1]
     group = 4
-    wt, w_first = packed.at[0:rows], packed.at[rows : rows + hid]
-    wo = packed[rows + hid : rows + hid + 16, 0:16]
-    wc = packed[rows + hid + 16 :, 0:16]
+    hid = mid.shape[1]
+    w_first = packed.at[0:hid]
+    wo = packed[hid : hid + 16, 0:16]
+    wc = packed[hid + 16 :, 0:16]
 
     @pl.when(s == 0)
     def _():
@@ -290,8 +302,7 @@
 
     planes = fcol.shape[2] // lanes
     group = 2
-    hid, rows = w_back.shape
-    w_first = packed.at[rows : rows + hid]
+    w_first = packed.at[0 : w_back.shape[0]]
     for x in range(0, planes, group):
         at = span(x, lanes, group)
         columns = [plane_taps(g2z, x + h, planes, nz, lanes) for h in range(group)]
@@ -484,6 +495,14 @@
         compiler_params=params(60),
         name="deposit",
     )(*flows, cross_count)
+    stay = pl.pallas_call(
+        hold_kernel,
+        out_shape=shape(stay.shape, F32),
+        in_specs=[VMEM],
+        out_specs=VMEM,
+        compiler_params=params(4),
+        name="hold",
+    )(stay)
     from_below = lax.ppermute(up, "slab", [(i, (i + 1) % n_slab) for i in range(n_slab)])
     from_above = lax.ppermute(down, "slab", [((i + 1) % n_slab, i) for i in range(n_slab)])
     own_feats, own_state = pl.pallas_call(
@@ -496,33 +515,45 @@
     )(stay, from_below, from_above)
 
     rows = 27 * block
-    own_feats, late_me, late_in, late_mid, late_out = lax.optimization_barrier((own_feats, me, w_in, w_mid, w_out))
-    packed, w_back = pl.pallas_call(
-        weight_kernel,
-        out_shape=(shape((rows + hid + 32, hid), BF16), shape((hid, rows), BF16)),
-        in_specs=[SMEM] + [VMEM] * 3,
-        out_specs=(VMEM,) * 2,
-        compiler_params=params(16),
-        cost_estimate=cost(1.5e9),
-        name="weights",
-    )(late_me[None], jnp.transpose(late_in, (1, 0, 2)), late_mid, late_out.T)
+    own_feats, late_me, late_in, late_out = lax.optimization_barrier((own_feats, me, w_in, w_out))
+    packed = pl.pallas_call(
+        outer_weight_kernel,
+        out_shape=shape((hid + 32, hid), BF16),
+        in_specs=[SMEM] + [VMEM] * 2,
+        out_specs=VMEM,
+        compiler_params=params(8),
+        name="outer_weights",
+    )(late_me[None], jnp.transpose(late_in, (1, 0, 2)), late_out.T)
 
     if fast:
         far, middle, close = (trade(own_feats, mask) for mask in (3, 2, 1))
         near_z = [close, middle, far]
-        packed, w_back, *near_z = lax.optimization_barrier((packed, w_back, *near_z))
+        packed, *near_z = lax.optimization_barrier((packed, *near_z))
         mine = jnp.stack([own_feats] + near_z)
+        mine, late_me, late_mid = lax.optimization_barrier((mine, me, w_mid))
         across = trade(mine, 8)
-        sources = [mine, across, trade(mine, 4), trade(across, 4)]
 
         def held_at(slabs):
             return 2 * ((slabs ^ slab) & 1) + (((slabs ^ slab) >> 1) & 1)
     else:
         sources = [lax.all_gather(own_feats, team)]
+        late_me, late_mid = me, w_mid
 
         def held_at(slabs):
             return slabs
 
+    wt, w_back = pl.pallas_call(
+        middle_weight_kernel,
+        out_shape=(shape((rows, hid), BF16), shape((hid, rows), BF16)),
+        in_specs=[SMEM, VMEM],
+        out_specs=(VMEM,) * 2,
+        compiler_params=params(16),
+        cost_estimate=cost(1.5e9),
+        name="middle_weights",
+    )(late_me[None], late_mid)
+    if fast:
+        across, wt, w_back = lax.optimization_barrier((across, wt, w_back))
+        sources = [mine, across, trade(mine, 4), trade(across, 4)]
     place = held_at(jnp.arange(n_slab, dtype=jnp.int32)) * samples
     near = held_at((slab + jnp.array([n_slab - 1, 1], jnp.int32)) % n_slab)
 
@@ -536,7 +567,7 @@
             shape((samples, 3, block, team_cells), BF16),
             shape((samples, 256, team_cells), BF16),
         ),
-        in_specs=[SMEM] + [VMEM] * (1 + len(sources)),
+        in_specs=[SMEM] + [VMEM] * (2 + len(sources)),
         out_specs=(
             whole_spec((rows + 16, hid)),
             pl.BlockSpec((1, all_planes, 16, lanes // 2), lambda s: (s, 0, 0, 0)),
@@ -556,7 +587,7 @@
         compiler_params=params(30 if all_planes <= 8 else 58),
         cost_estimate=cost(9e9),
         name="closure",
-    )(place, packed, *sources)
+    )(place, wt, packed, *sources)
 
     def first_part(lo, count, fcol, g2z):
         return pl.pallas_call(

time: 87.8 us -> 85.5 us (0.974)
  waiting for transfers between devices: 21.4 us -> 20.1 us
  starting transfers between devices: 22.8 us -> 21.8 us
    ppermute x7, starting transfers between devices: 6.9 us -> 5.54 us  [around(): lax.ppermute(v, team, [(device(at, c), device(at + by, c)) for at in rang...]
  transfers between devices with their start and end apart: 29 -> 29, of which waited for: 11 -> 12; matrix products, arithmetic and copies ran while one was open for 1% -> 1% of each run, Pallas kernels for 17% -> 18%
where the time goes in v7:
time: 85.5 us; the launch traced here: 85.2 us
  Pallas kernels  37.3 us (44%)
  starting transfers between devices  21.8 us (25%)
  waiting for transfers between devices  20.1 us (24%)
  local copies, waits for them, and re-layouts  4.44 us (5%)
  between operations  0.86 us (1%)
    ppermute x20, waiting for transfers between devices, trade(): return lax.ppermute(v, team, [(d, d ^ mask) for d in range(size)])  14.7 us
    pallas_call x1, Pallas kernels, shards(): pl.pallas_call(functools.partial(closure_kernel, nz, lanes, len(sources))...  14.1 us
    ppermute x20, starting transfers between devices, trade(): return lax.ppermute(v, team, [(d, d ^ mask) for d in range(size)])  13.7 us
    pallas_call x2, Pallas kernels, first_part(): pl.pallas_call(functools.partial(first_kernel, nz, lanes), grid=(count,),...  12.1 us
    ppermute x7, starting transfers between devices, around(): lax.ppermute(v, team, [(device(at, c), device(at + by, c)) for at in rang...  5.54 us
    pallas_call x1, Pallas kernels, shards(): pl.pallas_call(functools.partial(finish_kernel, len(pieces), weight_count...  5.19 us
    ppermute x7, waiting for transfers between devices, around(): lax.ppermute(v, team, [(device(at, c), device(at + by, c)) for at in rang...  4.55 us
    unnamed x8, local copies, waits for them, and re-layouts  4.44 us
  transfers between devices with their start and end apart: 29, of which 12 were waited for; matrix products, arithmetic and copies ran while one was open for 1% of the time, Pallas kernels for 18%

profile of v7, /device:TPU:0, one launch (start us, length us, event | category | flops | bytes accessed | tf_op | source)
XLA Modules:
  0.0 85.2 jit_solution(4756495725415034094)
XLA Ops:
  0.6 3.0 %deposit.1 = (f32[16,1024]{1,0:T(8,128)}, f32[4,1024]{1,0:T(4,128)}, f32[4,1024]{1,0:T(4,128)}) custom-call(f32[1,1024]{1,0:T(1,128)} %mass_in.1, f32[3,1,1024]{2,1,0:T(1,128)} %bitcast.51, s32[1,1024]{1,0:T(1,128)} %cell_in.1, s32[1,256]{1,0:T(1,128)} %listed_in.1, f32[1,5,2,4,128]{4,3,2,1,0:T(4,128)} %fields_in.1, f32[1,5,2,4,128]{4,3,2,1,0:T(4,128)} %cotangent_in.1, ...), custom_call_target="tpu_custom_call" | custom-call | tf_op jit(solution)/shard_map/deposit/pallas_call | solution.py:489
  3.6 0.5 collective-permute-start
  4.1 2.0 %collective-permute-start.1 = (f32[4,1024]{1,0:T(4,128)}, f32[4,1024]{1,0:T(4,128)S(1)}, u32[]{:S(2)}, u32[]{:S(2)}) collective-permute-start(f32[4,1024]{1,0:T(4,128)} %get-tuple-element.55), channel_id=1, source_target_pairs={{4,0},{8,4},{12,8},{0,12},{5,1},{9,5},{13,9},{1,13},{6,2},{10,6},{... | collective-permute-start | bytes 49160 | tf_op jit(solution)/shard_map/ppermute | solution.py:507
  6.2 0.8 copy-done.1
  7.0 0.7 collective-permute-done.below
  7.7 0.1 collective-permute-done.1.above
  7.8 2.4 %collective-permute-start.2 = (bf16[16,1024]{1,0:T(8,128)(2,1)S(1)}, bf16[16,1024]{1,0:T(8,128)(2,1)S(1)}, u32[]{:S(2)}, u32[]{:S(2)}) collective-permute-start(bf16[16,1024]{1,0:T(8,128)(2,1)S(1)} %get-tuple-element.57), channel_id=1, source_target_pairs={{0,1},{1,0},{2,3},{3,2},{4,5},{5,4},{6,7},{7,6},{8,9},{9,8},{10,11... | collective-permute-start | bytes 98312 | tf_op jit(solution)/shard_map/ppermute | solution.py:485
  10.2 2.6 %collective-permute-start.3 = (bf16[16,1024]{1,0:T(8,128)(2,1)S(1)}, bf16[16,1024]{1,0:T(8,128)(2,1)S(1)}, u32[]{:S(2)}, u32[]{:S(2)}) collective-permute-start(bf16[16,1024]{1,0:T(8,128)(2,1)S(1)} %get-tuple-element.57), channel_id=1, source_target_pairs={{0,2},{1,3},{2,0},{3,1},{4,6},{5,7},{6,4},{7,5},{8,10},{9,11},{10,... | collective-permute-start | bytes 98312 | tf_op jit(solution)/shard_map/ppermute | solution.py:485
  12.8 0.0 collective-permute-start.4
  12.8 0.7 and_add_fusion.place
  13.5 0.9 %copy-done = bf16[27,9,256]{2,0,1:T(8,128)(2,1)S(1)} copy-done((bf16[27,9,256]{2,0,1:T(8,128)(2,1)S(1)}, bf16[27,9,256]{2,0,1:T(8,128)(2,1)}, u32[]{:S(2)}) %copy-start) | copy-done | bytes 124440
  14.4 0.7 copy-done.2
  15.1 0.3 outer_weights.1.packed
  15.4 0.0 collective-permute-done.2
  15.4 0.5 collective-permute-done.3
  15.9 2.9 %collective-permute-done.4 = bf16[16,1024]{1,0:T(8,128)(2,1)S(1)} collective-permute-done((bf16[16,1024]{1,0:T(8,128)(2,1)S(1)}, bf16[16,1024]{1,0:T(8,128)(2,1)S(1)}, u32[]{:S(2)}, u32[]{:S(2)}) %collective-permute-start.4) | collective-permute-done | bytes 32800 | tf_op jit(solution)/shard_map/ppermute | solution.py:485
  18.8 1.3 %collective-permute-start.5 = (bf16[4,16,1024]{2,1,0:T(8,128)(2,1)S(1)}, bf16[4,16,1024]{2,1,0:T(8,128)(2,1)S(1)}, u32[]{:S(2)}, u32[]{:S(2)}) collective-permute-start(bf16[4,16,1024]{2,1,0:T(8,128)(2,1)S(1)} %pad_maximum_fusion.refs_0_), channel_id=1, source_target_pairs={{0,8},{1,9},{2,10},{3,11},{4,12},{5,13},{6,14},{7,15},{8,0},{9,1},... | collective-permute-start | bytes 393224 | tf_op jit(solution)/shard_map/ppermute | solution.py:485
  20.1 0.0 collective-permute-start.6
  20.1 2.0 %copy-done.3 = bf16[27,256,256]{2,1,0:T(8,128)(2,1)S(1)} copy-done((bf16[27,256,256]{2,1,0:T(8,128)(2,1)S(1)}, bf16[27,256,256]{2,1,0:T(8,128)(2,1)}, u32[]{:S(2)}) %copy-start.3) | copy-done | bytes 3538968
  22.1 1.2 %middle_weights.1 = (bf16[432,256]{1,0:T(8,128)(2,1)S(1)}, bf16[256,432]{1,0:T(8,128)(2,1)S(1)}) custom-call(s32[1]{0:T(128)} %bitcast.8.me, bf16[27,256,256]{2,1,0:T(8,128)(2,1)S(1)} %copy-done.3), custom_call_target="tpu_custom_call" | custom-call | flops 1500000000 | bytes 4194304 | tf_op jit(solution)/shard_map/middle_weights/pallas_call | solution.py:545
  23.3 1.1 %collective-permute-done.5.refs_1_ = bf16[4,16,1024]{2,1,0:T(8,128)(2,1)S(1)} collective-permute-done((bf16[4,16,1024]{2,1,0:T(8,128)(2,1)S(1)}, bf16[4,16,1024]{2,1,0:T(8,128)(2,1)S(1)}, u32[]{:S(2)}, u32[]{:S(2)}) %collective-permute-start.5) | collective-permute-done | bytes 131104 | tf_op jit(solution)/shard_map/ppermute | solution.py:485
  24.4 0.0 collective-permute-start.7
  24.4 0.0 collective-permute-done.6.refs_2_
  24.4 1.3 %collective-permute-done.7.refs_3_ = bf16[4,16,1024]{2,1,0:T(8,128)(2,1)S(1)} collective-permute-done((bf16[4,16,1024]{2,1,0:T(8,128)(2,1)S(1)}, bf16[4,16,1024]{2,1,0:T(8,128)(2,1)S(1)}, u32[]{:S(2)}, u32[]{:S(2)}) %collective-permute-start.7) | collective-permute-done | bytes 131104 | tf_op jit(solution)/shard_map/ppermute | solution.py:485
  25.7 14.1 %closure.1 = (bf16[448,256]{1,0:T(8,128)(2,1)S(1)}, bf16[4,8,16,256]{3,2,1,0:T(8,128)(2,1)S(1)}, bf16[4,3,16,4096]{3,2,1,0:T(8,128)(2,1)S(1)}, bf16[4,256,4096]{2,1,0:T(8,128)(2,1)S(1)}) custom-call(s32[4]{0:T(128)S(1)} %add_multiply_fusion.place, bf16[432,256]{1,0:T(8,128)(2,1)S(1)} %get-tuple-element.69.wt, bf16[288,256]{1,0:T(8,128)(2,1)S(1)} %outer_weights.1.packed, ...), custom_call_target="tpu_custom_call" | custom-call | flops 8999999488 | bytes 4194304 | tf_op jit(solution)/shard_map/closure/pallas_call | solution.py:561
  39.8 0.1 collective-permute-start.8
  39.9 2.0 %collective-permute-start.9 = (bf16[448,256]{1,0:T(8,128)(2,1)S(1)}, bf16[448,256]{1,0:T(8,128)(2,1)S(1)}, u32[]{:S(2)}, u32[]{:S(2)}) collective-permute-start(bf16[448,256]{1,0:T(8,128)(2,1)S(1)} %get-tuple-element.72), channel_id=1, source_target_pairs={{0,8},{4,12},{1,0},{5,4},{2,1},{6,5},{3,2},{7,6},{11,3},{15,7},{10... | collective-permute-start | bytes 688136 | tf_op jit(solution)/shard_map/ppermute | solution.py:621
  41.9 6.0 %first.2.one = f32[256,256]{1,0:T(8,128)S(1)} custom-call(bf16[288,256]{1,0:T(8,128)(2,1)S(1)} %outer_weights.1.packed, bf16[256,432]{1,0:T(8,128)(2,1)S(1)} %get-tuple-element.73.w_back, bf16[4,256,4096]{2,1,0:T(8,128)(2,1)S(1)} %get-tuple-element.81.fcol, bf16[4,3,16,4096]{3,2,1,0:T(8,128)(2,1)S(1)} %get-tuple-element.82.g2z), custom_call_target="tpu_custom_call" | custom-call | flops 3800000000 | bytes 4194304 | tf_op jit(solution)/shard_map/first/pallas_call | solution.py:593
  48.0 0.1 collective-permute-start.10
  48.1 2.0 %collective-permute-start.11 = (bf16[448,256]{1,0:T(8,128)(2,1)S(1)}, bf16[448,256]{1,0:T(8,128)(2,1)S(1)}, u32[]{:S(2)}, u32[]{:S(2)}) collective-permute-start(bf16[448,256]{1,0:T(8,128)(2,1)S(1)} %collective-permute-done.9), channel_id=1, source_target_pairs={{0,8},{4,12},{1,0},{5,4},{2,1},{6,5},{3,2},{7,6},{11,3},{15,7},{10... | collective-permute-start | bytes 688136 | tf_op jit(solution)/shard_map/ppermute | solution.py:621
  50.1 6.0 %first.3.two = f32[256,256]{1,0:T(8,128)S(1)} custom-call(bf16[288,256]{1,0:T(8,128)(2,1)S(1)} %outer_weights.1.packed, bf16[256,432]{1,0:T(8,128)(2,1)S(1)} %get-tuple-element.73.w_back, bf16[4,256,4096]{2,1,0:T(8,128)(2,1)S(1)} %get-tuple-element.81.fcol, bf16[4,3,16,4096]{3,2,1,0:T(8,128)(2,1)S(1)} %get-tuple-element.82.g2z), custom_call_target="tpu_custom_call" | custom-call | flops 3800000000 | bytes 4194304 | tf_op jit(solution)/shard_map/first/pallas_call | solution.py:593
  56.1 0.0 collective-permute-done.11
  56.1 0.1 split.1
  56.2 0.1 collective-permute-start.12
  56.3 0.5 collective-permute-start.21
  56.8 0.1 collective-permute-start.18
  56.9 0.0 collective-permute-start.22
  56.9 0.5 collective-permute-start.23
  57.4 0.6 collective-permute-done.12.got
  58.0 1.3 %collective-permute-start.19 = (bf16[448,256]{1,0:T(8,128)(2,1)S(1)}, bf16[448,256]{1,0:T(8,128)(2,1)S(1)}, u32[]{:S(2)}, u32[]{:S(2)}) collective-permute-start(bf16[448,256]{1,0:T(8,128)(2,1)S(1)} %collective-permute-done.11), channel_id=1, source_target_pairs={{0,8},{4,12},{1,0},{5,4},{2,1},{6,5},{3,2},{7,6},{11,3},{15,7},{10... | collective-permute-start | bytes 688136 | tf_op jit(solution)/shard_map/ppermute | solution.py:621
  59.3 0.1 merge.1
  59.4 1.3 %collective-permute-start.13 = (bf16[256,256]{1,0:T(8,128)(2,1)S(1)}, bf16[256,256]{1,0:T(8,128)(2,1)S(1)}, u32[]{:S(2)}, u32[]{:S(2)}) collective-permute-start(bf16[256,256]{1,0:T(8,128)(2,1)S(1)} %get-tuple-element.88.mine), channel_id=1, source_target_pairs={{0,8},{1,9},{2,10},{3,11},{4,12},{5,13},{6,14},{7,15},{8,0},{9,1},... | collective-permute-start | bytes 393224 | tf_op jit(solution)/shard_map/ppermute | solution.py:485
  60.7 4.5 %collective-permute-done.18 = bf16[448,256]{1,0:T(8,128)(2,1)S(1)} collective-permute-done((bf16[448,256]{1,0:T(8,128)(2,1)S(1)}, bf16[448,256]{1,0:T(8,128)(2,1)S(1)}, u32[]{:S(2)}, u32[]{:S(2)}) %collective-permute-start.18) | collective-permute-done | bytes 229408 | tf_op jit(solution)/shard_map/ppermute | solution.py:621
  65.2 0.0 collective-permute-start.20
  65.3 2.8 %collective-permute-done.13.got = bf16[256,256]{1,0:T(8,128)(2,1)S(1)} collective-permute-done((bf16[256,256]{1,0:T(8,128)(2,1)S(1)}, bf16[256,256]{1,0:T(8,128)(2,1)S(1)}, u32[]{:S(2)}, u32[]{:S(2)}) %collective-permute-start.13) | collective-permute-done | bytes 131104 | tf_op jit(solution)/shard_map/ppermute | solution.py:485
  68.1 0.0 collective-permute-start.24
  68.1 0.1 collective-permute-start.14
  68.2 0.0 collective-permute-done.23
  68.2 2.1 %collective-permute-start.15 = (bf16[160,256]{1,0:T(8,128)(2,1)S(1)}, bf16[160,256]{1,0:T(8,128)(2,1)S(1)}, u32[]{:S(2)}, u32[]{:S(2)}) collective-permute-start(bf16[160,256]{1,0:T(8,128)(2,1)S(1)} %get-tuple-element.92), channel_id=1, source_target_pairs={{0,2},{1,3},{2,0},{3,1},{4,6},{5,7},{6,4},{7,5},{8,10},{9,11},{10,... | collective-permute-start | bytes 245768 | tf_op jit(solution)/shard_map/ppermute | solution.py:485
  70.3 2.3 %collective-permute-start.16 = (bf16[160,256]{1,0:T(8,128)(2,1)S(1)}, bf16[160,256]{1,0:T(8,128)(2,1)S(1)}, u32[]{:S(2)}, u32[]{:S(2)}) collective-permute-start(bf16[160,256]{1,0:T(8,128)(2,1)S(1)} %get-tuple-element.93), channel_id=1, source_target_pairs={{0,3},{1,2},{2,1},{3,0},{4,7},{5,6},{6,5},{7,4},{8,11},{9,10},{10,... | collective-permute-start | bytes 245768 | tf_op jit(solution)/shard_map/ppermute | solution.py:485
  72.6 1.6 %collective-permute-done.14.one = bf16[160,256]{1,0:T(8,128)(2,1)S(1)} collective-permute-done((bf16[160,256]{1,0:T(8,128)(2,1)S(1)}, bf16[160,256]{1,0:T(8,128)(2,1)S(1)}, u32[]{:S(2)}, u32[]{:S(2)}) %collective-permute-start.14) | collective-permute-done | bytes 81952 | tf_op jit(solution)/shard_map/ppermute | solution.py:485
  74.2 0.0 collective-permute-start.26
  74.2 3.8 %collective-permute-done.15.two = bf16[160,256]{1,0:T(8,128)(2,1)S(1)} collective-permute-done((bf16[160,256]{1,0:T(8,128)(2,1)S(1)}, bf16[160,256]{1,0:T(8,128)(2,1)S(1)}, u32[]{:S(2)}, u32[]{:S(2)}) %collective-permute-start.15) | collective-permute-done | bytes 81952 | tf_op jit(solution)/shard_map/ppermute | solution.py:485
  78.0 0.0 collective-permute-start.27
  78.0 0.0 collective-permute-done.16.three
  78.0 0.5 collective-permute-start.28
  78.5 0.1 collective-permute-start.17
  78.6 1.3 %step.1 = f32[1,5,2,4,128]{4,3,2,1,0:T(4,128)} custom-call(s32[2]{0:T(128)S(1)} %and_add_fusion.place, f32[8,1024]{1,0:T(8,128)S(1)} %get-tuple-element.77.own, f32[32,256]{1,0:T(8,128)S(1)} %get-tuple-element.94.closure, bf16[4,16,1024]{2,1,0:T(8,128)(2,1)S(1)} %pad_maximum_fusion.refs_0_, bf16[4,16,1024]{2,1,0:T(8,128)(2,1)S(1)} %collective-permute-done.5.refs_1_, ...), custom_call_target="tpu_custom_call" | custom-call | tf_op jit(solution)/shard_map/step/pallas_call | solution.py:699
  79.9 0.0 collective-permute-done.25
  79.9 0.0 collective-permute-done.26
  79.9 0.0 collective-permute-done.27
  79.9 0.0 collective-permute-done.28
  79.9 0.1 collective-permute-done.17.other
  80.0 5.2 %finish.1 = (f32[27,256,256]{2,1,0:T(8,128)}, f32[9,27,256]{2,1,0:T(8,128)}, f32[5,256]{1,0:T(8,128)}) custom-call(s32[16]{0:T(128)S(1)} %fusion.3.place, s32[1]{0:T(128)} %bitcast.10.core, f32[128,256]{1,0:T(8,128)S(1)} %get-tuple-element.96.own, f32[128,256]{1,0:T(8,128)S(1)} %collective-permute-done.17.other, bf16[1,448,256]{2,1,0:T(8,128)(2,1)S(1)} %bitcast.29, ...), custom_call_target="tpu_custom_call" | custom-call | tf_op jit(solution)/shard_map/finish/pallas_call | solution.py:709
  (20 shorter events, 0.2 us)
Async XLA Ops:
  3.6 4.1 %collective-permute-start = (f32[4,1024]{1,0:T(4,128)}, f32[4,1024]{1,0:T(4,128)S(1)}, u32[]{:S(2)}, u32[]{:S(2)}) collective-permute-start(f32[4,1024]{1,0:T(4,128)} %get-tuple-element.54), channel_id=1, source_target_pairs={{0,4},{4,8},{8,12},{12,0},{1,5},{5,9},{9,13},{13,1},{2,6},{6,10},{... | collective-permute-start | bytes 49160 | tf_op jit(solution)/shard_map/ppermute | solution.py:506
  4.1 3.7 %collective-permute-start.1 = (f32[4,1024]{1,0:T(4,128)}, f32[4,1024]{1,0:T(4,128)S(1)}, u32[]{:S(2)}, u32[]{:S(2)}) collective-permute-start(f32[4,1024]{1,0:T(4,128)} %get-tuple-element.55), channel_id=1, source_target_pairs={{4,0},{8,4},{12,8},{0,12},{5,1},{9,5},{13,9},{1,13},{6,2},{10,6},{... | collective-permute-start | bytes 49160 | tf_op jit(solution)/shard_map/ppermute | solution.py:507
  6.1 0.8 copy-start.1
  7.8 7.5 %collective-permute-start.2 = (bf16[16,1024]{1,0:T(8,128)(2,1)S(1)}, bf16[16,1024]{1,0:T(8,128)(2,1)S(1)}, u32[]{:S(2)}, u32[]{:S(2)}) collective-permute-start(bf16[16,1024]{1,0:T(8,128)(2,1)S(1)} %get-tuple-element.57), channel_id=1, source_target_pairs={{0,1},{1,0},{2,3},{3,2},{4,5},{5,4},{6,7},{7,6},{8,9},{9,8},{10,11... | collective-permute-start | bytes 98312 | tf_op jit(solution)/shard_map/ppermute | solution.py:485
  10.2 5.7 %collective-permute-start.3 = (bf16[16,1024]{1,0:T(8,128)(2,1)S(1)}, bf16[16,1024]{1,0:T(8,128)(2,1)S(1)}, u32[]{:S(2)}, u32[]{:S(2)}) collective-permute-start(bf16[16,1024]{1,0:T(8,128)(2,1)S(1)} %get-tuple-element.57), channel_id=1, source_target_pairs={{0,2},{1,3},{2,0},{3,1},{4,6},{5,7},{6,4},{7,5},{8,10},{9,11},{10,... | collective-permute-start | bytes 98312 | tf_op jit(solution)/shard_map/ppermute | solution.py:485
  12.8 6.0 %collective-permute-start.4 = (bf16[16,1024]{1,0:T(8,128)(2,1)S(1)}, bf16[16,1024]{1,0:T(8,128)(2,1)S(1)}, u32[]{:S(2)}, u32[]{:S(2)}) collective-permute-start(bf16[16,1024]{1,0:T(8,128)(2,1)S(1)} %get-tuple-element.57), channel_id=1, source_target_pairs={{0,3},{1,2},{2,1},{3,0},{4,7},{5,6},{6,5},{7,4},{8,11},{9,10},{10,... | collective-permute-start | bytes 98312 | tf_op jit(solution)/shard_map/ppermute | solution.py:485
  13.5 0.9 %copy-start = (bf16[27,9,256]{2,0,1:T(8,128)(2,1)S(1)}, bf16[27,9,256]{2,0,1:T(8,128)(2,1)}, u32[]{:S(2)}) copy-start(bf16[27,9,256]{2,0,1:T(8,128)(2,1)} %param.17) | copy-start | bytes 373252
  14.4 0.7 copy-start.2
  18.8 5.6 %collective-permute-start.5 = (bf16[4,16,1024]{2,1,0:T(8,128)(2,1)S(1)}, bf16[4,16,1024]{2,1,0:T(8,128)(2,1)S(1)}, u32[]{:S(2)}, u32[]{:S(2)}) collective-permute-start(bf16[4,16,1024]{2,1,0:T(8,128)(2,1)S(1)} %pad_maximum_fusion.refs_0_), channel_id=1, source_target_pairs={{0,8},{1,9},{2,10},{3,11},{4,12},{5,13},{6,14},{7,15},{8,0},{9,1},... | collective-permute-start | bytes 393224 | tf_op jit(solution)/shard_map/ppermute | solution.py:485
  20.1 4.3 %collective-permute-start.6 = (bf16[4,16,1024]{2,1,0:T(8,128)(2,1)S(1)}, bf16[4,16,1024]{2,1,0:T(8,128)(2,1)S(1)}, u32[]{:S(2)}, u32[]{:S(2)}) collective-permute-start(bf16[4,16,1024]{2,1,0:T(8,128)(2,1)S(1)} %pad_maximum_fusion.refs_0_), channel_id=1, source_target_pairs={{0,4},{1,5},{2,6},{3,7},{4,0},{5,1},{6,2},{7,3},{8,12},{9,13},{10,... | collective-permute-start | bytes 393224 | tf_op jit(solution)/shard_map/ppermute | solution.py:485
  20.1 2.0 %copy-start.3 = (bf16[27,256,256]{2,1,0:T(8,128)(2,1)S(1)}, bf16[27,256,256]{2,1,0:T(8,128)(2,1)}, u32[]{:S(2)}) copy-start(bf16[27,256,256]{2,1,0:T(8,128)(2,1)} %w_mid) | copy-start | bytes 10616836
  24.4 1.3 %collective-permute-start.7 = (bf16[4,16,1024]{2,1,0:T(8,128)(2,1)S(1)}, bf16[4,16,1024]{2,1,0:T(8,128)(2,1)S(1)}, u32[]{:S(2)}, u32[]{:S(2)}) collective-permute-start(bf16[4,16,1024]{2,1,0:T(8,128)(2,1)S(1)} %collective-permute-done.5.refs_1_), channel_id=1, source_target_pairs={{0,4},{1,5},{2,6},{3,7},{4,0},{5,1},{6,2},{7,3},{8,12},{9,13},{10,... | collective-permute-start | bytes 393224 | tf_op jit(solution)/shard_map/ppermute | solution.py:485
  39.8 8.1 %collective-permute-start.8 = (bf16[448,256]{1,0:T(8,128)(2,1)S(1)}, bf16[448,256]{1,0:T(8,128)(2,1)S(1)}, u32[]{:S(2)}, u32[]{:S(2)}) collective-permute-start(bf16[448,256]{1,0:T(8,128)(2,1)S(1)} %get-tuple-element.72), channel_id=1, source_target_pairs={{0,1},{4,5},{1,2},{5,6},{2,3},{6,7},{3,11},{7,15},{11,10},{15,14},... | collective-permute-start | bytes 688136 | tf_op jit(solution)/shard_map/ppermute | solution.py:621
  39.9 8.1 %collective-permute-start.9 = (bf16[448,256]{1,0:T(8,128)(2,1)S(1)}, bf16[448,256]{1,0:T(8,128)(2,1)S(1)}, u32[]{:S(2)}, u32[]{:S(2)}) collective-permute-start(bf16[448,256]{1,0:T(8,128)(2,1)S(1)} %get-tuple-element.72), channel_id=1, source_target_pairs={{0,8},{4,12},{1,0},{5,4},{2,1},{6,5},{3,2},{7,6},{11,3},{15,7},{10... | collective-permute-start | bytes 688136 | tf_op jit(solution)/shard_map/ppermute | solution.py:621
  48.0 8.1 %collective-permute-start.10 = (bf16[448,256]{1,0:T(8,128)(2,1)S(1)}, bf16[448,256]{1,0:T(8,128)(2,1)S(1)}, u32[]{:S(2)}, u32[]{:S(2)}) collective-permute-start(bf16[448,256]{1,0:T(8,128)(2,1)S(1)} %collective-permute-done.8), channel_id=1, source_target_pairs={{0,1},{4,5},{1,2},{5,6},{2,3},{6,7},{3,11},{7,15},{11,10},{15,14},... | collective-permute-start | bytes 688136 | tf_op jit(solution)/shard_map/ppermute | solution.py:621
  48.1 8.0 %collective-permute-start.11 = (bf16[448,256]{1,0:T(8,128)(2,1)S(1)}, bf16[448,256]{1,0:T(8,128)(2,1)S(1)}, u32[]{:S(2)}, u32[]{:S(2)}) collective-permute-start(bf16[448,256]{1,0:T(8,128)(2,1)S(1)} %collective-permute-done.9), channel_id=1, source_target_pairs={{0,8},{4,12},{1,0},{5,4},{2,1},{6,5},{3,2},{7,6},{11,3},{15,7},{10... | collective-permute-start | bytes 688136 | tf_op jit(solution)/shard_map/ppermute | solution.py:621
  56.2 1.8 %collective-permute-start.12 = (f32[384,256]{1,0:T(8,128)S(1)}, f32[384,256]{1,0:T(8,128)S(1)}, u32[]{:S(2)}, u32[]{:S(2)}) collective-permute-start(f32[384,256]{1,0:T(8,128)S(1)} %get-tuple-element.85), channel_id=1, source_target_pairs={{0,4},{1,5},{2,6},{3,7},{4,0},{5,1},{6,2},{7,3},{8,12},{9,13},{10,... | collective-permute-start | bytes 1179656 | tf_op jit(solution)/shard_map/ppermute | solution.py:485
  56.3 3.1 %collective-permute-start.21 = (bf16[448,256]{1,0:T(8,128)(2,1)S(1)}, bf16[448,256]{1,0:T(8,128)(2,1)S(1)}, u32[]{:S(2)}, u32[]{:S(2)}) collective-permute-start(bf16[448,256]{1,0:T(8,128)(2,1)S(1)} %get-tuple-element.72), channel_id=1, source_target_pairs={{0,4},{1,5},{2,6},{3,7},{4,0},{5,1},{6,2},{7,3},{8,12},{9,13},{10,... | collective-permute-start | bytes 688136 | tf_op jit(solution)/shard_map/ppermute | solution.py:485
  56.8 8.5 %collective-permute-start.18 = (bf16[448,256]{1,0:T(8,128)(2,1)S(1)}, bf16[448,256]{1,0:T(8,128)(2,1)S(1)}, u32[]{:S(2)}, u32[]{:S(2)}) collective-permute-start(bf16[448,256]{1,0:T(8,128)(2,1)S(1)} %collective-permute-done.10), channel_id=1, source_target_pairs={{0,1},{4,5},{1,2},{5,6},{2,3},{6,7},{3,11},{7,15},{11,10},{15,14},... | collective-permute-start | bytes 688136 | tf_op jit(solution)/shard_map/ppermute | solution.py:621
  56.9 11.2 %collective-permute-start.22 = (bf16[448,256]{1,0:T(8,128)(2,1)S(1)}, bf16[448,256]{1,0:T(8,128)(2,1)S(1)}, u32[]{:S(2)}, u32[]{:S(2)}) collective-permute-start(bf16[448,256]{1,0:T(8,128)(2,1)S(1)} %collective-permute-done.8), channel_id=1, source_target_pairs={{0,4},{1,5},{2,6},{3,7},{4,0},{5,1},{6,2},{7,3},{8,12},{9,13},{10,... | collective-permute-start | bytes 688136 | tf_op jit(solution)/shard_map/ppermute | solution.py:485
  56.9 11.3 %collective-permute-start.23 = (bf16[448,256]{1,0:T(8,128)(2,1)S(1)}, bf16[448,256]{1,0:T(8,128)(2,1)S(1)}, u32[]{:S(2)}, u32[]{:S(2)}) collective-permute-start(bf16[448,256]{1,0:T(8,128)(2,1)S(1)} %collective-permute-done.9), channel_id=1, source_target_pairs={{0,4},{1,5},{2,6},{3,7},{4,0},{5,1},{6,2},{7,3},{8,12},{9,13},{10,... | collective-permute-start | bytes 688136 | tf_op jit(solution)/shard_map/ppermute | solution.py:485
  58.0 12.3 %collective-permute-start.19 = (bf16[448,256]{1,0:T(8,128)(2,1)S(1)}, bf16[448,256]{1,0:T(8,128)(2,1)S(1)}, u32[]{:S(2)}, u32[]{:S(2)}) collective-permute-start(bf16[448,256]{1,0:T(8,128)(2,1)S(1)} %collective-permute-done.11), channel_id=1, source_target_pairs={{0,8},{4,12},{1,0},{5,4},{2,1},{6,5},{3,2},{7,6},{11,3},{15,7},{10... | collective-permute-start | bytes 688136 | tf_op jit(solution)/shard_map/ppermute | solution.py:621
  59.4 8.7 %collective-permute-start.13 = (bf16[256,256]{1,0:T(8,128)(2,1)S(1)}, bf16[256,256]{1,0:T(8,128)(2,1)S(1)}, u32[]{:S(2)}, u32[]{:S(2)}) collective-permute-start(bf16[256,256]{1,0:T(8,128)(2,1)S(1)} %get-tuple-element.88.mine), channel_id=1, source_target_pairs={{0,8},{1,9},{2,10},{3,11},{4,12},{5,13},{6,14},{7,15},{8,0},{9,1},... | collective-permute-start | bytes 393224 | tf_op jit(solution)/shard_map/ppermute | solution.py:485
  65.2 7.3 %collective-permute-start.20 = (bf16[448,256]{1,0:T(8,128)(2,1)S(1)}, bf16[448,256]{1,0:T(8,128)(2,1)S(1)}, u32[]{:S(2)}, u32[]{:S(2)}) collective-permute-start(bf16[448,256]{1,0:T(8,128)(2,1)S(1)} %collective-permute-done.18), channel_id=1, source_target_pairs={{0,1},{4,5},{1,2},{5,6},{2,3},{6,7},{3,11},{7,15},{11,10},{15,14},... | collective-permute-start | bytes 688136 | tf_op jit(solution)/shard_map/ppermute | solution.py:621
  68.1 10.5 %collective-permute-start.24 = (bf16[448,256]{1,0:T(8,128)(2,1)S(1)}, bf16[448,256]{1,0:T(8,128)(2,1)S(1)}, u32[]{:S(2)}, u32[]{:S(2)}) collective-permute-start(bf16[448,256]{1,0:T(8,128)(2,1)S(1)} %collective-permute-done.10), channel_id=1, source_target_pairs={{0,4},{1,5},{2,6},{3,7},{4,0},{5,1},{6,2},{7,3},{8,12},{9,13},{10,... | collective-permute-start | bytes 688136 | tf_op jit(solution)/shard_map/ppermute | solution.py:485
  68.1 6.1 %collective-permute-start.14 = (bf16[160,256]{1,0:T(8,128)(2,1)S(1)}, bf16[160,256]{1,0:T(8,128)(2,1)S(1)}, u32[]{:S(2)}, u32[]{:S(2)}) collective-permute-start(bf16[160,256]{1,0:T(8,128)(2,1)S(1)} %get-tuple-element.90.mine), channel_id=1, source_target_pairs={{0,1},{1,0},{2,3},{3,2},{4,5},{5,4},{6,7},{7,6},{8,9},{9,8},{10,11... | collective-permute-start | bytes 245768 | tf_op jit(solution)/shard_map/ppermute | solution.py:485
  68.2 9.8 %collective-permute-start.15 = (bf16[160,256]{1,0:T(8,128)(2,1)S(1)}, bf16[160,256]{1,0:T(8,128)(2,1)S(1)}, u32[]{:S(2)}, u32[]{:S(2)}) collective-permute-start(bf16[160,256]{1,0:T(8,128)(2,1)S(1)} %get-tuple-element.92), channel_id=1, source_target_pairs={{0,2},{1,3},{2,0},{3,1},{4,6},{5,7},{6,4},{7,5},{8,10},{9,11},{10,... | collective-permute-start | bytes 245768 | tf_op jit(solution)/shard_map/ppermute | solution.py:485
  70.3 7.7 %collective-permute-start.16 = (bf16[160,256]{1,0:T(8,128)(2,1)S(1)}, bf16[160,256]{1,0:T(8,128)(2,1)S(1)}, u32[]{:S(2)}, u32[]{:S(2)}) collective-permute-start(bf16[160,256]{1,0:T(8,128)(2,1)S(1)} %get-tuple-element.93), channel_id=1, source_target_pairs={{0,3},{1,2},{2,1},{3,0},{4,7},{5,6},{6,5},{7,4},{8,11},{9,10},{10,... | collective-permute-start | bytes 245768 | tf_op jit(solution)/shard_map/ppermute | solution.py:485
  72.6 7.3 %collective-permute-start.25 = (bf16[448,256]{1,0:T(8,128)(2,1)S(1)}, bf16[448,256]{1,0:T(8,128)(2,1)S(1)}, u32[]{:S(2)}, u32[]{:S(2)}) collective-permute-start(bf16[448,256]{1,0:T(8,128)(2,1)S(1)} %collective-permute-done.11), channel_id=1, source_target_pairs={{0,4},{1,5},{2,6},{3,7},{4,0},{5,1},{6,2},{7,3},{8,12},{9,13},{10,... | collective-permute-start | bytes 688136 | tf_op jit(solution)/shard_map/ppermute | solution.py:485
  74.2 5.7 %collective-permute-start.26 = (bf16[448,256]{1,0:T(8,128)(2,1)S(1)}, bf16[448,256]{1,0:T(8,128)(2,1)S(1)}, u32[]{:S(2)}, u32[]{:S(2)}) collective-permute-start(bf16[448,256]{1,0:T(8,128)(2,1)S(1)} %collective-permute-done.18), channel_id=1, source_target_pairs={{0,4},{1,5},{2,6},{3,7},{4,0},{5,1},{6,2},{7,3},{8,12},{9,13},{10,... | collective-permute-start | bytes 688136 | tf_op jit(solution)/shard_map/ppermute | solution.py:485
  78.0 1.9 %collective-permute-start.27 = (bf16[448,256]{1,0:T(8,128)(2,1)S(1)}, bf16[448,256]{1,0:T(8,128)(2,1)S(1)}, u32[]{:S(2)}, u32[]{:S(2)}) collective-permute-start(bf16[448,256]{1,0:T(8,128)(2,1)S(1)} %collective-permute-done.19), channel_id=1, source_target_pairs={{0,4},{1,5},{2,6},{3,7},{4,0},{5,1},{6,2},{7,3},{8,12},{9,13},{10,... | collective-permute-start | bytes 688136 | tf_op jit(solution)/shard_map/ppermute | solution.py:485
  78.0 1.9 %collective-permute-start.28 = (bf16[448,256]{1,0:T(8,128)(2,1)S(1)}, bf16[448,256]{1,0:T(8,128)(2,1)S(1)}, u32[]{:S(2)}, u32[]{:S(2)}) collective-permute-start(bf16[448,256]{1,0:T(8,128)(2,1)S(1)} %collective-permute-done.20), channel_id=1, source_target_pairs={{0,4},{1,5},{2,6},{3,7},{4,0},{5,1},{6,2},{7,3},{8,12},{9,13},{10,... | collective-permute-start | bytes 688136 | tf_op jit(solution)/shard_map/ppermute | solution.py:485
  78.5 1.4 %collective-permute-start.17 = (f32[128,256]{1,0:T(8,128)S(1)}, f32[128,256]{1,0:T(8,128)S(1)}, u32[]{:S(2)}, u32[]{:S(2)}) collective-permute-start(f32[128,256]{1,0:T(8,128)S(1)} %get-tuple-element.96.own), channel_id=1, source_target_pairs={{0,4},{1,5},{2,6},{3,7},{4,0},{5,1},{6,2},{7,3},{8,12},{9,13},{10,... | collective-permute-start | bytes 393224 | tf_op jit(solution)/shard_map/ppermute | solution.py:485

commit v8 on v7

--- a/solution.py
+++ b/solution.py
@@ -155,10 +155,10 @@
     return slice(x * lanes, (x + count) * lanes)
 
 
-def plane_taps(g2z, x, planes, nz, lanes):
+def plane_taps(g2z, s, x, planes, nz, lanes):
     parts = []
     for ox, oy, oz in offsets:
-        parts.append(ahead_y(g2z[0, oz + 1, :, span((x - ox) % planes, lanes)], -oy, nz))
+        parts.append(ahead_y(g2z[s, oz + 1, :, span((x - ox) % planes, lanes)], -oy, nz))
     return jnp.concatenate(parts, 0)
 
 
@@ -221,14 +221,14 @@
         pieces += [eighth[:, n] for n in near]
         tail = jnp.where(sub == 0, ninth[:, near[0]], jnp.where(sub == 1, ninth[:, near[1]], ninth[:, near[2]]))
         pieces += [jnp.where(sub < 3, tail, 0.0), jnp.zeros((8, lanes), F32)]
-        fcol[0, :, near[1]] = jnp.concatenate(pieces, 0).astype(BF16)
+        fcol[s, :, near[1]] = jnp.concatenate(pieces, 0).astype(BF16)
 
     for x in range(planes):
         patches(x)
 
     def first(x):
         at = span(x, lanes)
-        half = dot(w_first[...], fcol[0, :, at])
+        half = dot(w_first[...], fcol[s, :, at])
         hidden[:, at] = (half * jnp.tanh(half) + half).astype(BF16)
 
     for x in range(planes):
@@ -258,16 +258,16 @@
         active = (pre * sig).astype(BF16)
         out = dot(wc, active)
         for h in range(per):
-            for k in range(2):
-                start = h * lanes + k * (lanes // 2)
-                closure[0, j * per + h, 8 * k : 8 * k + 8] = out[0:8, start : start + lanes // 2].astype(BF16)
+            left, right = h * lanes, h * lanes + lanes // 2
+            both = [out[0:8, left:right], out[0:8, right : right + lanes // 2]]
+            closure[s, j * per + h] = jnp.concatenate(both, 0).astype(BF16)
         grad = dot(wo, here) * (sig * (1.0 + pre * (1.0 - sig)))
         last[...] += dot_nt(here, active)
         rounded = grad.astype(BF16)
         grad = rounded.astype(F32)
-        g2z[0, 0, :, at] = roll_z(grad, -1, nz).astype(BF16)
-        g2z[0, 1, :, at] = rounded
-        g2z[0, 2, :, at] = roll_z(grad, 1, nz).astype(BF16)
+        g2z[s, 0, :, at] = roll_z(grad, -1, nz).astype(BF16)
+        g2z[s, 1, :, at] = rounded
+        g2z[s, 2, :, at] = roll_z(grad, 1, nz).astype(BF16)
 
     for j in range(slabs):
         gradient(j)
@@ -275,7 +275,7 @@
     @pl.when(s >= 0)
     def _():
         for x in range(0, planes, group):
-            columns = [plane_taps(g2z, x + h, planes, nz, lanes) for h in range(group)]
+            columns = [plane_taps(g2z, s, x + h, planes, nz, lanes) for h in range(group)]
             mid[...] += dot_nt(jnp.concatenate(columns, 1), hidden[:, span(x, lanes, group)])
 
     @pl.when(s == samples - 1)
@@ -295,7 +295,9 @@
         piece[taps:] = extra.astype(BF16)
 
 
-def first_kernel(nz, lanes, packed, w_back, fcol, g2z, out):
+def first_kernel(nz, lanes, lo, packed, w_back, fcol, g2z, out):
+    s = lo + pl.program_id(0)
+
     @pl.when(pl.program_id(0) == 0)
     def _():
         out[...] = jnp.zeros_like(out)
@@ -305,9 +307,9 @@
     w_first = packed.at[0 : w_back.shape[0]]
     for x in range(0, planes, group):
         at = span(x, lanes, group)
-        columns = [plane_taps(g2z, x + h, planes, nz, lanes) for h in range(group)]
+        columns = [plane_taps(g2z, s, x + h, planes, nz, lanes) for h in range(group)]
         back = dot(w_back[...], jnp.concatenate(columns, 1))
-        column = fcol[0, :, at]
+        column = fcol[s, :, at]
         half = dot(w_first[...], column)
         double = 1.0 + jnp.tanh(half)
         grad = (back * (double * (0.5 + half - 0.5 * half * double))).astype(BF16)
@@ -569,10 +571,10 @@
         ),
         in_specs=[SMEM] + [VMEM] * (2 + len(sources)),
         out_specs=(
-            whole_spec((rows + 16, hid)),
-            pl.BlockSpec((1, all_planes, 16, lanes // 2), lambda s: (s, 0, 0, 0)),
-            pl.BlockSpec((1, 3, block, team_cells), lambda s: (s, 0, 0, 0)),
-            pl.BlockSpec((1, 256, team_cells), lambda s: (s, 0, 0)),
+            VMEM,
+            VMEM,
+            VMEM,
+            VMEM,
         ),
         scratch_shapes=[
             pltpu.VMEM((size, 16, cells), BF16),
@@ -591,16 +593,11 @@
 
     def first_part(lo, count, fcol, g2z):
         return pl.pallas_call(
-            functools.partial(first_kernel, nz, lanes),
+            functools.partial(first_kernel, nz, lanes, lo),
             grid=(count,),
             out_shape=shape((256, hid), F32),
-            in_specs=[
-                whole_spec(packed.shape),
-                whole_spec((hid, rows)),
-                pl.BlockSpec((1, 256, team_cells), lambda s: (s + lo, 0, 0)),
-                pl.BlockSpec((1, 3, block, team_cells), lambda s: (s + lo, 0, 0, 0)),
-            ],
-            out_specs=whole_spec((256, hid)),
+            in_specs=[VMEM] * 4,
+            out_specs=VMEM,
             compiler_params=params(18 if all_planes <= 8 else 58),
             cost_estimate=cost(7.6e9 * count / samples),
             name="first",

time: 85.5 us -> 85.4 us (level)
  no operation moved by 1% of the time
where the time goes in v8:
time: 85.4 us; the launch traced here: 85.1 us
  Pallas kernels  37.3 us (44%)
  starting transfers between devices  21.8 us (26%)
  waiting for transfers between devices  20.1 us (24%)
  local copies, waits for them, and re-layouts  4.44 us (5%)
  between operations  0.86 us (1%)
    ppermute x20, waiting for transfers between devices, trade(): return lax.ppermute(v, team, [(d, d ^ mask) for d in range(size)])  14.7 us
    pallas_call x1, Pallas kernels, shards(): pl.pallas_call(functools.partial(closure_kernel, nz, lanes, len(sources))...  14.1 us
    ppermute x20, starting transfers between devices, trade(): return lax.ppermute(v, team, [(d, d ^ mask) for d in range(size)])  13.7 us
    pallas_call x2, Pallas kernels, first_part(): pl.pallas_call(functools.partial(first_kernel, nz, lanes, lo), grid=(coun...  12.1 us
    ppermute x7, starting transfers between devices, around(): lax.ppermute(v, team, [(device(at, c), device(at + by, c)) for at in rang...  5.54 us
    pallas_call x1, Pallas kernels, shards(): pl.pallas_call(functools.partial(finish_kernel, len(pieces), weight_count...  5.19 us
    ppermute x7, waiting for transfers between devices, around(): lax.ppermute(v, team, [(device(at, c), device(at + by, c)) for at in rang...  4.55 us
    unnamed x8, local copies, waits for them, and re-layouts  4.44 us
  transfers between devices with their start and end apart: 29, of which 12 were waited for; matrix products, arithmetic and copies ran while one was open for 1% of the time, Pallas kernels for 18%

profile of v8, /device:TPU:0, one launch (start us, length us, event | category | flops | bytes accessed | tf_op | source)
XLA Modules:
  0.0 85.1 jit_solution(2676138438864886679)
XLA Ops:
  0.6 3.0 %deposit.1 = (f32[16,1024]{1,0:T(8,128)}, f32[4,1024]{1,0:T(4,128)}, f32[4,1024]{1,0:T(4,128)}) custom-call(f32[1,1024]{1,0:T(1,128)} %mass_in.1, f32[3,1,1024]{2,1,0:T(1,128)} %bitcast.51, s32[1,1024]{1,0:T(1,128)} %cell_in.1, s32[1,256]{1,0:T(1,128)} %listed_in.1, f32[1,5,2,4,128]{4,3,2,1,0:T(4,128)} %fields_in.1, f32[1,5,2,4,128]{4,3,2,1,0:T(4,128)} %cotangent_in.1, ...), custom_call_target="tpu_custom_call" | custom-call | tf_op jit(solution)/shard_map/deposit/pallas_call | solution.py:491
  3.6 0.5 collective-permute-start
  4.1 2.0 %collective-permute-start.1 = (f32[4,1024]{1,0:T(4,128)}, f32[4,1024]{1,0:T(4,128)S(1)}, u32[]{:S(2)}, u32[]{:S(2)}) collective-permute-start(f32[4,1024]{1,0:T(4,128)} %get-tuple-element.55), channel_id=1, source_target_pairs={{4,0},{8,4},{12,8},{0,12},{5,1},{9,5},{13,9},{1,13},{6,2},{10,6},{... | collective-permute-start | bytes 49160 | tf_op jit(solution)/shard_map/ppermute | solution.py:509
  6.2 0.8 copy-done.1
  7.0 0.7 collective-permute-done.below
  7.7 0.1 collective-permute-done.1.above
  7.8 2.4 %collective-permute-start.2 = (bf16[16,1024]{1,0:T(8,128)(2,1)S(1)}, bf16[16,1024]{1,0:T(8,128)(2,1)S(1)}, u32[]{:S(2)}, u32[]{:S(2)}) collective-permute-start(bf16[16,1024]{1,0:T(8,128)(2,1)S(1)} %get-tuple-element.57), channel_id=1, source_target_pairs={{0,1},{1,0},{2,3},{3,2},{4,5},{5,4},{6,7},{7,6},{8,9},{9,8},{10,11... | collective-permute-start | bytes 98312 | tf_op jit(solution)/shard_map/ppermute | solution.py:487
  10.2 2.6 %collective-permute-start.3 = (bf16[16,1024]{1,0:T(8,128)(2,1)S(1)}, bf16[16,1024]{1,0:T(8,128)(2,1)S(1)}, u32[]{:S(2)}, u32[]{:S(2)}) collective-permute-start(bf16[16,1024]{1,0:T(8,128)(2,1)S(1)} %get-tuple-element.57), channel_id=1, source_target_pairs={{0,2},{1,3},{2,0},{3,1},{4,6},{5,7},{6,4},{7,5},{8,10},{9,11},{10,... | collective-permute-start | bytes 98312 | tf_op jit(solution)/shard_map/ppermute | solution.py:487
  12.8 0.0 collective-permute-start.4
  12.8 0.7 and_add_fusion.place
  13.5 0.9 %copy-done = bf16[27,9,256]{2,0,1:T(8,128)(2,1)S(1)} copy-done((bf16[27,9,256]{2,0,1:T(8,128)(2,1)S(1)}, bf16[27,9,256]{2,0,1:T(8,128)(2,1)}, u32[]{:S(2)}) %copy-start) | copy-done | bytes 124440
  14.4 0.7 copy-done.2
  15.1 0.3 outer_weights.1.packed
  15.4 0.0 collective-permute-done.2
  15.4 0.5 collective-permute-done.3
  15.9 2.9 %collective-permute-done.4 = bf16[16,1024]{1,0:T(8,128)(2,1)S(1)} collective-permute-done((bf16[16,1024]{1,0:T(8,128)(2,1)S(1)}, bf16[16,1024]{1,0:T(8,128)(2,1)S(1)}, u32[]{:S(2)}, u32[]{:S(2)}) %collective-permute-start.4) | collective-permute-done | bytes 32800 | tf_op jit(solution)/shard_map/ppermute | solution.py:487
  18.8 1.3 %collective-permute-start.5 = (bf16[4,16,1024]{2,1,0:T(8,128)(2,1)S(1)}, bf16[4,16,1024]{2,1,0:T(8,128)(2,1)S(1)}, u32[]{:S(2)}, u32[]{:S(2)}) collective-permute-start(bf16[4,16,1024]{2,1,0:T(8,128)(2,1)S(1)} %pad_maximum_fusion.refs_0_), channel_id=1, source_target_pairs={{0,8},{1,9},{2,10},{3,11},{4,12},{5,13},{6,14},{7,15},{8,0},{9,1},... | collective-permute-start | bytes 393224 | tf_op jit(solution)/shard_map/ppermute | solution.py:487
  20.1 0.0 collective-permute-start.6
  20.1 2.0 %copy-done.3 = bf16[27,256,256]{2,1,0:T(8,128)(2,1)S(1)} copy-done((bf16[27,256,256]{2,1,0:T(8,128)(2,1)S(1)}, bf16[27,256,256]{2,1,0:T(8,128)(2,1)}, u32[]{:S(2)}) %copy-start.3) | copy-done | bytes 3538968
  22.1 1.2 %middle_weights.1 = (bf16[432,256]{1,0:T(8,128)(2,1)S(1)}, bf16[256,432]{1,0:T(8,128)(2,1)S(1)}) custom-call(s32[1]{0:T(128)} %bitcast.8.me, bf16[27,256,256]{2,1,0:T(8,128)(2,1)S(1)} %copy-done.3), custom_call_target="tpu_custom_call" | custom-call | flops 1500000000 | bytes 4194304 | tf_op jit(solution)/shard_map/middle_weights/pallas_call | solution.py:547
  23.3 1.1 %collective-permute-done.5.refs_1_ = bf16[4,16,1024]{2,1,0:T(8,128)(2,1)S(1)} collective-permute-done((bf16[4,16,1024]{2,1,0:T(8,128)(2,1)S(1)}, bf16[4,16,1024]{2,1,0:T(8,128)(2,1)S(1)}, u32[]{:S(2)}, u32[]{:S(2)}) %collective-permute-start.5) | collective-permute-done | bytes 131104 | tf_op jit(solution)/shard_map/ppermute | solution.py:487
  24.4 0.0 collective-permute-start.7
  24.4 0.0 collective-permute-done.6.refs_2_
  24.4 1.3 %collective-permute-done.7.refs_3_ = bf16[4,16,1024]{2,1,0:T(8,128)(2,1)S(1)} collective-permute-done((bf16[4,16,1024]{2,1,0:T(8,128)(2,1)S(1)}, bf16[4,16,1024]{2,1,0:T(8,128)(2,1)S(1)}, u32[]{:S(2)}, u32[]{:S(2)}) %collective-permute-start.7) | collective-permute-done | bytes 131104 | tf_op jit(solution)/shard_map/ppermute | solution.py:487
  25.7 14.1 %closure.1 = (bf16[448,256]{1,0:T(8,128)(2,1)S(1)}, bf16[4,8,16,256]{3,2,1,0:T(8,128)(2,1)S(1)}, bf16[4,3,16,4096]{3,2,1,0:T(8,128)(2,1)S(1)}, bf16[4,256,4096]{2,1,0:T(8,128)(2,1)S(1)}) custom-call(s32[4]{0:T(128)S(1)} %add_multiply_fusion.place, bf16[432,256]{1,0:T(8,128)(2,1)S(1)} %get-tuple-element.69.wt, bf16[288,256]{1,0:T(8,128)(2,1)S(1)} %outer_weights.1.packed, ...), custom_call_target="tpu_custom_call" | custom-call | flops 8999999488 | bytes 4194304 | tf_op jit(solution)/shard_map/closure/pallas_call | solution.py:563
  39.8 0.1 collective-permute-start.8
  39.9 2.0 %collective-permute-start.9 = (bf16[448,256]{1,0:T(8,128)(2,1)S(1)}, bf16[448,256]{1,0:T(8,128)(2,1)S(1)}, u32[]{:S(2)}, u32[]{:S(2)}) collective-permute-start(bf16[448,256]{1,0:T(8,128)(2,1)S(1)} %get-tuple-element.72), channel_id=1, source_target_pairs={{0,8},{4,12},{1,0},{5,4},{2,1},{6,5},{3,2},{7,6},{11,3},{15,7},{10... | collective-permute-start | bytes 688136 | tf_op jit(solution)/shard_map/ppermute | solution.py:618
  41.9 6.0 %first.2.one = f32[256,256]{1,0:T(8,128)S(1)} custom-call(bf16[288,256]{1,0:T(8,128)(2,1)S(1)} %outer_weights.1.packed, bf16[256,432]{1,0:T(8,128)(2,1)S(1)} %get-tuple-element.73.w_back, bf16[4,256,4096]{2,1,0:T(8,128)(2,1)S(1)} %get-tuple-element.81.fcol, bf16[4,3,16,4096]{3,2,1,0:T(8,128)(2,1)S(1)} %get-tuple-element.82.g2z), custom_call_target="tpu_custom_call" | custom-call | flops 3800000000 | bytes 4194304 | tf_op jit(solution)/shard_map/first/pallas_call | solution.py:595
  47.9 0.0 collective-permute-done.8
  47.9 0.0 collective-permute-done.9
  47.9 0.1 collective-permute-start.10
  48.1 2.0 %collective-permute-start.11 = (bf16[448,256]{1,0:T(8,128)(2,1)S(1)}, bf16[448,256]{1,0:T(8,128)(2,1)S(1)}, u32[]{:S(2)}, u32[]{:S(2)}) collective-permute-start(bf16[448,256]{1,0:T(8,128)(2,1)S(1)} %collective-permute-done.9), channel_id=1, source_target_pairs={{0,8},{4,12},{1,0},{5,4},{2,1},{6,5},{3,2},{7,6},{11,3},{15,7},{10... | collective-permute-start | bytes 688136 | tf_op jit(solution)/shard_map/ppermute | solution.py:618
  50.0 6.0 %first.3.two = f32[256,256]{1,0:T(8,128)S(1)} custom-call(bf16[288,256]{1,0:T(8,128)(2,1)S(1)} %outer_weights.1.packed, bf16[256,432]{1,0:T(8,128)(2,1)S(1)} %get-tuple-element.73.w_back, bf16[4,256,4096]{2,1,0:T(8,128)(2,1)S(1)} %get-tuple-element.81.fcol, bf16[4,3,16,4096]{3,2,1,0:T(8,128)(2,1)S(1)} %get-tuple-element.82.g2z), custom_call_target="tpu_custom_call" | custom-call | flops 3800000000 | bytes 4194304 | tf_op jit(solution)/shard_map/first/pallas_call | solution.py:595
  56.1 0.0 collective-permute-done.10
  56.1 0.1 split.1
  56.2 0.1 collective-permute-start.12
  56.2 0.5 collective-permute-start.21
  56.7 0.1 collective-permute-start.18
  56.8 0.0 collective-permute-start.22
  56.8 0.5 collective-permute-start.23
  57.3 0.6 collective-permute-done.12.got
  58.0 1.3 %collective-permute-start.19 = (bf16[448,256]{1,0:T(8,128)(2,1)S(1)}, bf16[448,256]{1,0:T(8,128)(2,1)S(1)}, u32[]{:S(2)}, u32[]{:S(2)}) collective-permute-start(bf16[448,256]{1,0:T(8,128)(2,1)S(1)} %collective-permute-done.11), channel_id=1, source_target_pairs={{0,8},{4,12},{1,0},{5,4},{2,1},{6,5},{3,2},{7,6},{11,3},{15,7},{10... | collective-permute-start | bytes 688136 | tf_op jit(solution)/shard_map/ppermute | solution.py:618
  59.3 0.1 merge.1
  59.3 0.0 collective-permute-done.21
  59.3 1.3 %collective-permute-start.13 = (bf16[256,256]{1,0:T(8,128)(2,1)S(1)}, bf16[256,256]{1,0:T(8,128)(2,1)S(1)}, u32[]{:S(2)}, u32[]{:S(2)}) collective-permute-start(bf16[256,256]{1,0:T(8,128)(2,1)S(1)} %get-tuple-element.88.mine), channel_id=1, source_target_pairs={{0,8},{1,9},{2,10},{3,11},{4,12},{5,13},{6,14},{7,15},{8,0},{9,1},... | collective-permute-start | bytes 393224 | tf_op jit(solution)/shard_map/ppermute | solution.py:487
  60.7 4.5 %collective-permute-done.18 = bf16[448,256]{1,0:T(8,128)(2,1)S(1)} collective-permute-done((bf16[448,256]{1,0:T(8,128)(2,1)S(1)}, bf16[448,256]{1,0:T(8,128)(2,1)S(1)}, u32[]{:S(2)}, u32[]{:S(2)}) %collective-permute-start.18) | collective-permute-done | bytes 229408 | tf_op jit(solution)/shard_map/ppermute | solution.py:618
  65.2 0.0 collective-permute-start.20
  65.2 2.8 %collective-permute-done.13.got = bf16[256,256]{1,0:T(8,128)(2,1)S(1)} collective-permute-done((bf16[256,256]{1,0:T(8,128)(2,1)S(1)}, bf16[256,256]{1,0:T(8,128)(2,1)S(1)}, u32[]{:S(2)}, u32[]{:S(2)}) %collective-permute-start.13) | collective-permute-done | bytes 131104 | tf_op jit(solution)/shard_map/ppermute | solution.py:487
  68.0 0.0 collective-permute-done.22
  68.1 0.1 collective-permute-start.14
  68.1 2.1 %collective-permute-start.15 = (bf16[160,256]{1,0:T(8,128)(2,1)S(1)}, bf16[160,256]{1,0:T(8,128)(2,1)S(1)}, u32[]{:S(2)}, u32[]{:S(2)}) collective-permute-start(bf16[160,256]{1,0:T(8,128)(2,1)S(1)} %get-tuple-element.92), channel_id=1, source_target_pairs={{0,2},{1,3},{2,0},{3,1},{4,6},{5,7},{6,4},{7,5},{8,10},{9,11},{10,... | collective-permute-start | bytes 245768 | tf_op jit(solution)/shard_map/ppermute | solution.py:487
  70.2 2.3 %collective-permute-start.16 = (bf16[160,256]{1,0:T(8,128)(2,1)S(1)}, bf16[160,256]{1,0:T(8,128)(2,1)S(1)}, u32[]{:S(2)}, u32[]{:S(2)}) collective-permute-start(bf16[160,256]{1,0:T(8,128)(2,1)S(1)} %get-tuple-element.93), channel_id=1, source_target_pairs={{0,3},{1,2},{2,1},{3,0},{4,7},{5,6},{6,5},{7,4},{8,11},{9,10},{10,... | collective-permute-start | bytes 245768 | tf_op jit(solution)/shard_map/ppermute | solution.py:487
  72.5 0.0 collective-permute-done.20
  72.5 0.0 collective-permute-start.25
  72.5 1.6 %collective-permute-done.14.one = bf16[160,256]{1,0:T(8,128)(2,1)S(1)} collective-permute-done((bf16[160,256]{1,0:T(8,128)(2,1)S(1)}, bf16[160,256]{1,0:T(8,128)(2,1)S(1)}, u32[]{:S(2)}, u32[]{:S(2)}) %collective-permute-start.14) | collective-permute-done | bytes 81952 | tf_op jit(solution)/shard_map/ppermute | solution.py:487
  74.1 0.0 collective-permute-start.26
  74.1 3.8 %collective-permute-done.15.two = bf16[160,256]{1,0:T(8,128)(2,1)S(1)} collective-permute-done((bf16[160,256]{1,0:T(8,128)(2,1)S(1)}, bf16[160,256]{1,0:T(8,128)(2,1)S(1)}, u32[]{:S(2)}, u32[]{:S(2)}) %collective-permute-start.15) | collective-permute-done | bytes 81952 | tf_op jit(solution)/shard_map/ppermute | solution.py:487
  77.9 0.5 collective-permute-start.28
  78.5 0.0 collective-permute-done.24
  78.5 0.1 collective-permute-start.17
  78.6 1.3 %step.1 = f32[1,5,2,4,128]{4,3,2,1,0:T(4,128)} custom-call(s32[2]{0:T(128)S(1)} %and_add_fusion.place, f32[8,1024]{1,0:T(8,128)S(1)} %get-tuple-element.77.own, f32[32,256]{1,0:T(8,128)S(1)} %get-tuple-element.94.closure, bf16[4,16,1024]{2,1,0:T(8,128)(2,1)S(1)} %pad_maximum_fusion.refs_0_, bf16[4,16,1024]{2,1,0:T(8,128)(2,1)S(1)} %collective-permute-done.5.refs_1_, ...), custom_call_target="tpu_custom_call" | custom-call | tf_op jit(solution)/shard_map/step/pallas_call | solution.py:696
  79.8 0.0 collective-permute-done.27
  79.8 0.1 collective-permute-done.17.other
  79.9 5.2 %finish.1 = (f32[27,256,256]{2,1,0:T(8,128)}, f32[9,27,256]{2,1,0:T(8,128)}, f32[5,256]{1,0:T(8,128)}) custom-call(s32[16]{0:T(128)S(1)} %fusion.3.place, s32[1]{0:T(128)} %bitcast.10.core, f32[128,256]{1,0:T(8,128)S(1)} %get-tuple-element.96.own, f32[128,256]{1,0:T(8,128)S(1)} %collective-permute-done.17.other, bf16[1,448,256]{2,1,0:T(8,128)(2,1)S(1)} %bitcast.29, ...), custom_call_target="tpu_custom_call" | custom-call | tf_op jit(solution)/shard_map/finish/pallas_call | solution.py:706
  (20 shorter events, 0.2 us)
Async XLA Ops:
  3.6 4.1 %collective-permute-start = (f32[4,1024]{1,0:T(4,128)}, f32[4,1024]{1,0:T(4,128)S(1)}, u32[]{:S(2)}, u32[]{:S(2)}) collective-permute-start(f32[4,1024]{1,0:T(4,128)} %get-tuple-element.54), channel_id=1, source_target_pairs={{0,4},{4,8},{8,12},{12,0},{1,5},{5,9},{9,13},{13,1},{2,6},{6,10},{... | collective-permute-start | bytes 49160 | tf_op jit(solution)/shard_map/ppermute | solution.py:508
  4.1 3.7 %collective-permute-start.1 = (f32[4,1024]{1,0:T(4,128)}, f32[4,1024]{1,0:T(4,128)S(1)}, u32[]{:S(2)}, u32[]{:S(2)}) collective-permute-start(f32[4,1024]{1,0:T(4,128)} %get-tuple-element.55), channel_id=1, source_target_pairs={{4,0},{8,4},{12,8},{0,12},{5,1},{9,5},{13,9},{1,13},{6,2},{10,6},{... | collective-permute-start | bytes 49160 | tf_op jit(solution)/shard_map/ppermute | solution.py:509
  6.1 0.8 copy-start.1
  7.8 7.5 %collective-permute-start.2 = (bf16[16,1024]{1,0:T(8,128)(2,1)S(1)}, bf16[16,1024]{1,0:T(8,128)(2,1)S(1)}, u32[]{:S(2)}, u32[]{:S(2)}) collective-permute-start(bf16[16,1024]{1,0:T(8,128)(2,1)S(1)} %get-tuple-element.57), channel_id=1, source_target_pairs={{0,1},{1,0},{2,3},{3,2},{4,5},{5,4},{6,7},{7,6},{8,9},{9,8},{10,11... | collective-permute-start | bytes 98312 | tf_op jit(solution)/shard_map/ppermute | solution.py:487
  10.2 5.7 %collective-permute-start.3 = (bf16[16,1024]{1,0:T(8,128)(2,1)S(1)}, bf16[16,1024]{1,0:T(8,128)(2,1)S(1)}, u32[]{:S(2)}, u32[]{:S(2)}) collective-permute-start(bf16[16,1024]{1,0:T(8,128)(2,1)S(1)} %get-tuple-element.57), channel_id=1, source_target_pairs={{0,2},{1,3},{2,0},{3,1},{4,6},{5,7},{6,4},{7,5},{8,10},{9,11},{10,... | collective-permute-start | bytes 98312 | tf_op jit(solution)/shard_map/ppermute | solution.py:487
  12.8 6.0 %collective-permute-start.4 = (bf16[16,1024]{1,0:T(8,128)(2,1)S(1)}, bf16[16,1024]{1,0:T(8,128)(2,1)S(1)}, u32[]{:S(2)}, u32[]{:S(2)}) collective-permute-start(bf16[16,1024]{1,0:T(8,128)(2,1)S(1)} %get-tuple-element.57), channel_id=1, source_target_pairs={{0,3},{1,2},{2,1},{3,0},{4,7},{5,6},{6,5},{7,4},{8,11},{9,10},{10,... | collective-permute-start | bytes 98312 | tf_op jit(solution)/shard_map/ppermute | solution.py:487
  13.5 0.9 %copy-start = (bf16[27,9,256]{2,0,1:T(8,128)(2,1)S(1)}, bf16[27,9,256]{2,0,1:T(8,128)(2,1)}, u32[]{:S(2)}) copy-start(bf16[27,9,256]{2,0,1:T(8,128)(2,1)} %param.17) | copy-start | bytes 373252
  14.4 0.7 copy-start.2
  18.8 5.6 %collective-permute-start.5 = (bf16[4,16,1024]{2,1,0:T(8,128)(2,1)S(1)}, bf16[4,16,1024]{2,1,0:T(8,128)(2,1)S(1)}, u32[]{:S(2)}, u32[]{:S(2)}) collective-permute-start(bf16[4,16,1024]{2,1,0:T(8,128)(2,1)S(1)} %pad_maximum_fusion.refs_0_), channel_id=1, source_target_pairs={{0,8},{1,9},{2,10},{3,11},{4,12},{5,13},{6,14},{7,15},{8,0},{9,1},... | collective-permute-start | bytes 393224 | tf_op jit(solution)/shard_map/ppermute | solution.py:487
  20.1 4.3 %collective-permute-start.6 = (bf16[4,16,1024]{2,1,0:T(8,128)(2,1)S(1)}, bf16[4,16,1024]{2,1,0:T(8,128)(2,1)S(1)}, u32[]{:S(2)}, u32[]{:S(2)}) collective-permute-start(bf16[4,16,1024]{2,1,0:T(8,128)(2,1)S(1)} %pad_maximum_fusion.refs_0_), channel_id=1, source_target_pairs={{0,4},{1,5},{2,6},{3,7},{4,0},{5,1},{6,2},{7,3},{8,12},{9,13},{10,... | collective-permute-start | bytes 393224 | tf_op jit(solution)/shard_map/ppermute | solution.py:487
  20.1 2.0 %copy-start.3 = (bf16[27,256,256]{2,1,0:T(8,128)(2,1)S(1)}, bf16[27,256,256]{2,1,0:T(8,128)(2,1)}, u32[]{:S(2)}) copy-start(bf16[27,256,256]{2,1,0:T(8,128)(2,1)} %w_mid) | copy-start | bytes 10616836
  24.4 1.3 %collective-permute-start.7 = (bf16[4,16,1024]{2,1,0:T(8,128)(2,1)S(1)}, bf16[4,16,1024]{2,1,0:T(8,128)(2,1)S(1)}, u32[]{:S(2)}, u32[]{:S(2)}) collective-permute-start(bf16[4,16,1024]{2,1,0:T(8,128)(2,1)S(1)} %collective-permute-done.5.refs_1_), channel_id=1, source_target_pairs={{0,4},{1,5},{2,6},{3,7},{4,0},{5,1},{6,2},{7,3},{8,12},{9,13},{10,... | collective-permute-start | bytes 393224 | tf_op jit(solution)/shard_map/ppermute | solution.py:487
  39.8 8.1 %collective-permute-start.8 = (bf16[448,256]{1,0:T(8,128)(2,1)S(1)}, bf16[448,256]{1,0:T(8,128)(2,1)S(1)}, u32[]{:S(2)}, u32[]{:S(2)}) collective-permute-start(bf16[448,256]{1,0:T(8,128)(2,1)S(1)} %get-tuple-element.72), channel_id=1, source_target_pairs={{0,1},{4,5},{1,2},{5,6},{2,3},{6,7},{3,11},{7,15},{11,10},{15,14},... | collective-permute-start | bytes 688136 | tf_op jit(solution)/shard_map/ppermute | solution.py:618
  39.9 8.1 %collective-permute-start.9 = (bf16[448,256]{1,0:T(8,128)(2,1)S(1)}, bf16[448,256]{1,0:T(8,128)(2,1)S(1)}, u32[]{:S(2)}, u32[]{:S(2)}) collective-permute-start(bf16[448,256]{1,0:T(8,128)(2,1)S(1)} %get-tuple-element.72), channel_id=1, source_target_pairs={{0,8},{4,12},{1,0},{5,4},{2,1},{6,5},{3,2},{7,6},{11,3},{15,7},{10... | collective-permute-start | bytes 688136 | tf_op jit(solution)/shard_map/ppermute | solution.py:618
  47.9 8.1 %collective-permute-start.10 = (bf16[448,256]{1,0:T(8,128)(2,1)S(1)}, bf16[448,256]{1,0:T(8,128)(2,1)S(1)}, u32[]{:S(2)}, u32[]{:S(2)}) collective-permute-start(bf16[448,256]{1,0:T(8,128)(2,1)S(1)} %collective-permute-done.8), channel_id=1, source_target_pairs={{0,1},{4,5},{1,2},{5,6},{2,3},{6,7},{3,11},{7,15},{11,10},{15,14},... | collective-permute-start | bytes 688136 | tf_op jit(solution)/shard_map/ppermute | solution.py:618
  48.1 8.0 %collective-permute-start.11 = (bf16[448,256]{1,0:T(8,128)(2,1)S(1)}, bf16[448,256]{1,0:T(8,128)(2,1)S(1)}, u32[]{:S(2)}, u32[]{:S(2)}) collective-permute-start(bf16[448,256]{1,0:T(8,128)(2,1)S(1)} %collective-permute-done.9), channel_id=1, source_target_pairs={{0,8},{4,12},{1,0},{5,4},{2,1},{6,5},{3,2},{7,6},{11,3},{15,7},{10... | collective-permute-start | bytes 688136 | tf_op jit(solution)/shard_map/ppermute | solution.py:618
  56.2 1.8 %collective-permute-start.12 = (f32[384,256]{1,0:T(8,128)S(1)}, f32[384,256]{1,0:T(8,128)S(1)}, u32[]{:S(2)}, u32[]{:S(2)}) collective-permute-start(f32[384,256]{1,0:T(8,128)S(1)} %get-tuple-element.85), channel_id=1, source_target_pairs={{0,4},{1,5},{2,6},{3,7},{4,0},{5,1},{6,2},{7,3},{8,12},{9,13},{10,... | collective-permute-start | bytes 1179656 | tf_op jit(solution)/shard_map/ppermute | solution.py:487
  56.2 3.1 %collective-permute-start.21 = (bf16[448,256]{1,0:T(8,128)(2,1)S(1)}, bf16[448,256]{1,0:T(8,128)(2,1)S(1)}, u32[]{:S(2)}, u32[]{:S(2)}) collective-permute-start(bf16[448,256]{1,0:T(8,128)(2,1)S(1)} %get-tuple-element.72), channel_id=1, source_target_pairs={{0,4},{1,5},{2,6},{3,7},{4,0},{5,1},{6,2},{7,3},{8,12},{9,13},{10,... | collective-permute-start | bytes 688136 | tf_op jit(solution)/shard_map/ppermute | solution.py:487
  56.7 8.5 %collective-permute-start.18 = (bf16[448,256]{1,0:T(8,128)(2,1)S(1)}, bf16[448,256]{1,0:T(8,128)(2,1)S(1)}, u32[]{:S(2)}, u32[]{:S(2)}) collective-permute-start(bf16[448,256]{1,0:T(8,128)(2,1)S(1)} %collective-permute-done.10), channel_id=1, source_target_pairs={{0,1},{4,5},{1,2},{5,6},{2,3},{6,7},{3,11},{7,15},{11,10},{15,14},... | collective-permute-start | bytes 688136 | tf_op jit(solution)/shard_map/ppermute | solution.py:618
  56.8 11.2 %collective-permute-start.22 = (bf16[448,256]{1,0:T(8,128)(2,1)S(1)}, bf16[448,256]{1,0:T(8,128)(2,1)S(1)}, u32[]{:S(2)}, u32[]{:S(2)}) collective-permute-start(bf16[448,256]{1,0:T(8,128)(2,1)S(1)} %collective-permute-done.8), channel_id=1, source_target_pairs={{0,4},{1,5},{2,6},{3,7},{4,0},{5,1},{6,2},{7,3},{8,12},{9,13},{10,... | collective-permute-start | bytes 688136 | tf_op jit(solution)/shard_map/ppermute | solution.py:487
  56.8 11.3 %collective-permute-start.23 = (bf16[448,256]{1,0:T(8,128)(2,1)S(1)}, bf16[448,256]{1,0:T(8,128)(2,1)S(1)}, u32[]{:S(2)}, u32[]{:S(2)}) collective-permute-start(bf16[448,256]{1,0:T(8,128)(2,1)S(1)} %collective-permute-done.9), channel_id=1, source_target_pairs={{0,4},{1,5},{2,6},{3,7},{4,0},{5,1},{6,2},{7,3},{8,12},{9,13},{10,... | collective-permute-start | bytes 688136 | tf_op jit(solution)/shard_map/ppermute | solution.py:487
  58.0 12.3 %collective-permute-start.19 = (bf16[448,256]{1,0:T(8,128)(2,1)S(1)}, bf16[448,256]{1,0:T(8,128)(2,1)S(1)}, u32[]{:S(2)}, u32[]{:S(2)}) collective-permute-start(bf16[448,256]{1,0:T(8,128)(2,1)S(1)} %collective-permute-done.11), channel_id=1, source_target_pairs={{0,8},{4,12},{1,0},{5,4},{2,1},{6,5},{3,2},{7,6},{11,3},{15,7},{10... | collective-permute-start | bytes 688136 | tf_op jit(solution)/shard_map/ppermute | solution.py:618
  59.3 8.7 %collective-permute-start.13 = (bf16[256,256]{1,0:T(8,128)(2,1)S(1)}, bf16[256,256]{1,0:T(8,128)(2,1)S(1)}, u32[]{:S(2)}, u32[]{:S(2)}) collective-permute-start(bf16[256,256]{1,0:T(8,128)(2,1)S(1)} %get-tuple-element.88.mine), channel_id=1, source_target_pairs={{0,8},{1,9},{2,10},{3,11},{4,12},{5,13},{6,14},{7,15},{8,0},{9,1},... | collective-permute-start | bytes 393224 | tf_op jit(solution)/shard_map/ppermute | solution.py:487
  65.2 7.3 %collective-permute-start.20 = (bf16[448,256]{1,0:T(8,128)(2,1)S(1)}, bf16[448,256]{1,0:T(8,128)(2,1)S(1)}, u32[]{:S(2)}, u32[]{:S(2)}) collective-permute-start(bf16[448,256]{1,0:T(8,128)(2,1)S(1)} %collective-permute-done.18), channel_id=1, source_target_pairs={{0,1},{4,5},{1,2},{5,6},{2,3},{6,7},{3,11},{7,15},{11,10},{15,14},... | collective-permute-start | bytes 688136 | tf_op jit(solution)/shard_map/ppermute | solution.py:618
  68.0 10.5 %collective-permute-start.24 = (bf16[448,256]{1,0:T(8,128)(2,1)S(1)}, bf16[448,256]{1,0:T(8,128)(2,1)S(1)}, u32[]{:S(2)}, u32[]{:S(2)}) collective-permute-start(bf16[448,256]{1,0:T(8,128)(2,1)S(1)} %collective-permute-done.10), channel_id=1, source_target_pairs={{0,4},{1,5},{2,6},{3,7},{4,0},{5,1},{6,2},{7,3},{8,12},{9,13},{10,... | collective-permute-start | bytes 688136 | tf_op jit(solution)/shard_map/ppermute | solution.py:487
  68.1 6.1 %collective-permute-start.14 = (bf16[160,256]{1,0:T(8,128)(2,1)S(1)}, bf16[160,256]{1,0:T(8,128)(2,1)S(1)}, u32[]{:S(2)}, u32[]{:S(2)}) collective-permute-start(bf16[160,256]{1,0:T(8,128)(2,1)S(1)} %get-tuple-element.90.mine), channel_id=1, source_target_pairs={{0,1},{1,0},{2,3},{3,2},{4,5},{5,4},{6,7},{7,6},{8,9},{9,8},{10,11... | collective-permute-start | bytes 245768 | tf_op jit(solution)/shard_map/ppermute | solution.py:487
  68.1 9.8 %collective-permute-start.15 = (bf16[160,256]{1,0:T(8,128)(2,1)S(1)}, bf16[160,256]{1,0:T(8,128)(2,1)S(1)}, u32[]{:S(2)}, u32[]{:S(2)}) collective-permute-start(bf16[160,256]{1,0:T(8,128)(2,1)S(1)} %get-tuple-element.92), channel_id=1, source_target_pairs={{0,2},{1,3},{2,0},{3,1},{4,6},{5,7},{6,4},{7,5},{8,10},{9,11},{10,... | collective-permute-start | bytes 245768 | tf_op jit(solution)/shard_map/ppermute | solution.py:487
  70.2 7.7 %collective-permute-start.16 = (bf16[160,256]{1,0:T(8,128)(2,1)S(1)}, bf16[160,256]{1,0:T(8,128)(2,1)S(1)}, u32[]{:S(2)}, u32[]{:S(2)}) collective-permute-start(bf16[160,256]{1,0:T(8,128)(2,1)S(1)} %get-tuple-element.93), channel_id=1, source_target_pairs={{0,3},{1,2},{2,1},{3,0},{4,7},{5,6},{6,5},{7,4},{8,11},{9,10},{10,... | collective-permute-start | bytes 245768 | tf_op jit(solution)/shard_map/ppermute | solution.py:487
  72.5 7.3 %collective-permute-start.25 = (bf16[448,256]{1,0:T(8,128)(2,1)S(1)}, bf16[448,256]{1,0:T(8,128)(2,1)S(1)}, u32[]{:S(2)}, u32[]{:S(2)}) collective-permute-start(bf16[448,256]{1,0:T(8,128)(2,1)S(1)} %collective-permute-done.11), channel_id=1, source_target_pairs={{0,4},{1,5},{2,6},{3,7},{4,0},{5,1},{6,2},{7,3},{8,12},{9,13},{10,... | collective-permute-start | bytes 688136 | tf_op jit(solution)/shard_map/ppermute | solution.py:487
  74.1 5.7 %collective-permute-start.26 = (bf16[448,256]{1,0:T(8,128)(2,1)S(1)}, bf16[448,256]{1,0:T(8,128)(2,1)S(1)}, u32[]{:S(2)}, u32[]{:S(2)}) collective-permute-start(bf16[448,256]{1,0:T(8,128)(2,1)S(1)} %collective-permute-done.18), channel_id=1, source_target_pairs={{0,4},{1,5},{2,6},{3,7},{4,0},{5,1},{6,2},{7,3},{8,12},{9,13},{10,... | collective-permute-start | bytes 688136 | tf_op jit(solution)/shard_map/ppermute | solution.py:487
  77.9 1.9 %collective-permute-start.27 = (bf16[448,256]{1,0:T(8,128)(2,1)S(1)}, bf16[448,256]{1,0:T(8,128)(2,1)S(1)}, u32[]{:S(2)}, u32[]{:S(2)}) collective-permute-start(bf16[448,256]{1,0:T(8,128)(2,1)S(1)} %collective-permute-done.19), channel_id=1, source_target_pairs={{0,4},{1,5},{2,6},{3,7},{4,0},{5,1},{6,2},{7,3},{8,12},{9,13},{10,... | collective-permute-start | bytes 688136 | tf_op jit(solution)/shard_map/ppermute | solution.py:487
  77.9 1.9 %collective-permute-start.28 = (bf16[448,256]{1,0:T(8,128)(2,1)S(1)}, bf16[448,256]{1,0:T(8,128)(2,1)S(1)}, u32[]{:S(2)}, u32[]{:S(2)}) collective-permute-start(bf16[448,256]{1,0:T(8,128)(2,1)S(1)} %collective-permute-done.20), channel_id=1, source_target_pairs={{0,4},{1,5},{2,6},{3,7},{4,0},{5,1},{6,2},{7,3},{8,12},{9,13},{10,... | collective-permute-start | bytes 688136 | tf_op jit(solution)/shard_map/ppermute | solution.py:487
  78.5 1.4 %collective-permute-start.17 = (f32[128,256]{1,0:T(8,128)S(1)}, f32[128,256]{1,0:T(8,128)S(1)}, u32[]{:S(2)}, u32[]{:S(2)}) collective-permute-start(f32[128,256]{1,0:T(8,128)S(1)} %get-tuple-element.96.own), channel_id=1, source_target_pairs={{0,4},{1,5},{2,6},{3,7},{4,0},{5,1},{6,2},{7,3},{8,12},{9,13},{10,... | collective-permute-start | bytes 393224 | tf_op jit(solution)/shard_map/ppermute | solution.py:487
